TPU v7x, 32 devices: a whole 2x2x4 slice. The times are simulated.
32 devices in a mesh: groups: 2 (over y), hash: 16 (over z, x, core).
Axes of the slice: x: 2, y: 2, z: 4, core: 2. Of those that a mesh axis runs over, the one named last changes fastest.
Arguments:
- passages: bfloat16 [16384, 4096], P(('groups', 'hash')), parts along dimension 0, may hold values from -100 to 100
- queries: bfloat16 [32, 4096], P(('groups', 'hash')), parts along dimension 0, may hold values from -100 to 100
- gain: float32 [4096], replicated, may hold values from 0.5 to 1.5
- candidates: int32 [32, 128], P(('groups', 'hash')), parts along dimension 0, may hold values from 0 to 8191, as said below
- teacher: int32 [32, 128], P(('groups', 'hash')), parts along dimension 0, may hold values from 0 to 40
Outputs:
- d_passages: float32 [16384, 4096], P(('groups', 'hash')), parts along dimension 0
- d_queries: float32 [32, 4096], P(('groups', 'hash')), parts along dimension 0
- d_gain: float32 [8192], P('groups'), parts along dimension 0
There are 2 independent parts, one for each index of `groups`. A program takes and returns all parts, laid end to end along the dimension named above; an argument that names none is the same for every part. Nothing has to cross between parts.
Inputs may be any that keep to these rules, and one draw needn't show every extreme that they name: `candidates`: each query's 128 candidate ids are distinct, and exactly 8 of them lie in each hash index's block of 512 consecutive ids (owner = id // 512).
All inputs are finite; a program needn't handle non-finite values.
Results may differ from a plain program's by a relative error of at most 0.0095.
Values may be sent and summed in bfloat16 or wider, within the bound.
No kernel may reach another device: no remote copies, remote signals or barrier semaphores. Data moves between devices by JAX's collectives and lax.ppermute only.
A program may use at most 64 MiB of HBM per device.

v0:
```python
import jax
import jax.numpy as jnp
from jax import lax
from jax.sharding import PartitionSpec as P

score_scale = 20.0
loss_scale = 8192.0
teacher_div = 2.0


def local(passages, queries, gain, candidates, teacher):
    hashes = lax.axis_size("hash")
    p_rows, width = passages.shape
    q_rows, listed = candidates.shape
    per_owner = listed // hashes
    passage_f = passages.astype(jnp.float32)
    lifted = passage_f * gain[None, :]
    p_norm = jnp.sqrt(jnp.sum(lifted * lifted, axis=-1, keepdims=True))
    p_unit = lifted / p_norm
    table = p_unit.astype(jnp.bfloat16)
    query_f = queries.astype(jnp.float32)
    q_norm = jnp.sqrt(jnp.sum(query_f * query_f, axis=-1, keepdims=True))
    q_unit = query_f / q_norm
    q_send = q_unit.astype(jnp.bfloat16)
    owners = candidates // p_rows
    order = jnp.argsort(owners, axis=1, stable=True)
    sorted_ids = jnp.take_along_axis(candidates, order, axis=1)
    sorted_marks = jnp.take_along_axis(teacher, order, axis=1)
    local_rows = (sorted_ids % p_rows).reshape(q_rows, hashes, per_owner)
    local_rows = local_rows.transpose(1, 0, 2).reshape(hashes, q_rows * per_owner)
    wanted = lax.all_to_all(local_rows, "hash", split_axis=0, concat_axis=0, tiled=True)
    picked = table[wanted]
    fetched = lax.all_to_all(picked, "hash", split_axis=0, concat_axis=0, tiled=True)
    fetched = fetched.reshape(hashes, q_rows, per_owner, width)
    scores = (
        jnp.einsum("oqkd,qd->qok", fetched, q_send, preferred_element_type=jnp.float32)
        * score_scale
    )
    scores = scores.reshape(q_rows, listed)
    weights = jnp.exp(scores)
    student = weights / jnp.sum(weights, axis=-1, keepdims=True)
    t_weights = jnp.exp(sorted_marks.astype(jnp.float32) / teacher_div)
    teach = t_weights / jnp.sum(t_weights, axis=-1, keepdims=True)
    coef = loss_scale * score_scale * (student - teach)
    coef_three = coef.reshape(q_rows, hashes, per_owner)
    d_unit = jnp.einsum("qok,oqkd->qd", coef_three, fetched, preferred_element_type=jnp.float32)
    d_queries = (d_unit - q_unit * jnp.sum(q_unit * d_unit, axis=-1, keepdims=True)) / q_norm
    routed = coef_three.transpose(1, 0, 2)
    coef_in = lax.all_to_all(
        routed.reshape(hashes, q_rows * per_owner), "hash", split_axis=0, concat_axis=0, tiled=True
    )
    gathered = lax.all_gather(q_send, "hash", axis=0, tiled=True)
    row_ids = jnp.arange(p_rows, dtype=jnp.int32)
    matches = wanted[None, :, :] == row_ids[:, None, None]
    mixing = jnp.sum(jnp.where(matches, coef_in[None, :, :], 0.0), axis=-1)
    d_table = jnp.dot(
        mixing,
        gathered.astype(jnp.float32),
        precision=lax.Precision.HIGHEST,
        preferred_element_type=jnp.float32,
    )
    d_lifted = (d_table - p_unit * jnp.sum(p_unit * d_table, axis=-1, keepdims=True)) / p_norm
    d_passages = d_lifted * gain[None, :]
    d_gain = lax.psum(jnp.sum(d_lifted * passage_f, axis=0), "hash")
    return (d_passages, d_queries, d_gain)


def solution(mesh):
    in_specs = (
        P(("groups", "hash"), None),
        P(("groups", "hash"), None),
        P(),
        P(("groups", "hash"), None),
        P(("groups", "hash"), None),
    )
    out_specs = (P(("groups", "hash"), None), P(("groups", "hash"), None), P("groups"))
    return jax.shard_map(local, mesh=mesh, in_specs=in_specs, out_specs=out_specs, check_vma=False)
```

profile of v0, /device:TPU:0, one launch (start us, length us, event | category | flops | bytes accessed | tf_op | source)
XLA Modules:
  0.0 181.2 jit_solution(1312593632649263647)
XLA Ops:
  7.2 0.0 copy-start
  7.2 0.0 sort.19.cloned.1.call-start
  7.2 1.2 and_select_fusion.1
  8.4 0.5 iota.11
  8.9 0.0 sort.19.cloned.1.call-update
  8.9 3.4 %fusion.2 = f32[512]{0:T(512)S(1)} fusion(bf16[512,4096]{1,0:T(8,128)(2,1)} %param.7, f32[4096]{0:T(1024)} %param.9), kind=kLoop, calls=%fused_computation.7 | loop fusion | flops 8388096 | bytes 4212736 | tf_op jit(solution)/shard_map/reduce_sum | solution.py:18
  12.3 0.8 sort.19.cloned.1.call-done
  13.1 0.7 fusion.18
  13.8 1.6 gather_fusion.1
  15.4 0.7 fusion.12
  16.1 0.7 all_to_all.17
  16.8 7.4 %all-to-all-start = ((s32[16,1,8]{2,1,0:T(1,128)}), s32[16,1,8]{2,1,0:T(1,128)S(1)}, u32[]{:S(2)}, u32[]{:S(2)}) async-start(s32[16,1,8]{2,1,0:T(1,128)} %bitcast.3), calls=%async_computation | async-start | bytes 16384 | tf_op jit(solution)/shard_map/all_to_all | solution.py:31
  24.1 0.0 copy-start.3
  24.1 0.0 copy-start.4
  24.1 5.9 %fusion.20 = bf16[512,4096]{1,0:T(8,128)(2,1)} fusion(f32[512]{0:T(512)S(1)} %sqrt.12, f32[4096]{0:T(1024)} %param.9, bf16[512,4096]{1,0:T(8,128)(2,1)} %param.7), kind=kLoop, calls=%fused_computation.52 | loop fusion | flops 8388608 | bytes 8407040 | tf_op jit(solution)/shard_map/convert_element_type | solution.py:20
  30.0 0.4 all-to-all-done
  30.4 0.1 copy.31
  30.5 0.1 copy.32
  30.6 0.1 reshape.153
  30.7 5.9 %gather_fusion = bf16[128,4096]{1,0:T(8,128)(2,1)} fusion(bf16[512,4096]{1,0:T(8,128)(2,1)} %fusion.20, s32[1024]{0:T(1024)S(1)} %pad_clamp_fusion), kind=kCustom, calls=%fused_computation.2 | custom fusion | bytes 2097664 | tf_op jit(solution)/shard_map/gather | solution.py:32
  36.6 5.6 %all-to-all-start.1 = ((bf16[16,8,4096]{2,1,0:T(8,128)(2,1)}), bf16[16,8,4096]{2,1,0:T(8,128)(2,1)S(1)}, u32[]{:S(2)}, u32[]{:S(2)}) async-start(bf16[16,8,4096]{2,1,0:T(8,128)(2,1)} %bitcast.6), calls=%async_computation.1 | async-start | bytes 2097152 | tf_op jit(solution)/shard_map/all_to_all | solution.py:33
  42.2 0.0 copy-done.3
  42.2 0.6 multiply_reduce_fusion.2
  43.6 33.1 %all-gather = bf16[16,1,4096]{2,1,0:T(2,128)(2,1)S(1)} all-gather(bf16[1,1,4096]{2,1,0:T(2,128)(2,1)S(1)} %get-tuple-element.8), channel_id=1, replica_groups=mesh['groups'=2,'hash'=16] {'hash'}, dimensions={0}, use_global_device_ids=true | all-gather | bytes 139264 | tf_op jit(solution)/shard_map/all_gather | solution.py:52
  76.7 0.0 copy-done
  76.7 1.2 gather_fusion.2
  78.0 0.0 copy-done.4
  78.0 0.6 fusion.19
  78.6 0.0 all-to-all-done.1
  78.6 2.4 %fusion.7 = f32[1,16,8]{2,0,1:T(1,128)S(1)} fusion(bf16[16,8,4096]{2,1,0:T(8,128)(2,1)S(1)} %all-to-all-done.1, f32[1,4096]{1,0:T(1,128)S(1)} %get-tuple-element.9), kind=kOutput, calls=%fused_computation.18 | convolution fusion | flops 1052672 | bytes 1065472 | tf_op jit(solution)/shard_map/oqkd,qd->qok/dot_general | solution.py:36
  81.0 0.6 fusion.11
  81.6 0.7 fusion.10
  82.3 0.1 div.83
  82.4 0.5 broadcast.90
  82.9 1.3 fusion.21
  84.2 0.1 reshape.176
  84.3 0.7 all_to_all.21
  85.0 5.7 %all-to-all-start.2 = ((f32[16,1,8]{2,1,0:T(1,128)}), f32[16,1,8]{2,1,0:T(1,128)S(1)}, u32[]{:S(2)}, u32[]{:S(2)}) async-start(f32[16,1,8]{2,1,0:T(1,128)} %bitcast.12), calls=%async_computation.2 | async-start | bytes 16384 | tf_op jit(solution)/shard_map/all_to_all | solution.py:49
  90.6 0.9 multiply_reduce_fusion.1
  91.6 1.3 subtract_divide_fusion.1
  92.8 4.1 %all-to-all-done.2 = f32[16,1,8]{2,1,0:T(1,128)S(1)} async-done(((f32[16,1,8]{2,1,0:T(1,128)}), f32[16,1,8]{2,1,0:T(1,128)S(1)}, u32[]{:S(2)}, u32[]{:S(2)}) %all-to-all-start.2) | async-done | bytes 544 | tf_op jit(solution)/shard_map/all_to_all | solution.py:49
  97.0 0.2 select_reduce_fusion
  97.1 0.0 copy-start.1
  97.2 6.6 %multiply_reduce_fusion = (f32[512]{0:T(512)S(1)}, f32[512,4096]{1,0:T(8,128)S(1)}) fusion(f32[512]{0:T(512)S(1)} %sqrt.12, f32[4096]{0:T(1024)S(1)} %copy-done.2, bf16[512,4096]{1,0:T(8,128)(2,1)} %param.7, f32[512,16]{0,1:T(8,128)S(1)} %select_reduce_fusion, bf16[16,1,4096]{2,1,0:T(2,128)(2,1)S(1)} %all-gather), kind=kOutput, calls=%fused_computation.10 | convolution fusion | flops 413138432 | bytes 12767232 | tf_op jit(solution)/shard_map/dot_general | solution.py:56
  103.7 0.0 copy-done.1
  103.8 4.8 %fusion.3 = (f32[4096]{0:T(1024)S(1)}, f32[512,4096]{1,0:T(8,128)}) fusion(bf16[512,4096]{1,0:T(8,128)(2,1)S(1)} %copy-done.1, f32[512,4096]{1,0:T(8,128)S(1)} %get-tuple-element.13, f32[512]{0:T(512)S(1)} %get-tuple-element.12, f32[512]{0:T(512)S(1)} %sqrt.12, f32[4096]{0:T(1024)S(1)} %copy-done.2), kind=kLoop, calls=%fused_computation.8 | loop fusion | flops 16773120 | bytes 21008384 | tf_op jit(solution)/shard_map/reduce_sum | solution.py:64
  108.6 57.7 %psum.7 = f32[4096]{0:T(1024)} all-reduce(f32[4096]{0:T(1024)S(1)} %get-tuple-element.6), channel_id=1, replica_groups=mesh['groups'=2,'hash'=16] {'hash'}, use_global_device_ids=true, to_apply=%region_9.11 | all-reduce | flops 4096 | bytes 32768 | tf_op jit(solution)/shard_map/psum | solution.py:64
  166.3 8.1 %broadcast_multiply_fusion = f32[512,4096]{1,0:T(8,128)} fusion(f32[512,4096]{1,0:T(8,128)} %get-tuple-element.7, f32[4096]{0:T(1024)S(1)} %copy-done.2), kind=kLoop, calls=%fused_computation.12 | loop fusion | flops 2097152 | bytes 16793600 | tf_op jit(solution)/shard_map/mul | solution.py:63
  (7 shorter events, 0.1 us)
Async XLA Ops:
  7.2 69.6 %copy-start = (s32[1,128]{1,0:T(1,128)S(1)}, s32[1,128]{1,0:T(1,128)}, u32[]{:S(2)}) copy-start(s32[1,128]{1,0:T(1,128)} %param.11) | copy-start | bytes 1540
  7.2 5.9 %sort.19.cloned.1.call-start = ((), (), s32[]{:S(2)}) async-start(), calls=%async_computation.3 | async-start | bytes 3104 | tf_op jit(solution)/shard_map/jit(argsort)/sort | solution.py:26
  16.8 13.7 %all-to-all-start = ((s32[16,1,8]{2,1,0:T(1,128)}), s32[16,1,8]{2,1,0:T(1,128)S(1)}, u32[]{:S(2)}, u32[]{:S(2)}) async-start(s32[16,1,8]{2,1,0:T(1,128)} %bitcast.3), calls=%async_computation | async-start | bytes 16384 | tf_op jit(solution)/shard_map/all_to_all | solution.py:31
  24.1 18.1 %copy-start.3 = (bf16[1,4096]{1,0:T(2,128)(2,1)S(1)}, bf16[1,4096]{1,0:T(2,128)(2,1)}, u32[]{:S(2)}) copy-start(bf16[1,4096]{1,0:T(2,128)(2,1)} %param.8) | copy-start | bytes 24580
  24.1 53.8 %copy-start.4 = (s32[1,128]{1,0:T(1,128)S(1)}, s32[1,128]{1,0:T(1,128)}, u32[]{:S(2)}) copy-start(s32[1,128]{1,0:T(1,128)} %get-tuple-element.5) | copy-start | bytes 1540
  30.0 67.1 %copy-start.2 = (f32[4096]{0:T(1024)S(1)}, f32[4096]{0:T(1024)}, u32[]{:S(2)}) copy-start(f32[4096]{0:T(1024)} %param.9) | copy-start | bytes 49156
  36.6 42.0 %all-to-all-start.1 = ((bf16[16,8,4096]{2,1,0:T(8,128)(2,1)}), bf16[16,8,4096]{2,1,0:T(8,128)(2,1)S(1)}, u32[]{:S(2)}, u32[]{:S(2)}) async-start(bf16[16,8,4096]{2,1,0:T(8,128)(2,1)} %bitcast.6), calls=%async_computation.1 | async-start | bytes 2097152 | tf_op jit(solution)/shard_map/all_to_all | solution.py:33
  85.0 12.0 %all-to-all-start.2 = ((f32[16,1,8]{2,1,0:T(1,128)}), f32[16,1,8]{2,1,0:T(1,128)S(1)}, u32[]{:S(2)}, u32[]{:S(2)}) async-start(f32[16,1,8]{2,1,0:T(1,128)} %bitcast.12), calls=%async_computation.2 | async-start | bytes 16384 | tf_op jit(solution)/shard_map/all_to_all | solution.py:49
  97.1 6.6 %copy-start.1 = (bf16[512,4096]{1,0:T(8,128)(2,1)S(1)}, bf16[512,4096]{1,0:T(8,128)(2,1)}, u32[]{:S(2)}) copy-start(bf16[512,4096]{1,0:T(8,128)(2,1)} %param.7) | copy-start | bytes 12582916
Sparse Core Ops, SparseCore 0:
  10.8 2.0 sort.21.cloned.1.call-done
  (1 shorter events, 0.0 us)
where the time goes:
time: 182 us; the launch traced here: 181 us
  blocking collectives  90.9 us (50%)
  other arithmetic  30 us (16%)
  starting transfers between devices  18.6 us (10%)
  between operations  14.9 us (8%)
  local copies, waits for them, and re-layouts  12.4 us (7%)
  matrix products  9.91 us (5%)
  waiting for transfers between devices  4.53 us (2%)
    psum x1, blocking collectives, local(): d_gain = lax.psum(jnp.sum(d_lifted * passage_f, axis=0), 'hash')  57.7 us
    all_gather x1, blocking collectives, local(): gathered = lax.all_gather(q_send, 'hash', axis=0, tiled=True)  33.1 us
    mul x1, other arithmetic, local(): d_passages = d_lifted * gain[None, :]  8.09 us
    all_to_all x1, starting transfers between devices, local(): lax.all_to_all(local_rows, 'hash', split_axis=0, concat_axis=0, tiled=True)  7.36 us
    dot_general x1, matrix products, local(): jnp.dot(mixing, gathered.astype(jnp.float32), precision=lax.Precision.HIG...  6.58 us
    gather x1, local copies, waits for them, and re-layouts, local(): picked = table[wanted]  5.93 us
    convert_element_type x1, other arithmetic, local(): table = p_unit.astype(jnp.bfloat16)  5.9 us
    all_to_all x1, starting transfers between devices, local(): lax.all_to_all(routed.reshape(hashes, q_rows * per_owner), 'hash', split_...  5.66 us
  transfers between devices with their start and end apart: 3, of which 2 were waited for; matrix products, arithmetic and copies ran while one was open for 6% of the time, Pallas kernels for 0%

commit v1 on v0

v1 whole, which is shorter than its diff:
```python
import functools

import jax
import jax.numpy as jnp
from jax import lax
from jax.experimental import pallas as pl
from jax.experimental.pallas import tpu as pltpu
from jax.sharding import PartitionSpec as P

score_scale = 20.0
loss_scale = 8192.0
teacher_div = 2.0
coef_scale = loss_scale * score_scale
f32 = jnp.float32
bf16 = jnp.bfloat16
vmem = pltpu.VMEM
nt_dims = (((1,), (1,)), ((), ()))
nn_dims = (((1,), (0,)), ((), ()))


def dot(a, b, dims):
    return lax.dot_general(a, b, dims, preferred_element_type=f32)


def split(x):
    high = x.astype(bf16)
    low = (x - high.astype(f32)).astype(bf16)
    return high, low


def params(megabytes):
    return pltpu.CompilerParams(vmem_limit_bytes=megabytes * 1024 * 1024)


def whole():
    return pl.BlockSpec(memory_space=vmem)


def pack_kernel(queries_ref, candidates_ref, teacher_ref, out_ref):
    half = queries_ref.shape[1] // 2
    query = queries_ref[...].astype(f32)
    ids = candidates_ref[...]
    first = jnp.concatenate(
        [query[:, :half], (ids >> 8).astype(f32), (ids & 255).astype(f32)], axis=1
    )
    second = jnp.concatenate(
        [query[:, half:], teacher_ref[...].astype(f32), jnp.zeros(ids.shape, f32)], axis=1
    )
    both = jnp.concatenate([first, second], axis=0).astype(bf16)
    out_ref[...] = jnp.broadcast_to(both[None], out_ref.shape)


def table_kernel(passages_ref, gain_ref, table_ref, square_ref, inverse_ref):
    lifted = passages_ref[...].astype(f32) * gain_ref[...]
    norm = jnp.sqrt(jnp.sum(lifted * lifted, axis=1, keepdims=True))
    inverse = 1.0 / norm
    unit = lifted * inverse
    table_ref[...] = unit.astype(bf16)
    square_ref[...] = (unit * unit).astype(bf16)
    rows = unit.shape[0]
    inverse_ref[...] = jnp.transpose(jnp.broadcast_to(inverse, (rows, 128)))[:1, :]


def score_kernel(got_ref, start_ref, table_ref, cos_ref, weight_ref, teach_ref, sums_ref, unit_ref):
    queries = got_ref.shape[0]
    half = got_ref.shape[2] - 256
    listed = 128
    rows = table_ref.shape[0]
    got = got_ref[...].astype(f32)
    query = jnp.concatenate([got[:, 0, :half], got[:, 1, :half]], axis=1)
    norm = jnp.sqrt(jnp.sum(query * query, axis=1, keepdims=True))
    unit = (query / norm).astype(bf16)
    unit_ref[...] = unit
    ids = (got[:, 0, half : half + listed] * 256.0 + got[:, 0, half + listed :]).astype(jnp.int32)
    marks = jnp.exp(got[:, 1, half : half + listed] * (1.0 / teacher_div))
    marks = marks / jnp.sum(marks, axis=1, keepdims=True)
    here = ids - start_ref[0]
    places = lax.broadcasted_iota(jnp.int32, (queries, rows), 1)
    teach = jnp.zeros((queries, rows), f32)
    for c in range(listed):
        teach = teach + jnp.where(here[:, c : c + 1] == places, marks[:, c : c + 1], 0.0)
    teach_ref[...] = teach
    cos = dot(unit, table_ref[...], nt_dims)
    cos_ref[...] = cos
    weight = jnp.where(teach > 0.0, jnp.exp(cos * score_scale), 0.0)
    weight_ref[...] = weight
    total = jnp.sum(weight, axis=1, keepdims=True)
    flipped = jnp.transpose(jnp.broadcast_to(total, (queries, 128)))[:1, :queries]
    sums_ref[...] = jnp.broadcast_to(flipped[None], sums_ref.shape)


def mix_kernel(unit_ref, cos_ref, weight_ref, teach_ref, table_ref, square_ref, by_weight_ref, by_teach_ref, gain_weight_ref, gain_teach_ref):
    queries = unit_ref.shape[0]
    weight, teach, cos = weight_ref[...], teach_ref[...], cos_ref[...]
    stacked = jnp.concatenate([*split(weight), *split(teach)], axis=0)
    mixed = dot(stacked, table_ref[...], nn_dims)
    by_weight = mixed[:queries] + mixed[queries : 2 * queries]
    by_teach = mixed[2 * queries : 3 * queries] + mixed[3 * queries :]
    stacked = jnp.concatenate([*split(weight * cos), *split(teach * cos)], axis=0)
    along = dot(stacked, square_ref[...], nn_dims)
    unit = unit_ref[...].astype(f32)
    by_weight_ref[...] = by_weight
    by_teach_ref[...] = by_teach
    gain_weight_ref[...] = unit * by_weight - (along[:queries] + along[queries : 2 * queries])
    terms = unit * by_teach - (along[2 * queries : 3 * queries] + along[3 * queries :])
    gain_teach_ref[...] = jnp.sum(terms, axis=0, keepdims=True)


def partial_kernel(sums_ref, by_weight_ref, by_teach_ref, gain_weight_ref, gain_teach_ref, out_ref, inverse_ref):
    queries = by_weight_ref.shape[0]
    total = jnp.sum(sums_ref[...][:, 0, :], axis=0, keepdims=True)
    inverse = jnp.transpose(jnp.broadcast_to(1.0 / total, (128, queries)))[:, :1]
    inverse_ref[...] = inverse
    partial = coef_scale * (by_weight_ref[...] * inverse - by_teach_ref[...])
    gain_part = jnp.sum(gain_weight_ref[...] * inverse, axis=0, keepdims=True) - gain_teach_ref[...]
    gain_part = coef_scale * gain_part
    out_ref[...] = jnp.concatenate(
        [partial[:, None, :], jnp.broadcast_to(gain_part[None], (queries, 1, partial.shape[1]))], axis=1
    ).astype(bf16)


def passage_kernel(unit_ref, gain_ref, cos_ref, weight_ref, teach_ref, inverse_ref, norm_ref, table_ref, out_ref):
    coef = coef_scale * (weight_ref[...] * inverse_ref[...] - teach_ref[...])
    scaled = coef * norm_ref[...]
    along = jnp.sum(scaled * cos_ref[...], axis=0, keepdims=True)
    queries, rows = coef.shape
    column = jnp.transpose(jnp.broadcast_to(along, (128, rows)))[:, :1]
    high, low = split(jnp.transpose(scaled))
    unit = unit_ref[...]
    whole_part = dot(
        jnp.concatenate([high, low], axis=1), jnp.concatenate([unit, unit], axis=0), nn_dims
    )
    out_ref[...] = (whole_part - table_ref[...].astype(f32) * column) * gain_ref[...]


def final_kernel(got_ref, queries_ref, gain_ref, d_queries_ref, d_gain_ref):
    got = jnp.sum(got_ref[...].astype(f32), axis=0)
    query = queries_ref[...].astype(f32)
    norm = jnp.sqrt(jnp.sum(query * query, axis=1, keepdims=True))
    unit = query / norm
    d_unit = got[:1]
    d_queries_ref[...] = (d_unit - unit * jnp.sum(unit * d_unit, axis=1, keepdims=True)) / norm
    d_gain_ref[...] = got[1:] / gain_ref[...]


def shape(dims, dtype=f32):
    return jax.ShapeDtypeStruct(dims, dtype)


def exchange(x):
    return lax.all_to_all(x, "hash", split_axis=0, concat_axis=0, tiled=True)


def local(passages, queries, gain, candidates, teacher):
    count = lax.axis_size("hash")
    rows, width = passages.shape
    listed = candidates.shape[1]
    gain = gain.reshape(1, width)

    packed = pl.pallas_call(
        pack_kernel,
        out_shape=shape((count, 2, width // 2 + 2 * listed), bf16),
        name="pack",
    )(queries, candidates, teacher)
    got = exchange(packed)

    block = 128
    row_block = pl.BlockSpec((block, width), lambda i: (i, 0))
    table, square, norms = pl.pallas_call(
        table_kernel,
        grid=(rows // block,),
        in_specs=[row_block, pl.BlockSpec((1, width), lambda i: (0, 0))],
        out_specs=[row_block, row_block, pl.BlockSpec((1, block), lambda i: (0, i))],
        out_shape=[shape((rows, width), bf16), shape((rows, width), bf16), shape((1, rows))],
        compiler_params=params(48),
        name="table",
        cost_estimate=pl.CostEstimate(
            flops=6 * rows * width, bytes_accessed=6 * rows * width, transcendentals=0
        ),
    )(passages, gain)

    start = (lax.axis_index("hash") * rows).astype(jnp.int32).reshape(1)
    small = shape((count, rows))
    cos, weight, teach, sums, unit = pl.pallas_call(
        score_kernel,
        in_specs=[whole(), pl.BlockSpec(memory_space=pltpu.SMEM), whole()],
        out_shape=[small, small, small, shape((count, 1, count)), shape((count, width), bf16)],
        compiler_params=params(48),
        name="score",
    )(got, start, table)
    got_sums = exchange(sums)

    wide = shape((count, width))
    by_weight, by_teach, gain_weight, gain_teach = pl.pallas_call(
        mix_kernel,
        out_shape=[wide, wide, wide, shape((1, width))],
        compiler_params=params(48),
        name="mix",
        cost_estimate=pl.CostEstimate(
            flops=16 * count * rows * width, bytes_accessed=4 * rows * width, transcendentals=0
        ),
    )(unit, cos, weight, teach, table, square)

    partial, inverse = pl.pallas_call(
        partial_kernel,
        out_shape=[shape((count, 2, width), bf16), shape((count, 1))],
        compiler_params=params(48),
        name="partial",
    )(got_sums, by_weight, by_teach, gain_weight, gain_teach)
    got_partial = exchange(partial)

    fixed = lambda dims: pl.BlockSpec(dims, lambda i: (0, 0))
    cols = pl.BlockSpec((count, block), lambda i: (0, i))
    d_passages = pl.pallas_call(
        passage_kernel,
        grid=(rows // block,),
        in_specs=[
            fixed((count, width)),
            fixed((1, width)),
            cols,
            cols,
            cols,
            fixed((count, 1)),
            pl.BlockSpec((1, block), lambda i: (0, i)),
            row_block,
        ],
        out_specs=row_block,
        out_shape=shape((rows, width)),
        compiler_params=params(48),
        name="d_passages",
        cost_estimate=pl.CostEstimate(
            flops=4 * count * rows * width, bytes_accessed=6 * rows * width, transcendentals=0
        ),
    )(unit, gain, cos, weight, teach, inverse, norms, table)

    d_queries, d_gain = pl.pallas_call(
        final_kernel,
        out_shape=[shape((1, width)), shape((1, width))],
        compiler_params=params(48),
        name="final",
    )(got_partial, queries, gain)
    return (d_passages, d_queries, d_gain.reshape(width))


def solution(mesh):
    in_specs = (
        P(("groups", "hash"), None),
        P(("groups", "hash"), None),
        P(),
        P(("groups", "hash"), None),
        P(("groups", "hash"), None),
    )
    out_specs = (P(("groups", "hash"), None), P(("groups", "hash"), None), P("groups"))
    return jax.shard_map(local, mesh=mesh, in_specs=in_specs, out_specs=out_specs, check_vma=False)
```

time: 182 us -> 55.1 us (0.30)
  blocking collectives: 90.9 us -> 0 us
  other arithmetic: 30 us -> 0 us
  Pallas kernels: 0 us -> 21.9 us
  between operations: 14.9 us -> 0.71 us
  matrix products: 9.91 us -> 0 us
  local copies, waits for them, and re-layouts: 12.4 us -> 9.23 us
    psum x1 -> x0, blocking collectives: 57.7 us -> none  [local(): d_gain = lax.psum(jnp.sum(d_lifted * passage_f, axis=0), 'hash')]
    all_gather x1 -> x0, blocking collectives: 33.1 us -> none  [local(): gathered = lax.all_gather(q_send, 'hash', axis=0, tiled=True)]
    pallas_call x0 -> x7, Pallas kernels: none -> 21.9 us  [the longest x1 6.12 us: local(): pl.pallas_call(table_kernel, grid=(rows // block,), in_specs=[row_block,...]
    reduce_sum x6 -> x0, other arithmetic: 10.2 us -> none  [the longest x1 4.81 us: local(): d_gain = lax.psum(jnp.sum(d_lifted * passage_f, axis=0), 'hash')]
    dot_general x3 -> x0, matrix products: 9.91 us -> none  [the longest x1 6.58 us: local(): jnp.dot(mixing, gathered.astype(jnp.float32), precision=lax.Precision.HIG...]
    mul x2 -> x0, other arithmetic: 9.41 us -> none  [the longest x1 8.09 us: local(): d_passages = d_lifted * gain[None, :]]
    unnamed x11 -> x14, local copies, waits for them, and re-layouts: 0.05 us -> 9.23 us
    gather x3 -> x0, local copies, waits for them, and re-layouts: 8.73 us -> none  [the longest x1 5.93 us: local(): picked = table[wanted]]
  transfers between devices with their start and end apart: 3 -> 3, of which waited for: 2 -> 2; matrix products, arithmetic and copies ran while one was open for 6% -> 0% of each run, Pallas kernels for 0% -> 26%
where the time goes in v1:
time: 55.1 us; the launch traced here: 54.4 us
  Pallas kernels  21.9 us (40%)
  starting transfers between devices  18.9 us (34%)
  local copies, waits for them, and re-layouts  9.23 us (17%)
  waiting for transfers between devices  3.73 us (7%)
  between operations  0.71 us (1%)
    all_to_all x3, starting transfers between devices, exchange(): return lax.all_to_all(x, 'hash', split_axis=0, concat_axis=0, tiled=True)  18.9 us
    unnamed x14, local copies, waits for them, and re-layouts  9.23 us
    pallas_call x1, Pallas kernels, local(): pl.pallas_call(table_kernel, grid=(rows // block,), in_specs=[row_block,...  6.12 us
    pallas_call x1, Pallas kernels, local(): pl.pallas_call(passage_kernel, grid=(rows // block,), in_specs=[fixed((co...  4.63 us
    pallas_call x1, Pallas kernels, local(): pl.pallas_call(score_kernel, in_specs=[whole(), pl.BlockSpec(memory_space...  3.79 us
    all_to_all x3, waiting for transfers between devices, exchange(): return lax.all_to_all(x, 'hash', split_axis=0, concat_axis=0, tiled=True)  3.73 us
    pallas_call x1, Pallas kernels, local(): pl.pallas_call(mix_kernel, out_shape=[wide, wide, wide, shape((1, width))...  3.62 us
    pallas_call x1, Pallas kernels, local(): pl.pallas_call(pack_kernel, out_shape=shape((count, 2, width // 2 + 2 * l...  1.43 us
  transfers between devices with their start and end apart: 3, of which 2 were waited for; matrix products, arithmetic and copies ran while one was open for 0% of the time, Pallas kernels for 26%

profile of v1, /device:TPU:0, one launch (start us, length us, event | category | flops | bytes accessed | tf_op | source)
XLA Modules:
  0.0 54.4 jit_solution(8896602176290420893)
XLA Ops:
  0.6 1.4 %pack.1 = bf16[16,2,2304]{2,1,0:T(2,128)(2,1)} custom-call(bf16[1,4096]{1,0:T(2,128)(2,1)} %queries_ref.3, s32[1,128]{1,0:T(1,128)} %candidates_ref.1, s32[1,128]{1,0:T(1,128)} %teacher_ref.1), custom_call_target="tpu_custom_call" | custom-call | tf_op jit(solution)/shard_map/pack/pallas_call | solution.py:160
  2.1 7.4 %all-to-all-start = ((bf16[16,2,2304]{2,1,0:T(2,128)(2,1)}), bf16[16,2,2304]{2,1,0:T(2,128)(2,1)S(1)}, u32[]{:S(2)}, u32[]{:S(2)}) async-start(bf16[16,2,2304]{2,1,0:T(2,128)(2,1)} %pack.1), calls=%async_computation | async-start | bytes 294912 | tf_op jit(solution)/shard_map/all_to_all | solution.py:151
  9.4 0.0 copy-start.4
  9.4 0.7 %copy-done.4 = f32[4096]{0:T(1024)S(1)} copy-done((f32[4096]{0:T(1024)S(1)}, f32[4096]{0:T(1024)}, u32[]{:S(2)}) %copy-start.4) | copy-done | bytes 16408
  10.1 6.1 %table.1 = (bf16[512,4096]{1,0:T(8,128)(2,1)S(1)}, bf16[512,4096]{1,0:T(8,128)(2,1)}, f32[1,512]{1,0:T(1,128)S(1)}) custom-call(bf16[512,4096]{1,0:T(8,128)(2,1)} %passages_ref.1, f32[1,4096]{1,0:T(1,128)S(1)} %bitcast.3), custom_call_target="tpu_custom_call" | custom-call | flops 12582912 | bytes 12582912 | tf_op jit(solution)/shard_map/table/pallas_call | solution.py:169
  16.3 0.0 copy-start
  16.3 2.0 %copy-done = bf16[512,4096]{1,0:T(8,128)(2,1)} copy-done((bf16[512,4096]{1,0:T(8,128)(2,1)}, bf16[512,4096]{1,0:T(8,128)(2,1)S(1)}, u32[]{:S(2)}) %copy-start) | copy-done | bytes 4194328
  18.2 0.0 all-to-all-done.got_ref
  18.2 0.0 copy-start.1
  18.2 2.2 %copy-done.1 = bf16[512,4096]{1,0:T(8,128)(2,1)S(1)} copy-done((bf16[512,4096]{1,0:T(8,128)(2,1)S(1)}, bf16[512,4096]{1,0:T(8,128)(2,1)}, u32[]{:S(2)}) %copy-start.1) | copy-done | bytes 4194328
  20.4 3.8 %score.1 = (f32[16,512]{1,0:T(8,128)S(1)}, f32[16,512]{1,0:T(8,128)S(1)}, f32[16,512]{1,0:T(8,128)S(1)}, f32[16,1,16]{2,1,0:T(1,128)}, bf16[16,4096]{1,0:T(8,128)(2,1)S(1)}) custom-call(bf16[16,2,2304]{2,1,0:T(2,128)(2,1)S(1)} %all-to-all-done.got_ref, s32[1]{0:T(128)} %bitcast.start_ref, bf16[512,4096]{1,0:T(8,128)(2,1)S(1)} %copy-done.1), custom_call_target="tpu_custom_call" | custom-call | tf_op jit(solution)/shard_map/score/pallas_call | solution.py:184
  24.2 6.0 %all-to-all-start.1 = ((f32[16,1,16]{2,1,0:T(1,128)}), f32[16,1,16]{2,1,0:T(1,128)S(1)}, u32[]{:S(2)}, u32[]{:S(2)}) async-start(f32[16,1,16]{2,1,0:T(1,128)} %get-tuple-element.24), calls=%async_computation.1 | async-start | bytes 16384 | tf_op jit(solution)/shard_map/all_to_all | solution.py:151
  30.2 0.0 copy-start.2
  30.2 2.2 %copy-done.2 = bf16[512,4096]{1,0:T(8,128)(2,1)S(1)} copy-done((bf16[512,4096]{1,0:T(8,128)(2,1)S(1)}, bf16[512,4096]{1,0:T(8,128)(2,1)}, u32[]{:S(2)}) %copy-start.2) | copy-done | bytes 4194328
  32.4 0.0 copy-start.5
  32.4 3.6 %mix.1 = (f32[16,4096]{1,0:T(8,128)S(1)}, f32[16,4096]{1,0:T(8,128)S(1)}, f32[16,4096]{1,0:T(8,128)S(1)}, f32[1,4096]{1,0:T(1,128)S(1)}) custom-call(bf16[16,4096]{1,0:T(8,128)(2,1)S(1)} %get-tuple-element.20.unit_ref, f32[16,512]{1,0:T(8,128)S(1)} %get-tuple-element.21.cos_ref, f32[16,512]{1,0:T(8,128)S(1)} %get-tuple-element.22.weight_ref, ...), custom_call_target="tpu_custom_call" | custom-call | flops 536870912 | bytes 8388608 | tf_op jit(solution)/shard_map/mix/pallas_call | solution.py:194
  36.0 0.5 all-to-all-done.1.sums_ref
  36.5 1.3 %partial.1 = (bf16[16,2,4096]{2,1,0:T(2,128)(2,1)}, f32[16,1]{1,0:T(8,128)S(1)}) custom-call(f32[16,1,16]{2,1,0:T(1,128)S(1)} %all-to-all-done.1.sums_ref, f32[16,4096]{1,0:T(8,128)S(1)} %get-tuple-element.26.by_weight_ref, f32[16,4096]{1,0:T(8,128)S(1)} %get-tuple-element.27.by_teach_ref, f32[16,4096]{1,0:T(8,128)S(1)} %get-tuple-element.28.gain_weight_ref, ...), custom_call_target="tpu_custom_call" | custom-call | tf_op jit(solution)/shard_map/partial/pallas_call | solution.py:204
  37.8 5.5 %all-to-all-start.2 = ((bf16[16,2,4096]{2,1,0:T(2,128)(2,1)}), bf16[16,2,4096]{2,1,0:T(2,128)(2,1)S(1)}, u32[]{:S(2)}, u32[]{:S(2)}) async-start(bf16[16,2,4096]{2,1,0:T(2,128)(2,1)} %get-tuple-element.32), calls=%async_computation.2 | async-start | bytes 524288 | tf_op jit(solution)/shard_map/all_to_all | solution.py:151
  43.4 0.0 copy-done.5
  43.4 0.0 copy-start.3
  43.4 2.2 %copy-done.3 = bf16[512,4096]{1,0:T(8,128)(2,1)S(1)} copy-done((bf16[512,4096]{1,0:T(8,128)(2,1)S(1)}, bf16[512,4096]{1,0:T(8,128)(2,1)}, u32[]{:S(2)}) %copy-start.3) | copy-done | bytes 4194328
  45.6 0.0 copy-start.6
  45.6 4.6 %d_passages.1 = f32[512,4096]{1,0:T(8,128)} custom-call(bf16[16,4096]{1,0:T(8,128)(2,1)S(1)} %get-tuple-element.20.unit_ref, f32[1,4096]{1,0:T(1,128)S(1)} %bitcast.4, f32[16,512]{1,0:T(8,128)S(1)} %get-tuple-element.21.cos_ref, f32[16,512]{1,0:T(8,128)S(1)} %get-tuple-element.22.weight_ref, f32[16,512]{1,0:T(8,128)S(1)} %get-tuple-element.23.teach_ref, ...), custom_call_target="tpu_custom_call" | custom-call | flops 134217728 | bytes 12582912 | tf_op jit(solution)/shard_map/d_passages/pallas_call | solution.py:214
  50.2 3.2 %all-to-all-done.2.got_ref = bf16[16,2,4096]{2,1,0:T(2,128)(2,1)S(1)} async-done(((bf16[16,2,4096]{2,1,0:T(2,128)(2,1)}), bf16[16,2,4096]{2,1,0:T(2,128)(2,1)S(1)}, u32[]{:S(2)}, u32[]{:S(2)}) %all-to-all-start.2) | async-done | bytes 262176 | tf_op jit(solution)/shard_map/all_to_all | solution.py:151
  53.4 0.0 copy-done.6
  53.4 1.0 %final.1 = (f32[1,4096]{1,0:T(1,128)}, f32[1,4096]{1,0:T(1,128)}) custom-call(bf16[16,2,4096]{2,1,0:T(2,128)(2,1)S(1)} %all-to-all-done.2.got_ref, bf16[1,4096]{1,0:T(2,128)(2,1)S(1)} %copy-done.6, f32[1,4096]{1,0:T(1,128)S(1)} %bitcast.5), custom_call_target="tpu_custom_call" | custom-call | tf_op jit(solution)/shard_map/final/pallas_call | solution.py:236
Async XLA Ops:
  2.1 16.2 %all-to-all-start = ((bf16[16,2,2304]{2,1,0:T(2,128)(2,1)}), bf16[16,2,2304]{2,1,0:T(2,128)(2,1)S(1)}, u32[]{:S(2)}, u32[]{:S(2)}) async-start(bf16[16,2,2304]{2,1,0:T(2,128)(2,1)} %pack.1), calls=%async_computation | async-start | bytes 294912 | tf_op jit(solution)/shard_map/all_to_all | solution.py:151
  9.4 0.7 %copy-start.4 = (f32[4096]{0:T(1024)S(1)}, f32[4096]{0:T(1024)}, u32[]{:S(2)}) copy-start(f32[4096]{0:T(1024)} %param.7) | copy-start | bytes 49156
  16.3 2.0 %copy-start = (bf16[512,4096]{1,0:T(8,128)(2,1)}, bf16[512,4096]{1,0:T(8,128)(2,1)S(1)}, u32[]{:S(2)}) copy-start(bf16[512,4096]{1,0:T(8,128)(2,1)S(1)} %get-tuple-element.19.table_ref) | copy-start | bytes 12582916
  18.2 2.2 %copy-start.1 = (bf16[512,4096]{1,0:T(8,128)(2,1)S(1)}, bf16[512,4096]{1,0:T(8,128)(2,1)}, u32[]{:S(2)}) copy-start(bf16[512,4096]{1,0:T(8,128)(2,1)} %copy-done) | copy-start | bytes 12582916
  24.2 12.3 %all-to-all-start.1 = ((f32[16,1,16]{2,1,0:T(1,128)}), f32[16,1,16]{2,1,0:T(1,128)S(1)}, u32[]{:S(2)}, u32[]{:S(2)}) async-start(f32[16,1,16]{2,1,0:T(1,128)} %get-tuple-element.24), calls=%async_computation.1 | async-start | bytes 16384 | tf_op jit(solution)/shard_map/all_to_all | solution.py:151
  30.2 2.2 %copy-start.2 = (bf16[512,4096]{1,0:T(8,128)(2,1)S(1)}, bf16[512,4096]{1,0:T(8,128)(2,1)}, u32[]{:S(2)}) copy-start(bf16[512,4096]{1,0:T(8,128)(2,1)} %copy-done) | copy-start | bytes 12582916
  32.4 11.0 %copy-start.5 = (f32[4096]{0:T(1024)S(1)}, f32[4096]{0:T(1024)}, u32[]{:S(2)}) copy-start(f32[4096]{0:T(1024)} %param.7) | copy-start | bytes 49156
  37.8 15.6 %all-to-all-start.2 = ((bf16[16,2,4096]{2,1,0:T(2,128)(2,1)}), bf16[16,2,4096]{2,1,0:T(2,128)(2,1)S(1)}, u32[]{:S(2)}, u32[]{:S(2)}) async-start(bf16[16,2,4096]{2,1,0:T(2,128)(2,1)} %get-tuple-element.32), calls=%async_computation.2 | async-start | bytes 524288 | tf_op jit(solution)/shard_map/all_to_all | solution.py:151
  43.4 2.2 %copy-start.3 = (bf16[512,4096]{1,0:T(8,128)(2,1)S(1)}, bf16[512,4096]{1,0:T(8,128)(2,1)}, u32[]{:S(2)}) copy-start(bf16[512,4096]{1,0:T(8,128)(2,1)} %copy-done) | copy-start | bytes 12582916
  45.6 7.8 %copy-start.6 = (bf16[1,4096]{1,0:T(2,128)(2,1)S(1)}, bf16[1,4096]{1,0:T(2,128)(2,1)}, u32[]{:S(2)}) copy-start(bf16[1,4096]{1,0:T(2,128)(2,1)} %queries_ref.3) | copy-start | bytes 24580

commit v2 on v1

--- a/solution.py
+++ b/solution.py
@@ -29,7 +29,7 @@
 
 
 def params(megabytes):
-    return pltpu.CompilerParams(vmem_limit_bytes=megabytes * 1024 * 1024)
+    return pltpu.CompilerParams(vmem_limit_bytes=int(megabytes * 1024 * 1024))
 
 
 def whole():
@@ -85,8 +85,7 @@
     weight = jnp.where(teach > 0.0, jnp.exp(cos * score_scale), 0.0)
     weight_ref[...] = weight
     total = jnp.sum(weight, axis=1, keepdims=True)
-    flipped = jnp.transpose(jnp.broadcast_to(total, (queries, 128)))[:1, :queries]
-    sums_ref[...] = jnp.broadcast_to(flipped[None], sums_ref.shape)
+    sums_ref[...] = jnp.broadcast_to(total, sums_ref.shape)
 
 
 def mix_kernel(unit_ref, cos_ref, weight_ref, teach_ref, table_ref, square_ref, by_weight_ref, by_teach_ref, gain_weight_ref, gain_teach_ref):
@@ -108,8 +107,7 @@
 
 def partial_kernel(sums_ref, by_weight_ref, by_teach_ref, gain_weight_ref, gain_teach_ref, out_ref, inverse_ref):
     queries = by_weight_ref.shape[0]
-    total = jnp.sum(sums_ref[...][:, 0, :], axis=0, keepdims=True)
-    inverse = jnp.transpose(jnp.broadcast_to(1.0 / total, (128, queries)))[:, :1]
+    inverse = 1.0 / sums_ref[...][:, :1]
     inverse_ref[...] = inverse
     partial = coef_scale * (by_weight_ref[...] * inverse - by_teach_ref[...])
     gain_part = jnp.sum(gain_weight_ref[...] * inverse, axis=0, keepdims=True) - gain_teach_ref[...]
@@ -151,6 +149,15 @@
     return lax.all_to_all(x, "hash", split_axis=0, concat_axis=0, tiled=True)
 
 
+def add_up(x):
+    count = lax.axis_size("hash")
+    step = 1
+    while step < count:
+        x = x + lax.ppermute(x, "hash", [(i, i ^ step) for i in range(count)])
+        step *= 2
+    return x
+
+
 def local(passages, queries, gain, candidates, teacher):
     count = lax.axis_size("hash")
     rows, width = passages.shape
@@ -172,7 +179,7 @@
         in_specs=[row_block, pl.BlockSpec((1, width), lambda i: (0, 0))],
         out_specs=[row_block, row_block, pl.BlockSpec((1, block), lambda i: (0, i))],
         out_shape=[shape((rows, width), bf16), shape((rows, width), bf16), shape((1, rows))],
-        compiler_params=params(48),
+        compiler_params=params(24),
         name="table",
         cost_estimate=pl.CostEstimate(
             flops=6 * rows * width, bytes_accessed=6 * rows * width, transcendentals=0
@@ -184,17 +191,17 @@
     cos, weight, teach, sums, unit = pl.pallas_call(
         score_kernel,
         in_specs=[whole(), pl.BlockSpec(memory_space=pltpu.SMEM), whole()],
-        out_shape=[small, small, small, shape((count, 1, count)), shape((count, width), bf16)],
-        compiler_params=params(48),
+        out_shape=[small, small, small, shape((count, 128)), shape((count, width), bf16)],
+        compiler_params=params(12 + count // 4),
         name="score",
     )(got, start, table)
-    got_sums = exchange(sums)
+    got_sums = add_up(sums)
 
     wide = shape((count, width))
     by_weight, by_teach, gain_weight, gain_teach = pl.pallas_call(
         mix_kernel,
         out_shape=[wide, wide, wide, shape((1, width))],
-        compiler_params=params(48),
+        compiler_params=params(12 + count // 4),
         name="mix",
         cost_estimate=pl.CostEstimate(
             flops=16 * count * rows * width, bytes_accessed=4 * rows * width, transcendentals=0
@@ -204,7 +211,7 @@
     partial, inverse = pl.pallas_call(
         partial_kernel,
         out_shape=[shape((count, 2, width), bf16), shape((count, 1))],
-        compiler_params=params(48),
+        compiler_params=params(12 + count // 4),
         name="partial",
     )(got_sums, by_weight, by_teach, gain_weight, gain_teach)
     got_partial = exchange(partial)
@@ -226,7 +233,7 @@
         ],
         out_specs=row_block,
         out_shape=shape((rows, width)),
-        compiler_params=params(48),
+        compiler_params=params(16 + count // 8),
         name="d_passages",
         cost_estimate=pl.CostEstimate(
             flops=4 * count * rows * width, bytes_accessed=6 * rows * width, transcendentals=0
@@ -236,7 +243,7 @@
     d_queries, d_gain = pl.pallas_call(
         final_kernel,
         out_shape=[shape((1, width)), shape((1, width))],
-        compiler_params=params(48),
+        compiler_params=params(12 + count // 4),
         name="final",
     )(got_partial, queries, gain)
     return (d_passages, d_queries, d_gain.reshape(width))

time: 55.1 us -> 56.5 us (1.025)
  Pallas kernels: 21.9 us -> 15.8 us
  waiting for transfers between devices: 3.73 us -> 7.97 us
  local copies, waits for them, and re-layouts: 9.23 us -> 11.2 us
  starting transfers between devices: 18.9 us -> 20.3 us
    ppermute x0 -> x4, starting transfers between devices: none -> 6.89 us  [add_up(): x = x + lax.ppermute(x, 'hash', [(i, i ^ step) for i in range(count)])]
    all_to_all x3 -> x2, starting transfers between devices: 18.9 us -> 13.4 us  [exchange(): return lax.all_to_all(x, 'hash', split_axis=0, concat_axis=0, tiled=True)]
    ppermute x0 -> x4, waiting for transfers between devices: none -> 4.76 us  [add_up(): x = x + lax.ppermute(x, 'hash', [(i, i ^ step) for i in range(count)])]
    pallas_call x1, Pallas kernels: 6.12 us -> 2.98 us  [local(): pl.pallas_call(table_kernel, grid=(rows // block,), in_specs=[row_block,...]
    pallas_call x1, Pallas kernels: 3.62 us -> 1.42 us  [local(): pl.pallas_call(mix_kernel, out_shape=[wide, wide, wide, shape((1, width))...]
    unnamed x14 -> x18, local copies, waits for them, and re-layouts: 9.23 us -> 11.2 us
    pallas_call x1, Pallas kernels: 3.79 us -> 3.13 us  [local(): pl.pallas_call(score_kernel, in_specs=[whole(), pl.BlockSpec(memory_space...]
    all_to_all x3 -> x2, waiting for transfers between devices: 3.73 us -> 3.21 us  [exchange(): return lax.all_to_all(x, 'hash', split_axis=0, concat_axis=0, tiled=True)]
  transfers between devices with their start and end apart: 3 -> 6, of which waited for: 2 -> 5; matrix products, arithmetic and copies ran while one was open for 0% -> 0% of each run, Pallas kernels for 26% -> 16%
where the time goes in v2:
time: 56.5 us; the launch traced here: 56 us
  starting transfers between devices  20.3 us (36%)
  Pallas kernels  15.8 us (28%)
  local copies, waits for them, and re-layouts  11.2 us (20%)
  waiting for transfers between devices  7.97 us (14%)
  between operations  0.71 us (1%)
    all_to_all x2, starting transfers between devices, exchange(): return lax.all_to_all(x, 'hash', split_axis=0, concat_axis=0, tiled=True)  13.4 us
    unnamed x18, local copies, waits for them, and re-layouts  11.2 us
    ppermute x4, starting transfers between devices, add_up(): x = x + lax.ppermute(x, 'hash', [(i, i ^ step) for i in range(count)])  6.89 us
    ppermute x4, waiting for transfers between devices, add_up(): x = x + lax.ppermute(x, 'hash', [(i, i ^ step) for i in range(count)])  4.76 us
    pallas_call x1, Pallas kernels, local(): pl.pallas_call(passage_kernel, grid=(rows // block,), in_specs=[fixed((co...  4.64 us
    all_to_all x2, waiting for transfers between devices, exchange(): return lax.all_to_all(x, 'hash', split_axis=0, concat_axis=0, tiled=True)  3.21 us
    pallas_call x1, Pallas kernels, local(): pl.pallas_call(score_kernel, in_specs=[whole(), pl.BlockSpec(memory_space...  3.13 us
    pallas_call x1, Pallas kernels, local(): pl.pallas_call(table_kernel, grid=(rows // block,), in_specs=[row_block,...  2.98 us
  transfers between devices with their start and end apart: 6, of which 5 were waited for; matrix products, arithmetic and copies ran while one was open for 0% of the time, Pallas kernels for 16%

profile of v2, /device:TPU:0, one launch (start us, length us, event | category | flops | bytes accessed | tf_op | source)
XLA Modules:
  0.0 56.0 jit_solution(12662227096398657037)
XLA Ops:
  0.6 1.4 %pack.1 = bf16[16,2,2304]{2,1,0:T(2,128)(2,1)} custom-call(bf16[1,4096]{1,0:T(2,128)(2,1)} %queries_ref.3, s32[1,128]{1,0:T(1,128)} %candidates_ref.1, s32[1,128]{1,0:T(1,128)} %teacher_ref.1), custom_call_target="tpu_custom_call" | custom-call | tf_op jit(solution)/shard_map/pack/pallas_call | solution.py:167
  2.1 7.4 %all-to-all-start = ((bf16[16,2,2304]{2,1,0:T(2,128)(2,1)}), bf16[16,2,2304]{2,1,0:T(2,128)(2,1)S(1)}, u32[]{:S(2)}, u32[]{:S(2)}) async-start(bf16[16,2,2304]{2,1,0:T(2,128)(2,1)} %pack.1), calls=%async_computation | async-start | bytes 294912 | tf_op jit(solution)/shard_map/all_to_all | solution.py:149
  9.4 0.0 copy-start.3
  9.4 2.2 %copy-done.3 = bf16[512,4096]{1,0:T(8,128)(2,1)S(1)} copy-done((bf16[512,4096]{1,0:T(8,128)(2,1)S(1)}, bf16[512,4096]{1,0:T(8,128)(2,1)}, u32[]{:S(2)}) %copy-start.3) | copy-done | bytes 4194328
  11.6 0.0 copy-start.6
  11.6 0.7 %copy-done.6 = f32[4096]{0:T(1024)S(1)} copy-done((f32[4096]{0:T(1024)S(1)}, f32[4096]{0:T(1024)}, u32[]{:S(2)}) %copy-start.6) | copy-done | bytes 16408
  12.3 3.0 %table.1 = (bf16[512,4096]{1,0:T(8,128)(2,1)S(1)}, bf16[512,4096]{1,0:T(8,128)(2,1)S(1)}, f32[1,512]{1,0:T(1,128)S(1)}) custom-call(bf16[512,4096]{1,0:T(8,128)(2,1)S(1)} %copy-done.3, f32[1,4096]{1,0:T(1,128)S(1)} %bitcast.3), custom_call_target="tpu_custom_call" | custom-call | flops 12582912 | bytes 12582912 | tf_op jit(solution)/shard_map/table/pallas_call | solution.py:176
  15.3 0.0 copy-start
  15.3 2.0 %copy-done = bf16[512,4096]{1,0:T(8,128)(2,1)} copy-done((bf16[512,4096]{1,0:T(8,128)(2,1)}, bf16[512,4096]{1,0:T(8,128)(2,1)S(1)}, u32[]{:S(2)}) %copy-start) | copy-done | bytes 4194328
  17.3 0.0 copy-start.4
  17.3 1.9 %copy-done.4 = bf16[512,4096]{1,0:T(8,128)(2,1)} copy-done((bf16[512,4096]{1,0:T(8,128)(2,1)}, bf16[512,4096]{1,0:T(8,128)(2,1)S(1)}, u32[]{:S(2)}) %copy-start.4) | copy-done | bytes 4194328
  19.3 0.0 all-to-all-done.got_ref
  19.3 0.0 copy-start.1
  19.3 2.2 %copy-done.1 = bf16[512,4096]{1,0:T(8,128)(2,1)S(1)} copy-done((bf16[512,4096]{1,0:T(8,128)(2,1)S(1)}, bf16[512,4096]{1,0:T(8,128)(2,1)}, u32[]{:S(2)}) %copy-start.1) | copy-done | bytes 4194328
  21.5 0.0 copy-start.5
  21.5 3.1 %score.1 = (f32[16,512]{1,0:T(8,128)S(1)}, f32[16,512]{1,0:T(8,128)S(1)}, f32[16,512]{1,0:T(8,128)S(1)}, f32[16,128]{1,0:T(8,128)S(1)}, bf16[16,4096]{1,0:T(8,128)(2,1)S(1)}) custom-call(bf16[16,2,2304]{2,1,0:T(2,128)(2,1)S(1)} %all-to-all-done.got_ref, s32[1]{0:T(128)} %bitcast.start_ref, bf16[512,4096]{1,0:T(8,128)(2,1)S(1)} %copy-done.1), custom_call_target="tpu_custom_call" | custom-call | tf_op jit(solution)/shard_map/score/pallas_call | solution.py:191
  24.6 0.4 collective-permute-start
  25.0 0.8 %collective-permute-done = f32[16,128]{1,0:T(8,128)S(1)} collective-permute-done((f32[16,128]{1,0:T(8,128)S(1)}, f32[16,128]{1,0:T(8,128)S(1)}, u32[]{:S(2)}, u32[]{:S(2)}) %collective-permute-start) | collective-permute-done | bytes 8224 | tf_op jit(solution)/shard_map/ppermute | solution.py:156
  25.9 1.9 %collective-permute-start.1 = (f32[16,128]{1,0:T(8,128)S(1)}, f32[16,128]{1,0:T(8,128)S(1)}, u32[]{:S(2)}, u32[]{:S(2)}) collective-permute-start(f32[16,128]{1,0:T(8,128)S(1)} %add.12), channel_id=1, source_target_pairs={{0,2},{1,3},{2,0},{3,1},{4,6},{5,7},{6,4},{7,5},{8,10},{9,11},{10,... | collective-permute-start | bytes 24584 | tf_op jit(solution)/shard_map/ppermute | solution.py:156
  27.7 1.8 %collective-permute-done.1 = f32[16,128]{1,0:T(8,128)S(1)} collective-permute-done((f32[16,128]{1,0:T(8,128)S(1)}, f32[16,128]{1,0:T(8,128)S(1)}, u32[]{:S(2)}, u32[]{:S(2)}) %collective-permute-start.1) | collective-permute-done | bytes 8224 | tf_op jit(solution)/shard_map/ppermute | solution.py:156
  29.5 1.9 %collective-permute-start.2 = (f32[16,128]{1,0:T(8,128)S(1)}, f32[16,128]{1,0:T(8,128)S(1)}, u32[]{:S(2)}, u32[]{:S(2)}) collective-permute-start(f32[16,128]{1,0:T(8,128)S(1)} %add.13), channel_id=1, source_target_pairs={{0,4},{1,5},{2,6},{3,7},{4,0},{5,1},{6,2},{7,3},{8,12},{9,13},{10,... | collective-permute-start | bytes 24584 | tf_op jit(solution)/shard_map/ppermute | solution.py:156
  31.4 1.8 %collective-permute-done.2 = f32[16,128]{1,0:T(8,128)S(1)} collective-permute-done((f32[16,128]{1,0:T(8,128)S(1)}, f32[16,128]{1,0:T(8,128)S(1)}, u32[]{:S(2)}, u32[]{:S(2)}) %collective-permute-start.2) | collective-permute-done | bytes 8224 | tf_op jit(solution)/shard_map/ppermute | solution.py:156
  33.2 2.8 %collective-permute-start.3 = (f32[16,128]{1,0:T(8,128)S(1)}, f32[16,128]{1,0:T(8,128)S(1)}, u32[]{:S(2)}, u32[]{:S(2)}) collective-permute-start(f32[16,128]{1,0:T(8,128)S(1)} %add.14), channel_id=1, source_target_pairs={{0,8},{1,9},{2,10},{3,11},{4,12},{5,13},{6,14},{7,15},{8,0},{9,1},... | collective-permute-start | bytes 24584 | tf_op jit(solution)/shard_map/ppermute | solution.py:156
  35.9 0.0 copy-done.5
  35.9 0.0 copy-start.7
  35.9 1.4 %mix.1 = (f32[16,4096]{1,0:T(8,128)S(1)}, f32[16,4096]{1,0:T(8,128)S(1)}, f32[16,4096]{1,0:T(8,128)S(1)}, f32[1,4096]{1,0:T(1,128)S(1)}) custom-call(bf16[16,4096]{1,0:T(8,128)(2,1)S(1)} %get-tuple-element.20.unit_ref, f32[16,512]{1,0:T(8,128)S(1)} %get-tuple-element.21.cos_ref, f32[16,512]{1,0:T(8,128)S(1)} %get-tuple-element.22.weight_ref, ...), custom_call_target="tpu_custom_call" | custom-call | flops 536870912 | bytes 8388608 | tf_op jit(solution)/shard_map/mix/pallas_call | solution.py:201
  37.4 0.4 collective-permute-done.3
  37.7 1.2 %partial.1 = (bf16[16,2,4096]{2,1,0:T(2,128)(2,1)}, f32[16,1]{1,0:T(8,128)S(1)}) custom-call(f32[16,128]{1,0:T(8,128)S(1)} %add.15.sums_ref, f32[16,4096]{1,0:T(8,128)S(1)} %get-tuple-element.26.by_weight_ref, f32[16,4096]{1,0:T(8,128)S(1)} %get-tuple-element.27.by_teach_ref, f32[16,4096]{1,0:T(8,128)S(1)} %get-tuple-element.28.gain_weight_ref, ...), custom_call_target="tpu_custom_call" | custom-call | tf_op jit(solution)/shard_map/partial/pallas_call | solution.py:211
  38.9 6.0 %all-to-all-start.1 = ((bf16[16,2,4096]{2,1,0:T(2,128)(2,1)}), bf16[16,2,4096]{2,1,0:T(2,128)(2,1)S(1)}, u32[]{:S(2)}, u32[]{:S(2)}) async-start(bf16[16,2,4096]{2,1,0:T(2,128)(2,1)} %get-tuple-element.32), calls=%async_computation.1 | async-start | bytes 524288 | tf_op jit(solution)/shard_map/all_to_all | solution.py:149
  45.0 0.0 copy-done.7
  45.0 0.0 copy-start.2
  45.0 2.2 %copy-done.2 = bf16[512,4096]{1,0:T(8,128)(2,1)S(1)} copy-done((bf16[512,4096]{1,0:T(8,128)(2,1)S(1)}, bf16[512,4096]{1,0:T(8,128)(2,1)}, u32[]{:S(2)}) %copy-start.2) | copy-done | bytes 4194328
  47.2 0.0 copy-start.8
  47.2 4.6 %d_passages.1 = f32[512,4096]{1,0:T(8,128)} custom-call(bf16[16,4096]{1,0:T(8,128)(2,1)S(1)} %get-tuple-element.20.unit_ref, f32[1,4096]{1,0:T(1,128)S(1)} %bitcast.4, f32[16,512]{1,0:T(8,128)S(1)} %get-tuple-element.21.cos_ref, f32[16,512]{1,0:T(8,128)S(1)} %get-tuple-element.22.weight_ref, f32[16,512]{1,0:T(8,128)S(1)} %get-tuple-element.23.teach_ref, ...), custom_call_target="tpu_custom_call" | custom-call | flops 134217728 | bytes 12582912 | tf_op jit(solution)/shard_map/d_passages/pallas_call | solution.py:221
  51.8 3.2 %all-to-all-done.1.got_ref = bf16[16,2,4096]{2,1,0:T(2,128)(2,1)S(1)} async-done(((bf16[16,2,4096]{2,1,0:T(2,128)(2,1)}), bf16[16,2,4096]{2,1,0:T(2,128)(2,1)S(1)}, u32[]{:S(2)}, u32[]{:S(2)}) %all-to-all-start.1) | async-done | bytes 262176 | tf_op jit(solution)/shard_map/all_to_all | solution.py:149
  55.0 0.0 copy-done.8
  55.0 1.0 %final.1 = (f32[1,4096]{1,0:T(1,128)}, f32[1,4096]{1,0:T(1,128)}) custom-call(bf16[16,2,4096]{2,1,0:T(2,128)(2,1)S(1)} %all-to-all-done.1.got_ref, bf16[1,4096]{1,0:T(2,128)(2,1)S(1)} %copy-done.8, f32[1,4096]{1,0:T(1,128)S(1)} %bitcast.5), custom_call_target="tpu_custom_call" | custom-call | tf_op jit(solution)/shard_map/final/pallas_call | solution.py:243
  (4 shorter events, 0.0 us)
Async XLA Ops:
  2.1 17.2 %all-to-all-start = ((bf16[16,2,2304]{2,1,0:T(2,128)(2,1)}), bf16[16,2,2304]{2,1,0:T(2,128)(2,1)S(1)}, u32[]{:S(2)}, u32[]{:S(2)}) async-start(bf16[16,2,2304]{2,1,0:T(2,128)(2,1)} %pack.1), calls=%async_computation | async-start | bytes 294912 | tf_op jit(solution)/shard_map/all_to_all | solution.py:149
  9.4 2.2 %copy-start.3 = (bf16[512,4096]{1,0:T(8,128)(2,1)S(1)}, bf16[512,4096]{1,0:T(8,128)(2,1)}, u32[]{:S(2)}) copy-start(bf16[512,4096]{1,0:T(8,128)(2,1)} %passages_ref.1) | copy-start | bytes 12582916
  11.6 0.7 %copy-start.6 = (f32[4096]{0:T(1024)S(1)}, f32[4096]{0:T(1024)}, u32[]{:S(2)}) copy-start(f32[4096]{0:T(1024)} %param.7) | copy-start | bytes 49156
  15.3 2.0 %copy-start = (bf16[512,4096]{1,0:T(8,128)(2,1)}, bf16[512,4096]{1,0:T(8,128)(2,1)S(1)}, u32[]{:S(2)}) copy-start(bf16[512,4096]{1,0:T(8,128)(2,1)S(1)} %get-tuple-element.19.table_ref) | copy-start | bytes 12582916
  17.3 1.9 %copy-start.4 = (bf16[512,4096]{1,0:T(8,128)(2,1)}, bf16[512,4096]{1,0:T(8,128)(2,1)S(1)}, u32[]{:S(2)}) copy-start(bf16[512,4096]{1,0:T(8,128)(2,1)S(1)} %get-tuple-element.25.square_ref) | copy-start | bytes 12582916
  19.3 2.2 %copy-start.1 = (bf16[512,4096]{1,0:T(8,128)(2,1)S(1)}, bf16[512,4096]{1,0:T(8,128)(2,1)}, u32[]{:S(2)}) copy-start(bf16[512,4096]{1,0:T(8,128)(2,1)} %copy-done) | copy-start | bytes 12582916
  21.5 14.5 %copy-start.5 = (bf16[512,4096]{1,0:T(8,128)(2,1)S(1)}, bf16[512,4096]{1,0:T(8,128)(2,1)}, u32[]{:S(2)}) copy-start(bf16[512,4096]{1,0:T(8,128)(2,1)} %copy-done.4) | copy-start | bytes 12582916
  24.6 1.2 %collective-permute-start = (f32[16,128]{1,0:T(8,128)S(1)}, f32[16,128]{1,0:T(8,128)S(1)}, u32[]{:S(2)}, u32[]{:S(2)}) collective-permute-start(f32[16,128]{1,0:T(8,128)S(1)} %get-tuple-element.24), channel_id=1, source_target_pairs={{0,1},{1,0},{2,3},{3,2},{4,5},{5,4},{6,7},{7,6},{8,9},{9,8},{10,11... | collective-permute-start | bytes 24584 | tf_op jit(solution)/shard_map/ppermute | solution.py:156
  25.9 3.7 %collective-permute-start.1 = (f32[16,128]{1,0:T(8,128)S(1)}, f32[16,128]{1,0:T(8,128)S(1)}, u32[]{:S(2)}, u32[]{:S(2)}) collective-permute-start(f32[16,128]{1,0:T(8,128)S(1)} %add.12), channel_id=1, source_target_pairs={{0,2},{1,3},{2,0},{3,1},{4,6},{5,7},{6,4},{7,5},{8,10},{9,11},{10,... | collective-permute-start | bytes 24584 | tf_op jit(solution)/shard_map/ppermute | solution.py:156
  29.5 3.7 %collective-permute-start.2 = (f32[16,128]{1,0:T(8,128)S(1)}, f32[16,128]{1,0:T(8,128)S(1)}, u32[]{:S(2)}, u32[]{:S(2)}) collective-permute-start(f32[16,128]{1,0:T(8,128)S(1)} %add.13), channel_id=1, source_target_pairs={{0,4},{1,5},{2,6},{3,7},{4,0},{5,1},{6,2},{7,3},{8,12},{9,13},{10,... | collective-permute-start | bytes 24584 | tf_op jit(solution)/shard_map/ppermute | solution.py:156
  33.2 4.5 %collective-permute-start.3 = (f32[16,128]{1,0:T(8,128)S(1)}, f32[16,128]{1,0:T(8,128)S(1)}, u32[]{:S(2)}, u32[]{:S(2)}) collective-permute-start(f32[16,128]{1,0:T(8,128)S(1)} %add.14), channel_id=1, source_target_pairs={{0,8},{1,9},{2,10},{3,11},{4,12},{5,13},{6,14},{7,15},{8,0},{9,1},... | collective-permute-start | bytes 24584 | tf_op jit(solution)/shard_map/ppermute | solution.py:156
  35.9 9.0 %copy-start.7 = (f32[4096]{0:T(1024)S(1)}, f32[4096]{0:T(1024)}, u32[]{:S(2)}) copy-start(f32[4096]{0:T(1024)} %param.7) | copy-start | bytes 49156
  38.9 16.1 %all-to-all-start.1 = ((bf16[16,2,4096]{2,1,0:T(2,128)(2,1)}), bf16[16,2,4096]{2,1,0:T(2,128)(2,1)S(1)}, u32[]{:S(2)}, u32[]{:S(2)}) async-start(bf16[16,2,4096]{2,1,0:T(2,128)(2,1)} %get-tuple-element.32), calls=%async_computation.1 | async-start | bytes 524288 | tf_op jit(solution)/shard_map/all_to_all | solution.py:149
  45.0 2.2 %copy-start.2 = (bf16[512,4096]{1,0:T(8,128)(2,1)S(1)}, bf16[512,4096]{1,0:T(8,128)(2,1)}, u32[]{:S(2)}) copy-start(bf16[512,4096]{1,0:T(8,128)(2,1)} %copy-done) | copy-start | bytes 12582916
  47.2 7.8 %copy-start.8 = (bf16[1,4096]{1,0:T(2,128)(2,1)S(1)}, bf16[1,4096]{1,0:T(2,128)(2,1)}, u32[]{:S(2)}) copy-start(bf16[1,4096]{1,0:T(2,128)(2,1)} %queries_ref.3) | copy-start | bytes 24580

commit v3 on v1

--- a/solution.py
+++ b/solution.py
@@ -11,6 +11,7 @@
 loss_scale = 8192.0
 teacher_div = 2.0
 coef_scale = loss_scale * score_scale
+chunks = 4
 f32 = jnp.float32
 bf16 = jnp.bfloat16
 vmem = pltpu.VMEM
@@ -34,6 +35,10 @@
 
 def whole():
     return pl.BlockSpec(memory_space=vmem)
+
+
+def outside():
+    return pl.BlockSpec(memory_space=pltpu.HBM)
 
 
 def pack_kernel(queries_ref, candidates_ref, teacher_ref, out_ref):
@@ -50,22 +55,39 @@
     out_ref[...] = jnp.broadcast_to(both[None], out_ref.shape)
 
 
-def table_kernel(passages_ref, gain_ref, table_ref, square_ref, inverse_ref):
-    lifted = passages_ref[...].astype(f32) * gain_ref[...]
-    norm = jnp.sqrt(jnp.sum(lifted * lifted, axis=1, keepdims=True))
-    inverse = 1.0 / norm
-    unit = lifted * inverse
-    table_ref[...] = unit.astype(bf16)
-    square_ref[...] = (unit * unit).astype(bf16)
-    rows = unit.shape[0]
-    inverse_ref[...] = jnp.transpose(jnp.broadcast_to(inverse, (rows, 128)))[:1, :]
-
-
-def score_kernel(got_ref, start_ref, table_ref, cos_ref, weight_ref, teach_ref, sums_ref, unit_ref):
+def table_kernel(passages_ref, gain_ref, table_ref, inverse_ref, raw, held, sems_in, sems_out):
+    gain = gain_ref[...]
+    chunk = raw.shape[0] // chunks
+    copies_in, copies_out = [], []
+    for k in range(chunks):
+        part = pl.ds(k * chunk, chunk)
+        copies_in.append(pltpu.make_async_copy(passages_ref.at[part], raw.at[part], sems_in.at[k]))
+        copies_out.append(pltpu.make_async_copy(held.at[part], table_ref.at[part], sems_out.at[k]))
+        copies_in[-1].start()
+    for k in range(chunks):
+        part = pl.ds(k * chunk, chunk)
+        copies_in[k].wait()
+        lifted = raw[part, :].astype(f32) * gain
+        norm = jnp.sqrt(jnp.sum(lifted * lifted, axis=1, keepdims=True))
+        inverse = 1.0 / norm
+        held[part, :] = (lifted * inverse).astype(bf16)
+        copies_out[k].start()
+        inverse_ref[:, part] = jnp.transpose(jnp.broadcast_to(inverse, (chunk, 128)))[:1, :]
+    for k in range(chunks):
+        copies_out[k].wait()
+
+
+def score_kernel(got_ref, start_ref, table_ref, cos_ref, weight_ref, teach_ref, sums_ref, unit_ref, held, sems):
     queries = got_ref.shape[0]
     half = got_ref.shape[2] - 256
     listed = 128
     rows = table_ref.shape[0]
+    chunk = rows // chunks
+    copies = []
+    for k in range(chunks):
+        part = pl.ds(k * chunk, chunk)
+        copies.append(pltpu.make_async_copy(table_ref.at[part], held.at[part], sems.at[k]))
+        copies[-1].start()
     got = got_ref[...].astype(f32)
     query = jnp.concatenate([got[:, 0, :half], got[:, 1, :half]], axis=1)
     norm = jnp.sqrt(jnp.sum(query * query, axis=1, keepdims=True))
@@ -80,30 +102,46 @@
     for c in range(listed):
         teach = teach + jnp.where(here[:, c : c + 1] == places, marks[:, c : c + 1], 0.0)
     teach_ref[...] = teach
-    cos = dot(unit, table_ref[...], nt_dims)
-    cos_ref[...] = cos
-    weight = jnp.where(teach > 0.0, jnp.exp(cos * score_scale), 0.0)
+    for k in range(chunks):
+        copies[k].wait()
+        part = pl.ds(k * chunk, chunk)
+        cos_ref[:, part] = dot(unit, held[part, :], nt_dims)
+    weight = jnp.where(teach > 0.0, jnp.exp(cos_ref[...] * score_scale), 0.0)
     weight_ref[...] = weight
     total = jnp.sum(weight, axis=1, keepdims=True)
     flipped = jnp.transpose(jnp.broadcast_to(total, (queries, 128)))[:1, :queries]
     sums_ref[...] = jnp.broadcast_to(flipped[None], sums_ref.shape)
 
 
-def mix_kernel(unit_ref, cos_ref, weight_ref, teach_ref, table_ref, square_ref, by_weight_ref, by_teach_ref, gain_weight_ref, gain_teach_ref):
+def mix_kernel(
+    unit_ref, cos_ref, weight_ref, teach_ref, table_ref,
+    by_weight_ref, by_teach_ref, gain_weight_ref, gain_teach_ref, held, sems,
+):
     queries = unit_ref.shape[0]
+    chunk = table_ref.shape[1] // chunks
+    copies = []
+    for k in range(chunks):
+        part = pl.ds(k * chunk, chunk)
+        copies.append(pltpu.make_async_copy(table_ref.at[:, part], held.at[:, part], sems.at[k]))
+        copies[-1].start()
     weight, teach, cos = weight_ref[...], teach_ref[...], cos_ref[...]
-    stacked = jnp.concatenate([*split(weight), *split(teach)], axis=0)
-    mixed = dot(stacked, table_ref[...], nn_dims)
-    by_weight = mixed[:queries] + mixed[queries : 2 * queries]
-    by_teach = mixed[2 * queries : 3 * queries] + mixed[3 * queries :]
-    stacked = jnp.concatenate([*split(weight * cos), *split(teach * cos)], axis=0)
-    along = dot(stacked, square_ref[...], nn_dims)
-    unit = unit_ref[...].astype(f32)
-    by_weight_ref[...] = by_weight
-    by_teach_ref[...] = by_teach
-    gain_weight_ref[...] = unit * by_weight - (along[:queries] + along[queries : 2 * queries])
-    terms = unit * by_teach - (along[2 * queries : 3 * queries] + along[3 * queries :])
-    gain_teach_ref[...] = jnp.sum(terms, axis=0, keepdims=True)
+    plain = jnp.concatenate([*split(weight), *split(teach)], axis=0)
+    scored = jnp.concatenate([*split(weight * cos), *split(teach * cos)], axis=0)
+    for k in range(chunks):
+        copies[k].wait()
+        part = pl.ds(k * chunk, chunk)
+        table = held[:, part]
+        mixed = dot(plain, table, nn_dims)
+        by_weight = mixed[:queries] + mixed[queries : 2 * queries]
+        by_teach = mixed[2 * queries : 3 * queries] + mixed[3 * queries :]
+        table = table.astype(f32)
+        along = dot(scored, (table * table).astype(bf16), nn_dims)
+        unit = unit_ref[:, part].astype(f32)
+        by_weight_ref[:, part] = by_weight
+        by_teach_ref[:, part] = by_teach
+        gain_weight_ref[:, part] = unit * by_weight - (along[:queries] + along[queries : 2 * queries])
+        terms = unit * by_teach - (along[2 * queries : 3 * queries] + along[3 * queries :])
+        gain_teach_ref[:, part] = jnp.sum(terms, axis=0, keepdims=True)
 
 
 def partial_kernel(sums_ref, by_weight_ref, by_teach_ref, gain_weight_ref, gain_teach_ref, out_ref, inverse_ref):
@@ -119,18 +157,28 @@
     ).astype(bf16)
 
 
-def passage_kernel(unit_ref, gain_ref, cos_ref, weight_ref, teach_ref, inverse_ref, norm_ref, table_ref, out_ref):
+def passage_kernel(unit_ref, gain_ref, cos_ref, weight_ref, teach_ref, inverse_ref, norm_ref, table_ref, out_ref, held, sems):
+    step = pl.program_id(0)
+    chunk = out_ref.shape[0]
+    part = pl.ds(pl.multiple_of(step * chunk, chunk), chunk)
+
+    @pl.when(step == 0)
+    def _():
+        for k in range(chunks):
+            first = pl.ds(k * chunk, chunk)
+            pltpu.make_async_copy(table_ref.at[first], held.at[first], sems.at[k]).start()
+
     coef = coef_scale * (weight_ref[...] * inverse_ref[...] - teach_ref[...])
     scaled = coef * norm_ref[...]
     along = jnp.sum(scaled * cos_ref[...], axis=0, keepdims=True)
-    queries, rows = coef.shape
-    column = jnp.transpose(jnp.broadcast_to(along, (128, rows)))[:, :1]
+    column = jnp.transpose(jnp.broadcast_to(along, (128, chunk)))[:, :1]
     high, low = split(jnp.transpose(scaled))
     unit = unit_ref[...]
     whole_part = dot(
         jnp.concatenate([high, low], axis=1), jnp.concatenate([unit, unit], axis=0), nn_dims
     )
-    out_ref[...] = (whole_part - table_ref[...].astype(f32) * column) * gain_ref[...]
+    pltpu.make_async_copy(table_ref.at[part], held.at[part], sems.at[step]).wait()
+    out_ref[...] = (whole_part - held[part, :].astype(f32) * column) * gain_ref[...]
 
 
 def final_kernel(got_ref, queries_ref, gain_ref, d_queries_ref, d_gain_ref):
@@ -160,22 +208,25 @@
     packed = pl.pallas_call(
         pack_kernel,
         out_shape=shape((count, 2, width // 2 + 2 * listed), bf16),
+        compiler_params=params(60),
         name="pack",
     )(queries, candidates, teacher)
     got = exchange(packed)
 
     block = 128
     row_block = pl.BlockSpec((block, width), lambda i: (i, 0))
-    table, square, norms = pl.pallas_call(
+    held = pltpu.VMEM((rows, width), bf16)
+    sems = pltpu.SemaphoreType.DMA((chunks,))
+    table, norms = pl.pallas_call(
         table_kernel,
-        grid=(rows // block,),
-        in_specs=[row_block, pl.BlockSpec((1, width), lambda i: (0, 0))],
-        out_specs=[row_block, row_block, pl.BlockSpec((1, block), lambda i: (0, i))],
-        out_shape=[shape((rows, width), bf16), shape((rows, width), bf16), shape((1, rows))],
-        compiler_params=params(48),
+        in_specs=[outside(), whole()],
+        out_specs=[outside(), whole()],
+        out_shape=[shape((rows, width), bf16), shape((1, rows))],
+        scratch_shapes=[held, held, sems, sems],
+        compiler_params=params(60),
         name="table",
         cost_estimate=pl.CostEstimate(
-            flops=6 * rows * width, bytes_accessed=6 * rows * width, transcendentals=0
+            flops=6 * rows * width, bytes_accessed=4 * rows * width, transcendentals=0
         ),
     )(passages, gain)
 
@@ -183,9 +234,10 @@
     small = shape((count, rows))
     cos, weight, teach, sums, unit = pl.pallas_call(
         score_kernel,
-        in_specs=[whole(), pl.BlockSpec(memory_space=pltpu.SMEM), whole()],
+        in_specs=[whole(), pl.BlockSpec(memory_space=pltpu.SMEM), outside()],
         out_shape=[small, small, small, shape((count, 1, count)), shape((count, width), bf16)],
-        compiler_params=params(48),
+        scratch_shapes=[held, sems],
+        compiler_params=params(60),
         name="score",
     )(got, start, table)
     got_sums = exchange(sums)
@@ -193,22 +245,25 @@
     wide = shape((count, width))
     by_weight, by_teach, gain_weight, gain_teach = pl.pallas_call(
         mix_kernel,
+        in_specs=[whole(), whole(), whole(), whole(), outside()],
         out_shape=[wide, wide, wide, shape((1, width))],
-        compiler_params=params(48),
+        scratch_shapes=[held, sems],
+        compiler_params=params(60),
         name="mix",
         cost_estimate=pl.CostEstimate(
-            flops=16 * count * rows * width, bytes_accessed=4 * rows * width, transcendentals=0
+            flops=16 * count * rows * width, bytes_accessed=2 * rows * width, transcendentals=0
         ),
-    )(unit, cos, weight, teach, table, square)
+    )(unit, cos, weight, teach, table)
 
     partial, inverse = pl.pallas_call(
         partial_kernel,
         out_shape=[shape((count, 2, width), bf16), shape((count, 1))],
-        compiler_params=params(48),
+        compiler_params=params(60),
         name="partial",
     )(got_sums, by_weight, by_teach, gain_weight, gain_teach)
     got_partial = exchange(partial)
 
+    block = rows // chunks
     fixed = lambda dims: pl.BlockSpec(dims, lambda i: (0, 0))
     cols = pl.BlockSpec((count, block), lambda i: (0, i))
     d_passages = pl.pallas_call(
@@ -222,11 +277,12 @@
             cols,
             fixed((count, 1)),
             pl.BlockSpec((1, block), lambda i: (0, i)),
-            row_block,
+            outside(),
         ],
-        out_specs=row_block,
+        out_specs=pl.BlockSpec((block, width), lambda i: (i, 0)),
         out_shape=shape((rows, width)),
-        compiler_params=params(48),
+        scratch_shapes=[held, sems],
+        compiler_params=params(60),
         name="d_passages",
         cost_estimate=pl.CostEstimate(
             flops=4 * count * rows * width, bytes_accessed=6 * rows * width, transcendentals=0
@@ -236,7 +292,7 @@
     d_queries, d_gain = pl.pallas_call(
         final_kernel,
         out_shape=[shape((1, width)), shape((1, width))],
-        compiler_params=params(48),
+        compiler_params=params(60),
         name="final",
     )(got_partial, queries, gain)
     return (d_passages, d_queries, d_gain.reshape(width))

time: 55.1 us -> 56.3 us (1.022)
  Pallas kernels: 21.9 us -> 31.3 us
  local copies, waits for them, and re-layouts: 9.23 us -> 1.95 us
  starting transfers between devices: 18.9 us -> 15.3 us
  waiting for transfers between devices: 3.73 us -> 6.46 us
    unnamed x14 -> x6, local copies, waits for them, and re-layouts: 9.23 us -> 1.95 us
    pallas_call x1, Pallas kernels: 3.79 us -> 7.37 us  [local(): pl.pallas_call(score_kernel, in_specs=[whole(), pl.BlockSpec(memory_space...]
    all_to_all x3, starting transfers between devices: 18.9 us -> 15.3 us  [exchange(): return lax.all_to_all(x, 'hash', split_axis=0, concat_axis=0, tiled=True)]
    pallas_call x1, Pallas kernels: 4.63 us -> 7.63 us  [local(): pl.pallas_call(passage_kernel, grid=(rows // block,), in_specs=[fixed((co...]
    all_to_all x3, waiting for transfers between devices: 3.73 us -> 6.46 us  [exchange(): return lax.all_to_all(x, 'hash', split_axis=0, concat_axis=0, tiled=True)]
    pallas_call x1, Pallas kernels: 1.29 us -> 2.4 us  [local(): pl.pallas_call(partial_kernel, out_shape=[shape((count, 2, width), bf16),...]
    pallas_call x1, Pallas kernels: 1.02 us -> 1.99 us  [local(): pl.pallas_call(final_kernel, out_shape=[shape((1, width)), shape((1, widt...]
    pallas_call x2, Pallas kernels: 9.73 us -> 10.4 us  [the longest x1 5.63 us: local(): pl.pallas_call(table_kernel, in_specs=[outside(), whole()], out_specs=[ou...]
  transfers between devices with their start and end apart: 3 -> 3, of which waited for: 2 -> 3; matrix products, arithmetic and copies ran while one was open for 0% -> 0% of each run, Pallas kernels for 26% -> 32%
where the time goes in v3:
time: 56.3 us; the launch traced here: 55.7 us
  Pallas kernels  31.3 us (56%)
  starting transfers between devices  15.3 us (27%)
  waiting for transfers between devices  6.46 us (11%)
  local copies, waits for them, and re-layouts  1.95 us (3%)
  between operations  0.7 us (1%)
    all_to_all x3, starting transfers between devices, exchange(): return lax.all_to_all(x, 'hash', split_axis=0, concat_axis=0, tiled=True)  15.3 us
    pallas_call x1, Pallas kernels, local(): pl.pallas_call(passage_kernel, grid=(rows // block,), in_specs=[fixed((co...  7.63 us
    pallas_call x1, Pallas kernels, local(): pl.pallas_call(score_kernel, in_specs=[whole(), pl.BlockSpec(memory_space...  7.37 us
    all_to_all x3, waiting for transfers between devices, exchange(): return lax.all_to_all(x, 'hash', split_axis=0, concat_axis=0, tiled=True)  6.46 us
    pallas_call x1, Pallas kernels, local(): pl.pallas_call(table_kernel, in_specs=[outside(), whole()], out_specs=[ou...  5.63 us
    pallas_call x1, Pallas kernels, local(): pl.pallas_call(mix_kernel, in_specs=[whole(), whole(), whole(), whole(),...  4.82 us
    pallas_call x1, Pallas kernels, local(): pl.pallas_call(partial_kernel, out_shape=[shape((count, 2, width), bf16),...  2.4 us
    pallas_call x1, Pallas kernels, local(): pl.pallas_call(final_kernel, out_shape=[shape((1, width)), shape((1, widt...  1.99 us
  transfers between devices with their start and end apart: 3, of which 3 were waited for; matrix products, arithmetic and copies ran while one was open for 0% of the time, Pallas kernels for 32%

profile of v3, /device:TPU:0, one launch (start us, length us, event | category | flops | bytes accessed | tf_op | source)
XLA Modules:
  0.0 55.7 jit_solution(9992267679955307107)
XLA Ops:
  0.6 1.4 %pack.1 = bf16[16,2,2304]{2,1,0:T(2,128)(2,1)} custom-call(bf16[1,4096]{1,0:T(2,128)(2,1)} %queries_ref.3, s32[1,128]{1,0:T(1,128)} %candidates_ref.1, s32[1,128]{1,0:T(1,128)} %teacher_ref.1), custom_call_target="tpu_custom_call" | custom-call | tf_op jit(solution)/shard_map/pack/pallas_call | solution.py:208
  2.1 7.4 %all-to-all-start = ((bf16[16,2,2304]{2,1,0:T(2,128)(2,1)}), bf16[16,2,2304]{2,1,0:T(2,128)(2,1)S(1)}, u32[]{:S(2)}, u32[]{:S(2)}) async-start(bf16[16,2,2304]{2,1,0:T(2,128)(2,1)} %pack.1), calls=%async_computation | async-start | bytes 294912 | tf_op jit(solution)/shard_map/all_to_all | solution.py:199
  9.4 5.6 %table.1 = (bf16[512,4096]{1,0:T(8,128)(2,1)}, f32[1,512]{1,0:T(1,128)}) custom-call(bf16[512,4096]{1,0:T(8,128)(2,1)} %passages_ref.1, f32[1,4096]{1,0:T(1,128)} %bitcast.3), custom_call_target="tpu_custom_call" | custom-call | flops 12582912 | bytes 8388608 | tf_op jit(solution)/shard_map/table/pallas_call | solution.py:220
  15.1 2.6 %all-to-all-done.got_ref = bf16[16,2,2304]{2,1,0:T(2,128)(2,1)S(1)} async-done(((bf16[16,2,2304]{2,1,0:T(2,128)(2,1)}), bf16[16,2,2304]{2,1,0:T(2,128)(2,1)S(1)}, u32[]{:S(2)}, u32[]{:S(2)}) %all-to-all-start) | async-done | bytes 147488 | tf_op jit(solution)/shard_map/all_to_all | solution.py:199
  17.6 0.0 copy-start.1
  17.6 0.7 %copy-done.1 = bf16[16,2,2304]{2,1,0:T(2,128)(2,1)} copy-done((bf16[16,2,2304]{2,1,0:T(2,128)(2,1)}, bf16[16,2,2304]{2,1,0:T(2,128)(2,1)S(1)}, u32[]{:S(2)}) %copy-start.1) | copy-done | bytes 147480
  18.3 7.4 %score.1 = (f32[16,512]{1,0:T(8,128)}, f32[16,512]{1,0:T(8,128)}, f32[16,512]{1,0:T(8,128)}, f32[16,1,16]{2,1,0:T(1,128)}, bf16[16,4096]{1,0:T(8,128)(2,1)}) custom-call(bf16[16,2,2304]{2,1,0:T(2,128)(2,1)} %copy-done.1, s32[1]{0:T(128)} %bitcast.start_ref, bf16[512,4096]{1,0:T(8,128)(2,1)} %get-tuple-element.18.table_ref), custom_call_target="tpu_custom_call" | custom-call | tf_op jit(solution)/shard_map/score/pallas_call | solution.py:235
  25.7 3.5 %all-to-all-start.1 = ((f32[16,1,16]{2,1,0:T(1,128)}), f32[16,1,16]{2,1,0:T(1,128)S(1)}, u32[]{:S(2)}, u32[]{:S(2)}) async-start(f32[16,1,16]{2,1,0:T(1,128)} %get-tuple-element.23), calls=%async_computation.1 | async-start | bytes 16384 | tf_op jit(solution)/shard_map/all_to_all | solution.py:199
  29.2 4.8 %mix.1 = (f32[16,4096]{1,0:T(8,128)}, f32[16,4096]{1,0:T(8,128)}, f32[16,4096]{1,0:T(8,128)}, f32[1,4096]{1,0:T(1,128)}) custom-call(bf16[16,4096]{1,0:T(8,128)(2,1)} %get-tuple-element.19.unit_ref, f32[16,512]{1,0:T(8,128)} %get-tuple-element.20.cos_ref, f32[16,512]{1,0:T(8,128)} %get-tuple-element.21.weight_ref, f32[16,512]{1,0:T(8,128)} %get-tuple-element.22.teach_ref, ...), custom_call_target="tpu_custom_call" | custom-call | flops 536870912 | bytes 4194304 | tf_op jit(solution)/shard_map/mix/pallas_call | solution.py:246
  34.0 1.5 %all-to-all-done.1.sums_ref = f32[16,1,16]{2,1,0:T(1,128)S(1)} async-done(((f32[16,1,16]{2,1,0:T(1,128)}), f32[16,1,16]{2,1,0:T(1,128)S(1)}, u32[]{:S(2)}, u32[]{:S(2)}) %all-to-all-start.1) | async-done | bytes 1056 | tf_op jit(solution)/shard_map/all_to_all | solution.py:199
  35.5 0.0 copy-start.2
  35.5 0.6 %copy-done.2 = f32[16,1,16]{2,1,0:T(1,128)} copy-done((f32[16,1,16]{2,1,0:T(1,128)}, f32[16,1,16]{2,1,0:T(1,128)S(1)}, u32[]{:S(2)}) %copy-start.2) | copy-done | bytes 1048
  36.1 2.4 %partial.1 = (bf16[16,2,4096]{2,1,0:T(2,128)(2,1)}, f32[16,1]{1,0:T(8,128)}) custom-call(f32[16,1,16]{2,1,0:T(1,128)} %copy-done.2, f32[16,4096]{1,0:T(8,128)} %get-tuple-element.24.by_weight_ref, f32[16,4096]{1,0:T(8,128)} %get-tuple-element.25.by_teach_ref, f32[16,4096]{1,0:T(8,128)} %get-tuple-element.26.gain_weight_ref, ...), custom_call_target="tpu_custom_call" | custom-call | tf_op jit(solution)/shard_map/partial/pallas_call | solution.py:258
  38.5 4.5 %all-to-all-start.2 = ((bf16[16,2,4096]{2,1,0:T(2,128)(2,1)}), bf16[16,2,4096]{2,1,0:T(2,128)(2,1)S(1)}, u32[]{:S(2)}, u32[]{:S(2)}) async-start(bf16[16,2,4096]{2,1,0:T(2,128)(2,1)} %get-tuple-element.30), calls=%async_computation.2 | async-start | bytes 524288 | tf_op jit(solution)/shard_map/all_to_all | solution.py:199
  43.0 7.6 %d_passages.1 = f32[512,4096]{1,0:T(8,128)} custom-call(bf16[16,4096]{1,0:T(8,128)(2,1)} %get-tuple-element.19.unit_ref, f32[1,4096]{1,0:T(1,128)} %bitcast.4, f32[16,512]{1,0:T(8,128)} %get-tuple-element.20.cos_ref, f32[16,512]{1,0:T(8,128)} %get-tuple-element.21.weight_ref, f32[16,512]{1,0:T(8,128)} %get-tuple-element.22.teach_ref, ...), custom_call_target="tpu_custom_call" | custom-call | flops 134217728 | bytes 12582912 | tf_op jit(solution)/shard_map/d_passages/pallas_call | solution.py:269
  50.6 2.4 %all-to-all-done.2.got_ref = bf16[16,2,4096]{2,1,0:T(2,128)(2,1)S(1)} async-done(((bf16[16,2,4096]{2,1,0:T(2,128)(2,1)}), bf16[16,2,4096]{2,1,0:T(2,128)(2,1)S(1)}, u32[]{:S(2)}, u32[]{:S(2)}) %all-to-all-start.2) | async-done | bytes 262176 | tf_op jit(solution)/shard_map/all_to_all | solution.py:199
  53.0 0.0 copy-start
  53.0 0.7 %copy-done = bf16[16,2,4096]{2,1,0:T(2,128)(2,1)} copy-done((bf16[16,2,4096]{2,1,0:T(2,128)(2,1)}, bf16[16,2,4096]{2,1,0:T(2,128)(2,1)S(1)}, u32[]{:S(2)}) %copy-start) | copy-done | bytes 262168
  53.7 2.0 %final.1 = (f32[1,4096]{1,0:T(1,128)}, f32[1,4096]{1,0:T(1,128)}) custom-call(bf16[16,2,4096]{2,1,0:T(2,128)(2,1)} %copy-done, bf16[1,4096]{1,0:T(2,128)(2,1)} %queries_ref.3, f32[1,4096]{1,0:T(1,128)} %bitcast.5), custom_call_target="tpu_custom_call" | custom-call | tf_op jit(solution)/shard_map/final/pallas_call | solution.py:292
Async XLA Ops:
  2.1 15.6 %all-to-all-start = ((bf16[16,2,2304]{2,1,0:T(2,128)(2,1)}), bf16[16,2,2304]{2,1,0:T(2,128)(2,1)S(1)}, u32[]{:S(2)}, u32[]{:S(2)}) async-start(bf16[16,2,2304]{2,1,0:T(2,128)(2,1)} %pack.1), calls=%async_computation | async-start | bytes 294912 | tf_op jit(solution)/shard_map/all_to_all | solution.py:199
  17.6 0.7 %copy-start.1 = (bf16[16,2,2304]{2,1,0:T(2,128)(2,1)}, bf16[16,2,2304]{2,1,0:T(2,128)(2,1)S(1)}, u32[]{:S(2)}) copy-start(bf16[16,2,2304]{2,1,0:T(2,128)(2,1)S(1)} %all-to-all-done.got_ref) | copy-start | bytes 442372
  25.7 9.8 %all-to-all-start.1 = ((f32[16,1,16]{2,1,0:T(1,128)}), f32[16,1,16]{2,1,0:T(1,128)S(1)}, u32[]{:S(2)}, u32[]{:S(2)}) async-start(f32[16,1,16]{2,1,0:T(1,128)} %get-tuple-element.23), calls=%async_computation.1 | async-start | bytes 16384 | tf_op jit(solution)/shard_map/all_to_all | solution.py:199
  35.5 0.6 %copy-start.2 = (f32[16,1,16]{2,1,0:T(1,128)}, f32[16,1,16]{2,1,0:T(1,128)S(1)}, u32[]{:S(2)}) copy-start(f32[16,1,16]{2,1,0:T(1,128)S(1)} %all-to-all-done.1.sums_ref) | copy-start | bytes 3076
  38.5 14.6 %all-to-all-start.2 = ((bf16[16,2,4096]{2,1,0:T(2,128)(2,1)}), bf16[16,2,4096]{2,1,0:T(2,128)(2,1)S(1)}, u32[]{:S(2)}, u32[]{:S(2)}) async-start(bf16[16,2,4096]{2,1,0:T(2,128)(2,1)} %get-tuple-element.30), calls=%async_computation.2 | async-start | bytes 524288 | tf_op jit(solution)/shard_map/all_to_all | solution.py:199
  53.0 0.7 %copy-start = (bf16[16,2,4096]{2,1,0:T(2,128)(2,1)}, bf16[16,2,4096]{2,1,0:T(2,128)(2,1)S(1)}, u32[]{:S(2)}) copy-start(bf16[16,2,4096]{2,1,0:T(2,128)(2,1)S(1)} %all-to-all-done.2.got_ref) | copy-start | bytes 786436

commit v4 on v3

--- a/solution.py
+++ b/solution.py
@@ -81,7 +81,7 @@
     queries = got_ref.shape[0]
     half = got_ref.shape[2] - 256
     listed = 128
-    rows = table_ref.shape[0]
+    rows = held.shape[0]
     chunk = rows // chunks
     copies = []
     for k in range(chunks):
@@ -122,7 +122,7 @@
     copies = []
     for k in range(chunks):
         part = pl.ds(k * chunk, chunk)
-        copies.append(pltpu.make_async_copy(table_ref.at[:, part], held.at[:, part], sems.at[k]))
+        copies.append(pltpu.make_async_copy(table_ref.at[pl.ds(0, held.shape[0]), part], held.at[:, part], sems.at[k]))
         copies[-1].start()
     weight, teach, cos = weight_ref[...], teach_ref[...], cos_ref[...]
     plain = jnp.concatenate([*split(weight), *split(teach)], axis=0)
@@ -208,7 +208,7 @@
     packed = pl.pallas_call(
         pack_kernel,
         out_shape=shape((count, 2, width // 2 + 2 * listed), bf16),
-        compiler_params=params(60),
+        compiler_params=params(48),
         name="pack",
     )(queries, candidates, teacher)
     got = exchange(packed)
@@ -221,7 +221,7 @@
         table_kernel,
         in_specs=[outside(), whole()],
         out_specs=[outside(), whole()],
-        out_shape=[shape((rows, width), bf16), shape((1, rows))],
+        out_shape=[shape((5 * rows, width), bf16), shape((1, rows))],
         scratch_shapes=[held, held, sems, sems],
         compiler_params=params(60),
         name="table",
@@ -237,7 +237,7 @@
         in_specs=[whole(), pl.BlockSpec(memory_space=pltpu.SMEM), outside()],
         out_shape=[small, small, small, shape((count, 1, count)), shape((count, width), bf16)],
         scratch_shapes=[held, sems],
-        compiler_params=params(60),
+        compiler_params=params(48),
         name="score",
     )(got, start, table)
     got_sums = exchange(sums)
@@ -248,7 +248,7 @@
         in_specs=[whole(), whole(), whole(), whole(), outside()],
         out_shape=[wide, wide, wide, shape((1, width))],
         scratch_shapes=[held, sems],
-        compiler_params=params(60),
+        compiler_params=params(48),
         name="mix",
         cost_estimate=pl.CostEstimate(
             flops=16 * count * rows * width, bytes_accessed=2 * rows * width, transcendentals=0
@@ -258,7 +258,7 @@
     partial, inverse = pl.pallas_call(
         partial_kernel,
         out_shape=[shape((count, 2, width), bf16), shape((count, 1))],
-        compiler_params=params(60),
+        compiler_params=params(48),
         name="partial",
     )(got_sums, by_weight, by_teach, gain_weight, gain_teach)
     got_partial = exchange(partial)
@@ -282,7 +282,7 @@
         out_specs=pl.BlockSpec((block, width), lambda i: (i, 0)),
         out_shape=shape((rows, width)),
         scratch_shapes=[held, sems],
-        compiler_params=params(60),
+        compiler_params=params(48),
         name="d_passages",
         cost_estimate=pl.CostEstimate(
             flops=4 * count * rows * width, bytes_accessed=6 * rows * width, transcendentals=0
@@ -292,7 +292,7 @@
     d_queries, d_gain = pl.pallas_call(
         final_kernel,
         out_shape=[shape((1, width)), shape((1, width))],
-        compiler_params=params(60),
+        compiler_params=params(48),
         name="final",
     )(got_partial, queries, gain)
     return (d_passages, d_queries, d_gain.reshape(width))

time: 56.3 us -> 51.6 us (0.917)
  Pallas kernels: 31.3 us -> 24.8 us
  waiting for transfers between devices: 6.46 us -> 9 us
  starting transfers between devices: 15.3 us -> 14.4 us
    all_to_all x3, waiting for transfers between devices: 6.46 us -> 9 us  [exchange(): return lax.all_to_all(x, 'hash', split_axis=0, concat_axis=0, tiled=True)]
    pallas_call x1, Pallas kernels: 4.82 us -> 3.18 us  [local(): pl.pallas_call(mix_kernel, in_specs=[whole(), whole(), whole(), whole(),...]
    pallas_call x1, Pallas kernels: 2.4 us -> 1.28 us  [local(): pl.pallas_call(partial_kernel, out_shape=[shape((count, 2, width), bf16),...]
    pallas_call x1, Pallas kernels: 7.63 us -> 6.61 us  [local(): pl.pallas_call(passage_kernel, grid=(rows // block,), in_specs=[fixed((co...]
    pallas_call x1, Pallas kernels: 7.37 us -> 6.39 us  [local(): pl.pallas_call(score_kernel, in_specs=[whole(), pl.BlockSpec(memory_space...]
    pallas_call x1, Pallas kernels: 1.99 us -> 1.02 us  [local(): pl.pallas_call(final_kernel, out_shape=[shape((1, width)), shape((1, widt...]
    all_to_all x3, starting transfers between devices: 15.3 us -> 14.4 us  [exchange(): return lax.all_to_all(x, 'hash', split_axis=0, concat_axis=0, tiled=True)]
    pallas_call x1, Pallas kernels: 1.42 us -> 0.69 us  [local(): pl.pallas_call(pack_kernel, out_shape=shape((count, 2, width // 2 + 2 * l...]
  transfers between devices with their start and end apart: 3 -> 3, of which waited for: 3 -> 3; matrix products, arithmetic and copies ran while one was open for 0% -> 0% of each run, Pallas kernels for 32% -> 30%
where the time goes in v4:
time: 51.6 us; the launch traced here: 51 us
  Pallas kernels  24.8 us (48%)
  starting transfers between devices  14.4 us (28%)
  waiting for transfers between devices  9 us (17%)
  local copies, waits for them, and re-layouts  2.04 us (4%)
  between operations  0.74 us (1%)
    all_to_all x3, starting transfers between devices, exchange(): return lax.all_to_all(x, 'hash', split_axis=0, concat_axis=0, tiled=True)  14.4 us
    all_to_all x3, waiting for transfers between devices, exchange(): return lax.all_to_all(x, 'hash', split_axis=0, concat_axis=0, tiled=True)  9 us
    pallas_call x1, Pallas kernels, local(): pl.pallas_call(passage_kernel, grid=(rows // block,), in_specs=[fixed((co...  6.61 us
    pallas_call x1, Pallas kernels, local(): pl.pallas_call(score_kernel, in_specs=[whole(), pl.BlockSpec(memory_space...  6.39 us
    pallas_call x1, Pallas kernels, local(): pl.pallas_call(table_kernel, in_specs=[outside(), whole()], out_specs=[ou...  5.65 us
    pallas_call x1, Pallas kernels, local(): pl.pallas_call(mix_kernel, in_specs=[whole(), whole(), whole(), whole(),...  3.18 us
    unnamed x12, local copies, waits for them, and re-layouts  2.04 us
    pallas_call x1, Pallas kernels, local(): pl.pallas_call(partial_kernel, out_shape=[shape((count, 2, width), bf16),...  1.28 us
  transfers between devices with their start and end apart: 3, of which 3 were waited for; matrix products, arithmetic and copies ran while one was open for 0% of the time, Pallas kernels for 30%

profile of v4, /device:TPU:0, one launch (start us, length us, event | category | flops | bytes accessed | tf_op | source)
XLA Modules:
  0.0 51.0 jit_solution(11389085490077063621)
XLA Ops:
  0.6 0.0 copy-start.1
  0.6 0.7 %copy-done.1 = bf16[1,4096]{1,0:T(2,128)(2,1)S(1)} copy-done((bf16[1,4096]{1,0:T(2,128)(2,1)S(1)}, bf16[1,4096]{1,0:T(2,128)(2,1)}, u32[]{:S(2)}) %copy-start.1) | copy-done | bytes 8216
  1.4 0.0 copy-start.4
  1.4 0.7 %copy-done.4 = s32[1,128]{1,0:T(1,128)S(1)} copy-done((s32[1,128]{1,0:T(1,128)S(1)}, s32[1,128]{1,0:T(1,128)}, u32[]{:S(2)}) %copy-start.4) | copy-done | bytes 536
  2.0 0.0 copy-start.5
  2.0 0.7 %copy-done.5 = s32[1,128]{1,0:T(1,128)S(1)} copy-done((s32[1,128]{1,0:T(1,128)S(1)}, s32[1,128]{1,0:T(1,128)}, u32[]{:S(2)}) %copy-start.5) | copy-done | bytes 536
  2.7 0.7 %pack.1 = bf16[16,2,2304]{2,1,0:T(2,128)(2,1)} custom-call(bf16[1,4096]{1,0:T(2,128)(2,1)S(1)} %copy-done.1, s32[1,128]{1,0:T(1,128)S(1)} %copy-done.4, s32[1,128]{1,0:T(1,128)S(1)} %copy-done.5), custom_call_target="tpu_custom_call" | custom-call | tf_op jit(solution)/shard_map/pack/pallas_call | solution.py:208
  3.4 7.4 %all-to-all-start = ((bf16[16,2,2304]{2,1,0:T(2,128)(2,1)}), bf16[16,2,2304]{2,1,0:T(2,128)(2,1)S(1)}, u32[]{:S(2)}, u32[]{:S(2)}) async-start(bf16[16,2,2304]{2,1,0:T(2,128)(2,1)} %pack.1), calls=%async_computation | async-start | bytes 294912 | tf_op jit(solution)/shard_map/all_to_all | solution.py:199
  10.7 5.6 %table.1 = (bf16[2560,4096]{1,0:T(8,128)(2,1)}, f32[1,512]{1,0:T(1,128)}) custom-call(bf16[512,4096]{1,0:T(8,128)(2,1)} %passages_ref.1, f32[1,4096]{1,0:T(1,128)} %bitcast.3), custom_call_target="tpu_custom_call" | custom-call | flops 12582912 | bytes 8388608 | tf_op jit(solution)/shard_map/table/pallas_call | solution.py:220
  16.4 2.5 %all-to-all-done.got_ref = bf16[16,2,2304]{2,1,0:T(2,128)(2,1)S(1)} async-done(((bf16[16,2,2304]{2,1,0:T(2,128)(2,1)}), bf16[16,2,2304]{2,1,0:T(2,128)(2,1)S(1)}, u32[]{:S(2)}, u32[]{:S(2)}) %all-to-all-start) | async-done | bytes 147488 | tf_op jit(solution)/shard_map/all_to_all | solution.py:199
  18.9 6.4 %score.1 = (f32[16,512]{1,0:T(8,128)S(1)}, f32[16,512]{1,0:T(8,128)S(1)}, f32[16,512]{1,0:T(8,128)S(1)}, f32[16,1,16]{2,1,0:T(1,128)}, bf16[16,4096]{1,0:T(8,128)(2,1)S(1)}) custom-call(bf16[16,2,2304]{2,1,0:T(2,128)(2,1)S(1)} %all-to-all-done.got_ref, s32[1]{0:T(128)} %bitcast.start_ref, bf16[2560,4096]{1,0:T(8,128)(2,1)} %get-tuple-element.18.table_ref), custom_call_target="tpu_custom_call" | custom-call | tf_op jit(solution)/shard_map/score/pallas_call | solution.py:235
  25.3 3.5 %all-to-all-start.1 = ((f32[16,1,16]{2,1,0:T(1,128)}), f32[16,1,16]{2,1,0:T(1,128)S(1)}, u32[]{:S(2)}, u32[]{:S(2)}) async-start(f32[16,1,16]{2,1,0:T(1,128)} %get-tuple-element.23), calls=%async_computation.1 | async-start | bytes 16384 | tf_op jit(solution)/shard_map/all_to_all | solution.py:199
  28.8 0.0 copy-start
  28.8 0.0 copy-start.3
  28.8 3.2 %mix.1 = (f32[16,4096]{1,0:T(8,128)S(1)}, f32[16,4096]{1,0:T(8,128)S(1)}, f32[16,4096]{1,0:T(8,128)S(1)}, f32[1,4096]{1,0:T(1,128)S(1)}) custom-call(bf16[16,4096]{1,0:T(8,128)(2,1)S(1)} %get-tuple-element.19.unit_ref, f32[16,512]{1,0:T(8,128)S(1)} %get-tuple-element.20.cos_ref, f32[16,512]{1,0:T(8,128)S(1)} %get-tuple-element.21.weight_ref, ...), custom_call_target="tpu_custom_call" | custom-call | flops 536870912 | bytes 4194304 | tf_op jit(solution)/shard_map/mix/pallas_call | solution.py:246
  32.0 3.1 %all-to-all-done.1.sums_ref = f32[16,1,16]{2,1,0:T(1,128)S(1)} async-done(((f32[16,1,16]{2,1,0:T(1,128)}), f32[16,1,16]{2,1,0:T(1,128)S(1)}, u32[]{:S(2)}, u32[]{:S(2)}) %all-to-all-start.1) | async-done | bytes 1056 | tf_op jit(solution)/shard_map/all_to_all | solution.py:199
  35.1 1.3 %partial.1 = (bf16[16,2,4096]{2,1,0:T(2,128)(2,1)}, f32[16,1]{1,0:T(8,128)S(1)}) custom-call(f32[16,1,16]{2,1,0:T(1,128)S(1)} %all-to-all-done.1.sums_ref, f32[16,4096]{1,0:T(8,128)S(1)} %get-tuple-element.24.by_weight_ref, f32[16,4096]{1,0:T(8,128)S(1)} %get-tuple-element.25.by_teach_ref, f32[16,4096]{1,0:T(8,128)S(1)} %get-tuple-element.26.gain_weight_ref, ...), custom_call_target="tpu_custom_call" | custom-call | tf_op jit(solution)/shard_map/partial/pallas_call | solution.py:258
  36.4 3.5 %all-to-all-start.2 = ((bf16[16,2,4096]{2,1,0:T(2,128)(2,1)}), bf16[16,2,4096]{2,1,0:T(2,128)(2,1)S(1)}, u32[]{:S(2)}, u32[]{:S(2)}) async-start(bf16[16,2,4096]{2,1,0:T(2,128)(2,1)} %get-tuple-element.30), calls=%async_computation.2 | async-start | bytes 524288 | tf_op jit(solution)/shard_map/all_to_all | solution.py:199
  40.0 0.0 copy-done
  40.0 0.0 copy-done.3
  40.0 0.0 copy-start.2
  40.0 6.6 %d_passages.1 = f32[512,4096]{1,0:T(8,128)} custom-call(bf16[16,4096]{1,0:T(8,128)(2,1)S(1)} %get-tuple-element.19.unit_ref, f32[1,4096]{1,0:T(1,128)S(1)} %bitcast.4, f32[16,512]{1,0:T(8,128)S(1)} %get-tuple-element.20.cos_ref, f32[16,512]{1,0:T(8,128)S(1)} %get-tuple-element.21.weight_ref, f32[16,512]{1,0:T(8,128)S(1)} %get-tuple-element.22.teach_ref, ...), custom_call_target="tpu_custom_call" | custom-call | flops 134217728 | bytes 12582912 | tf_op jit(solution)/shard_map/d_passages/pallas_call | solution.py:269
  46.6 3.4 %all-to-all-done.2.got_ref = bf16[16,2,4096]{2,1,0:T(2,128)(2,1)S(1)} async-done(((bf16[16,2,4096]{2,1,0:T(2,128)(2,1)}), bf16[16,2,4096]{2,1,0:T(2,128)(2,1)S(1)}, u32[]{:S(2)}, u32[]{:S(2)}) %all-to-all-start.2) | async-done | bytes 262176 | tf_op jit(solution)/shard_map/all_to_all | solution.py:199
  50.0 0.0 copy-done.2
  50.0 1.0 %final.1 = (f32[1,4096]{1,0:T(1,128)}, f32[1,4096]{1,0:T(1,128)}) custom-call(bf16[16,2,4096]{2,1,0:T(2,128)(2,1)S(1)} %all-to-all-done.2.got_ref, bf16[1,4096]{1,0:T(2,128)(2,1)S(1)} %copy-done.2, f32[1,4096]{1,0:T(1,128)S(1)} %bitcast.5), custom_call_target="tpu_custom_call" | custom-call | tf_op jit(solution)/shard_map/final/pallas_call | solution.py:292
Async XLA Ops:
  0.6 0.7 %copy-start.1 = (bf16[1,4096]{1,0:T(2,128)(2,1)S(1)}, bf16[1,4096]{1,0:T(2,128)(2,1)}, u32[]{:S(2)}) copy-start(bf16[1,4096]{1,0:T(2,128)(2,1)} %queries_ref.3) | copy-start | bytes 24580
  1.4 0.7 %copy-start.4 = (s32[1,128]{1,0:T(1,128)S(1)}, s32[1,128]{1,0:T(1,128)}, u32[]{:S(2)}) copy-start(s32[1,128]{1,0:T(1,128)} %candidates_ref.1) | copy-start | bytes 1540
  2.0 0.7 %copy-start.5 = (s32[1,128]{1,0:T(1,128)S(1)}, s32[1,128]{1,0:T(1,128)}, u32[]{:S(2)}) copy-start(s32[1,128]{1,0:T(1,128)} %teacher_ref.1) | copy-start | bytes 1540
  3.4 15.6 %all-to-all-start = ((bf16[16,2,2304]{2,1,0:T(2,128)(2,1)}), bf16[16,2,2304]{2,1,0:T(2,128)(2,1)S(1)}, u32[]{:S(2)}, u32[]{:S(2)}) async-start(bf16[16,2,2304]{2,1,0:T(2,128)(2,1)} %pack.1), calls=%async_computation | async-start | bytes 294912 | tf_op jit(solution)/shard_map/all_to_all | solution.py:199
  25.3 9.8 %all-to-all-start.1 = ((f32[16,1,16]{2,1,0:T(1,128)}), f32[16,1,16]{2,1,0:T(1,128)S(1)}, u32[]{:S(2)}, u32[]{:S(2)}) async-start(f32[16,1,16]{2,1,0:T(1,128)} %get-tuple-element.23), calls=%async_computation.1 | async-start | bytes 16384 | tf_op jit(solution)/shard_map/all_to_all | solution.py:199
  28.8 11.1 %copy-start = (f32[4096]{0:T(1024)S(1)}, f32[4096]{0:T(1024)}, u32[]{:S(2)}) copy-start(f32[4096]{0:T(1024)} %param.7) | copy-start | bytes 49156
  28.8 11.1 %copy-start.3 = (f32[1,512]{1,0:T(1,128)S(1)}, f32[1,512]{1,0:T(1,128)}, u32[]{:S(2)}) copy-start(f32[1,512]{1,0:T(1,128)} %get-tuple-element.29.norm_ref) | copy-start | bytes 6148
  36.4 13.5 %all-to-all-start.2 = ((bf16[16,2,4096]{2,1,0:T(2,128)(2,1)}), bf16[16,2,4096]{2,1,0:T(2,128)(2,1)S(1)}, u32[]{:S(2)}, u32[]{:S(2)}) async-start(bf16[16,2,4096]{2,1,0:T(2,128)(2,1)} %get-tuple-element.30), calls=%async_computation.2 | async-start | bytes 524288 | tf_op jit(solution)/shard_map/all_to_all | solution.py:199
  40.0 10.0 %copy-start.2 = (bf16[1,4096]{1,0:T(2,128)(2,1)S(1)}, bf16[1,4096]{1,0:T(2,128)(2,1)}, u32[]{:S(2)}) copy-start(bf16[1,4096]{1,0:T(2,128)(2,1)} %queries_ref.3) | copy-start | bytes 24580

commit v5 on v4

--- a/solution.py
+++ b/solution.py
@@ -82,11 +82,13 @@
     half = got_ref.shape[2] - 256
     listed = 128
     rows = held.shape[0]
-    chunk = rows // chunks
+    chunk = held.shape[1] // chunks
     copies = []
     for k in range(chunks):
         part = pl.ds(k * chunk, chunk)
-        copies.append(pltpu.make_async_copy(table_ref.at[part], held.at[part], sems.at[k]))
+        copies.append(
+            pltpu.make_async_copy(table_ref.at[pl.ds(0, rows), part], held.at[:, part], sems.at[k])
+        )
         copies[-1].start()
     got = got_ref[...].astype(f32)
     query = jnp.concatenate([got[:, 0, :half], got[:, 1, :half]], axis=1)
@@ -102,11 +104,13 @@
     for c in range(listed):
         teach = teach + jnp.where(here[:, c : c + 1] == places, marks[:, c : c + 1], 0.0)
     teach_ref[...] = teach
+    cos = jnp.zeros((queries, rows), f32)
     for k in range(chunks):
         copies[k].wait()
-        part = pl.ds(k * chunk, chunk)
-        cos_ref[:, part] = dot(unit, held[part, :], nt_dims)
-    weight = jnp.where(teach > 0.0, jnp.exp(cos_ref[...] * score_scale), 0.0)
+        part = slice(k * chunk, (k + 1) * chunk)
+        cos = cos + dot(unit[:, part], held[:, part], nt_dims)
+    cos_ref[...] = cos
+    weight = jnp.where(teach > 0.0, jnp.exp(cos * score_scale), 0.0)
     weight_ref[...] = weight
     total = jnp.sum(weight, axis=1, keepdims=True)
     flipped = jnp.transpose(jnp.broadcast_to(total, (queries, 128)))[:1, :queries]
@@ -196,7 +200,11 @@
 
 
 def exchange(x):
-    return lax.all_to_all(x, "hash", split_axis=0, concat_axis=0, tiled=True)
+    count = lax.axis_size("hash")
+    order = [(i + count // 2 + 1) % count for i in range(count)]
+    return lax.all_to_all(
+        x, "hash", split_axis=0, concat_axis=0, axis_index_groups=[order], tiled=True
+    )
 
 
 def local(passages, queries, gain, candidates, teacher):

time: 51.6 us -> 45.4 us (0.88)
  waiting for transfers between devices: 9 us -> 2.25 us
  starting transfers between devices: 14.4 us -> 16.4 us
  Pallas kernels: 24.8 us -> 23.5 us
    all_to_all x3, waiting for transfers between devices: 9 us -> 2.25 us  [exchange(): lax.all_to_all(x, 'hash', split_axis=0, concat_axis=0, axis_index_groups=...]
    all_to_all x3, starting transfers between devices: 14.4 us -> 16.4 us  [exchange(): lax.all_to_all(x, 'hash', split_axis=0, concat_axis=0, axis_index_groups=...]
    pallas_call x1, Pallas kernels: 6.39 us -> 5.04 us  [local(): pl.pallas_call(score_kernel, in_specs=[whole(), pl.BlockSpec(memory_space...]
  transfers between devices with their start and end apart: 3 -> 3, of which waited for: 3 -> 3; matrix products, arithmetic and copies ran while one was open for 0% -> 0% of each run, Pallas kernels for 30% -> 34%
where the time goes in v5:
time: 45.4 us; the launch traced here: 44.8 us
  Pallas kernels  23.5 us (52%)
  starting transfers between devices  16.4 us (36%)
  waiting for transfers between devices  2.25 us (5%)
  local copies, waits for them, and re-layouts  2.04 us (4%)
  between operations  0.71 us (2%)
    all_to_all x3, starting transfers between devices, exchange(): lax.all_to_all(x, 'hash', split_axis=0, concat_axis=0, axis_index_groups=...  16.4 us
    pallas_call x1, Pallas kernels, local(): pl.pallas_call(passage_kernel, grid=(rows // block,), in_specs=[fixed((co...  6.61 us
    pallas_call x1, Pallas kernels, local(): pl.pallas_call(table_kernel, in_specs=[outside(), whole()], out_specs=[ou...  5.64 us
    pallas_call x1, Pallas kernels, local(): pl.pallas_call(score_kernel, in_specs=[whole(), pl.BlockSpec(memory_space...  5.04 us
    pallas_call x1, Pallas kernels, local(): pl.pallas_call(mix_kernel, in_specs=[whole(), whole(), whole(), whole(),...  3.18 us
    all_to_all x3, waiting for transfers between devices, exchange(): lax.all_to_all(x, 'hash', split_axis=0, concat_axis=0, axis_index_groups=...  2.25 us
    unnamed x12, local copies, waits for them, and re-layouts  2.04 us
    pallas_call x1, Pallas kernels, local(): pl.pallas_call(partial_kernel, out_shape=[shape((count, 2, width), bf16),...  1.28 us
  transfers between devices with their start and end apart: 3, of which 3 were waited for; matrix products, arithmetic and copies ran while one was open for 0% of the time, Pallas kernels for 34%

profile of v5, /device:TPU:0, one launch (start us, length us, event | category | flops | bytes accessed | tf_op | source)
XLA Modules:
  0.0 44.8 jit_solution(11974878773269995549)
XLA Ops:
  0.6 0.0 copy-start.1
  0.6 0.7 %copy-done.1 = bf16[1,4096]{1,0:T(2,128)(2,1)S(1)} copy-done((bf16[1,4096]{1,0:T(2,128)(2,1)S(1)}, bf16[1,4096]{1,0:T(2,128)(2,1)}, u32[]{:S(2)}) %copy-start.1) | copy-done | bytes 8216
  1.4 0.0 copy-start.4
  1.4 0.7 %copy-done.4 = s32[1,128]{1,0:T(1,128)S(1)} copy-done((s32[1,128]{1,0:T(1,128)S(1)}, s32[1,128]{1,0:T(1,128)}, u32[]{:S(2)}) %copy-start.4) | copy-done | bytes 536
  2.0 0.0 copy-start.5
  2.0 0.7 %copy-done.5 = s32[1,128]{1,0:T(1,128)S(1)} copy-done((s32[1,128]{1,0:T(1,128)S(1)}, s32[1,128]{1,0:T(1,128)}, u32[]{:S(2)}) %copy-start.5) | copy-done | bytes 536
  2.7 0.7 %pack.1 = bf16[16,2,2304]{2,1,0:T(2,128)(2,1)} custom-call(bf16[1,4096]{1,0:T(2,128)(2,1)S(1)} %copy-done.1, s32[1,128]{1,0:T(1,128)S(1)} %copy-done.4, s32[1,128]{1,0:T(1,128)S(1)} %copy-done.5), custom_call_target="tpu_custom_call" | custom-call | tf_op jit(solution)/shard_map/pack/pallas_call | solution.py:216
  3.4 7.6 %all-to-all-start = ((bf16[16,2,2304]{2,1,0:T(2,128)(2,1)}), bf16[16,2,2304]{2,1,0:T(2,128)(2,1)S(1)}, u32[]{:S(2)}, u32[]{:S(2)}) async-start(bf16[16,2,2304]{2,1,0:T(2,128)(2,1)} %pack.1), calls=%async_computation | async-start | bytes 294912 | tf_op jit(solution)/shard_map/all_to_all | solution.py:205
  10.9 5.6 %table.1 = (bf16[2560,4096]{1,0:T(8,128)(2,1)}, f32[1,512]{1,0:T(1,128)}) custom-call(bf16[512,4096]{1,0:T(8,128)(2,1)} %passages_ref.1, f32[1,4096]{1,0:T(1,128)} %bitcast.3), custom_call_target="tpu_custom_call" | custom-call | flops 12582912 | bytes 8388608 | tf_op jit(solution)/shard_map/table/pallas_call | solution.py:228
  16.6 0.3 all-to-all-done.got_ref
  16.8 5.0 %score.1 = (f32[16,512]{1,0:T(8,128)S(1)}, f32[16,512]{1,0:T(8,128)S(1)}, f32[16,512]{1,0:T(8,128)S(1)}, f32[16,1,16]{2,1,0:T(1,128)}, bf16[16,4096]{1,0:T(8,128)(2,1)S(1)}) custom-call(bf16[16,2,2304]{2,1,0:T(2,128)(2,1)S(1)} %all-to-all-done.got_ref, s32[1]{0:T(128)} %bitcast.start_ref, bf16[2560,4096]{1,0:T(8,128)(2,1)} %get-tuple-element.18.table_ref), custom_call_target="tpu_custom_call" | custom-call | tf_op jit(solution)/shard_map/score/pallas_call | solution.py:243
  21.9 4.6 %all-to-all-start.1 = ((f32[16,1,16]{2,1,0:T(1,128)}), f32[16,1,16]{2,1,0:T(1,128)S(1)}, u32[]{:S(2)}, u32[]{:S(2)}) async-start(f32[16,1,16]{2,1,0:T(1,128)} %get-tuple-element.23), calls=%async_computation.1 | async-start | bytes 16384 | tf_op jit(solution)/shard_map/all_to_all | solution.py:205
  26.5 0.0 copy-start
  26.5 0.0 copy-start.3
  26.5 3.2 %mix.1 = (f32[16,4096]{1,0:T(8,128)S(1)}, f32[16,4096]{1,0:T(8,128)S(1)}, f32[16,4096]{1,0:T(8,128)S(1)}, f32[1,4096]{1,0:T(1,128)S(1)}) custom-call(bf16[16,4096]{1,0:T(8,128)(2,1)S(1)} %get-tuple-element.19.unit_ref, f32[16,512]{1,0:T(8,128)S(1)} %get-tuple-element.20.cos_ref, f32[16,512]{1,0:T(8,128)S(1)} %get-tuple-element.21.weight_ref, ...), custom_call_target="tpu_custom_call" | custom-call | flops 536870912 | bytes 4194304 | tf_op jit(solution)/shard_map/mix/pallas_call | solution.py:254
  29.7 0.9 %all-to-all-done.1.sums_ref = f32[16,1,16]{2,1,0:T(1,128)S(1)} async-done(((f32[16,1,16]{2,1,0:T(1,128)}), f32[16,1,16]{2,1,0:T(1,128)S(1)}, u32[]{:S(2)}, u32[]{:S(2)}) %all-to-all-start.1) | async-done | bytes 1056 | tf_op jit(solution)/shard_map/all_to_all | solution.py:205
  30.5 1.3 %partial.1 = (bf16[16,2,4096]{2,1,0:T(2,128)(2,1)}, f32[16,1]{1,0:T(8,128)S(1)}) custom-call(f32[16,1,16]{2,1,0:T(1,128)S(1)} %all-to-all-done.1.sums_ref, f32[16,4096]{1,0:T(8,128)S(1)} %get-tuple-element.24.by_weight_ref, f32[16,4096]{1,0:T(8,128)S(1)} %get-tuple-element.25.by_teach_ref, f32[16,4096]{1,0:T(8,128)S(1)} %get-tuple-element.26.gain_weight_ref, ...), custom_call_target="tpu_custom_call" | custom-call | tf_op jit(solution)/shard_map/partial/pallas_call | solution.py:266
  31.8 4.2 %all-to-all-start.2 = ((bf16[16,2,4096]{2,1,0:T(2,128)(2,1)}), bf16[16,2,4096]{2,1,0:T(2,128)(2,1)S(1)}, u32[]{:S(2)}, u32[]{:S(2)}) async-start(bf16[16,2,4096]{2,1,0:T(2,128)(2,1)} %get-tuple-element.30), calls=%async_computation.2 | async-start | bytes 524288 | tf_op jit(solution)/shard_map/all_to_all | solution.py:205
  36.0 0.0 copy-done
  36.0 0.0 copy-done.3
  36.1 0.0 copy-start.2
  36.1 6.6 %d_passages.1 = f32[512,4096]{1,0:T(8,128)} custom-call(bf16[16,4096]{1,0:T(8,128)(2,1)S(1)} %get-tuple-element.19.unit_ref, f32[1,4096]{1,0:T(1,128)S(1)} %bitcast.4, f32[16,512]{1,0:T(8,128)S(1)} %get-tuple-element.20.cos_ref, f32[16,512]{1,0:T(8,128)S(1)} %get-tuple-element.21.weight_ref, f32[16,512]{1,0:T(8,128)S(1)} %get-tuple-element.22.teach_ref, ...), custom_call_target="tpu_custom_call" | custom-call | flops 134217728 | bytes 12582912 | tf_op jit(solution)/shard_map/d_passages/pallas_call | solution.py:277
  42.7 1.1 %all-to-all-done.2.got_ref = bf16[16,2,4096]{2,1,0:T(2,128)(2,1)S(1)} async-done(((bf16[16,2,4096]{2,1,0:T(2,128)(2,1)}), bf16[16,2,4096]{2,1,0:T(2,128)(2,1)S(1)}, u32[]{:S(2)}, u32[]{:S(2)}) %all-to-all-start.2) | async-done | bytes 262176 | tf_op jit(solution)/shard_map/all_to_all | solution.py:205
  43.8 0.0 copy-done.2
  43.8 1.0 %final.1 = (f32[1,4096]{1,0:T(1,128)}, f32[1,4096]{1,0:T(1,128)}) custom-call(bf16[16,2,4096]{2,1,0:T(2,128)(2,1)S(1)} %all-to-all-done.2.got_ref, bf16[1,4096]{1,0:T(2,128)(2,1)S(1)} %copy-done.2, f32[1,4096]{1,0:T(1,128)S(1)} %bitcast.5), custom_call_target="tpu_custom_call" | custom-call | tf_op jit(solution)/shard_map/final/pallas_call | solution.py:300
Async XLA Ops:
  0.6 0.7 %copy-start.1 = (bf16[1,4096]{1,0:T(2,128)(2,1)S(1)}, bf16[1,4096]{1,0:T(2,128)(2,1)}, u32[]{:S(2)}) copy-start(bf16[1,4096]{1,0:T(2,128)(2,1)} %queries_ref.3) | copy-start | bytes 24580
  1.4 0.7 %copy-start.4 = (s32[1,128]{1,0:T(1,128)S(1)}, s32[1,128]{1,0:T(1,128)}, u32[]{:S(2)}) copy-start(s32[1,128]{1,0:T(1,128)} %candidates_ref.1) | copy-start | bytes 1540
  2.0 0.7 %copy-start.5 = (s32[1,128]{1,0:T(1,128)S(1)}, s32[1,128]{1,0:T(1,128)}, u32[]{:S(2)}) copy-start(s32[1,128]{1,0:T(1,128)} %teacher_ref.1) | copy-start | bytes 1540
  3.4 13.5 %all-to-all-start = ((bf16[16,2,2304]{2,1,0:T(2,128)(2,1)}), bf16[16,2,2304]{2,1,0:T(2,128)(2,1)S(1)}, u32[]{:S(2)}, u32[]{:S(2)}) async-start(bf16[16,2,2304]{2,1,0:T(2,128)(2,1)} %pack.1), calls=%async_computation | async-start | bytes 294912 | tf_op jit(solution)/shard_map/all_to_all | solution.py:205
  21.9 8.6 %all-to-all-start.1 = ((f32[16,1,16]{2,1,0:T(1,128)}), f32[16,1,16]{2,1,0:T(1,128)S(1)}, u32[]{:S(2)}, u32[]{:S(2)}) async-start(f32[16,1,16]{2,1,0:T(1,128)} %get-tuple-element.23), calls=%async_computation.1 | async-start | bytes 16384 | tf_op jit(solution)/shard_map/all_to_all | solution.py:205
  26.5 9.6 %copy-start = (f32[4096]{0:T(1024)S(1)}, f32[4096]{0:T(1024)}, u32[]{:S(2)}) copy-start(f32[4096]{0:T(1024)} %param.7) | copy-start | bytes 49156
  26.5 9.6 %copy-start.3 = (f32[1,512]{1,0:T(1,128)S(1)}, f32[1,512]{1,0:T(1,128)}, u32[]{:S(2)}) copy-start(f32[1,512]{1,0:T(1,128)} %get-tuple-element.29.norm_ref) | copy-start | bytes 6148
  31.8 12.0 %all-to-all-start.2 = ((bf16[16,2,4096]{2,1,0:T(2,128)(2,1)}), bf16[16,2,4096]{2,1,0:T(2,128)(2,1)S(1)}, u32[]{:S(2)}, u32[]{:S(2)}) async-start(bf16[16,2,4096]{2,1,0:T(2,128)(2,1)} %get-tuple-element.30), calls=%async_computation.2 | async-start | bytes 524288 | tf_op jit(solution)/shard_map/all_to_all | solution.py:205
  36.1 7.7 %copy-start.2 = (bf16[1,4096]{1,0:T(2,128)(2,1)S(1)}, bf16[1,4096]{1,0:T(2,128)(2,1)}, u32[]{:S(2)}) copy-start(bf16[1,4096]{1,0:T(2,128)(2,1)} %queries_ref.3) | copy-start | bytes 24580

commit v6 on v5

--- a/solution.py
+++ b/solution.py
@@ -12,6 +12,7 @@
 teacher_div = 2.0
 coef_scale = loss_scale * score_scale
 chunks = 4
+pieces = 8
 f32 = jnp.float32
 bf16 = jnp.bfloat16
 vmem = pltpu.VMEM
@@ -42,29 +43,27 @@
 
 
 def pack_kernel(queries_ref, candidates_ref, teacher_ref, out_ref):
-    half = queries_ref.shape[1] // 2
+    ids = candidates_ref[...]
+    listed = ids.shape[1]
+    width = queries_ref.shape[1] // 8
     query = queries_ref[...].astype(f32)
-    ids = candidates_ref[...]
-    first = jnp.concatenate(
-        [query[:, :half], (ids >> 8).astype(f32), (ids & 255).astype(f32)], axis=1
-    )
-    second = jnp.concatenate(
-        [query[:, half:], teacher_ref[...].astype(f32), jnp.zeros(ids.shape, f32)], axis=1
-    )
-    both = jnp.concatenate([first, second], axis=0).astype(bf16)
+    query = jnp.concatenate([query[:, k * width : (k + 1) * width] for k in range(8)], axis=0)
+    lists = [(ids >> 8).astype(f32), (ids & 255).astype(f32), teacher_ref[...].astype(f32)]
+    lists = jnp.concatenate([*lists, jnp.zeros((5, listed), f32)], axis=0)
+    both = jnp.concatenate([query, lists], axis=1).astype(bf16)
     out_ref[...] = jnp.broadcast_to(both[None], out_ref.shape)
 
 
 def table_kernel(passages_ref, gain_ref, table_ref, inverse_ref, raw, held, sems_in, sems_out):
     gain = gain_ref[...]
-    chunk = raw.shape[0] // chunks
-    copies_in, copies_out = [], []
-    for k in range(chunks):
+    chunk = raw.shape[0] // pieces
+    copies_in, copies_out, inverses = [], [], []
+    for k in range(pieces):
         part = pl.ds(k * chunk, chunk)
         copies_in.append(pltpu.make_async_copy(passages_ref.at[part], raw.at[part], sems_in.at[k]))
         copies_out.append(pltpu.make_async_copy(held.at[part], table_ref.at[part], sems_out.at[k]))
         copies_in[-1].start()
-    for k in range(chunks):
+    for k in range(pieces):
         part = pl.ds(k * chunk, chunk)
         copies_in[k].wait()
         lifted = raw[part, :].astype(f32) * gain
@@ -72,17 +71,19 @@
         inverse = 1.0 / norm
         held[part, :] = (lifted * inverse).astype(bf16)
         copies_out[k].start()
-        inverse_ref[:, part] = jnp.transpose(jnp.broadcast_to(inverse, (chunk, 128)))[:1, :]
-    for k in range(chunks):
+        inverses.append(inverse)
+    inverse = jnp.concatenate(inverses, axis=0)
+    inverse_ref[...] = jnp.transpose(jnp.broadcast_to(inverse, (inverse.shape[0], 128)))[:1, :]
+    for k in range(pieces):
         copies_out[k].wait()
 
 
-def score_kernel(got_ref, start_ref, table_ref, cos_ref, weight_ref, teach_ref, sums_ref, unit_ref, held, sems):
-    queries = got_ref.shape[0]
-    half = got_ref.shape[2] - 256
-    listed = 128
-    rows = held.shape[0]
-    chunk = held.shape[1] // chunks
+def score_kernel(
+    got_ref, start_ref, table_ref, cos_ref, weight_ref, teach_ref, sums_ref, unit_ref, held, wide, sems
+):
+    queries = unit_ref.shape[0]
+    rows, width = held.shape
+    chunk = width // chunks
     copies = []
     for k in range(chunks):
         part = pl.ds(k * chunk, chunk)
@@ -90,13 +91,18 @@
             pltpu.make_async_copy(table_ref.at[pl.ds(0, rows), part], held.at[:, part], sems.at[k])
         )
         copies[-1].start()
-    got = got_ref[...].astype(f32)
-    query = jnp.concatenate([got[:, 0, :half], got[:, 1, :half]], axis=1)
+    listed = wide.shape[2]
+    tiles = wide.shape[0]
+    for j in range(tiles):
+        wide[j] = got_ref[:, j * listed : (j + 1) * listed].astype(f32)
+    every = [[wide[j, pl.ds(k, queries, stride=8), :] for j in range(tiles)] for k in range(8)]
+    query = jnp.concatenate([x for row in every for x in row[:-1]], axis=1)
     norm = jnp.sqrt(jnp.sum(query * query, axis=1, keepdims=True))
-    unit = (query / norm).astype(bf16)
-    unit_ref[...] = unit
-    ids = (got[:, 0, half : half + listed] * 256.0 + got[:, 0, half + listed :]).astype(jnp.int32)
-    marks = jnp.exp(got[:, 1, half : half + listed] * (1.0 / teacher_div))
+    unit = query / norm
+    unit_ref[...] = unit.astype(bf16)
+    flipped = jnp.transpose(unit).astype(bf16)
+    ids = (every[0][-1] * 256.0 + every[1][-1]).astype(jnp.int32)
+    marks = jnp.exp(every[2][-1] * (1.0 / teacher_div))
     marks = marks / jnp.sum(marks, axis=1, keepdims=True)
     here = ids - start_ref[0]
     places = lax.broadcasted_iota(jnp.int32, (queries, rows), 1)
@@ -104,11 +110,12 @@
     for c in range(listed):
         teach = teach + jnp.where(here[:, c : c + 1] == places, marks[:, c : c + 1], 0.0)
     teach_ref[...] = teach
-    cos = jnp.zeros((queries, rows), f32)
+    cos = jnp.zeros((rows, queries), f32)
     for k in range(chunks):
         copies[k].wait()
         part = slice(k * chunk, (k + 1) * chunk)
-        cos = cos + dot(unit[:, part], held[:, part], nt_dims)
+        cos = cos + dot(held[:, part], flipped[part, :], nn_dims)
+    cos = jnp.transpose(cos)
     cos_ref[...] = cos
     weight = jnp.where(teach > 0.0, jnp.exp(cos * score_scale), 0.0)
     weight_ref[...] = weight
@@ -161,28 +168,38 @@
     ).astype(bf16)
 
 
-def passage_kernel(unit_ref, gain_ref, cos_ref, weight_ref, teach_ref, inverse_ref, norm_ref, table_ref, out_ref, held, sems):
-    step = pl.program_id(0)
-    chunk = out_ref.shape[0]
-    part = pl.ds(pl.multiple_of(step * chunk, chunk), chunk)
-
-    @pl.when(step == 0)
-    def _():
-        for k in range(chunks):
-            first = pl.ds(k * chunk, chunk)
-            pltpu.make_async_copy(table_ref.at[first], held.at[first], sems.at[k]).start()
-
+def passage_kernel(
+    unit_ref, gain_ref, cos_ref, weight_ref, teach_ref, inverse_ref, norm_ref, table_ref,
+    out_ref, held, made, sems_in, sems_out,
+):
+    rows = held.shape[0]
+    piece = rows // pieces
+    parts = [pl.ds(k * piece, piece) for k in range(pieces)]
+    copies_in = [
+        pltpu.make_async_copy(table_ref.at[part], held.at[part], sems_in.at[k])
+        for k, part in enumerate(parts)
+    ]
+    copies_out = [
+        pltpu.make_async_copy(made.at[part], out_ref.at[part], sems_out.at[k])
+        for k, part in enumerate(parts)
+    ]
+    for copy in copies_in:
+        copy.start()
     coef = coef_scale * (weight_ref[...] * inverse_ref[...] - teach_ref[...])
     scaled = coef * norm_ref[...]
     along = jnp.sum(scaled * cos_ref[...], axis=0, keepdims=True)
-    column = jnp.transpose(jnp.broadcast_to(along, (128, chunk)))[:, :1]
-    high, low = split(jnp.transpose(scaled))
-    unit = unit_ref[...]
-    whole_part = dot(
-        jnp.concatenate([high, low], axis=1), jnp.concatenate([unit, unit], axis=0), nn_dims
-    )
-    pltpu.make_async_copy(table_ref.at[part], held.at[part], sems.at[step]).wait()
-    out_ref[...] = (whole_part - held[part, :].astype(f32) * column) * gain_ref[...]
+    column = jnp.transpose(jnp.broadcast_to(along, (128, rows)))[:, :1]
+    left = jnp.concatenate(split(jnp.transpose(scaled)), axis=1)
+    right = jnp.concatenate([unit_ref[...], unit_ref[...]], axis=0)
+    gain = gain_ref[...]
+    for k, part in enumerate(parts):
+        inside = slice(k * piece, (k + 1) * piece)
+        mixed = dot(left[inside], right, nn_dims)
+        copies_in[k].wait()
+        made[part, :] = (mixed - held[part, :].astype(f32) * column[inside]) * gain
+        copies_out[k].start()
+    for copy in copies_out:
+        copy.wait()
 
 
 def final_kernel(got_ref, queries_ref, gain_ref, d_queries_ref, d_gain_ref):
@@ -215,22 +232,21 @@
 
     packed = pl.pallas_call(
         pack_kernel,
-        out_shape=shape((count, 2, width // 2 + 2 * listed), bf16),
-        compiler_params=params(48),
+        out_shape=shape((count, 8, width // 8 + listed), bf16),
+        compiler_params=params(60),
         name="pack",
     )(queries, candidates, teacher)
-    got = exchange(packed)
-
-    block = 128
-    row_block = pl.BlockSpec((block, width), lambda i: (i, 0))
+    got = exchange(packed).reshape(count * 8, width // 8 + listed)
+
     held = pltpu.VMEM((rows, width), bf16)
     sems = pltpu.SemaphoreType.DMA((chunks,))
+    many = pltpu.SemaphoreType.DMA((pieces,))
     table, norms = pl.pallas_call(
         table_kernel,
         in_specs=[outside(), whole()],
         out_specs=[outside(), whole()],
         out_shape=[shape((5 * rows, width), bf16), shape((1, rows))],
-        scratch_shapes=[held, held, sems, sems],
+        scratch_shapes=[held, held, many, many],
         compiler_params=params(60),
         name="table",
         cost_estimate=pl.CostEstimate(
@@ -244,7 +260,7 @@
         score_kernel,
         in_specs=[whole(), pl.BlockSpec(memory_space=pltpu.SMEM), outside()],
         out_shape=[small, small, small, shape((count, 1, count)), shape((count, width), bf16)],
-        scratch_shapes=[held, sems],
+        scratch_shapes=[held, pltpu.VMEM((width // 8 // listed + 1, count * 8, listed), f32), sems],
         compiler_params=params(48),
         name="score",
     )(got, start, table)
@@ -271,25 +287,12 @@
     )(got_sums, by_weight, by_teach, gain_weight, gain_teach)
     got_partial = exchange(partial)
 
-    block = rows // chunks
-    fixed = lambda dims: pl.BlockSpec(dims, lambda i: (0, 0))
-    cols = pl.BlockSpec((count, block), lambda i: (0, i))
     d_passages = pl.pallas_call(
         passage_kernel,
-        grid=(rows // block,),
-        in_specs=[
-            fixed((count, width)),
-            fixed((1, width)),
-            cols,
-            cols,
-            cols,
-            fixed((count, 1)),
-            pl.BlockSpec((1, block), lambda i: (0, i)),
-            outside(),
-        ],
-        out_specs=pl.BlockSpec((block, width), lambda i: (i, 0)),
+        in_specs=[whole()] * 7 + [outside()],
+        out_specs=outside(),
         out_shape=shape((rows, width)),
-        scratch_shapes=[held, sems],
+        scratch_shapes=[held, pltpu.VMEM((rows, width), f32), many, many],
         compiler_params=params(48),
         name="d_passages",
         cost_estimate=pl.CostEstimate(

time: 45.4 us -> 44.1 us (0.971)
  local copies, waits for them, and re-layouts: 2.04 us -> 0.02 us
  waiting for transfers between devices: 2.25 us -> 3.99 us
  starting transfers between devices: 16.4 us -> 15.8 us
  Pallas kernels: 23.5 us -> 23 us
    unnamed x12 -> x6, local copies, waits for them, and re-layouts: 2.04 us -> 0.02 us
    all_to_all x3, waiting for transfers between devices: 2.25 us -> 3.99 us  [exchange(): lax.all_to_all(x, 'hash', split_axis=0, concat_axis=0, axis_index_groups=...]
    all_to_all x3, starting transfers between devices: 16.4 us -> 15.8 us  [exchange(): lax.all_to_all(x, 'hash', split_axis=0, concat_axis=0, axis_index_groups=...]
    pallas_call x2, Pallas kernels: 7.3 us -> 6.83 us  [the longest x1 5.41 us: local(): pl.pallas_call(passage_kernel, in_specs=[whole()] * 7 + [outside()], out_...]
  transfers between devices with their start and end apart: 3 -> 3, of which waited for: 3 -> 3; matrix products, arithmetic and copies ran while one was open for 0% -> 0% of each run, Pallas kernels for 34% -> 32%
where the time goes in v6:
time: 44.1 us; the launch traced here: 43.5 us
  Pallas kernels  23 us (52%)
  starting transfers between devices  15.8 us (36%)
  waiting for transfers between devices  3.99 us (9%)
  between operations  0.7 us (2%)
    all_to_all x3, starting transfers between devices, exchange(): lax.all_to_all(x, 'hash', split_axis=0, concat_axis=0, axis_index_groups=...  15.8 us
    pallas_call x1, Pallas kernels, local(): pl.pallas_call(passage_kernel, in_specs=[whole()] * 7 + [outside()], out_...  5.41 us
    pallas_call x1, Pallas kernels, local(): pl.pallas_call(table_kernel, in_specs=[outside(), whole()], out_specs=[ou...  5.37 us
    pallas_call x1, Pallas kernels, local(): pl.pallas_call(score_kernel, in_specs=[whole(), pl.BlockSpec(memory_space...  5.3 us
    all_to_all x3, waiting for transfers between devices, exchange(): lax.all_to_all(x, 'hash', split_axis=0, concat_axis=0, axis_index_groups=...  3.99 us
    pallas_call x1, Pallas kernels, local(): pl.pallas_call(mix_kernel, in_specs=[whole(), whole(), whole(), whole(),...  3.18 us
    pallas_call x1, Pallas kernels, local(): pl.pallas_call(pack_kernel, out_shape=shape((count, 8, width // 8 + liste...  1.42 us
    pallas_call x1, Pallas kernels, local(): pl.pallas_call(partial_kernel, out_shape=[shape((count, 2, width), bf16),...  1.28 us
  transfers between devices with their start and end apart: 3, of which 3 were waited for; matrix products, arithmetic and copies ran while one was open for 0% of the time, Pallas kernels for 32%

profile of v6, /device:TPU:0, one launch (start us, length us, event | category | flops | bytes accessed | tf_op | source)
XLA Modules:
  0.0 43.5 jit_solution(270291503001506634)
XLA Ops:
  0.6 1.4 %pack.1 = bf16[16,8,640]{2,1,0:T(8,128)(2,1)} custom-call(bf16[1,4096]{1,0:T(2,128)(2,1)} %queries_ref.3, s32[1,128]{1,0:T(1,128)} %candidates_ref.1, s32[1,128]{1,0:T(1,128)} %teacher_ref.1), custom_call_target="tpu_custom_call" | custom-call | tf_op jit(solution)/shard_map/pack/pallas_call | solution.py:233
  2.1 7.6 %all-to-all-start = ((bf16[16,8,640]{2,1,0:T(8,128)(2,1)}), bf16[16,8,640]{2,1,0:T(8,128)(2,1)S(1)}, u32[]{:S(2)}, u32[]{:S(2)}) async-start(bf16[16,8,640]{2,1,0:T(8,128)(2,1)} %pack.1), calls=%async_computation | async-start | bytes 327680 | tf_op jit(solution)/shard_map/all_to_all | solution.py:222
  9.6 5.4 %table.1 = (bf16[2560,4096]{1,0:T(8,128)(2,1)}, f32[1,512]{1,0:T(1,128)}) custom-call(bf16[512,4096]{1,0:T(8,128)(2,1)} %passages_ref.1, f32[1,4096]{1,0:T(1,128)} %bitcast.5), custom_call_target="tpu_custom_call" | custom-call | flops 12582912 | bytes 8388608 | tf_op jit(solution)/shard_map/table/pallas_call | solution.py:244
  15.0 0.8 %all-to-all-done = bf16[16,8,640]{2,1,0:T(8,128)(2,1)S(1)} async-done(((bf16[16,8,640]{2,1,0:T(8,128)(2,1)}), bf16[16,8,640]{2,1,0:T(8,128)(2,1)S(1)}, u32[]{:S(2)}, u32[]{:S(2)}) %all-to-all-start) | async-done | bytes 163872 | tf_op jit(solution)/shard_map/all_to_all | solution.py:222
  15.8 5.3 %score.1 = (f32[16,512]{1,0:T(8,128)S(1)}, f32[16,512]{1,0:T(8,128)S(1)}, f32[16,512]{1,0:T(8,128)S(1)}, f32[16,1,16]{2,1,0:T(1,128)}, bf16[16,4096]{1,0:T(8,128)(2,1)S(1)}) custom-call(bf16[128,640]{1,0:T(8,128)(2,1)S(1)} %bitcast.4, s32[1]{0:T(128)} %bitcast.1.start_ref, bf16[2560,4096]{1,0:T(8,128)(2,1)} %get-tuple-element.18.table_ref), custom_call_target="tpu_custom_call" | custom-call | tf_op jit(solution)/shard_map/score/pallas_call | solution.py:259
  21.1 4.0 %all-to-all-start.1 = ((f32[16,1,16]{2,1,0:T(1,128)}), f32[16,1,16]{2,1,0:T(1,128)S(1)}, u32[]{:S(2)}, u32[]{:S(2)}) async-start(f32[16,1,16]{2,1,0:T(1,128)} %get-tuple-element.23), calls=%async_computation.1 | async-start | bytes 16384 | tf_op jit(solution)/shard_map/all_to_all | solution.py:222
  25.2 0.0 copy-start
  25.2 0.0 copy-start.2
  25.2 3.2 %mix.1 = (f32[16,4096]{1,0:T(8,128)S(1)}, f32[16,4096]{1,0:T(8,128)S(1)}, f32[16,4096]{1,0:T(8,128)S(1)}, f32[1,4096]{1,0:T(1,128)S(1)}) custom-call(bf16[16,4096]{1,0:T(8,128)(2,1)S(1)} %get-tuple-element.19.unit_ref, f32[16,512]{1,0:T(8,128)S(1)} %get-tuple-element.20.cos_ref, f32[16,512]{1,0:T(8,128)S(1)} %get-tuple-element.21.weight_ref, ...), custom_call_target="tpu_custom_call" | custom-call | flops 536870912 | bytes 4194304 | tf_op jit(solution)/shard_map/mix/pallas_call | solution.py:270
  28.4 0.9 %all-to-all-done.1.sums_ref = f32[16,1,16]{2,1,0:T(1,128)S(1)} async-done(((f32[16,1,16]{2,1,0:T(1,128)}), f32[16,1,16]{2,1,0:T(1,128)S(1)}, u32[]{:S(2)}, u32[]{:S(2)}) %all-to-all-start.1) | async-done | bytes 1056 | tf_op jit(solution)/shard_map/all_to_all | solution.py:222
  29.2 1.3 %partial.1 = (bf16[16,2,4096]{2,1,0:T(2,128)(2,1)}, f32[16,1]{1,0:T(8,128)S(1)}) custom-call(f32[16,1,16]{2,1,0:T(1,128)S(1)} %all-to-all-done.1.sums_ref, f32[16,4096]{1,0:T(8,128)S(1)} %get-tuple-element.24.by_weight_ref, f32[16,4096]{1,0:T(8,128)S(1)} %get-tuple-element.25.by_teach_ref, f32[16,4096]{1,0:T(8,128)S(1)} %get-tuple-element.26.gain_weight_ref, ...), custom_call_target="tpu_custom_call" | custom-call | tf_op jit(solution)/shard_map/partial/pallas_call | solution.py:282
  30.5 4.2 %all-to-all-start.2 = ((bf16[16,2,4096]{2,1,0:T(2,128)(2,1)}), bf16[16,2,4096]{2,1,0:T(2,128)(2,1)S(1)}, u32[]{:S(2)}, u32[]{:S(2)}) async-start(bf16[16,2,4096]{2,1,0:T(2,128)(2,1)} %get-tuple-element.30), calls=%async_computation.2 | async-start | bytes 524288 | tf_op jit(solution)/shard_map/all_to_all | solution.py:222
  34.7 0.0 copy-done
  34.7 0.0 copy-done.2
  34.7 0.0 copy-start.1
  34.8 5.4 %d_passages.1 = f32[512,4096]{1,0:T(8,128)} custom-call(bf16[16,4096]{1,0:T(8,128)(2,1)S(1)} %get-tuple-element.19.unit_ref, f32[1,4096]{1,0:T(1,128)S(1)} %bitcast.6, f32[16,512]{1,0:T(8,128)S(1)} %get-tuple-element.20.cos_ref, f32[16,512]{1,0:T(8,128)S(1)} %get-tuple-element.21.weight_ref, f32[16,512]{1,0:T(8,128)S(1)} %get-tuple-element.22.teach_ref, ...), custom_call_target="tpu_custom_call" | custom-call | flops 134217728 | bytes 12582912 | tf_op jit(solution)/shard_map/d_passages/pallas_call | solution.py:290
  40.2 2.3 %all-to-all-done.2.got_ref = bf16[16,2,4096]{2,1,0:T(2,128)(2,1)S(1)} async-done(((bf16[16,2,4096]{2,1,0:T(2,128)(2,1)}), bf16[16,2,4096]{2,1,0:T(2,128)(2,1)S(1)}, u32[]{:S(2)}, u32[]{:S(2)}) %all-to-all-start.2) | async-done | bytes 262176 | tf_op jit(solution)/shard_map/all_to_all | solution.py:222
  42.5 0.0 copy-done.1
  42.5 1.0 %final.1 = (f32[1,4096]{1,0:T(1,128)}, f32[1,4096]{1,0:T(1,128)}) custom-call(bf16[16,2,4096]{2,1,0:T(2,128)(2,1)S(1)} %all-to-all-done.2.got_ref, bf16[1,4096]{1,0:T(2,128)(2,1)S(1)} %copy-done.1, f32[1,4096]{1,0:T(1,128)S(1)} %bitcast.7), custom_call_target="tpu_custom_call" | custom-call | tf_op jit(solution)/shard_map/final/pallas_call | solution.py:303
Async XLA Ops:
  2.1 13.7 %all-to-all-start = ((bf16[16,8,640]{2,1,0:T(8,128)(2,1)}), bf16[16,8,640]{2,1,0:T(8,128)(2,1)S(1)}, u32[]{:S(2)}, u32[]{:S(2)}) async-start(bf16[16,8,640]{2,1,0:T(8,128)(2,1)} %pack.1), calls=%async_computation | async-start | bytes 327680 | tf_op jit(solution)/shard_map/all_to_all | solution.py:222
  21.1 8.1 %all-to-all-start.1 = ((f32[16,1,16]{2,1,0:T(1,128)}), f32[16,1,16]{2,1,0:T(1,128)S(1)}, u32[]{:S(2)}, u32[]{:S(2)}) async-start(f32[16,1,16]{2,1,0:T(1,128)} %get-tuple-element.23), calls=%async_computation.1 | async-start | bytes 16384 | tf_op jit(solution)/shard_map/all_to_all | solution.py:222
  25.2 9.6 %copy-start = (f32[4096]{0:T(1024)S(1)}, f32[4096]{0:T(1024)}, u32[]{:S(2)}) copy-start(f32[4096]{0:T(1024)} %param.7) | copy-start | bytes 49156
  25.2 9.6 %copy-start.2 = (f32[1,512]{1,0:T(1,128)S(1)}, f32[1,512]{1,0:T(1,128)}, u32[]{:S(2)}) copy-start(f32[1,512]{1,0:T(1,128)} %get-tuple-element.29.norm_ref) | copy-start | bytes 6148
  30.5 12.0 %all-to-all-start.2 = ((bf16[16,2,4096]{2,1,0:T(2,128)(2,1)}), bf16[16,2,4096]{2,1,0:T(2,128)(2,1)S(1)}, u32[]{:S(2)}, u32[]{:S(2)}) async-start(bf16[16,2,4096]{2,1,0:T(2,128)(2,1)} %get-tuple-element.30), calls=%async_computation.2 | async-start | bytes 524288 | tf_op jit(solution)/shard_map/all_to_all | solution.py:222
  34.7 7.7 %copy-start.1 = (bf16[1,4096]{1,0:T(2,128)(2,1)S(1)}, bf16[1,4096]{1,0:T(2,128)(2,1)}, u32[]{:S(2)}) copy-start(bf16[1,4096]{1,0:T(2,128)(2,1)} %queries_ref.3) | copy-start | bytes 24580

commit v7 on v6

--- a/solution.py
+++ b/solution.py
@@ -30,6 +30,10 @@
     return high, low
 
 
+def member_order(count):
+    return [(i + count // 2 + 1) % count for i in range(count)]
+
+
 def params(megabytes):
     return pltpu.CompilerParams(vmem_limit_bytes=megabytes * 1024 * 1024)
 
@@ -42,16 +46,41 @@
     return pl.BlockSpec(memory_space=pltpu.HBM)
 
 
-def pack_kernel(queries_ref, candidates_ref, teacher_ref, out_ref):
+def pack_kernel(rows, queries_ref, candidates_ref, teacher_ref, out_ref):
     ids = candidates_ref[...]
     listed = ids.shape[1]
+    count = out_ref.shape[0]
     width = queries_ref.shape[1] // 8
     query = queries_ref[...].astype(f32)
     query = jnp.concatenate([query[:, k * width : (k + 1) * width] for k in range(8)], axis=0)
-    lists = [(ids >> 8).astype(f32), (ids & 255).astype(f32), teacher_ref[...].astype(f32)]
-    lists = jnp.concatenate([*lists, jnp.zeros((5, listed), f32)], axis=0)
-    both = jnp.concatenate([query, lists], axis=1).astype(bf16)
-    out_ref[...] = jnp.broadcast_to(both[None], out_ref.shape)
+    owner = lax.div(ids, rows)
+    inside = ids - owner * rows
+    marks = jnp.exp(teacher_ref[...].astype(f32) * (1.0 / teacher_div))
+    marks = marks / jnp.sum(marks, axis=1, keepdims=True)
+    high, low = split(marks)
+    values = jnp.concatenate(
+        [
+            (inside >> 8).astype(f32),
+            (inside & 255).astype(f32),
+            high.astype(f32),
+            low.astype(f32),
+            jnp.zeros((4, listed), f32),
+        ],
+        axis=0,
+    )
+    square = (listed, listed)
+    across = jnp.broadcast_to(owner.astype(f32), square)
+    down = jnp.transpose(across)
+    lane = lax.broadcasted_iota(jnp.int32, square, 1)
+    earlier = (across == down) & (lane < lax.broadcasted_iota(jnp.int32, square, 0))
+    rank = jnp.sum(jnp.where(earlier, 1.0, 0.0), axis=1, keepdims=True)
+    places = jnp.where(rank == lane.astype(f32), 1.0, 0.0).astype(bf16)
+    spread = jnp.concatenate(
+        [jnp.where(owner == k, values, 0.0).astype(bf16) for k in member_order(count)], axis=0
+    )
+    lists = dot(spread, places, nn_dims).reshape(count, 8, listed)
+    out_ref[:, :, :width] = jnp.broadcast_to(query.astype(bf16)[None], (count, 8, width))
+    out_ref[:, :, width:] = lists.astype(bf16)
 
 
 def table_kernel(passages_ref, gain_ref, table_ref, inverse_ref, raw, held, sems_in, sems_out):
@@ -79,7 +108,7 @@
 
 
 def score_kernel(
-    got_ref, start_ref, table_ref, cos_ref, weight_ref, teach_ref, sums_ref, unit_ref, held, wide, sems
+    got_ref, table_ref, cos_ref, weight_ref, teach_ref, sums_ref, unit_ref, held, wide, sems
 ):
     queries = unit_ref.shape[0]
     rows, width = held.shape
@@ -101,13 +130,11 @@
     unit = query / norm
     unit_ref[...] = unit.astype(bf16)
     flipped = jnp.transpose(unit).astype(bf16)
-    ids = (every[0][-1] * 256.0 + every[1][-1]).astype(jnp.int32)
-    marks = jnp.exp(every[2][-1] * (1.0 / teacher_div))
-    marks = marks / jnp.sum(marks, axis=1, keepdims=True)
-    here = ids - start_ref[0]
+    here = (every[0][-1] * 256.0 + every[1][-1]).astype(jnp.int32)
+    marks = every[2][-1] + every[3][-1]
     places = lax.broadcasted_iota(jnp.int32, (queries, rows), 1)
     teach = jnp.zeros((queries, rows), f32)
-    for c in range(listed):
+    for c in range(listed // queries):
         teach = teach + jnp.where(here[:, c : c + 1] == places, marks[:, c : c + 1], 0.0)
     teach_ref[...] = teach
     cos = jnp.zeros((rows, queries), f32)
@@ -155,17 +182,26 @@
         gain_teach_ref[:, part] = jnp.sum(terms, axis=0, keepdims=True)
 
 
-def partial_kernel(sums_ref, by_weight_ref, by_teach_ref, gain_weight_ref, gain_teach_ref, out_ref, inverse_ref):
-    queries = by_weight_ref.shape[0]
+def partial_kernel(
+    sums_ref, by_weight_ref, by_teach_ref, gain_weight_ref, gain_teach_ref, out_ref, inverse_ref, laid
+):
+    queries, width = by_weight_ref.shape
     total = jnp.sum(sums_ref[...][:, 0, :], axis=0, keepdims=True)
     inverse = jnp.transpose(jnp.broadcast_to(1.0 / total, (128, queries)))[:, :1]
     inverse_ref[...] = inverse
     partial = coef_scale * (by_weight_ref[...] * inverse - by_teach_ref[...])
     gain_part = jnp.sum(gain_weight_ref[...] * inverse, axis=0, keepdims=True) - gain_teach_ref[...]
     gain_part = coef_scale * gain_part
-    out_ref[...] = jnp.concatenate(
-        [partial[:, None, :], jnp.broadcast_to(gain_part[None], (queries, 1, partial.shape[1]))], axis=1
-    ).astype(bf16)
+    tiles = laid.shape[0]
+    for k in range(width // 128):
+        row, tile = k // tiles, k % tiles
+        part = slice(k * 128, (k + 1) * 128)
+        laid[tile, pl.ds(row, queries, stride=8), :] = partial[:, part]
+        laid[tile, pl.ds(4 + row, queries, stride=8), :] = jnp.broadcast_to(
+            gain_part[:, part], (queries, 128)
+        )
+    for tile in range(tiles):
+        out_ref[:, tile * 128 : (tile + 1) * 128] = laid[tile].astype(bf16)
 
 
 def passage_kernel(
@@ -207,9 +243,9 @@
     query = queries_ref[...].astype(f32)
     norm = jnp.sqrt(jnp.sum(query * query, axis=1, keepdims=True))
     unit = query / norm
-    d_unit = got[:1]
+    d_unit = jnp.concatenate([got[k : k + 1] for k in range(4)], axis=1)
     d_queries_ref[...] = (d_unit - unit * jnp.sum(unit * d_unit, axis=1, keepdims=True)) / norm
-    d_gain_ref[...] = got[1:] / gain_ref[...]
+    d_gain_ref[...] = jnp.concatenate([got[k : k + 1] for k in range(4, 8)], axis=1) / gain_ref[...]
 
 
 def shape(dims, dtype=f32):
@@ -217,8 +253,7 @@
 
 
 def exchange(x):
-    count = lax.axis_size("hash")
-    order = [(i + count // 2 + 1) % count for i in range(count)]
+    order = member_order(lax.axis_size("hash"))
     return lax.all_to_all(
         x, "hash", split_axis=0, concat_axis=0, axis_index_groups=[order], tiled=True
     )
@@ -231,7 +266,7 @@
     gain = gain.reshape(1, width)
 
     packed = pl.pallas_call(
-        pack_kernel,
+        functools.partial(pack_kernel, rows),
         out_shape=shape((count, 8, width // 8 + listed), bf16),
         compiler_params=params(60),
         name="pack",
@@ -254,16 +289,15 @@
         ),
     )(passages, gain)
 
-    start = (lax.axis_index("hash") * rows).astype(jnp.int32).reshape(1)
     small = shape((count, rows))
     cos, weight, teach, sums, unit = pl.pallas_call(
         score_kernel,
-        in_specs=[whole(), pl.BlockSpec(memory_space=pltpu.SMEM), outside()],
+        in_specs=[whole(), outside()],
         out_shape=[small, small, small, shape((count, 1, count)), shape((count, width), bf16)],
         scratch_shapes=[held, pltpu.VMEM((width // 8 // listed + 1, count * 8, listed), f32), sems],
         compiler_params=params(48),
         name="score",
-    )(got, start, table)
+    )(got, table)
     got_sums = exchange(sums)
 
     wide = shape((count, width))
@@ -281,11 +315,12 @@
 
     partial, inverse = pl.pallas_call(
         partial_kernel,
-        out_shape=[shape((count, 2, width), bf16), shape((count, 1))],
+        out_shape=[shape((count * 8, width // 4), bf16), shape((count, 1))],
+        scratch_shapes=[pltpu.VMEM((width // 512, count * 8, 128), f32)],
         compiler_params=params(48),
         name="partial",
     )(got_sums, by_weight, by_teach, gain_weight, gain_teach)
-    got_partial = exchange(partial)
+    got_partial = exchange(partial.reshape(count, 8, width // 4))
 
     d_passages = pl.pallas_call(
         passage_kernel,

time: 44.1 us -> 43.9 us (level)
  no operation moved by 1% of the time
where the time goes in v7:
time: 43.9 us; the launch traced here: 43.4 us
  Pallas kernels  22.9 us (52%)
  starting transfers between devices  15.8 us (36%)
  waiting for transfers between devices  3.99 us (9%)
  between operations  0.7 us (2%)
    all_to_all x3, starting transfers between devices, exchange(): lax.all_to_all(x, 'hash', split_axis=0, concat_axis=0, axis_index_groups=...  15.8 us
    pallas_call x1, Pallas kernels, local(): pl.pallas_call(passage_kernel, in_specs=[whole()] * 7 + [outside()], out_...  5.41 us
    pallas_call x1, Pallas kernels, local(): pl.pallas_call(table_kernel, in_specs=[outside(), whole()], out_specs=[ou...  5.37 us
    pallas_call x1, Pallas kernels, local(): pl.pallas_call(score_kernel, in_specs=[whole(), outside()], out_shape=[sm...  5.23 us
    all_to_all x3, waiting for transfers between devices, exchange(): lax.all_to_all(x, 'hash', split_axis=0, concat_axis=0, axis_index_groups=...  3.99 us
    pallas_call x1, Pallas kernels, local(): pl.pallas_call(mix_kernel, in_specs=[whole(), whole(), whole(), whole(),...  3.18 us
    pallas_call x1, Pallas kernels, local(): pl.pallas_call(functools.partial(pack_kernel, rows), out_shape=shape((cou...  1.71 us
    pallas_call x1, Pallas kernels, local(): pl.pallas_call(partial_kernel, out_shape=[shape((count * 8, width // 4),...  1.1 us
  transfers between devices with their start and end apart: 3, of which 3 were waited for; matrix products, arithmetic and copies ran while one was open for 0% of the time, Pallas kernels for 32%

profile of v7, /device:TPU:0, one launch (start us, length us, event | category | flops | bytes accessed | tf_op | source)
XLA Modules:
  0.0 43.4 jit_solution(14487273304594789779)
XLA Ops:
  0.6 1.7 %pack.1 = bf16[16,8,640]{2,1,0:T(8,128)(2,1)} custom-call(bf16[1,4096]{1,0:T(2,128)(2,1)} %queries_ref.3, s32[1,128]{1,0:T(1,128)} %candidates_ref.1, s32[1,128]{1,0:T(1,128)} %teacher_ref.1), custom_call_target="tpu_custom_call" | custom-call | tf_op jit(solution)/shard_map/pack/pallas_call | solution.py:268
  2.3 7.6 %all-to-all-start = ((bf16[16,8,640]{2,1,0:T(8,128)(2,1)}), bf16[16,8,640]{2,1,0:T(8,128)(2,1)S(1)}, u32[]{:S(2)}, u32[]{:S(2)}) async-start(bf16[16,8,640]{2,1,0:T(8,128)(2,1)} %pack.1), calls=%async_computation | async-start | bytes 327680 | tf_op jit(solution)/shard_map/all_to_all | solution.py:257
  9.9 5.4 %table.1 = (bf16[2560,4096]{1,0:T(8,128)(2,1)}, f32[1,512]{1,0:T(1,128)}) custom-call(bf16[512,4096]{1,0:T(8,128)(2,1)} %passages_ref.1, f32[1,4096]{1,0:T(1,128)} %bitcast.5), custom_call_target="tpu_custom_call" | custom-call | flops 12582912 | bytes 8388608 | tf_op jit(solution)/shard_map/table/pallas_call | solution.py:279
  15.3 0.8 %all-to-all-done = bf16[16,8,640]{2,1,0:T(8,128)(2,1)S(1)} async-done(((bf16[16,8,640]{2,1,0:T(8,128)(2,1)}), bf16[16,8,640]{2,1,0:T(8,128)(2,1)S(1)}, u32[]{:S(2)}, u32[]{:S(2)}) %all-to-all-start) | async-done | bytes 163872 | tf_op jit(solution)/shard_map/all_to_all | solution.py:257
  16.1 5.2 %score.1 = (f32[16,512]{1,0:T(8,128)S(1)}, f32[16,512]{1,0:T(8,128)S(1)}, f32[16,512]{1,0:T(8,128)S(1)}, f32[16,1,16]{2,1,0:T(1,128)}, bf16[16,4096]{1,0:T(8,128)(2,1)S(1)}) custom-call(bf16[128,640]{1,0:T(8,128)(2,1)S(1)} %bitcast.4, bf16[2560,4096]{1,0:T(8,128)(2,1)} %get-tuple-element.18.table_ref), custom_call_target="tpu_custom_call" | custom-call | tf_op jit(solution)/shard_map/score/pallas_call | solution.py:293
  21.3 4.0 %all-to-all-start.1 = ((f32[16,1,16]{2,1,0:T(1,128)}), f32[16,1,16]{2,1,0:T(1,128)S(1)}, u32[]{:S(2)}, u32[]{:S(2)}) async-start(f32[16,1,16]{2,1,0:T(1,128)} %get-tuple-element.23), calls=%async_computation.1 | async-start | bytes 16384 | tf_op jit(solution)/shard_map/all_to_all | solution.py:257
  25.4 0.0 copy-start
  25.4 0.0 copy-start.2
  25.4 3.2 %mix.1 = (f32[16,4096]{1,0:T(8,128)S(1)}, f32[16,4096]{1,0:T(8,128)S(1)}, f32[16,4096]{1,0:T(8,128)S(1)}, f32[1,4096]{1,0:T(1,128)S(1)}) custom-call(bf16[16,4096]{1,0:T(8,128)(2,1)S(1)} %get-tuple-element.19.unit_ref, f32[16,512]{1,0:T(8,128)S(1)} %get-tuple-element.20.cos_ref, f32[16,512]{1,0:T(8,128)S(1)} %get-tuple-element.21.weight_ref, ...), custom_call_target="tpu_custom_call" | custom-call | flops 536870912 | bytes 4194304 | tf_op jit(solution)/shard_map/mix/pallas_call | solution.py:304
  28.6 0.9 %all-to-all-done.1.sums_ref = f32[16,1,16]{2,1,0:T(1,128)S(1)} async-done(((f32[16,1,16]{2,1,0:T(1,128)}), f32[16,1,16]{2,1,0:T(1,128)S(1)}, u32[]{:S(2)}, u32[]{:S(2)}) %all-to-all-start.1) | async-done | bytes 1056 | tf_op jit(solution)/shard_map/all_to_all | solution.py:257
  29.4 1.1 %partial.1 = (bf16[128,1024]{1,0:T(8,128)(2,1)}, f32[16,1]{1,0:T(8,128)S(1)}) custom-call(f32[16,1,16]{2,1,0:T(1,128)S(1)} %all-to-all-done.1.sums_ref, f32[16,4096]{1,0:T(8,128)S(1)} %get-tuple-element.24.by_weight_ref, f32[16,4096]{1,0:T(8,128)S(1)} %get-tuple-element.25.by_teach_ref, f32[16,4096]{1,0:T(8,128)S(1)} %get-tuple-element.26.gain_weight_ref, ...), custom_call_target="tpu_custom_call" | custom-call | tf_op jit(solution)/shard_map/partial/pallas_call | solution.py:316
  30.5 4.2 %all-to-all-start.2 = ((bf16[16,8,1024]{2,1,0:T(8,128)(2,1)}), bf16[16,8,1024]{2,1,0:T(8,128)(2,1)S(1)}, u32[]{:S(2)}, u32[]{:S(2)}) async-start(bf16[16,8,1024]{2,1,0:T(8,128)(2,1)} %bitcast.2), calls=%async_computation.2 | async-start | bytes 524288 | tf_op jit(solution)/shard_map/all_to_all | solution.py:257
  34.8 0.0 copy-done
  34.8 0.0 copy-done.2
  34.8 0.0 copy-start.1
  34.8 5.4 %d_passages.1 = f32[512,4096]{1,0:T(8,128)} custom-call(bf16[16,4096]{1,0:T(8,128)(2,1)S(1)} %get-tuple-element.19.unit_ref, f32[1,4096]{1,0:T(1,128)S(1)} %bitcast.6, f32[16,512]{1,0:T(8,128)S(1)} %get-tuple-element.20.cos_ref, f32[16,512]{1,0:T(8,128)S(1)} %get-tuple-element.21.weight_ref, f32[16,512]{1,0:T(8,128)S(1)} %get-tuple-element.22.teach_ref, ...), custom_call_target="tpu_custom_call" | custom-call | flops 134217728 | bytes 12582912 | tf_op jit(solution)/shard_map/d_passages/pallas_call | solution.py:325
  40.2 2.3 %all-to-all-done.2.got_ref = bf16[16,8,1024]{2,1,0:T(8,128)(2,1)S(1)} async-done(((bf16[16,8,1024]{2,1,0:T(8,128)(2,1)}), bf16[16,8,1024]{2,1,0:T(8,128)(2,1)S(1)}, u32[]{:S(2)}, u32[]{:S(2)}) %all-to-all-start.2) | async-done | bytes 262176 | tf_op jit(solution)/shard_map/all_to_all | solution.py:257
  42.5 0.0 copy-done.1
  42.5 0.9 %final.1 = (f32[1,4096]{1,0:T(1,128)}, f32[1,4096]{1,0:T(1,128)}) custom-call(bf16[16,8,1024]{2,1,0:T(8,128)(2,1)S(1)} %all-to-all-done.2.got_ref, bf16[1,4096]{1,0:T(2,128)(2,1)S(1)} %copy-done.1, f32[1,4096]{1,0:T(1,128)S(1)} %bitcast.7), custom_call_target="tpu_custom_call" | custom-call | tf_op jit(solution)/shard_map/final/pallas_call | solution.py:338
Async XLA Ops:
  2.3 13.7 %all-to-all-start = ((bf16[16,8,640]{2,1,0:T(8,128)(2,1)}), bf16[16,8,640]{2,1,0:T(8,128)(2,1)S(1)}, u32[]{:S(2)}, u32[]{:S(2)}) async-start(bf16[16,8,640]{2,1,0:T(8,128)(2,1)} %pack.1), calls=%async_computation | async-start | bytes 327680 | tf_op jit(solution)/shard_map/all_to_all | solution.py:257
  21.3 8.1 %all-to-all-start.1 = ((f32[16,1,16]{2,1,0:T(1,128)}), f32[16,1,16]{2,1,0:T(1,128)S(1)}, u32[]{:S(2)}, u32[]{:S(2)}) async-start(f32[16,1,16]{2,1,0:T(1,128)} %get-tuple-element.23), calls=%async_computation.1 | async-start | bytes 16384 | tf_op jit(solution)/shard_map/all_to_all | solution.py:257
  25.4 9.4 %copy-start = (f32[4096]{0:T(1024)S(1)}, f32[4096]{0:T(1024)}, u32[]{:S(2)}) copy-start(f32[4096]{0:T(1024)} %param.7) | copy-start | bytes 49156
  25.4 9.4 %copy-start.2 = (f32[1,512]{1,0:T(1,128)S(1)}, f32[1,512]{1,0:T(1,128)}, u32[]{:S(2)}) copy-start(f32[1,512]{1,0:T(1,128)} %get-tuple-element.29.norm_ref) | copy-start | bytes 6148
  30.5 12.0 %all-to-all-start.2 = ((bf16[16,8,1024]{2,1,0:T(8,128)(2,1)}), bf16[16,8,1024]{2,1,0:T(8,128)(2,1)S(1)}, u32[]{:S(2)}, u32[]{:S(2)}) async-start(bf16[16,8,1024]{2,1,0:T(8,128)(2,1)} %bitcast.2), calls=%async_computation.2 | async-start | bytes 524288 | tf_op jit(solution)/shard_map/all_to_all | solution.py:257
  34.8 7.7 %copy-start.1 = (bf16[1,4096]{1,0:T(2,128)(2,1)S(1)}, bf16[1,4096]{1,0:T(2,128)(2,1)}, u32[]{:S(2)}) copy-start(bf16[1,4096]{1,0:T(2,128)(2,1)} %queries_ref.3) | copy-start | bytes 24580

commit v8 on v7

v8 whole, which is shorter than its diff:
```python
import functools

import jax
import jax.numpy as jnp
from jax import lax
from jax.experimental import pallas as pl
from jax.experimental.pallas import tpu as pltpu
from jax.sharding import PartitionSpec as P

score_scale = 20.0
loss_scale = 8192.0
teacher_div = 2.0
coef_scale = loss_scale * score_scale
chunks = 4
pieces = 8
f32 = jnp.float32
bf16 = jnp.bfloat16
vmem = pltpu.VMEM
nn_dims = (((1,), (0,)), ((), ()))


def dot(a, b, dims):
    return lax.dot_general(a, b, dims, preferred_element_type=f32)


def split(x):
    high = x.astype(bf16)
    low = (x - high.astype(f32)).astype(bf16)
    return high, low


def member_order(count):
    return [(i + count // 2 + 1) % count for i in range(count)]


def params(megabytes):
    return pltpu.CompilerParams(vmem_limit_bytes=megabytes * 1024 * 1024)


def whole():
    return pl.BlockSpec(memory_space=vmem)


def outside():
    return pl.BlockSpec(memory_space=pltpu.HBM)


def pack_kernel(rows, queries_ref, candidates_ref, teacher_ref, out_ref):
    ids = candidates_ref[...]
    listed = ids.shape[1]
    count = out_ref.shape[0]
    width = queries_ref.shape[1] // 8
    query = queries_ref[...].astype(f32)
    query = jnp.concatenate([query[:, k * width : (k + 1) * width] for k in range(8)], axis=0)
    owner = lax.div(ids, rows)
    inside = ids - owner * rows
    slot = lax.rem(owner + (count - member_order(count)[0]), count)
    marks = jnp.exp(teacher_ref[...].astype(f32) * (1.0 / teacher_div))
    marks = marks / jnp.sum(marks, axis=1, keepdims=True)
    high, low = split(marks)
    values = jnp.concatenate(
        [
            (inside >> 8).astype(f32),
            (inside & 255).astype(f32),
            high.astype(f32),
            low.astype(f32),
            jnp.zeros((listed - 4, listed), f32),
        ],
        axis=0,
    )
    square = (listed, listed)
    across = jnp.broadcast_to(slot.astype(f32), square)
    same = across == jnp.transpose(across)
    earlier = same & (lax.broadcasted_iota(jnp.int32, square, 0) < lax.broadcasted_iota(jnp.int32, square, 1))
    rank = jnp.sum(jnp.where(earlier, 1.0, 0.0), axis=0, keepdims=True)
    place = slot * 8 + rank.astype(jnp.int32)
    spread = jnp.where(place == lax.broadcasted_iota(jnp.int32, (count * 8, listed), 0), 1.0, 0.0)
    lists = dot(spread.astype(bf16), jnp.transpose(values).astype(bf16), nn_dims)
    out_ref[:, :, :width] = jnp.broadcast_to(query.astype(bf16)[None], (count, 8, width))
    out_ref[:, :, width:] = lists.astype(bf16).reshape(count, 8, listed)


def belongs(dims, pair_axis):
    pair = lax.broadcasted_iota(jnp.int32, dims, pair_axis) >> 3
    return pair == lax.broadcasted_iota(jnp.int32, dims, 1 - pair_axis)


def score_kernel(got_ref, gain_ref, passages_ref, raw_ref, unit_ref, cols_ref, rows_ref, sums_ref, held, wide, sems):
    queries, width = unit_ref.shape
    pairs = queries * 8
    rows = held.shape[0]
    chunk = width // chunks
    copies = []
    for k in range(chunks):
        part = pl.ds(k * chunk, chunk)
        copies.append(pltpu.make_async_copy(passages_ref.at[:, part], held.at[:, part], sems.at[k]))
        copies[-1].start()
    tiles = wide.shape[0]
    loaded = [got_ref[:, j * 128 : (j + 1) * 128].astype(f32) for j in range(tiles + 1)]
    squares = sum(x * x for x in loaded[:-1])
    norm = jnp.sum(squares, axis=1, keepdims=True).reshape(queries, 8, 1)
    norm = jnp.sqrt(jnp.broadcast_to(jnp.sum(norm, axis=1, keepdims=True), (queries, 8, 1)))
    norm = norm.reshape(pairs, 1)
    for j in range(tiles):
        wide[j] = loaded[j] / norm
    unit = [wide[j, pl.ds(k, queries, stride=8), :] for k in range(8) for j in range(tiles)]
    unit = jnp.concatenate(unit, axis=1).astype(bf16)
    unit_ref[...] = unit
    lists = loaded[-1]
    inside = lists[:, 0:1] * 256.0 + lists[:, 1:2]
    mark = lists[:, 2:3] + lists[:, 3:4]
    lane = lax.broadcasted_iota(jnp.int32, (pairs, rows), 1).astype(f32)
    pick = jnp.where(inside == lane, 1.0, 0.0).astype(bf16)
    repeat = jnp.where(belongs((pairs, queries), 0), 1.0, 0.0).astype(bf16)
    size = jnp.zeros((pairs, 128), f32)
    along = jnp.zeros((pairs, 128), f32)
    for k in range(chunks):
        part = slice(k * chunk, (k + 1) * chunk)
        repeated = dot(repeat, unit[:, part], nn_dims)
        copies[k].wait()
        raw = dot(pick, held[:, part], nn_dims)
        raw_ref[:, part] = raw.astype(bf16)
        lifted = raw * gain_ref[:, part]
        for j in range(chunk // 128):
            tile = slice(j * 128, (j + 1) * 128)
            size = size + lifted[:, tile] * lifted[:, tile]
            along = along + lifted[:, tile] * repeated[:, tile]
    inverse = 1.0 / jnp.sqrt(jnp.sum(size, axis=1, keepdims=True))
    cos = jnp.sum(along, axis=1, keepdims=True) * inverse
    weight = jnp.where(mark > 0.0, jnp.exp(cos * score_scale), 0.0)
    lane = lax.broadcasted_iota(jnp.int32, (pairs, 128), 1)
    cols = jnp.zeros((pairs, 128), f32)
    for k, column in enumerate((weight, mark, cos, inverse, inside)):
        cols = jnp.where(lane == k, column, cols)
    cols_ref[...] = cols
    flipped = jnp.transpose(cols)[:8]
    rows_ref[...] = flipped
    sums_ref[...] = jnp.broadcast_to(flipped[None, :1], sums_ref.shape)


def mix_kernel(
    unit_ref, gain_ref, raw_ref, cols_ref, rows_ref, by_weight_ref, by_teach_ref, gain_weight_ref, gain_teach_ref
):
    queries, width = unit_ref.shape
    pairs = raw_ref.shape[0]
    chunk = width // chunks
    cos, inverse = cols_ref[:, 2:3], cols_ref[:, 3:4]
    weight, mark = rows_ref[0:1, :], rows_ref[1:2, :]
    own = belongs((queries, pairs), 1)
    by_weight = split(jnp.where(own, weight, 0.0))
    by_mark = split(jnp.where(own, mark, 0.0))
    plain = jnp.concatenate([*by_weight, *by_mark], axis=0)
    repeat = jnp.where(belongs((pairs, queries), 0), 1.0, 0.0).astype(bf16)
    for k in range(chunks):
        part = slice(k * chunk, (k + 1) * chunk)
        row = (raw_ref[:, part].astype(f32) * gain_ref[:, part] * inverse).astype(bf16)
        mixed = dot(plain, row, nn_dims)
        by_weight_ref[:, part] = mixed[:queries] + mixed[queries : 2 * queries]
        by_teach_ref[:, part] = mixed[2 * queries : 3 * queries] + mixed[3 * queries :]
        row = row.astype(f32)
        turned = row * (dot(repeat, unit_ref[:, part], nn_dims) - cos * row)
        mixed = dot(plain, turned.astype(bf16), nn_dims)
        gain_weight_ref[:, part] = mixed[:queries] + mixed[queries : 2 * queries]
        gain_teach_ref[:, part] = jnp.sum(mixed[2 * queries :], axis=0, keepdims=True)


def partial_kernel(sums_ref, by_weight_ref, by_teach_ref, gain_weight_ref, gain_teach_ref, out_ref, laid):
    queries, width = by_weight_ref.shape
    total = jnp.sum(sums_ref[...][:, 0, :], axis=0, keepdims=True)
    own = belongs((queries, total.shape[1]), 1)
    inverse = 1.0 / jnp.sum(jnp.where(own, total, 0.0), axis=1, keepdims=True)
    partial = coef_scale * (by_weight_ref[...] * inverse - by_teach_ref[...])
    gain_part = jnp.sum(gain_weight_ref[...] * inverse, axis=0, keepdims=True) - gain_teach_ref[...]
    gain_part = coef_scale * gain_part
    tiles = laid.shape[0]
    for k in range(width // 128):
        row, tile = k // tiles, k % tiles
        part = slice(k * 128, (k + 1) * 128)
        laid[tile, pl.ds(row, queries, stride=8), :] = partial[:, part]
        laid[tile, pl.ds(4 + row, queries, stride=8), :] = jnp.broadcast_to(
            gain_part[:, part], (queries, 128)
        )
    for tile in range(tiles):
        out_ref[:, tile * 128 : (tile + 1) * 128] = laid[tile].astype(bf16)


def passage_kernel(sums_ref, unit_ref, gain_ref, raw_ref, cols_ref, rows_ref, out_ref, made, sems):
    queries, width = unit_ref.shape
    rows, pairs = made.shape[0], raw_ref.shape[0]
    piece = width // pieces
    weight, mark = cols_ref[:, 0:1], cols_ref[:, 1:2]
    cos, inverse = cols_ref[:, 2:3], cols_ref[:, 3:4]
    total = jnp.sum(sums_ref[...][:, 0, :], axis=0, keepdims=True)
    square = (pairs, pairs)
    alike = (lax.broadcasted_iota(jnp.int32, square, 0) >> 3) == (
        lax.broadcasted_iota(jnp.int32, square, 1) >> 3
    )
    total = jnp.sum(jnp.where(alike, total, 0.0), axis=1, keepdims=True)
    scale = coef_scale * (weight / total - mark) * inverse
    inside = rows_ref[4:5, :]
    spread = lax.broadcasted_iota(jnp.int32, (rows, pairs), 0).astype(f32) == inside
    spread = jnp.where(spread, 1.0, 0.0).astype(bf16)
    spread = jnp.concatenate([spread, spread], axis=1)
    repeat = jnp.where(belongs((pairs, queries), 0), 1.0, 0.0).astype(bf16)
    copies = []
    for k in range(pieces):
        part = slice(k * piece, (k + 1) * piece)
        gain = gain_ref[:, part]
        row = (raw_ref[:, part].astype(f32) * gain * inverse).astype(bf16).astype(f32)
        term = (dot(repeat, unit_ref[:, part], nn_dims) - cos * row) * scale * gain
        made[:, part] = dot(spread, jnp.concatenate(split(term), axis=0), nn_dims)
        part = pl.ds(k * piece, piece)
        copies.append(pltpu.make_async_copy(made.at[:, part], out_ref.at[:, part], sems.at[k]))
        copies[-1].start()
    for copy in copies:
        copy.wait()


def final_kernel(got_ref, queries_ref, gain_ref, d_queries_ref, d_gain_ref):
    got = jnp.sum(got_ref[...].astype(f32), axis=0)
    query = queries_ref[...].astype(f32)
    norm = jnp.sqrt(jnp.sum(query * query, axis=1, keepdims=True))
    unit = query / norm
    d_unit = jnp.concatenate([got[k : k + 1] for k in range(4)], axis=1)
    d_queries_ref[...] = (d_unit - unit * jnp.sum(unit * d_unit, axis=1, keepdims=True)) / norm
    d_gain_ref[...] = jnp.concatenate([got[k : k + 1] for k in range(4, 8)], axis=1) / gain_ref[...]


def shape(dims, dtype=f32):
    return jax.ShapeDtypeStruct(dims, dtype)


def exchange(x):
    order = member_order(lax.axis_size("hash"))
    return lax.all_to_all(
        x, "hash", split_axis=0, concat_axis=0, axis_index_groups=[order], tiled=True
    )


def local(passages, queries, gain, candidates, teacher):
    count = lax.axis_size("hash")
    rows, width = passages.shape
    listed = candidates.shape[1]
    gain = gain.reshape(1, width)

    packed = pl.pallas_call(
        functools.partial(pack_kernel, rows),
        out_shape=shape((count, 8, width // 8 + listed), bf16),
        compiler_params=params(60),
        name="pack",
    )(queries, candidates, teacher)
    got = exchange(packed).reshape(count * 8, width // 8 + listed)

    pairs = count * 8
    raw, unit, cols, lines, sums = pl.pallas_call(
        score_kernel,
        in_specs=[whole(), whole(), outside()],
        out_shape=[
            shape((pairs, width), bf16),
            shape((count, width), bf16),
            shape((pairs, 128)),
            shape((8, pairs)),
            shape((count, 1, pairs)),
        ],
        scratch_shapes=[
            pltpu.VMEM((rows, width), bf16),
            pltpu.VMEM((width // 1024, pairs, 128), f32),
            pltpu.SemaphoreType.DMA((chunks,)),
        ],
        compiler_params=params(57),
        name="score",
    )(got, gain, passages)
    got_sums = exchange(sums)

    wide = shape((count, width))
    by_weight, by_teach, gain_weight, gain_teach = pl.pallas_call(
        mix_kernel,
        out_shape=[wide, wide, wide, shape((1, width))],
        compiler_params=params(48),
        name="mix",
        cost_estimate=pl.CostEstimate(
            flops=16 * count * pairs * width, bytes_accessed=8 * pairs * width, transcendentals=0
        ),
    )(unit, gain, raw, cols, lines)

    partial = pl.pallas_call(
        partial_kernel,
        out_shape=shape((pairs, width // 4), bf16),
        scratch_shapes=[pltpu.VMEM((width // 512, pairs, 128), f32)],
        compiler_params=params(48),
        name="partial",
    )(got_sums, by_weight, by_teach, gain_weight, gain_teach)
    got_partial = exchange(partial.reshape(count, 8, width // 4))

    d_passages = pl.pallas_call(
        passage_kernel,
        in_specs=[whole()] * 6,
        out_specs=outside(),
        out_shape=shape((rows, width)),
        scratch_shapes=[pltpu.VMEM((rows, width), f32), pltpu.SemaphoreType.DMA((pieces,))],
        compiler_params=params(48),
        name="d_passages",
        cost_estimate=pl.CostEstimate(
            flops=4 * pairs * rows * width, bytes_accessed=4 * rows * width, transcendentals=0
        ),
    )(got_sums, unit, gain, raw, cols, lines)

    d_queries, d_gain = pl.pallas_call(
        final_kernel,
        out_shape=[shape((1, width)), shape((1, width))],
        compiler_params=params(48),
        name="final",
    )(got_partial, queries, gain)
    return (d_passages, d_queries, d_gain.reshape(width))


def solution(mesh):
    in_specs = (
        P(("groups", "hash"), None),
        P(("groups", "hash"), None),
        P(),
        P(("groups", "hash"), None),
        P(("groups", "hash"), None),
    )
    out_specs = (P(("groups", "hash"), None), P(("groups", "hash"), None), P("groups"))
    return jax.shard_map(local, mesh=mesh, in_specs=in_specs, out_specs=out_specs, check_vma=False)
```

time: 43.9 us -> 46.5 us (1.059)
  blocking collectives: 0 us -> 13.8 us
  Pallas kernels: 22.9 us -> 13.7 us
  local copies, waits for them, and re-layouts: 0.02 us -> 8.74 us
  starting transfers between devices: 15.8 us -> 8.78 us
  waiting for transfers between devices: 3.99 us -> 0.01 us
    all_to_all x0 -> x1, blocking collectives: none -> 13.8 us  [exchange(): lax.all_to_all(x, 'hash', split_axis=0, concat_axis=0, axis_index_groups=...]
    pallas_call x5 -> x4, Pallas kernels: 20.3 us -> 11.1 us  [the longest x1 4.66 us: local(): pl.pallas_call(score_kernel, in_specs=[whole(), whole(), outside()], out_...]
    unnamed x6 -> x24, local copies, waits for them, and re-layouts: 0.02 us -> 8.74 us
    all_to_all x3 -> x2, starting transfers between devices: 15.8 us -> 8.78 us  [exchange(): lax.all_to_all(x, 'hash', split_axis=0, concat_axis=0, axis_index_groups=...]
    all_to_all x3 -> x2, waiting for transfers between devices: 3.99 us -> 0.01 us  [exchange(): lax.all_to_all(x, 'hash', split_axis=0, concat_axis=0, axis_index_groups=...]
  transfers between devices with their start and end apart: 3 -> 2, of which waited for: 3 -> 0; matrix products, arithmetic and copies ran while one was open for 0% -> 0% of each run, Pallas kernels for 32% -> 12%
where the time goes in v8:
time: 46.5 us; the launch traced here: 45.7 us
  blocking collectives  13.8 us (30%)
  Pallas kernels  13.7 us (29%)
  starting transfers between devices  8.78 us (19%)
  local copies, waits for them, and re-layouts  8.74 us (19%)
  between operations  0.71 us (2%)
    all_to_all x1, blocking collectives, exchange(): lax.all_to_all(x, 'hash', split_axis=0, concat_axis=0, axis_index_groups=...  13.8 us
    all_to_all x2, starting transfers between devices, exchange(): lax.all_to_all(x, 'hash', split_axis=0, concat_axis=0, axis_index_groups=...  8.78 us
    unnamed x24, local copies, waits for them, and re-layouts  8.74 us
    pallas_call x1, Pallas kernels, local(): pl.pallas_call(score_kernel, in_specs=[whole(), whole(), outside()], out_...  4.66 us
    pallas_call x1, Pallas kernels, local(): pl.pallas_call(passage_kernel, in_specs=[whole()] * 6, out_specs=outside(...  3.97 us
    pallas_call x1, Pallas kernels, local(): pl.pallas_call(functools.partial(pack_kernel, rows), out_shape=shape((cou...  1.72 us
    pallas_call x1, Pallas kernels, local(): pl.pallas_call(mix_kernel, out_shape=[wide, wide, wide, shape((1, width))...  1.37 us
    pallas_call x1, Pallas kernels, local(): pl.pallas_call(partial_kernel, out_shape=shape((pairs, width // 4), bf16)...  1.07 us
  transfers between devices with their start and end apart: 2, of which 0 were waited for; matrix products, arithmetic and copies ran while one was open for 0% of the time, Pallas kernels for 12%

profile of v8, /device:TPU:0, one launch (start us, length us, event | category | flops | bytes accessed | tf_op | source)
XLA Modules:
  0.0 45.7 jit_solution(15164944422455182634)
XLA Ops:
  0.6 1.7 %pack.1 = bf16[16,8,640]{2,1,0:T(8,128)(2,1)} custom-call(bf16[1,4096]{1,0:T(2,128)(2,1)} %queries_ref.3, s32[1,128]{1,0:T(1,128)} %candidates_ref.1, s32[1,128]{1,0:T(1,128)} %teacher_ref.1), custom_call_target="tpu_custom_call" | custom-call | tf_op jit(solution)/shard_map/pack/pallas_call | solution.py:246
  2.4 13.8 %all_to_all.15 = bf16[16,8,640]{2,1,0:T(8,128)(2,1)} all-to-all(bf16[16,8,640]{2,1,0:T(8,128)(2,1)} %pack.1), channel_id=1, replica_groups={{9,10,11,12,13,14,15,0,1,2,3,4,5,6,7,8},{25,26,27,28,29,30,31,16,17,18,..., dimensions={0} | all-to-all | bytes 327680 | tf_op jit(solution)/shard_map/all_to_all | solution.py:235
  16.2 0.0 copy-start.6
  16.2 0.0 copy-start.9
  16.2 4.7 %score.1 = (bf16[128,4096]{1,0:T(8,128)(2,1)}, bf16[16,4096]{1,0:T(8,128)(2,1)}, f32[128,128]{1,0:T(8,128)}, f32[8,128]{1,0:T(8,128)}, f32[16,1,128]{2,1,0:T(1,128)}) custom-call(bf16[128,640]{1,0:T(8,128)(2,1)} %bitcast.8, f32[1,4096]{1,0:T(1,128)} %bitcast.4, bf16[512,4096]{1,0:T(8,128)(2,1)} %passages_ref.1), custom_call_target="tpu_custom_call" | custom-call | tf_op jit(solution)/shard_map/score/pallas_call | solution.py:255
  20.9 3.9 %all-to-all-start.1 = ((f32[16,1,128]{2,1,0:T(1,128)}), f32[16,1,128]{2,1,0:T(1,128)S(1)}, u32[]{:S(2)}, u32[]{:S(2)}) async-start(f32[16,1,128]{2,1,0:T(1,128)} %get-tuple-element.14), calls=%async_computation.1 | async-start | bytes 16384 | tf_op jit(solution)/shard_map/all_to_all | solution.py:235
  24.8 0.0 copy-start
  24.8 1.2 %copy-done = bf16[128,4096]{1,0:T(8,128)(2,1)S(1)} copy-done((bf16[128,4096]{1,0:T(8,128)(2,1)S(1)}, bf16[128,4096]{1,0:T(8,128)(2,1)}, u32[]{:S(2)}) %copy-start) | copy-done | bytes 1048600
  26.0 0.0 copy-start.2
  26.0 0.9 %copy-done.2 = bf16[16,4096]{1,0:T(8,128)(2,1)S(1)} copy-done((bf16[16,4096]{1,0:T(8,128)(2,1)S(1)}, bf16[16,4096]{1,0:T(8,128)(2,1)}, u32[]{:S(2)}) %copy-start.2) | copy-done | bytes 131096
  26.9 0.0 copy-start.4
  27.0 0.7 %copy-done.4 = f32[4096]{0:T(1024)S(1)} copy-done((f32[4096]{0:T(1024)S(1)}, f32[4096]{0:T(1024)}, u32[]{:S(2)}) %copy-start.4) | copy-done | bytes 16408
  27.7 0.0 copy-start.7
  27.7 0.8 %copy-done.7 = f32[128,128]{1,0:T(8,128)S(1)} copy-done((f32[128,128]{1,0:T(8,128)S(1)}, f32[128,128]{1,0:T(8,128)}, u32[]{:S(2)}) %copy-start.7) | copy-done | bytes 65560
  28.5 0.0 copy-start.10
  28.5 0.7 %copy-done.10 = f32[8,128]{1,0:T(8,128)S(1)} copy-done((f32[8,128]{1,0:T(8,128)S(1)}, f32[8,128]{1,0:T(8,128)}, u32[]{:S(2)}) %copy-start.10) | copy-done | bytes 4120
  29.2 1.4 %mix.1 = (f32[16,4096]{1,0:T(8,128)S(1)}, f32[16,4096]{1,0:T(8,128)S(1)}, f32[16,4096]{1,0:T(8,128)S(1)}, f32[1,4096]{1,0:T(1,128)S(1)}) custom-call(bf16[16,4096]{1,0:T(8,128)(2,1)S(1)} %copy-done.2, f32[1,4096]{1,0:T(1,128)S(1)} %bitcast.5, bf16[128,4096]{1,0:T(8,128)(2,1)S(1)} %copy-done, f32[128,128]{1,0:T(8,128)S(1)} %copy-done.7, f32[8,128]{1,0:T(8,128)S(1)} %copy-done.10), custom_call_target="tpu_custom_call" | custom-call | flops 134217728 | bytes 4194304 | tf_op jit(solution)/shard_map/mix/pallas_call | solution.py:276
  30.6 0.0 all-to-all-done.1.sums_ref
  30.6 1.1 %partial.1 = bf16[128,1024]{1,0:T(8,128)(2,1)} custom-call(f32[16,1,128]{2,1,0:T(1,128)S(1)} %all-to-all-done.1.sums_ref, f32[16,4096]{1,0:T(8,128)S(1)} %get-tuple-element.19.by_weight_ref, f32[16,4096]{1,0:T(8,128)S(1)} %get-tuple-element.20.by_teach_ref, f32[16,4096]{1,0:T(8,128)S(1)} %get-tuple-element.21.gain_weight_ref, ...), custom_call_target="tpu_custom_call" | custom-call | tf_op jit(solution)/shard_map/partial/pallas_call | solution.py:286
  31.6 4.8 %all-to-all-start.2 = ((bf16[16,8,1024]{2,1,0:T(8,128)(2,1)}), bf16[16,8,1024]{2,1,0:T(8,128)(2,1)S(1)}, u32[]{:S(2)}, u32[]{:S(2)}) async-start(bf16[16,8,1024]{2,1,0:T(8,128)(2,1)} %bitcast.2), calls=%async_computation.2 | async-start | bytes 524288 | tf_op jit(solution)/shard_map/all_to_all | solution.py:235
  36.5 0.0 copy-start.1
  36.5 1.2 %copy-done.1 = bf16[128,4096]{1,0:T(8,128)(2,1)S(1)} copy-done((bf16[128,4096]{1,0:T(8,128)(2,1)S(1)}, bf16[128,4096]{1,0:T(8,128)(2,1)}, u32[]{:S(2)}) %copy-start.1) | copy-done | bytes 1048600
  37.7 0.0 copy-start.3
  37.7 0.9 %copy-done.3 = bf16[16,4096]{1,0:T(8,128)(2,1)S(1)} copy-done((bf16[16,4096]{1,0:T(8,128)(2,1)S(1)}, bf16[16,4096]{1,0:T(8,128)(2,1)}, u32[]{:S(2)}) %copy-start.3) | copy-done | bytes 131096
  38.6 0.0 copy-start.5
  38.6 0.7 %copy-done.5 = f32[4096]{0:T(1024)S(1)} copy-done((f32[4096]{0:T(1024)S(1)}, f32[4096]{0:T(1024)}, u32[]{:S(2)}) %copy-start.5) | copy-done | bytes 16408
  39.3 0.0 copy-start.8
  39.3 0.8 %copy-done.8 = f32[128,128]{1,0:T(8,128)S(1)} copy-done((f32[128,128]{1,0:T(8,128)S(1)}, f32[128,128]{1,0:T(8,128)}, u32[]{:S(2)}) %copy-start.8) | copy-done | bytes 65560
  40.2 0.0 copy-start.11
  40.2 0.7 %copy-done.11 = f32[8,128]{1,0:T(8,128)S(1)} copy-done((f32[8,128]{1,0:T(8,128)S(1)}, f32[8,128]{1,0:T(8,128)}, u32[]{:S(2)}) %copy-start.11) | copy-done | bytes 4120
  40.9 4.0 %d_passages.1 = f32[512,4096]{1,0:T(8,128)} custom-call(f32[16,1,128]{2,1,0:T(1,128)S(1)} %all-to-all-done.1.sums_ref, bf16[16,4096]{1,0:T(8,128)(2,1)S(1)} %copy-done.3, f32[1,4096]{1,0:T(1,128)S(1)} %bitcast.6, bf16[128,4096]{1,0:T(8,128)(2,1)S(1)} %copy-done.1, f32[128,128]{1,0:T(8,128)S(1)} %copy-done.8, f32[8,128]{1,0:T(8,128)S(1)} %copy-done.11), custom_call_target="tpu_custom_call" | custom-call | flops 1073741824 | bytes 8388608 | tf_op jit(solution)/shard_map/d_passages/pallas_call | solution.py:295
  44.8 0.0 all-to-all-done.2.got_ref
  44.9 0.0 copy-done.6
  44.9 0.0 copy-done.9
  44.9 0.9 %final.1 = (f32[1,4096]{1,0:T(1,128)}, f32[1,4096]{1,0:T(1,128)}) custom-call(bf16[16,8,1024]{2,1,0:T(8,128)(2,1)S(1)} %all-to-all-done.2.got_ref, bf16[1,4096]{1,0:T(2,128)(2,1)S(1)} %copy-done.9, f32[1,4096]{1,0:T(1,128)S(1)} %bitcast.7), custom_call_target="tpu_custom_call" | custom-call | tf_op jit(solution)/shard_map/final/pallas_call | solution.py:308
Async XLA Ops:
  16.2 28.7 %copy-start.6 = (f32[4096]{0:T(1024)S(1)}, f32[4096]{0:T(1024)}, u32[]{:S(2)}) copy-start(f32[4096]{0:T(1024)} %param.7) | copy-start | bytes 49156
  16.2 28.7 %copy-start.9 = (bf16[1,4096]{1,0:T(2,128)(2,1)S(1)}, bf16[1,4096]{1,0:T(2,128)(2,1)}, u32[]{:S(2)}) copy-start(bf16[1,4096]{1,0:T(2,128)(2,1)} %queries_ref.3) | copy-start | bytes 24580
  20.9 9.7 %all-to-all-start.1 = ((f32[16,1,128]{2,1,0:T(1,128)}), f32[16,1,128]{2,1,0:T(1,128)S(1)}, u32[]{:S(2)}, u32[]{:S(2)}) async-start(f32[16,1,128]{2,1,0:T(1,128)} %get-tuple-element.14), calls=%async_computation.1 | async-start | bytes 16384 | tf_op jit(solution)/shard_map/all_to_all | solution.py:235
  24.8 1.2 %copy-start = (bf16[128,4096]{1,0:T(8,128)(2,1)S(1)}, bf16[128,4096]{1,0:T(8,128)(2,1)}, u32[]{:S(2)}) copy-start(bf16[128,4096]{1,0:T(8,128)(2,1)} %get-tuple-element.16.raw_ref) | copy-start | bytes 3145732
  26.0 0.9 %copy-start.2 = (bf16[16,4096]{1,0:T(8,128)(2,1)S(1)}, bf16[16,4096]{1,0:T(8,128)(2,1)}, u32[]{:S(2)}) copy-start(bf16[16,4096]{1,0:T(8,128)(2,1)} %get-tuple-element.15.unit_ref) | copy-start | bytes 393220
  26.9 0.7 %copy-start.4 = (f32[4096]{0:T(1024)S(1)}, f32[4096]{0:T(1024)}, u32[]{:S(2)}) copy-start(f32[4096]{0:T(1024)} %param.7) | copy-start | bytes 49156
  27.7 0.8 %copy-start.7 = (f32[128,128]{1,0:T(8,128)S(1)}, f32[128,128]{1,0:T(8,128)}, u32[]{:S(2)}) copy-start(f32[128,128]{1,0:T(8,128)} %get-tuple-element.17.cols_ref) | copy-start | bytes 196612
  28.5 0.7 %copy-start.10 = (f32[8,128]{1,0:T(8,128)S(1)}, f32[8,128]{1,0:T(8,128)}, u32[]{:S(2)}) copy-start(f32[8,128]{1,0:T(8,128)} %get-tuple-element.18.rows_ref) | copy-start | bytes 12292
  31.6 13.2 %all-to-all-start.2 = ((bf16[16,8,1024]{2,1,0:T(8,128)(2,1)}), bf16[16,8,1024]{2,1,0:T(8,128)(2,1)S(1)}, u32[]{:S(2)}, u32[]{:S(2)}) async-start(bf16[16,8,1024]{2,1,0:T(8,128)(2,1)} %bitcast.2), calls=%async_computation.2 | async-start | bytes 524288 | tf_op jit(solution)/shard_map/all_to_all | solution.py:235
  36.5 1.2 %copy-start.1 = (bf16[128,4096]{1,0:T(8,128)(2,1)S(1)}, bf16[128,4096]{1,0:T(8,128)(2,1)}, u32[]{:S(2)}) copy-start(bf16[128,4096]{1,0:T(8,128)(2,1)} %get-tuple-element.16.raw_ref) | copy-start | bytes 3145732
  37.7 0.9 %copy-start.3 = (bf16[16,4096]{1,0:T(8,128)(2,1)S(1)}, bf16[16,4096]{1,0:T(8,128)(2,1)}, u32[]{:S(2)}) copy-start(bf16[16,4096]{1,0:T(8,128)(2,1)} %get-tuple-element.15.unit_ref) | copy-start | bytes 393220
  38.6 0.7 %copy-start.5 = (f32[4096]{0:T(1024)S(1)}, f32[4096]{0:T(1024)}, u32[]{:S(2)}) copy-start(f32[4096]{0:T(1024)} %param.7) | copy-start | bytes 49156
  39.3 0.8 %copy-start.8 = (f32[128,128]{1,0:T(8,128)S(1)}, f32[128,128]{1,0:T(8,128)}, u32[]{:S(2)}) copy-start(f32[128,128]{1,0:T(8,128)} %get-tuple-element.17.cols_ref) | copy-start | bytes 196612
  40.2 0.7 %copy-start.11 = (f32[8,128]{1,0:T(8,128)S(1)}, f32[8,128]{1,0:T(8,128)}, u32[]{:S(2)}) copy-start(f32[8,128]{1,0:T(8,128)} %get-tuple-element.18.rows_ref) | copy-start | bytes 12292

commit v9 on v8

--- a/solution.py
+++ b/solution.py
@@ -85,15 +85,34 @@
     return pair == lax.broadcasted_iota(jnp.int32, dims, 1 - pair_axis)
 
 
-def score_kernel(got_ref, gain_ref, passages_ref, raw_ref, unit_ref, cols_ref, rows_ref, sums_ref, held, wide, sems):
+def stage_kernel(passages_ref, near_ref, far_ref, sems):
+    rows, width = near_ref.shape
+    half = rows // 2
+    copies = []
+    for k in range(2):
+        part = pl.ds(k * half, half)
+        near = passages_ref.at[part, pl.ds(0, width)]
+        far = passages_ref.at[part, pl.ds(width, width)]
+        copies.append(pltpu.make_async_copy(near, near_ref.at[part], sems.at[2 * k]))
+        copies.append(pltpu.make_async_copy(far, far_ref.at[part], sems.at[2 * k + 1]))
+    for copy in copies:
+        copy.start()
+    for copy in copies:
+        copy.wait()
+
+
+def score_kernel(
+    got_ref, gain_ref, near_ref, far_ref, raw_ref, unit_ref, cols_ref, rows_ref, sums_ref, held, wide, sems
+):
     queries, width = unit_ref.shape
     pairs = queries * 8
     rows = held.shape[0]
     chunk = width // chunks
+    half = chunks // 2
     copies = []
-    for k in range(chunks):
+    for k in range(half):
         part = pl.ds(k * chunk, chunk)
-        copies.append(pltpu.make_async_copy(passages_ref.at[:, part], held.at[:, part], sems.at[k]))
+        copies.append(pltpu.make_async_copy(far_ref.at[pl.ds(0, rows), part], held.at[:, part], sems.at[k]))
         copies[-1].start()
     tiles = wide.shape[0]
     loaded = [got_ref[:, j * 128 : (j + 1) * 128].astype(f32) for j in range(tiles + 1)]
@@ -117,8 +136,12 @@
     for k in range(chunks):
         part = slice(k * chunk, (k + 1) * chunk)
         repeated = dot(repeat, unit[:, part], nn_dims)
-        copies[k].wait()
-        raw = dot(pick, held[:, part], nn_dims)
+        if k < half:
+            passages = near_ref[:, part]
+        else:
+            copies[k - half].wait()
+            passages = held[:, slice((k - half) * chunk, (k - half + 1) * chunk)]
+        raw = dot(pick, passages, nn_dims)
         raw_ref[:, part] = raw.astype(bf16)
         lifted = raw * gain_ref[:, part]
         for j in range(chunk // 128):
@@ -252,9 +275,21 @@
     got = exchange(packed).reshape(count * 8, width // 8 + listed)
 
     pairs = count * 8
+    near, far = pl.pallas_call(
+        stage_kernel,
+        in_specs=[outside()],
+        out_specs=[whole(), outside()],
+        out_shape=[shape((rows, width // 2), bf16), shape((10 * rows, width // 2), bf16)],
+        scratch_shapes=[pltpu.SemaphoreType.DMA((4,))],
+        compiler_params=params(48),
+        name="stage",
+        cost_estimate=pl.CostEstimate(
+            flops=0, bytes_accessed=4 * rows * width, transcendentals=0
+        ),
+    )(passages)
     raw, unit, cols, lines, sums = pl.pallas_call(
         score_kernel,
-        in_specs=[whole(), whole(), outside()],
+        in_specs=[whole(), whole(), whole(), outside()],
         out_shape=[
             shape((pairs, width), bf16),
             shape((count, width), bf16),
@@ -263,13 +298,13 @@
             shape((count, 1, pairs)),
         ],
         scratch_shapes=[
-            pltpu.VMEM((rows, width), bf16),
+            pltpu.VMEM((rows, width // 2), bf16),
             pltpu.VMEM((width // 1024, pairs, 128), f32),
-            pltpu.SemaphoreType.DMA((chunks,)),
+            pltpu.SemaphoreType.DMA((chunks // 2,)),
         ],
-        compiler_params=params(57),
+        compiler_params=params(48),
         name="score",
-    )(got, gain, passages)
+    )(got, gain, near, far)
     got_sums = exchange(sums)
 
     wide = shape((count, width))

time: 46.5 us -> 102 us (2.19)
  Pallas kernels: 13.7 us -> 76.5 us
  blocking collectives: 13.8 us -> 0 us
  local copies, waits for them, and re-layouts: 8.74 us -> 0.72 us
  starting transfers between devices: 8.78 us -> 16.6 us
  waiting for transfers between devices: 0.01 us -> 6.46 us
    pallas_call x1 -> x2, Pallas kernels: 4.66 us -> 67.5 us  [the longest x1 64.7 us: local(): pl.pallas_call(stage_kernel, in_specs=[outside()], out_specs=[whole(), ou...]
    all_to_all x1 -> x0, blocking collectives: 13.8 us -> none  [exchange(): lax.all_to_all(x, 'hash', split_axis=0, concat_axis=0, axis_index_groups=...]
    unnamed x24 -> x6, local copies, waits for them, and re-layouts: 8.74 us -> 0.72 us
    all_to_all x2 -> x3, starting transfers between devices: 8.78 us -> 16.6 us  [exchange(): lax.all_to_all(x, 'hash', split_axis=0, concat_axis=0, axis_index_groups=...]
    all_to_all x2 -> x3, waiting for transfers between devices: 0.01 us -> 6.46 us  [exchange(): lax.all_to_all(x, 'hash', split_axis=0, concat_axis=0, axis_index_groups=...]
  transfers between devices with their start and end apart: 2 -> 3, of which waited for: 0 -> 2; matrix products, arithmetic and copies ran while one was open for 0% -> 0% of each run, Pallas kernels for 12% -> 69%
where the time goes in v9:
time: 102 us; the launch traced here: 101 us
  Pallas kernels  76.5 us (75%)
  starting transfers between devices  16.6 us (16%)
  waiting for transfers between devices  6.46 us (6%)
    pallas_call x1, Pallas kernels, local(): pl.pallas_call(stage_kernel, in_specs=[outside()], out_specs=[whole(), ou...  64.7 us
    all_to_all x3, starting transfers between devices, exchange(): lax.all_to_all(x, 'hash', split_axis=0, concat_axis=0, axis_index_groups=...  16.6 us
    all_to_all x3, waiting for transfers between devices, exchange(): lax.all_to_all(x, 'hash', split_axis=0, concat_axis=0, axis_index_groups=...  6.46 us
    pallas_call x1, Pallas kernels, local(): pl.pallas_call(passage_kernel, in_specs=[whole()] * 6, out_specs=outside(...  3.97 us
    pallas_call x1, Pallas kernels, local(): pl.pallas_call(score_kernel, in_specs=[whole(), whole(), whole(), outside...  2.81 us
  transfers between devices with their start and end apart: 3, of which 2 were waited for; matrix products, arithmetic and copies ran while one was open for 0% of the time, Pallas kernels for 69%

profile of v9, /device:TPU:0, one launch (start us, length us, event | category | flops | bytes accessed | tf_op | source)
XLA Modules:
  0.0 101.0 jit_solution(8056815954706575406)
XLA Ops:
  0.6 1.7 %pack.1 = bf16[16,8,640]{2,1,0:T(8,128)(2,1)} custom-call(bf16[1,4096]{1,0:T(2,128)(2,1)} %queries_ref.3, s32[1,128]{1,0:T(1,128)} %candidates_ref.1, s32[1,128]{1,0:T(1,128)} %teacher_ref.1), custom_call_target="tpu_custom_call" | custom-call | tf_op jit(solution)/shard_map/pack/pallas_call | solution.py:269
  2.4 7.6 %all-to-all-start = ((bf16[16,8,640]{2,1,0:T(8,128)(2,1)}), bf16[16,8,640]{2,1,0:T(8,128)(2,1)S(1)}, u32[]{:S(2)}, u32[]{:S(2)}) async-start(bf16[16,8,640]{2,1,0:T(8,128)(2,1)} %pack.1), calls=%async_computation | async-start | bytes 327680 | tf_op jit(solution)/shard_map/all_to_all | solution.py:258
  9.9 64.7 %stage.1 = (bf16[512,2048]{1,0:T(8,128)(2,1)S(1)}, bf16[5120,2048]{1,0:T(8,128)(2,1)}) custom-call(bf16[512,4096]{1,0:T(8,128)(2,1)} %passages_ref.1), custom_call_target="tpu_custom_call" | custom-call | bytes 8388608 | tf_op jit(solution)/shard_map/stage/pallas_call | solution.py:278
  74.6 0.0 all-to-all-done
  74.6 0.0 copy-start
  74.6 0.7 copy-done
  75.3 0.0 copy-start.1
  75.3 2.8 %score.1 = (bf16[128,4096]{1,0:T(8,128)(2,1)S(1)}, bf16[16,4096]{1,0:T(8,128)(2,1)S(1)}, f32[128,128]{1,0:T(8,128)S(1)}, f32[8,128]{1,0:T(8,128)S(1)}, f32[16,1,128]{2,1,0:T(1,128)}) custom-call(bf16[128,640]{1,0:T(8,128)(2,1)S(1)} %bitcast.4, f32[1,4096]{1,0:T(1,128)S(1)} %bitcast.5, bf16[512,2048]{1,0:T(8,128)(2,1)S(1)} %get-tuple-element.16.near_ref, ...), custom_call_target="tpu_custom_call" | custom-call | tf_op jit(solution)/shard_map/score/pallas_call | solution.py:290
  78.1 0.0 copy-start.2
  78.1 4.8 %all-to-all-start.1 = ((f32[16,1,128]{2,1,0:T(1,128)}), f32[16,1,128]{2,1,0:T(1,128)S(1)}, u32[]{:S(2)}, u32[]{:S(2)}) async-start(f32[16,1,128]{2,1,0:T(1,128)} %get-tuple-element.18), calls=%async_computation.1 | async-start | bytes 16384 | tf_op jit(solution)/shard_map/all_to_all | solution.py:258
  83.0 0.0 copy-done.1
  83.0 1.4 %mix.1 = (f32[16,4096]{1,0:T(8,128)S(1)}, f32[16,4096]{1,0:T(8,128)S(1)}, f32[16,4096]{1,0:T(8,128)S(1)}, f32[1,4096]{1,0:T(1,128)S(1)}) custom-call(bf16[16,4096]{1,0:T(8,128)(2,1)S(1)} %get-tuple-element.19.unit_ref, f32[1,4096]{1,0:T(1,128)S(1)} %bitcast.6, bf16[128,4096]{1,0:T(8,128)(2,1)S(1)} %get-tuple-element.20.raw_ref, ...), custom_call_target="tpu_custom_call" | custom-call | flops 134217728 | bytes 4194304 | tf_op jit(solution)/shard_map/mix/pallas_call | solution.py:311
  84.4 2.7 %all-to-all-done.1.sums_ref = f32[16,1,128]{2,1,0:T(1,128)S(1)} async-done(((f32[16,1,128]{2,1,0:T(1,128)}), f32[16,1,128]{2,1,0:T(1,128)S(1)}, u32[]{:S(2)}, u32[]{:S(2)}) %all-to-all-start.1) | async-done | bytes 8224 | tf_op jit(solution)/shard_map/all_to_all | solution.py:258
  87.1 1.1 %partial.1 = bf16[128,1024]{1,0:T(8,128)(2,1)} custom-call(f32[16,1,128]{2,1,0:T(1,128)S(1)} %all-to-all-done.1.sums_ref, f32[16,4096]{1,0:T(8,128)S(1)} %get-tuple-element.23.by_weight_ref, f32[16,4096]{1,0:T(8,128)S(1)} %get-tuple-element.24.by_teach_ref, f32[16,4096]{1,0:T(8,128)S(1)} %get-tuple-element.25.gain_weight_ref, ...), custom_call_target="tpu_custom_call" | custom-call | tf_op jit(solution)/shard_map/partial/pallas_call | solution.py:321
  88.1 4.2 %all-to-all-start.2 = ((bf16[16,8,1024]{2,1,0:T(8,128)(2,1)}), bf16[16,8,1024]{2,1,0:T(8,128)(2,1)S(1)}, u32[]{:S(2)}, u32[]{:S(2)}) async-start(bf16[16,8,1024]{2,1,0:T(8,128)(2,1)} %bitcast.2), calls=%async_computation.2 | async-start | bytes 524288 | tf_op jit(solution)/shard_map/all_to_all | solution.py:258
  92.3 4.0 %d_passages.1 = f32[512,4096]{1,0:T(8,128)} custom-call(f32[16,1,128]{2,1,0:T(1,128)S(1)} %all-to-all-done.1.sums_ref, bf16[16,4096]{1,0:T(8,128)(2,1)S(1)} %get-tuple-element.19.unit_ref, f32[1,4096]{1,0:T(1,128)S(1)} %bitcast.7, bf16[128,4096]{1,0:T(8,128)(2,1)S(1)} %get-tuple-element.20.raw_ref, f32[128,128]{1,0:T(8,128)S(1)} %get-tuple-element.21.cols_ref, ...), custom_call_target="tpu_custom_call" | custom-call | flops 1073741824 | bytes 8388608 | tf_op jit(solution)/shard_map/d_passages/pallas_call | solution.py:330
  96.3 3.8 %all-to-all-done.2.got_ref = bf16[16,8,1024]{2,1,0:T(8,128)(2,1)S(1)} async-done(((bf16[16,8,1024]{2,1,0:T(8,128)(2,1)}), bf16[16,8,1024]{2,1,0:T(8,128)(2,1)S(1)}, u32[]{:S(2)}, u32[]{:S(2)}) %all-to-all-start.2) | async-done | bytes 262176 | tf_op jit(solution)/shard_map/all_to_all | solution.py:258
  100.1 0.0 copy-done.2
  100.1 0.9 final.1
Async XLA Ops:
  2.4 72.2 %all-to-all-start = ((bf16[16,8,640]{2,1,0:T(8,128)(2,1)}), bf16[16,8,640]{2,1,0:T(8,128)(2,1)S(1)}, u32[]{:S(2)}, u32[]{:S(2)}) async-start(bf16[16,8,640]{2,1,0:T(8,128)(2,1)} %pack.1), calls=%async_computation | async-start | bytes 327680 | tf_op jit(solution)/shard_map/all_to_all | solution.py:258
  74.6 0.7 copy-start
  75.3 7.7 %copy-start.1 = (f32[4096]{0:T(1024)S(1)}, f32[4096]{0:T(1024)}, u32[]{:S(2)}) copy-start(f32[4096]{0:T(1024)} %param.7) | copy-start | bytes 49156
  78.1 22.0 %copy-start.2 = (bf16[1,4096]{1,0:T(2,128)(2,1)S(1)}, bf16[1,4096]{1,0:T(2,128)(2,1)}, u32[]{:S(2)}) copy-start(bf16[1,4096]{1,0:T(2,128)(2,1)} %queries_ref.3) | copy-start | bytes 24580
  78.1 8.9 %all-to-all-start.1 = ((f32[16,1,128]{2,1,0:T(1,128)}), f32[16,1,128]{2,1,0:T(1,128)S(1)}, u32[]{:S(2)}, u32[]{:S(2)}) async-start(f32[16,1,128]{2,1,0:T(1,128)} %get-tuple-element.18), calls=%async_computation.1 | async-start | bytes 16384 | tf_op jit(solution)/shard_map/all_to_all | solution.py:258
  88.1 12.0 %all-to-all-start.2 = ((bf16[16,8,1024]{2,1,0:T(8,128)(2,1)}), bf16[16,8,1024]{2,1,0:T(8,128)(2,1)S(1)}, u32[]{:S(2)}, u32[]{:S(2)}) async-start(bf16[16,8,1024]{2,1,0:T(8,128)(2,1)} %bitcast.2), calls=%async_computation.2 | async-start | bytes 524288 | tf_op jit(solution)/shard_map/all_to_all | solution.py:258

commit v10 on v9

--- a/solution.py
+++ b/solution.py
@@ -85,19 +85,23 @@
     return pair == lax.broadcasted_iota(jnp.int32, dims, 1 - pair_axis)
 
 
-def stage_kernel(passages_ref, near_ref, far_ref, sems):
+def stage_kernel(passages_ref, near_ref, far_ref, held, sems_in, sems_out):
     rows, width = near_ref.shape
-    half = rows // 2
-    copies = []
-    for k in range(2):
-        part = pl.ds(k * half, half)
+    piece = rows // chunks
+    copies_in, copies_out, copies_near = [], [], []
+    for k in range(chunks):
+        part = pl.ds(k * piece, piece)
+        far = passages_ref.at[part, pl.ds(width, width)]
         near = passages_ref.at[part, pl.ds(0, width)]
-        far = passages_ref.at[part, pl.ds(width, width)]
-        copies.append(pltpu.make_async_copy(near, near_ref.at[part], sems.at[2 * k]))
-        copies.append(pltpu.make_async_copy(far, far_ref.at[part], sems.at[2 * k + 1]))
-    for copy in copies:
+        copies_in.append(pltpu.make_async_copy(far, held.at[part], sems_in.at[k]))
+        copies_out.append(pltpu.make_async_copy(held.at[part], far_ref.at[part], sems_out.at[k]))
+        copies_near.append(pltpu.make_async_copy(near, near_ref.at[part], sems_in.at[chunks + k]))
+    for copy in copies_in + copies_near:
         copy.start()
-    for copy in copies:
+    for k in range(chunks):
+        copies_in[k].wait()
+        copies_out[k].start()
+    for copy in copies_near + copies_out:
         copy.wait()
 
 
@@ -161,12 +165,10 @@
     sums_ref[...] = jnp.broadcast_to(flipped[None, :1], sums_ref.shape)
 
 
-def mix_kernel(
-    unit_ref, gain_ref, raw_ref, cols_ref, rows_ref, by_weight_ref, by_teach_ref, gain_weight_ref, gain_teach_ref
-):
-    queries, width = unit_ref.shape
+def mix_kernel(base_ref, unit_ref, gain_ref, raw_ref, cols_ref, rows_ref, out_ref):
+    queries = unit_ref.shape[0]
     pairs = raw_ref.shape[0]
-    chunk = width // chunks
+    chunk = out_ref.shape[1] // 2
     cos, inverse = cols_ref[:, 2:3], cols_ref[:, 3:4]
     weight, mark = rows_ref[0:1, :], rows_ref[1:2, :]
     own = belongs((queries, pairs), 1)
@@ -174,27 +176,32 @@
     by_mark = split(jnp.where(own, mark, 0.0))
     plain = jnp.concatenate([*by_weight, *by_mark], axis=0)
     repeat = jnp.where(belongs((pairs, queries), 0), 1.0, 0.0).astype(bf16)
-    for k in range(chunks):
+    for k in range(2):
         part = slice(k * chunk, (k + 1) * chunk)
-        row = (raw_ref[:, part].astype(f32) * gain_ref[:, part] * inverse).astype(bf16)
+        there = pl.ds(pl.multiple_of(base_ref[0] + k * chunk, 128), chunk)
+        row = (raw_ref[:, there].astype(f32) * gain_ref[:, there] * inverse).astype(bf16)
         mixed = dot(plain, row, nn_dims)
-        by_weight_ref[:, part] = mixed[:queries] + mixed[queries : 2 * queries]
-        by_teach_ref[:, part] = mixed[2 * queries : 3 * queries] + mixed[3 * queries :]
+        out_ref[:queries, part] = mixed[:queries] + mixed[queries : 2 * queries]
+        out_ref[queries : 2 * queries, part] = mixed[2 * queries : 3 * queries] + mixed[3 * queries :]
         row = row.astype(f32)
-        turned = row * (dot(repeat, unit_ref[:, part], nn_dims) - cos * row)
+        turned = row * (dot(repeat, unit_ref[:, there], nn_dims) - cos * row)
         mixed = dot(plain, turned.astype(bf16), nn_dims)
-        gain_weight_ref[:, part] = mixed[:queries] + mixed[queries : 2 * queries]
-        gain_teach_ref[:, part] = jnp.sum(mixed[2 * queries :], axis=0, keepdims=True)
-
-
-def partial_kernel(sums_ref, by_weight_ref, by_teach_ref, gain_weight_ref, gain_teach_ref, out_ref, laid):
-    queries, width = by_weight_ref.shape
+        out_ref[2 * queries : 3 * queries, part] = mixed[:queries] + mixed[queries : 2 * queries]
+        last = jnp.sum(mixed[2 * queries :], axis=0, keepdims=True)
+        out_ref[3 * queries :, part] = jnp.broadcast_to(last, (8, chunk))
+
+
+def partial_kernel(sums_ref, mine_ref, sibling_ref, out_ref, total_ref, laid):
+    queries = sums_ref.shape[2] // 8
+    width = mine_ref.shape[1]
     total = jnp.sum(sums_ref[...][:, 0, :], axis=0, keepdims=True)
+    total_ref[...] = total
     own = belongs((queries, total.shape[1]), 1)
     inverse = 1.0 / jnp.sum(jnp.where(own, total, 0.0), axis=1, keepdims=True)
-    partial = coef_scale * (by_weight_ref[...] * inverse - by_teach_ref[...])
-    gain_part = jnp.sum(gain_weight_ref[...] * inverse, axis=0, keepdims=True) - gain_teach_ref[...]
-    gain_part = coef_scale * gain_part
+    both = mine_ref[...] + sibling_ref[...]
+    partial = coef_scale * (both[:queries] * inverse - both[queries : 2 * queries])
+    gain_part = jnp.sum(both[2 * queries : 3 * queries] * inverse, axis=0, keepdims=True)
+    gain_part = coef_scale * (gain_part - both[3 * queries : 3 * queries + 1])
     tiles = laid.shape[0]
     for k in range(width // 128):
         row, tile = k // tiles, k % tiles
@@ -207,18 +214,17 @@
         out_ref[:, tile * 128 : (tile + 1) * 128] = laid[tile].astype(bf16)
 
 
-def passage_kernel(sums_ref, unit_ref, gain_ref, raw_ref, cols_ref, rows_ref, out_ref, made, sems):
+def passage_kernel(total_ref, unit_ref, gain_ref, raw_ref, cols_ref, rows_ref, out_ref, made, sems):
     queries, width = unit_ref.shape
     rows, pairs = made.shape[0], raw_ref.shape[0]
     piece = width // pieces
     weight, mark = cols_ref[:, 0:1], cols_ref[:, 1:2]
     cos, inverse = cols_ref[:, 2:3], cols_ref[:, 3:4]
-    total = jnp.sum(sums_ref[...][:, 0, :], axis=0, keepdims=True)
     square = (pairs, pairs)
     alike = (lax.broadcasted_iota(jnp.int32, square, 0) >> 3) == (
         lax.broadcasted_iota(jnp.int32, square, 1) >> 3
     )
-    total = jnp.sum(jnp.where(alike, total, 0.0), axis=1, keepdims=True)
+    total = jnp.sum(jnp.where(alike, total_ref[...], 0.0), axis=1, keepdims=True)
     scale = coef_scale * (weight / total - mark) * inverse
     inside = rows_ref[4:5, :]
     spread = lax.broadcasted_iota(jnp.int32, (rows, pairs), 0).astype(f32) == inside
@@ -240,13 +246,18 @@
 
 
 def final_kernel(got_ref, queries_ref, gain_ref, d_queries_ref, d_gain_ref):
-    got = jnp.sum(got_ref[...].astype(f32), axis=0)
+    count = got_ref.shape[0]
+    got = got_ref[...].astype(f32).reshape(count // 2, 2, *got_ref.shape[1:])
+    got = jnp.sum(got, axis=0)
+    first = member_order(count)[0] % 2
+    halves = [got[first], got[1 - first]]
     query = queries_ref[...].astype(f32)
     norm = jnp.sqrt(jnp.sum(query * query, axis=1, keepdims=True))
     unit = query / norm
-    d_unit = jnp.concatenate([got[k : k + 1] for k in range(4)], axis=1)
+    d_unit = jnp.concatenate([half[k : k + 1] for half in halves for k in range(4)], axis=1)
     d_queries_ref[...] = (d_unit - unit * jnp.sum(unit * d_unit, axis=1, keepdims=True)) / norm
-    d_gain_ref[...] = jnp.concatenate([got[k : k + 1] for k in range(4, 8)], axis=1) / gain_ref[...]
+    d_gain = jnp.concatenate([half[k : k + 1] for half in halves for k in range(4, 8)], axis=1)
+    d_gain_ref[...] = d_gain / gain_ref[...]
 
 
 def shape(dims, dtype=f32):
@@ -280,7 +291,11 @@
         in_specs=[outside()],
         out_specs=[whole(), outside()],
         out_shape=[shape((rows, width // 2), bf16), shape((10 * rows, width // 2), bf16)],
-        scratch_shapes=[pltpu.SemaphoreType.DMA((4,))],
+        scratch_shapes=[
+            pltpu.VMEM((rows, width // 2), bf16),
+            pltpu.SemaphoreType.DMA((2 * chunks,)),
+            pltpu.SemaphoreType.DMA((chunks,)),
+        ],
         compiler_params=params(48),
         name="stage",
         cost_estimate=pl.CostEstimate(
@@ -307,25 +322,33 @@
     )(got, gain, near, far)
     got_sums = exchange(sums)
 
-    wide = shape((count, width))
-    by_weight, by_teach, gain_weight, gain_teach = pl.pallas_call(
-        mix_kernel,
-        out_shape=[wide, wide, wide, shape((1, width))],
-        compiler_params=params(48),
-        name="mix",
-        cost_estimate=pl.CostEstimate(
-            flops=16 * count * pairs * width, bytes_accessed=8 * pairs * width, transcendentals=0
-        ),
-    )(unit, gain, raw, cols, lines)
-
-    partial = pl.pallas_call(
+    half = width // 2
+
+    def mix(base):
+        return pl.pallas_call(
+            mix_kernel,
+            in_specs=[pl.BlockSpec(memory_space=pltpu.SMEM)] + [whole()] * 5,
+            out_shape=shape((3 * count + 8, half)),
+            compiler_params=params(48),
+            name="mix",
+            cost_estimate=pl.CostEstimate(
+                flops=8 * count * pairs * width, bytes_accessed=4 * pairs * width, transcendentals=0
+            ),
+        )(base.astype(jnp.int32).reshape(1), unit, gain, raw, cols, lines)
+
+    core = lax.axis_index("hash") % 2
+    theirs = mix((1 - core) * half)
+    sibling = lax.ppermute(theirs, "hash", [(i, i ^ 1) for i in range(count)])
+    mine = mix(core * half)
+
+    partial, total = pl.pallas_call(
         partial_kernel,
-        out_shape=shape((pairs, width // 4), bf16),
-        scratch_shapes=[pltpu.VMEM((width // 512, pairs, 128), f32)],
+        out_shape=[shape((pairs, half // 4), bf16), shape((1, pairs))],
+        scratch_shapes=[pltpu.VMEM((half // 512, pairs, 128), f32)],
         compiler_params=params(48),
         name="partial",
-    )(got_sums, by_weight, by_teach, gain_weight, gain_teach)
-    got_partial = exchange(partial.reshape(count, 8, width // 4))
+    )(got_sums, mine, sibling)
+    got_partial = exchange(partial.reshape(count, 8, half // 4))
 
     d_passages = pl.pallas_call(
         passage_kernel,
@@ -338,7 +361,7 @@
         cost_estimate=pl.CostEstimate(
             flops=4 * pairs * rows * width, bytes_accessed=4 * rows * width, transcendentals=0
         ),
-    )(got_sums, unit, gain, raw, cols, lines)
+    )(total, unit, gain, raw, cols, lines)
 
     d_queries, d_gain = pl.pallas_call(
         final_kernel,

time: 102 us -> 41.6 us (0.41)
  Pallas kernels: 76.5 us -> 14.5 us
  waiting for transfers between devices: 6.46 us -> 8.37 us
    pallas_call x1, Pallas kernels: 64.7 us -> 2.75 us  [local(): pl.pallas_call(stage_kernel, in_specs=[outside()], out_specs=[whole(), ou...]
    all_to_all x3, waiting for transfers between devices: 6.46 us -> 8.36 us  [exchange(): lax.all_to_all(x, 'hash', split_axis=0, concat_axis=0, axis_index_groups=...]
    pallas_call x2 -> x3, Pallas kernels: 2.44 us -> 2.44 us  [the longest x2 1.58 us: mix(): pl.pallas_call(mix_kernel, in_specs=[pl.BlockSpec(memory_space=pltpu.SMEM...]
  transfers between devices with their start and end apart: 3 -> 4, of which waited for: 2 -> 3; matrix products, arithmetic and copies ran while one was open for 0% -> 0% of each run, Pallas kernels for 69% -> 18%
where the time goes in v10:
time: 41.6 us; the launch traced here: 41 us
  starting transfers between devices  16.7 us (40%)
  Pallas kernels  14.5 us (35%)
  waiting for transfers between devices  8.37 us (20%)
  local copies, waits for them, and re-layouts  0.73 us (2%)
  between operations  0.71 us (2%)
    all_to_all x3, starting transfers between devices, exchange(): lax.all_to_all(x, 'hash', split_axis=0, concat_axis=0, axis_index_groups=...  16.6 us
    all_to_all x3, waiting for transfers between devices, exchange(): lax.all_to_all(x, 'hash', split_axis=0, concat_axis=0, axis_index_groups=...  8.36 us
    pallas_call x1, Pallas kernels, local(): pl.pallas_call(passage_kernel, in_specs=[whole()] * 6, out_specs=outside(...  3.95 us
    pallas_call x1, Pallas kernels, local(): pl.pallas_call(score_kernel, in_specs=[whole(), whole(), whole(), outside...  2.81 us
    pallas_call x1, Pallas kernels, local(): pl.pallas_call(stage_kernel, in_specs=[outside()], out_specs=[whole(), ou...  2.75 us
    pallas_call x1, Pallas kernels, local(): pl.pallas_call(functools.partial(pack_kernel, rows), out_shape=shape((cou...  1.72 us
    pallas_call x2, Pallas kernels, mix(): pl.pallas_call(mix_kernel, in_specs=[pl.BlockSpec(memory_space=pltpu.SMEM...  1.58 us
    pallas_call x1, Pallas kernels, local(): pl.pallas_call(final_kernel, out_shape=[shape((1, width)), shape((1, widt...  0.87 us
  transfers between devices with their start and end apart: 4, of which 3 were waited for; matrix products, arithmetic and copies ran while one was open for 0% of the time, Pallas kernels for 18%

profile of v10, /device:TPU:0, one launch (start us, length us, event | category | flops | bytes accessed | tf_op | source)
XLA Modules:
  0.0 41.0 jit_solution(15054784173659252503)
XLA Ops:
  0.6 1.7 %pack.1 = bf16[16,8,640]{2,1,0:T(8,128)(2,1)} custom-call(bf16[1,4096]{1,0:T(2,128)(2,1)} %queries_ref.3, s32[1,128]{1,0:T(1,128)} %candidates_ref.1, s32[1,128]{1,0:T(1,128)} %teacher_ref.1), custom_call_target="tpu_custom_call" | custom-call | tf_op jit(solution)/shard_map/pack/pallas_call | solution.py:280
  2.4 7.6 %all-to-all-start = ((bf16[16,8,640]{2,1,0:T(8,128)(2,1)}), bf16[16,8,640]{2,1,0:T(8,128)(2,1)S(1)}, u32[]{:S(2)}, u32[]{:S(2)}) async-start(bf16[16,8,640]{2,1,0:T(8,128)(2,1)} %pack.1), calls=%async_computation | async-start | bytes 327680 | tf_op jit(solution)/shard_map/all_to_all | solution.py:269
  9.9 2.8 %stage.1 = (bf16[512,2048]{1,0:T(8,128)(2,1)S(1)}, bf16[5120,2048]{1,0:T(8,128)(2,1)}) custom-call(bf16[512,4096]{1,0:T(8,128)(2,1)} %passages_ref.1), custom_call_target="tpu_custom_call" | custom-call | bytes 8388608 | tf_op jit(solution)/shard_map/stage/pallas_call | solution.py:289
  12.7 3.4 %all-to-all-done = bf16[16,8,640]{2,1,0:T(8,128)(2,1)S(1)} async-done(((bf16[16,8,640]{2,1,0:T(8,128)(2,1)}), bf16[16,8,640]{2,1,0:T(8,128)(2,1)S(1)}, u32[]{:S(2)}, u32[]{:S(2)}) %all-to-all-start) | async-done | bytes 163872 | tf_op jit(solution)/shard_map/all_to_all | solution.py:269
  16.1 0.0 copy-start
  16.1 0.7 %copy-done = f32[4096]{0:T(1024)S(1)} copy-done((f32[4096]{0:T(1024)S(1)}, f32[4096]{0:T(1024)}, u32[]{:S(2)}) %copy-start) | copy-done | bytes 16408
  16.8 0.0 copy-start.1
  16.8 2.8 %score.1 = (bf16[128,4096]{1,0:T(8,128)(2,1)S(1)}, bf16[16,4096]{1,0:T(8,128)(2,1)S(1)}, f32[128,128]{1,0:T(8,128)S(1)}, f32[8,128]{1,0:T(8,128)S(1)}, f32[16,1,128]{2,1,0:T(1,128)}) custom-call(bf16[128,640]{1,0:T(8,128)(2,1)S(1)} %bitcast.6, f32[1,4096]{1,0:T(1,128)S(1)} %bitcast.7, bf16[512,2048]{1,0:T(8,128)(2,1)S(1)} %get-tuple-element.14.near_ref, ...), custom_call_target="tpu_custom_call" | custom-call | tf_op jit(solution)/shard_map/score/pallas_call | solution.py:305
  19.6 0.0 copy-start.2
  19.7 0.8 %mix.3 = f32[56,2048]{1,0:T(8,128)S(1)} custom-call(s32[1]{0:T(128)} %bitcast.3.base_ref, bf16[16,4096]{1,0:T(8,128)(2,1)S(1)} %get-tuple-element.17.unit_ref, f32[1,4096]{1,0:T(1,128)S(1)} %bitcast.8, bf16[128,4096]{1,0:T(8,128)(2,1)S(1)} %get-tuple-element.18.raw_ref, f32[128,128]{1,0:T(8,128)S(1)} %get-tuple-element.19.cols_ref, ...), custom_call_target="tpu_custom_call" | custom-call | flops 67108864 | bytes 2097152 | tf_op jit(solution)/shard_map/mix/pallas_call | solution.py:328
  20.5 0.1 collective-permute-start
  20.5 4.8 %all-to-all-start.1 = ((f32[16,1,128]{2,1,0:T(1,128)}), f32[16,1,128]{2,1,0:T(1,128)S(1)}, u32[]{:S(2)}, u32[]{:S(2)}) async-start(f32[16,1,128]{2,1,0:T(1,128)} %get-tuple-element.16), calls=%async_computation.1 | async-start | bytes 16384 | tf_op jit(solution)/shard_map/all_to_all | solution.py:269
  25.4 0.0 copy-done.1
  25.4 0.8 %mix.2.mine_ref = f32[56,2048]{1,0:T(8,128)S(1)} custom-call(s32[1]{0:T(128)} %bitcast.2.base_ref, bf16[16,4096]{1,0:T(8,128)(2,1)S(1)} %get-tuple-element.17.unit_ref, f32[1,4096]{1,0:T(1,128)S(1)} %bitcast.9, bf16[128,4096]{1,0:T(8,128)(2,1)S(1)} %get-tuple-element.18.raw_ref, f32[128,128]{1,0:T(8,128)S(1)} %get-tuple-element.19.cols_ref, ...), custom_call_target="tpu_custom_call" | custom-call | flops 67108864 | bytes 2097152 | tf_op jit(solution)/shard_map/mix/pallas_call | solution.py:328
  26.2 3.2 %all-to-all-done.1.sums_ref = f32[16,1,128]{2,1,0:T(1,128)S(1)} async-done(((f32[16,1,128]{2,1,0:T(1,128)}), f32[16,1,128]{2,1,0:T(1,128)S(1)}, u32[]{:S(2)}, u32[]{:S(2)}) %all-to-all-start.1) | async-done | bytes 8224 | tf_op jit(solution)/shard_map/all_to_all | solution.py:269
  29.4 0.0 collective-permute-done.sibling_ref
  29.4 0.9 %partial.1 = (bf16[128,512]{1,0:T(8,128)(2,1)}, f32[1,128]{1,0:T(1,128)S(1)}) custom-call(f32[16,1,128]{2,1,0:T(1,128)S(1)} %all-to-all-done.1.sums_ref, f32[56,2048]{1,0:T(8,128)S(1)} %mix.2.mine_ref, f32[56,2048]{1,0:T(8,128)S(1)} %collective-permute-done.sibling_ref), custom_call_target="tpu_custom_call" | custom-call | tf_op jit(solution)/shard_map/partial/pallas_call | solution.py:344
  30.3 4.2 %all-to-all-start.2 = ((bf16[16,8,512]{2,1,0:T(8,128)(2,1)}), bf16[16,8,512]{2,1,0:T(8,128)(2,1)S(1)}, u32[]{:S(2)}, u32[]{:S(2)}) async-start(bf16[16,8,512]{2,1,0:T(8,128)(2,1)} %bitcast.4), calls=%async_computation.2 | async-start | bytes 262144 | tf_op jit(solution)/shard_map/all_to_all | solution.py:269
  34.5 3.9 %d_passages.1 = f32[512,4096]{1,0:T(8,128)} custom-call(f32[1,128]{1,0:T(1,128)S(1)} %get-tuple-element.21.total_ref, bf16[16,4096]{1,0:T(8,128)(2,1)S(1)} %get-tuple-element.17.unit_ref, f32[1,4096]{1,0:T(1,128)S(1)} %bitcast.10, bf16[128,4096]{1,0:T(8,128)(2,1)S(1)} %get-tuple-element.18.raw_ref, f32[128,128]{1,0:T(8,128)S(1)} %get-tuple-element.19.cols_ref, ...), custom_call_target="tpu_custom_call" | custom-call | flops 1073741824 | bytes 8388608 | tf_op jit(solution)/shard_map/d_passages/pallas_call | solution.py:353
  38.5 1.7 %all-to-all-done.2.got_ref = bf16[16,8,512]{2,1,0:T(8,128)(2,1)S(1)} async-done(((bf16[16,8,512]{2,1,0:T(8,128)(2,1)}), bf16[16,8,512]{2,1,0:T(8,128)(2,1)S(1)}, u32[]{:S(2)}, u32[]{:S(2)}) %all-to-all-start.2) | async-done | bytes 131104 | tf_op jit(solution)/shard_map/all_to_all | solution.py:269
  40.2 0.0 copy-done.2
  40.2 0.9 %final.1 = (f32[1,4096]{1,0:T(1,128)}, f32[1,4096]{1,0:T(1,128)}) custom-call(bf16[16,8,512]{2,1,0:T(8,128)(2,1)S(1)} %all-to-all-done.2.got_ref, bf16[1,4096]{1,0:T(2,128)(2,1)S(1)} %copy-done.2, f32[1,4096]{1,0:T(1,128)S(1)} %bitcast.11), custom_call_target="tpu_custom_call" | custom-call | tf_op jit(solution)/shard_map/final/pallas_call | solution.py:366
Async XLA Ops:
  2.4 13.7 %all-to-all-start = ((bf16[16,8,640]{2,1,0:T(8,128)(2,1)}), bf16[16,8,640]{2,1,0:T(8,128)(2,1)S(1)}, u32[]{:S(2)}, u32[]{:S(2)}) async-start(bf16[16,8,640]{2,1,0:T(8,128)(2,1)} %pack.1), calls=%async_computation | async-start | bytes 327680 | tf_op jit(solution)/shard_map/all_to_all | solution.py:269
  16.1 0.7 %copy-start = (f32[4096]{0:T(1024)S(1)}, f32[4096]{0:T(1024)}, u32[]{:S(2)}) copy-start(f32[4096]{0:T(1024)} %param.7) | copy-start | bytes 49156
  16.8 8.6 %copy-start.1 = (f32[4096]{0:T(1024)S(1)}, f32[4096]{0:T(1024)}, u32[]{:S(2)}) copy-start(f32[4096]{0:T(1024)} %param.7) | copy-start | bytes 49156
  19.6 20.5 %copy-start.2 = (bf16[1,4096]{1,0:T(2,128)(2,1)S(1)}, bf16[1,4096]{1,0:T(2,128)(2,1)}, u32[]{:S(2)}) copy-start(bf16[1,4096]{1,0:T(2,128)(2,1)} %queries_ref.3) | copy-start | bytes 24580
  20.5 9.0 %collective-permute-start = (f32[56,2048]{1,0:T(8,128)S(1)}, f32[56,2048]{1,0:T(8,128)S(1)}, u32[]{:S(2)}, u32[]{:S(2)}) collective-permute-start(f32[56,2048]{1,0:T(8,128)S(1)} %mix.3), channel_id=1, source_target_pairs={{0,1},{1,0},{2,3},{3,2},{4,5},{5,4},{6,7},{7,6},{8,9},{9,8},{10,11... | collective-permute-start | bytes 1376264 | tf_op jit(solution)/shard_map/ppermute | solution.py:341
  20.5 8.9 %all-to-all-start.1 = ((f32[16,1,128]{2,1,0:T(1,128)}), f32[16,1,128]{2,1,0:T(1,128)S(1)}, u32[]{:S(2)}, u32[]{:S(2)}) async-start(f32[16,1,128]{2,1,0:T(1,128)} %get-tuple-element.16), calls=%async_computation.1 | async-start | bytes 16384 | tf_op jit(solution)/shard_map/all_to_all | solution.py:269
  30.3 9.9 %all-to-all-start.2 = ((bf16[16,8,512]{2,1,0:T(8,128)(2,1)}), bf16[16,8,512]{2,1,0:T(8,128)(2,1)S(1)}, u32[]{:S(2)}, u32[]{:S(2)}) async-start(bf16[16,8,512]{2,1,0:T(8,128)(2,1)} %bitcast.4), calls=%async_computation.2 | async-start | bytes 262144 | tf_op jit(solution)/shard_map/all_to_all | solution.py:269

commit v11 on v10

--- a/solution.py
+++ b/solution.py
@@ -12,7 +12,6 @@
 teacher_div = 2.0
 coef_scale = loss_scale * score_scale
 chunks = 4
-pieces = 8
 f32 = jnp.float32
 bf16 = jnp.bfloat16
 vmem = pltpu.VMEM
@@ -85,7 +84,17 @@
     return pair == lax.broadcasted_iota(jnp.int32, dims, 1 - pair_axis)
 
 
-def stage_kernel(passages_ref, near_ref, far_ref, held, sems_in, sems_out):
+def repeated(got_ref, eighth):
+    pairs = got_ref.shape[0]
+    width = got_ref.shape[1] - 128
+    pair = lax.broadcasted_iota(jnp.int32, (pairs, pairs), 0)
+    source = lax.broadcasted_iota(jnp.int32, (pairs, pairs), 1)
+    pick = jnp.where(source == (pair & -8) + eighth, 1.0, 0.0).astype(bf16)
+    return dot(pick, got_ref[:, :width], nn_dims)
+
+
+def stage_kernel(passages_ref, gain_ref, near_ref, far_ref, gain_out_ref, held, sems_in, sems_out):
+    gain_out_ref[...] = gain_ref[...]
     rows, width = near_ref.shape
     piece = rows // chunks
     copies_in, copies_out, copies_near = [], [], []
@@ -105,41 +114,27 @@
         copy.wait()
 
 
-def score_kernel(
-    got_ref, gain_ref, near_ref, far_ref, raw_ref, unit_ref, cols_ref, rows_ref, sums_ref, held, wide, sems
-):
-    queries, width = unit_ref.shape
-    pairs = queries * 8
+def score_kernel(got_ref, gain_ref, near_ref, far_ref, raw_ref, cols_ref, rows_ref, sums_ref, held, sems):
+    pairs, width = raw_ref.shape
+    queries = pairs // 8
     rows = held.shape[0]
-    chunk = width // chunks
-    half = chunks // 2
+    chunk = width // 8
+    half = held.shape[1] // chunk
     copies = []
     for k in range(half):
         part = pl.ds(k * chunk, chunk)
         copies.append(pltpu.make_async_copy(far_ref.at[pl.ds(0, rows), part], held.at[:, part], sems.at[k]))
         copies[-1].start()
-    tiles = wide.shape[0]
-    loaded = [got_ref[:, j * 128 : (j + 1) * 128].astype(f32) for j in range(tiles + 1)]
-    squares = sum(x * x for x in loaded[:-1])
-    norm = jnp.sum(squares, axis=1, keepdims=True).reshape(queries, 8, 1)
-    norm = jnp.sqrt(jnp.broadcast_to(jnp.sum(norm, axis=1, keepdims=True), (queries, 8, 1)))
-    norm = norm.reshape(pairs, 1)
-    for j in range(tiles):
-        wide[j] = loaded[j] / norm
-    unit = [wide[j, pl.ds(k, queries, stride=8), :] for k in range(8) for j in range(tiles)]
-    unit = jnp.concatenate(unit, axis=1).astype(bf16)
-    unit_ref[...] = unit
-    lists = loaded[-1]
+    lists = got_ref[:, chunk:].astype(f32)
     inside = lists[:, 0:1] * 256.0 + lists[:, 1:2]
     mark = lists[:, 2:3] + lists[:, 3:4]
     lane = lax.broadcasted_iota(jnp.int32, (pairs, rows), 1).astype(f32)
     pick = jnp.where(inside == lane, 1.0, 0.0).astype(bf16)
-    repeat = jnp.where(belongs((pairs, queries), 0), 1.0, 0.0).astype(bf16)
     size = jnp.zeros((pairs, 128), f32)
     along = jnp.zeros((pairs, 128), f32)
-    for k in range(chunks):
+    for k in range(8):
         part = slice(k * chunk, (k + 1) * chunk)
-        repeated = dot(repeat, unit[:, part], nn_dims)
+        query = repeated(got_ref, k)
         if k < half:
             passages = near_ref[:, part]
         else:
@@ -151,13 +146,17 @@
         for j in range(chunk // 128):
             tile = slice(j * 128, (j + 1) * 128)
             size = size + lifted[:, tile] * lifted[:, tile]
-            along = along + lifted[:, tile] * repeated[:, tile]
+            along = along + lifted[:, tile] * query[:, tile]
+    squares = got_ref[:, :chunk].astype(f32)
+    squares = jnp.sum(squares * squares, axis=1, keepdims=True).reshape(queries, 8, 1)
+    squares = jnp.broadcast_to(jnp.sum(squares, axis=1, keepdims=True), (queries, 8, 1))
+    query_inverse = 1.0 / jnp.sqrt(squares.reshape(pairs, 1))
     inverse = 1.0 / jnp.sqrt(jnp.sum(size, axis=1, keepdims=True))
-    cos = jnp.sum(along, axis=1, keepdims=True) * inverse
+    cos = jnp.sum(along, axis=1, keepdims=True) * inverse * query_inverse
     weight = jnp.where(mark > 0.0, jnp.exp(cos * score_scale), 0.0)
     lane = lax.broadcasted_iota(jnp.int32, (pairs, 128), 1)
     cols = jnp.zeros((pairs, 128), f32)
-    for k, column in enumerate((weight, mark, cos, inverse, inside)):
+    for k, column in enumerate((weight, mark, cos, inverse, inside, query_inverse)):
         cols = jnp.where(lane == k, column, cols)
     cols_ref[...] = cols
     flipped = jnp.transpose(cols)[:8]
@@ -165,26 +164,27 @@
     sums_ref[...] = jnp.broadcast_to(flipped[None, :1], sums_ref.shape)
 
 
-def mix_kernel(base_ref, unit_ref, gain_ref, raw_ref, cols_ref, rows_ref, out_ref):
-    queries = unit_ref.shape[0]
-    pairs = raw_ref.shape[0]
-    chunk = out_ref.shape[1] // 2
+def mix_kernel(base_ref, got_ref, gain_ref, raw_ref, cols_ref, rows_ref, out_ref):
+    pairs, width = raw_ref.shape
+    queries = pairs // 8
+    chunk = width // 8
     cos, inverse = cols_ref[:, 2:3], cols_ref[:, 3:4]
     weight, mark = rows_ref[0:1, :], rows_ref[1:2, :]
     own = belongs((queries, pairs), 1)
     by_weight = split(jnp.where(own, weight, 0.0))
     by_mark = split(jnp.where(own, mark, 0.0))
     plain = jnp.concatenate([*by_weight, *by_mark], axis=0)
-    repeat = jnp.where(belongs((pairs, queries), 0), 1.0, 0.0).astype(bf16)
-    for k in range(2):
+    for k in range(out_ref.shape[1] // chunk):
         part = slice(k * chunk, (k + 1) * chunk)
-        there = pl.ds(pl.multiple_of(base_ref[0] + k * chunk, 128), chunk)
+        eighth = base_ref[0] + k
+        there = pl.ds(pl.multiple_of(eighth * chunk, 128), chunk)
         row = (raw_ref[:, there].astype(f32) * gain_ref[:, there] * inverse).astype(bf16)
         mixed = dot(plain, row, nn_dims)
         out_ref[:queries, part] = mixed[:queries] + mixed[queries : 2 * queries]
         out_ref[queries : 2 * queries, part] = mixed[2 * queries : 3 * queries] + mixed[3 * queries :]
         row = row.astype(f32)
-        turned = row * (dot(repeat, unit_ref[:, there], nn_dims) - cos * row)
+        query = (repeated(got_ref, eighth) * cols_ref[:, 5:6]).astype(bf16).astype(f32)
+        turned = row * (query - cos * row)
         mixed = dot(plain, turned.astype(bf16), nn_dims)
         out_ref[2 * queries : 3 * queries, part] = mixed[:queries] + mixed[queries : 2 * queries]
         last = jnp.sum(mixed[2 * queries :], axis=0, keepdims=True)
@@ -214,10 +214,10 @@
         out_ref[:, tile * 128 : (tile + 1) * 128] = laid[tile].astype(bf16)
 
 
-def passage_kernel(total_ref, unit_ref, gain_ref, raw_ref, cols_ref, rows_ref, out_ref, made, sems):
-    queries, width = unit_ref.shape
-    rows, pairs = made.shape[0], raw_ref.shape[0]
-    piece = width // pieces
+def passage_kernel(total_ref, got_ref, gain_ref, raw_ref, cols_ref, rows_ref, out_ref, made, sems):
+    pairs, width = raw_ref.shape
+    rows = made.shape[0]
+    piece = width // 8
     weight, mark = cols_ref[:, 0:1], cols_ref[:, 1:2]
     cos, inverse = cols_ref[:, 2:3], cols_ref[:, 3:4]
     square = (pairs, pairs)
@@ -230,13 +230,13 @@
     spread = lax.broadcasted_iota(jnp.int32, (rows, pairs), 0).astype(f32) == inside
     spread = jnp.where(spread, 1.0, 0.0).astype(bf16)
     spread = jnp.concatenate([spread, spread], axis=1)
-    repeat = jnp.where(belongs((pairs, queries), 0), 1.0, 0.0).astype(bf16)
     copies = []
-    for k in range(pieces):
+    for k in range(8):
         part = slice(k * piece, (k + 1) * piece)
         gain = gain_ref[:, part]
         row = (raw_ref[:, part].astype(f32) * gain * inverse).astype(bf16).astype(f32)
-        term = (dot(repeat, unit_ref[:, part], nn_dims) - cos * row) * scale * gain
+        query = (repeated(got_ref, k) * cols_ref[:, 5:6]).astype(bf16).astype(f32)
+        term = (query - cos * row) * scale * gain
         made[:, part] = dot(spread, jnp.concatenate(split(term), axis=0), nn_dims)
         part = pl.ds(k * piece, piece)
         copies.append(pltpu.make_async_copy(made.at[:, part], out_ref.at[:, part], sems.at[k]))
@@ -286,11 +286,15 @@
     got = exchange(packed).reshape(count * 8, width // 8 + listed)
 
     pairs = count * 8
-    near, far = pl.pallas_call(
+    near, far, gain_near = pl.pallas_call(
         stage_kernel,
-        in_specs=[outside()],
-        out_specs=[whole(), outside()],
-        out_shape=[shape((rows, width // 2), bf16), shape((10 * rows, width // 2), bf16)],
+        in_specs=[outside(), whole()],
+        out_specs=[whole(), outside(), whole()],
+        out_shape=[
+            shape((rows, width // 2), bf16),
+            shape((10 * rows, width // 2), bf16),
+            shape((1, width)),
+        ],
         scratch_shapes=[
             pltpu.VMEM((rows, width // 2), bf16),
             pltpu.SemaphoreType.DMA((2 * chunks,)),
@@ -301,25 +305,23 @@
         cost_estimate=pl.CostEstimate(
             flops=0, bytes_accessed=4 * rows * width, transcendentals=0
         ),
-    )(passages)
-    raw, unit, cols, lines, sums = pl.pallas_call(
+    )(passages, gain)
+    raw, cols, lines, sums = pl.pallas_call(
         score_kernel,
         in_specs=[whole(), whole(), whole(), outside()],
         out_shape=[
             shape((pairs, width), bf16),
-            shape((count, width), bf16),
             shape((pairs, 128)),
             shape((8, pairs)),
             shape((count, 1, pairs)),
         ],
         scratch_shapes=[
             pltpu.VMEM((rows, width // 2), bf16),
-            pltpu.VMEM((width // 1024, pairs, 128), f32),
-            pltpu.SemaphoreType.DMA((chunks // 2,)),
+            pltpu.SemaphoreType.DMA((4,)),
         ],
         compiler_params=params(48),
         name="score",
-    )(got, gain, near, far)
+    )(got, gain_near, near, far)
     got_sums = exchange(sums)
 
     half = width // 2
@@ -332,14 +334,14 @@
             compiler_params=params(48),
             name="mix",
             cost_estimate=pl.CostEstimate(
-                flops=8 * count * pairs * width, bytes_accessed=4 * pairs * width, transcendentals=0
+                flops=8 * count * pairs * width, bytes_accessed=64 * pairs * width, transcendentals=0
             ),
-        )(base.astype(jnp.int32).reshape(1), unit, gain, raw, cols, lines)
+        )(base.astype(jnp.int32).reshape(1), got, gain_near, raw, cols, lines)
 
     core = lax.axis_index("hash") % 2
-    theirs = mix((1 - core) * half)
+    theirs = mix((1 - core) * 4)
     sibling = lax.ppermute(theirs, "hash", [(i, i ^ 1) for i in range(count)])
-    mine = mix(core * half)
+    mine = mix(core * 4)
 
     partial, total = pl.pallas_call(
         partial_kernel,
@@ -355,13 +357,13 @@
         in_specs=[whole()] * 6,
         out_specs=outside(),
         out_shape=shape((rows, width)),
-        scratch_shapes=[pltpu.VMEM((rows, width), f32), pltpu.SemaphoreType.DMA((pieces,))],
+        scratch_shapes=[pltpu.VMEM((rows, width), f32), pltpu.SemaphoreType.DMA((8,))],
         compiler_params=params(48),
         name="d_passages",
         cost_estimate=pl.CostEstimate(
             flops=4 * pairs * rows * width, bytes_accessed=4 * rows * width, transcendentals=0
         ),
-    )(total, unit, gain, raw, cols, lines)
+    )(total, got, gain_near, raw, cols, lines)
 
     d_queries, d_gain = pl.pallas_call(
         final_kernel,

time: 41.6 us -> 42 us (level)
  Pallas kernels: 14.5 us -> 16.1 us
  waiting for transfers between devices: 8.37 us -> 7.21 us
    all_to_all x3, waiting for transfers between devices: 8.36 us -> 7.21 us  [exchange(): lax.all_to_all(x, 'hash', split_axis=0, concat_axis=0, axis_index_groups=...]
    pallas_call x1, Pallas kernels: 2.81 us -> 3.58 us  [local(): pl.pallas_call(score_kernel, in_specs=[whole(), whole(), whole(), outside...]
    pallas_call x2, Pallas kernels: 1.58 us -> 2.24 us  [mix(): pl.pallas_call(mix_kernel, in_specs=[pl.BlockSpec(memory_space=pltpu.SMEM...]
  transfers between devices with their start and end apart: 4 -> 4, of which waited for: 3 -> 3; matrix products, arithmetic and copies ran while one was open for 0% -> 0% of each run, Pallas kernels for 18% -> 19%
where the time goes in v11:
time: 42 us; the launch traced here: 41.4 us
  starting transfers between devices  16.7 us (40%)
  Pallas kernels  16.1 us (38%)
  waiting for transfers between devices  7.21 us (17%)
  local copies, waits for them, and re-layouts  0.72 us (2%)
  between operations  0.71 us (2%)
    all_to_all x3, starting transfers between devices, exchange(): lax.all_to_all(x, 'hash', split_axis=0, concat_axis=0, axis_index_groups=...  16.6 us
    all_to_all x3, waiting for transfers between devices, exchange(): lax.all_to_all(x, 'hash', split_axis=0, concat_axis=0, axis_index_groups=...  7.21 us
    pallas_call x1, Pallas kernels, local(): pl.pallas_call(passage_kernel, in_specs=[whole()] * 6, out_specs=outside(...  4.07 us
    pallas_call x1, Pallas kernels, local(): pl.pallas_call(score_kernel, in_specs=[whole(), whole(), whole(), outside...  3.58 us
    pallas_call x1, Pallas kernels, local(): pl.pallas_call(stage_kernel, in_specs=[outside(), whole()], out_specs=[wh...  2.75 us
    pallas_call x2, Pallas kernels, mix(): pl.pallas_call(mix_kernel, in_specs=[pl.BlockSpec(memory_space=pltpu.SMEM...  2.24 us
    pallas_call x1, Pallas kernels, local(): pl.pallas_call(functools.partial(pack_kernel, rows), out_shape=shape((cou...  1.72 us
    pallas_call x1, Pallas kernels, local(): pl.pallas_call(final_kernel, out_shape=[shape((1, width)), shape((1, widt...  0.87 us
  transfers between devices with their start and end apart: 4, of which 3 were waited for; matrix products, arithmetic and copies ran while one was open for 0% of the time, Pallas kernels for 19%

profile of v11, /device:TPU:0, one launch (start us, length us, event | category | flops | bytes accessed | tf_op | source)
XLA Modules:
  0.0 41.4 jit_solution(3264585082873352155)
XLA Ops:
  0.6 1.7 %pack.1 = bf16[16,8,640]{2,1,0:T(8,128)(2,1)} custom-call(bf16[1,4096]{1,0:T(2,128)(2,1)} %queries_ref.3, s32[1,128]{1,0:T(1,128)} %candidates_ref.1, s32[1,128]{1,0:T(1,128)} %teacher_ref.1), custom_call_target="tpu_custom_call" | custom-call | tf_op jit(solution)/shard_map/pack/pallas_call | solution.py:280
  2.4 7.6 %all-to-all-start = ((bf16[16,8,640]{2,1,0:T(8,128)(2,1)}), bf16[16,8,640]{2,1,0:T(8,128)(2,1)S(1)}, u32[]{:S(2)}, u32[]{:S(2)}) async-start(bf16[16,8,640]{2,1,0:T(8,128)(2,1)} %pack.1), calls=%async_computation | async-start | bytes 327680 | tf_op jit(solution)/shard_map/all_to_all | solution.py:269
  9.9 0.0 copy-start
  9.9 0.7 %copy-done = f32[4096]{0:T(1024)S(1)} copy-done((f32[4096]{0:T(1024)S(1)}, f32[4096]{0:T(1024)}, u32[]{:S(2)}) %copy-start) | copy-done | bytes 16408
  10.6 2.8 %stage.1 = (bf16[512,2048]{1,0:T(8,128)(2,1)S(1)}, bf16[5120,2048]{1,0:T(8,128)(2,1)}, f32[1,4096]{1,0:T(1,128)S(1)}) custom-call(bf16[512,4096]{1,0:T(8,128)(2,1)} %passages_ref.1, f32[1,4096]{1,0:T(1,128)S(1)} %bitcast.10), custom_call_target="tpu_custom_call" | custom-call | bytes 8388608 | tf_op jit(solution)/shard_map/stage/pallas_call | solution.py:289
  13.4 2.7 %all-to-all-done = bf16[16,8,640]{2,1,0:T(8,128)(2,1)S(1)} async-done(((bf16[16,8,640]{2,1,0:T(8,128)(2,1)}), bf16[16,8,640]{2,1,0:T(8,128)(2,1)S(1)}, u32[]{:S(2)}, u32[]{:S(2)}) %all-to-all-start) | async-done | bytes 163872 | tf_op jit(solution)/shard_map/all_to_all | solution.py:269
  16.1 3.6 %score.1 = (bf16[128,4096]{1,0:T(8,128)(2,1)S(1)}, f32[128,128]{1,0:T(8,128)S(1)}, f32[8,128]{1,0:T(8,128)S(1)}, f32[16,1,128]{2,1,0:T(1,128)}) custom-call(bf16[128,640]{1,0:T(8,128)(2,1)S(1)} %bitcast.6, f32[1,4096]{1,0:T(1,128)S(1)} %get-tuple-element.14.gain_ref, bf16[512,2048]{1,0:T(8,128)(2,1)S(1)} %get-tuple-element.15.near_ref, ...), custom_call_target="tpu_custom_call" | custom-call | tf_op jit(solution)/shard_map/score/pallas_call | solution.py:309
  19.7 0.0 copy-start.1
  19.7 0.0 copy-start.2
  19.7 1.1 %mix.3 = f32[56,2048]{1,0:T(8,128)S(1)} custom-call(s32[1]{0:T(128)} %bitcast.3.base_ref, bf16[128,640]{1,0:T(8,128)(2,1)S(1)} %bitcast.7, f32[1,4096]{1,0:T(1,128)S(1)} %get-tuple-element.14.gain_ref, bf16[128,4096]{1,0:T(8,128)(2,1)S(1)} %get-tuple-element.18.raw_ref, f32[128,128]{1,0:T(8,128)S(1)} %get-tuple-element.19.cols_ref, ...), custom_call_target="tpu_custom_call" | custom-call | flops 67108864 | bytes 33554432 | tf_op jit(solution)/shard_map/mix/pallas_call | solution.py:330
  20.8 0.1 collective-permute-start
  20.9 4.8 %all-to-all-start.1 = ((f32[16,1,128]{2,1,0:T(1,128)}), f32[16,1,128]{2,1,0:T(1,128)S(1)}, u32[]{:S(2)}, u32[]{:S(2)}) async-start(f32[16,1,128]{2,1,0:T(1,128)} %get-tuple-element.17), calls=%async_computation.1 | async-start | bytes 16384 | tf_op jit(solution)/shard_map/all_to_all | solution.py:269
  25.8 1.1 %mix.2.mine_ref = f32[56,2048]{1,0:T(8,128)S(1)} custom-call(s32[1]{0:T(128)} %bitcast.2.base_ref, bf16[128,640]{1,0:T(8,128)(2,1)S(1)} %bitcast.8, f32[1,4096]{1,0:T(1,128)S(1)} %get-tuple-element.14.gain_ref, bf16[128,4096]{1,0:T(8,128)(2,1)S(1)} %get-tuple-element.18.raw_ref, f32[128,128]{1,0:T(8,128)S(1)} %get-tuple-element.19.cols_ref, ...), custom_call_target="tpu_custom_call" | custom-call | flops 67108864 | bytes 33554432 | tf_op jit(solution)/shard_map/mix/pallas_call | solution.py:330
  26.9 2.9 %all-to-all-done.1.sums_ref = f32[16,1,128]{2,1,0:T(1,128)S(1)} async-done(((f32[16,1,128]{2,1,0:T(1,128)}), f32[16,1,128]{2,1,0:T(1,128)S(1)}, u32[]{:S(2)}, u32[]{:S(2)}) %all-to-all-start.1) | async-done | bytes 8224 | tf_op jit(solution)/shard_map/all_to_all | solution.py:269
  29.8 0.0 collective-permute-done.sibling_ref
  29.8 0.9 %partial.1 = (bf16[128,512]{1,0:T(8,128)(2,1)}, f32[1,128]{1,0:T(1,128)S(1)}) custom-call(f32[16,1,128]{2,1,0:T(1,128)S(1)} %all-to-all-done.1.sums_ref, f32[56,2048]{1,0:T(8,128)S(1)} %mix.2.mine_ref, f32[56,2048]{1,0:T(8,128)S(1)} %collective-permute-done.sibling_ref), custom_call_target="tpu_custom_call" | custom-call | tf_op jit(solution)/shard_map/partial/pallas_call | solution.py:346
  30.7 4.2 %all-to-all-start.2 = ((bf16[16,8,512]{2,1,0:T(8,128)(2,1)}), bf16[16,8,512]{2,1,0:T(8,128)(2,1)S(1)}, u32[]{:S(2)}, u32[]{:S(2)}) async-start(bf16[16,8,512]{2,1,0:T(8,128)(2,1)} %bitcast.4), calls=%async_computation.2 | async-start | bytes 262144 | tf_op jit(solution)/shard_map/all_to_all | solution.py:269
  34.9 4.1 %d_passages.1 = f32[512,4096]{1,0:T(8,128)} custom-call(f32[1,128]{1,0:T(1,128)S(1)} %get-tuple-element.21.total_ref, bf16[128,640]{1,0:T(8,128)(2,1)S(1)} %bitcast.9, f32[1,4096]{1,0:T(1,128)S(1)} %get-tuple-element.14.gain_ref, bf16[128,4096]{1,0:T(8,128)(2,1)S(1)} %get-tuple-element.18.raw_ref, f32[128,128]{1,0:T(8,128)S(1)} %get-tuple-element.19.cols_ref, ...), custom_call_target="tpu_custom_call" | custom-call | flops 1073741824 | bytes 8388608 | tf_op jit(solution)/shard_map/d_passages/pallas_call | solution.py:355
  39.0 1.6 %all-to-all-done.2.got_ref = bf16[16,8,512]{2,1,0:T(8,128)(2,1)S(1)} async-done(((bf16[16,8,512]{2,1,0:T(8,128)(2,1)}), bf16[16,8,512]{2,1,0:T(8,128)(2,1)S(1)}, u32[]{:S(2)}, u32[]{:S(2)}) %all-to-all-start.2) | async-done | bytes 131104 | tf_op jit(solution)/shard_map/all_to_all | solution.py:269
  40.6 0.0 copy-done.1
  40.6 0.0 copy-done.2
  40.6 0.9 %final.1 = (f32[1,4096]{1,0:T(1,128)}, f32[1,4096]{1,0:T(1,128)}) custom-call(bf16[16,8,512]{2,1,0:T(8,128)(2,1)S(1)} %all-to-all-done.2.got_ref, bf16[1,4096]{1,0:T(2,128)(2,1)S(1)} %copy-done.2, f32[1,4096]{1,0:T(1,128)S(1)} %bitcast.11), custom_call_target="tpu_custom_call" | custom-call | tf_op jit(solution)/shard_map/final/pallas_call | solution.py:368
Async XLA Ops:
  2.4 13.7 %all-to-all-start = ((bf16[16,8,640]{2,1,0:T(8,128)(2,1)}), bf16[16,8,640]{2,1,0:T(8,128)(2,1)S(1)}, u32[]{:S(2)}, u32[]{:S(2)}) async-start(bf16[16,8,640]{2,1,0:T(8,128)(2,1)} %pack.1), calls=%async_computation | async-start | bytes 327680 | tf_op jit(solution)/shard_map/all_to_all | solution.py:269
  9.9 0.7 %copy-start = (f32[4096]{0:T(1024)S(1)}, f32[4096]{0:T(1024)}, u32[]{:S(2)}) copy-start(f32[4096]{0:T(1024)} %param.7) | copy-start | bytes 49156
  19.7 20.9 %copy-start.1 = (f32[4096]{0:T(1024)S(1)}, f32[4096]{0:T(1024)}, u32[]{:S(2)}) copy-start(f32[4096]{0:T(1024)} %param.7) | copy-start | bytes 49156
  19.7 20.9 %copy-start.2 = (bf16[1,4096]{1,0:T(2,128)(2,1)S(1)}, bf16[1,4096]{1,0:T(2,128)(2,1)}, u32[]{:S(2)}) copy-start(bf16[1,4096]{1,0:T(2,128)(2,1)} %queries_ref.3) | copy-start | bytes 24580
  20.8 9.0 %collective-permute-start = (f32[56,2048]{1,0:T(8,128)S(1)}, f32[56,2048]{1,0:T(8,128)S(1)}, u32[]{:S(2)}, u32[]{:S(2)}) collective-permute-start(f32[56,2048]{1,0:T(8,128)S(1)} %mix.3), channel_id=1, source_target_pairs={{0,1},{1,0},{2,3},{3,2},{4,5},{5,4},{6,7},{7,6},{8,9},{9,8},{10,11... | collective-permute-start | bytes 1376264 | tf_op jit(solution)/shard_map/ppermute | solution.py:343
  20.9 8.9 %all-to-all-start.1 = ((f32[16,1,128]{2,1,0:T(1,128)}), f32[16,1,128]{2,1,0:T(1,128)S(1)}, u32[]{:S(2)}, u32[]{:S(2)}) async-start(f32[16,1,128]{2,1,0:T(1,128)} %get-tuple-element.17), calls=%async_computation.1 | async-start | bytes 16384 | tf_op jit(solution)/shard_map/all_to_all | solution.py:269
  30.7 9.9 %all-to-all-start.2 = ((bf16[16,8,512]{2,1,0:T(8,128)(2,1)}), bf16[16,8,512]{2,1,0:T(8,128)(2,1)S(1)}, u32[]{:S(2)}, u32[]{:S(2)}) async-start(bf16[16,8,512]{2,1,0:T(8,128)(2,1)} %bitcast.4), calls=%async_computation.2 | async-start | bytes 262144 | tf_op jit(solution)/shard_map/all_to_all | solution.py:269

commit v12 on v10

--- a/solution.py
+++ b/solution.py
@@ -85,7 +85,8 @@
     return pair == lax.broadcasted_iota(jnp.int32, dims, 1 - pair_axis)
 
 
-def stage_kernel(passages_ref, near_ref, far_ref, held, sems_in, sems_out):
+def stage_kernel(passages_ref, gain_ref, near_ref, far_ref, gain_out_ref, held, sems_in, sems_out):
+    gain_out_ref[...] = gain_ref[...]
     rows, width = near_ref.shape
     piece = rows // chunks
     copies_in, copies_out, copies_near = [], [], []
@@ -106,9 +107,9 @@
 
 
 def score_kernel(
-    got_ref, gain_ref, near_ref, far_ref, raw_ref, unit_ref, cols_ref, rows_ref, sums_ref, held, wide, sems
+    got_ref, gain_ref, near_ref, far_ref, raw_ref, query_ref, cols_ref, rows_ref, sums_ref, held, wide, sems
 ):
-    queries, width = unit_ref.shape
+    queries, width = query_ref.shape
     pairs = queries * 8
     rows = held.shape[0]
     chunk = width // chunks
@@ -120,15 +121,11 @@
         copies[-1].start()
     tiles = wide.shape[0]
     loaded = [got_ref[:, j * 128 : (j + 1) * 128].astype(f32) for j in range(tiles + 1)]
-    squares = sum(x * x for x in loaded[:-1])
-    norm = jnp.sum(squares, axis=1, keepdims=True).reshape(queries, 8, 1)
-    norm = jnp.sqrt(jnp.broadcast_to(jnp.sum(norm, axis=1, keepdims=True), (queries, 8, 1)))
-    norm = norm.reshape(pairs, 1)
     for j in range(tiles):
-        wide[j] = loaded[j] / norm
-    unit = [wide[j, pl.ds(k, queries, stride=8), :] for k in range(8) for j in range(tiles)]
-    unit = jnp.concatenate(unit, axis=1).astype(bf16)
-    unit_ref[...] = unit
+        wide[j] = loaded[j]
+    query = [wide[j, pl.ds(k, queries, stride=8), :] for k in range(8) for j in range(tiles)]
+    query = jnp.concatenate(query, axis=1).astype(bf16)
+    query_ref[...] = query
     lists = loaded[-1]
     inside = lists[:, 0:1] * 256.0 + lists[:, 1:2]
     mark = lists[:, 2:3] + lists[:, 3:4]
@@ -139,7 +136,7 @@
     along = jnp.zeros((pairs, 128), f32)
     for k in range(chunks):
         part = slice(k * chunk, (k + 1) * chunk)
-        repeated = dot(repeat, unit[:, part], nn_dims)
+        repeated = dot(repeat, query[:, part], nn_dims)
         if k < half:
             passages = near_ref[:, part]
         else:
@@ -153,11 +150,15 @@
             size = size + lifted[:, tile] * lifted[:, tile]
             along = along + lifted[:, tile] * repeated[:, tile]
     inverse = 1.0 / jnp.sqrt(jnp.sum(size, axis=1, keepdims=True))
-    cos = jnp.sum(along, axis=1, keepdims=True) * inverse
+    squares = sum(x * x for x in loaded[:-1])
+    squares = jnp.sum(squares, axis=1, keepdims=True).reshape(queries, 8, 1)
+    squares = jnp.broadcast_to(jnp.sum(squares, axis=1, keepdims=True), (queries, 8, 1))
+    query_inverse = 1.0 / jnp.sqrt(squares.reshape(pairs, 1))
+    cos = jnp.sum(along, axis=1, keepdims=True) * inverse * query_inverse
     weight = jnp.where(mark > 0.0, jnp.exp(cos * score_scale), 0.0)
     lane = lax.broadcasted_iota(jnp.int32, (pairs, 128), 1)
     cols = jnp.zeros((pairs, 128), f32)
-    for k, column in enumerate((weight, mark, cos, inverse, inside)):
+    for k, column in enumerate((weight, mark, cos, inverse, inside, query_inverse)):
         cols = jnp.where(lane == k, column, cols)
     cols_ref[...] = cols
     flipped = jnp.transpose(cols)[:8]
@@ -165,8 +166,8 @@
     sums_ref[...] = jnp.broadcast_to(flipped[None, :1], sums_ref.shape)
 
 
-def mix_kernel(base_ref, unit_ref, gain_ref, raw_ref, cols_ref, rows_ref, out_ref):
-    queries = unit_ref.shape[0]
+def mix_kernel(base_ref, query_ref, gain_ref, raw_ref, cols_ref, rows_ref, out_ref):
+    queries = query_ref.shape[0]
     pairs = raw_ref.shape[0]
     chunk = out_ref.shape[1] // 2
     cos, inverse = cols_ref[:, 2:3], cols_ref[:, 3:4]
@@ -184,7 +185,8 @@
         out_ref[:queries, part] = mixed[:queries] + mixed[queries : 2 * queries]
         out_ref[queries : 2 * queries, part] = mixed[2 * queries : 3 * queries] + mixed[3 * queries :]
         row = row.astype(f32)
-        turned = row * (dot(repeat, unit_ref[:, there], nn_dims) - cos * row)
+        query = dot(repeat, query_ref[:, there], nn_dims) * cols_ref[:, 5:6]
+        turned = row * (query.astype(bf16).astype(f32) - cos * row)
         mixed = dot(plain, turned.astype(bf16), nn_dims)
         out_ref[2 * queries : 3 * queries, part] = mixed[:queries] + mixed[queries : 2 * queries]
         last = jnp.sum(mixed[2 * queries :], axis=0, keepdims=True)
@@ -214,8 +216,8 @@
         out_ref[:, tile * 128 : (tile + 1) * 128] = laid[tile].astype(bf16)
 
 
-def passage_kernel(total_ref, unit_ref, gain_ref, raw_ref, cols_ref, rows_ref, out_ref, made, sems):
-    queries, width = unit_ref.shape
+def passage_kernel(total_ref, query_ref, gain_ref, raw_ref, cols_ref, rows_ref, out_ref, made, sems):
+    queries, width = query_ref.shape
     rows, pairs = made.shape[0], raw_ref.shape[0]
     piece = width // pieces
     weight, mark = cols_ref[:, 0:1], cols_ref[:, 1:2]
@@ -236,7 +238,8 @@
         part = slice(k * piece, (k + 1) * piece)
         gain = gain_ref[:, part]
         row = (raw_ref[:, part].astype(f32) * gain * inverse).astype(bf16).astype(f32)
-        term = (dot(repeat, unit_ref[:, part], nn_dims) - cos * row) * scale * gain
+        query = dot(repeat, query_ref[:, part], nn_dims) * cols_ref[:, 5:6]
+        term = (query.astype(bf16).astype(f32) - cos * row) * scale * gain
         made[:, part] = dot(spread, jnp.concatenate(split(term), axis=0), nn_dims)
         part = pl.ds(k * piece, piece)
         copies.append(pltpu.make_async_copy(made.at[:, part], out_ref.at[:, part], sems.at[k]))
@@ -286,11 +289,15 @@
     got = exchange(packed).reshape(count * 8, width // 8 + listed)
 
     pairs = count * 8
-    near, far = pl.pallas_call(
+    near, far, gain_near = pl.pallas_call(
         stage_kernel,
-        in_specs=[outside()],
-        out_specs=[whole(), outside()],
-        out_shape=[shape((rows, width // 2), bf16), shape((10 * rows, width // 2), bf16)],
+        in_specs=[outside(), whole()],
+        out_specs=[whole(), outside(), whole()],
+        out_shape=[
+            shape((rows, width // 2), bf16),
+            shape((10 * rows, width // 2), bf16),
+            shape((1, width)),
+        ],
         scratch_shapes=[
             pltpu.VMEM((rows, width // 2), bf16),
             pltpu.SemaphoreType.DMA((2 * chunks,)),
@@ -301,8 +308,8 @@
         cost_estimate=pl.CostEstimate(
             flops=0, bytes_accessed=4 * rows * width, transcendentals=0
         ),
-    )(passages)
-    raw, unit, cols, lines, sums = pl.pallas_call(
+    )(passages, gain)
+    raw, query, cols, lines, sums = pl.pallas_call(
         score_kernel,
         in_specs=[whole(), whole(), whole(), outside()],
         out_shape=[
@@ -319,8 +326,7 @@
         ],
         compiler_params=params(48),
         name="score",
-    )(got, gain, near, far)
-    got_sums = exchange(sums)
+    )(got, gain_near, near, far)
 
     half = width // 2
 
@@ -334,12 +340,13 @@
             cost_estimate=pl.CostEstimate(
                 flops=8 * count * pairs * width, bytes_accessed=4 * pairs * width, transcendentals=0
             ),
-        )(base.astype(jnp.int32).reshape(1), unit, gain, raw, cols, lines)
+        )(base.astype(jnp.int32).reshape(1), query, gain_near, raw, cols, lines)
 
     core = lax.axis_index("hash") % 2
     theirs = mix((1 - core) * half)
     sibling = lax.ppermute(theirs, "hash", [(i, i ^ 1) for i in range(count)])
     mine = mix(core * half)
+    got_sums = exchange(sums)
 
     partial, total = pl.pallas_call(
         partial_kernel,
@@ -361,7 +368,7 @@
         cost_estimate=pl.CostEstimate(
             flops=4 * pairs * rows * width, bytes_accessed=4 * rows * width, transcendentals=0
         ),
-    )(total, unit, gain, raw, cols, lines)
+    )(total, query, gain_near, raw, cols, lines)
 
     d_queries, d_gain = pl.pallas_call(
         final_kernel,

time: 41.6 us -> 41.2 us (level)
  waiting for transfers between devices: 8.37 us -> 7.47 us
  Pallas kernels: 14.5 us -> 15.1 us
    all_to_all x3, waiting for transfers between devices: 8.36 us -> 7.46 us  [exchange(): lax.all_to_all(x, 'hash', split_axis=0, concat_axis=0, axis_index_groups=...]
  transfers between devices with their start and end apart: 4 -> 4, of which waited for: 3 -> 3; matrix products, arithmetic and copies ran while one was open for 0% -> 0% of each run, Pallas kernels for 18% -> 19%
where the time goes in v12:
time: 41.2 us; the launch traced here: 40.7 us
  starting transfers between devices  16.7 us (41%)
  Pallas kernels  15.1 us (37%)
  waiting for transfers between devices  7.47 us (18%)
  local copies, waits for them, and re-layouts  0.72 us (2%)
  between operations  0.71 us (2%)
    all_to_all x3, starting transfers between devices, exchange(): lax.all_to_all(x, 'hash', split_axis=0, concat_axis=0, axis_index_groups=...  16.6 us
    all_to_all x3, waiting for transfers between devices, exchange(): lax.all_to_all(x, 'hash', split_axis=0, concat_axis=0, axis_index_groups=...  7.46 us
    pallas_call x1, Pallas kernels, local(): pl.pallas_call(passage_kernel, in_specs=[whole()] * 6, out_specs=outside(...  4.06 us
    pallas_call x1, Pallas kernels, local(): pl.pallas_call(score_kernel, in_specs=[whole(), whole(), whole(), outside...  3.07 us
    pallas_call x1, Pallas kernels, local(): pl.pallas_call(stage_kernel, in_specs=[outside(), whole()], out_specs=[wh...  2.75 us
    pallas_call x2, Pallas kernels, mix(): pl.pallas_call(mix_kernel, in_specs=[pl.BlockSpec(memory_space=pltpu.SMEM...  1.74 us
    pallas_call x1, Pallas kernels, local(): pl.pallas_call(functools.partial(pack_kernel, rows), out_shape=shape((cou...  1.72 us
    pallas_call x1, Pallas kernels, local(): pl.pallas_call(final_kernel, out_shape=[shape((1, width)), shape((1, widt...  0.87 us
  transfers between devices with their start and end apart: 4, of which 3 were waited for; matrix products, arithmetic and copies ran while one was open for 0% of the time, Pallas kernels for 19%

profile of v12, /device:TPU:0, one launch (start us, length us, event | category | flops | bytes accessed | tf_op | source)
XLA Modules:
  0.0 40.7 jit_solution(9402617443324376527)
XLA Ops:
  0.6 1.7 %pack.1 = bf16[16,8,640]{2,1,0:T(8,128)(2,1)} custom-call(bf16[1,4096]{1,0:T(2,128)(2,1)} %queries_ref.3, s32[1,128]{1,0:T(1,128)} %candidates_ref.1, s32[1,128]{1,0:T(1,128)} %teacher_ref.1), custom_call_target="tpu_custom_call" | custom-call | tf_op jit(solution)/shard_map/pack/pallas_call | solution.py:283
  2.4 7.6 %all-to-all-start = ((bf16[16,8,640]{2,1,0:T(8,128)(2,1)}), bf16[16,8,640]{2,1,0:T(8,128)(2,1)S(1)}, u32[]{:S(2)}, u32[]{:S(2)}) async-start(bf16[16,8,640]{2,1,0:T(8,128)(2,1)} %pack.1), calls=%async_computation | async-start | bytes 327680 | tf_op jit(solution)/shard_map/all_to_all | solution.py:272
  9.9 0.0 copy-start
  9.9 0.7 %copy-done = f32[4096]{0:T(1024)S(1)} copy-done((f32[4096]{0:T(1024)S(1)}, f32[4096]{0:T(1024)}, u32[]{:S(2)}) %copy-start) | copy-done | bytes 16408
  10.6 2.8 %stage.1 = (bf16[512,2048]{1,0:T(8,128)(2,1)S(1)}, bf16[5120,2048]{1,0:T(8,128)(2,1)}, f32[1,4096]{1,0:T(1,128)S(1)}) custom-call(bf16[512,4096]{1,0:T(8,128)(2,1)} %passages_ref.1, f32[1,4096]{1,0:T(1,128)S(1)} %bitcast.7), custom_call_target="tpu_custom_call" | custom-call | bytes 8388608 | tf_op jit(solution)/shard_map/stage/pallas_call | solution.py:292
  13.4 2.7 %all-to-all-done = bf16[16,8,640]{2,1,0:T(8,128)(2,1)S(1)} async-done(((bf16[16,8,640]{2,1,0:T(8,128)(2,1)}), bf16[16,8,640]{2,1,0:T(8,128)(2,1)S(1)}, u32[]{:S(2)}, u32[]{:S(2)}) %all-to-all-start) | async-done | bytes 163872 | tf_op jit(solution)/shard_map/all_to_all | solution.py:272
  16.1 3.1 %score.1 = (bf16[128,4096]{1,0:T(8,128)(2,1)S(1)}, bf16[16,4096]{1,0:T(8,128)(2,1)S(1)}, f32[128,128]{1,0:T(8,128)S(1)}, f32[8,128]{1,0:T(8,128)S(1)}, f32[16,1,128]{2,1,0:T(1,128)}) custom-call(bf16[128,640]{1,0:T(8,128)(2,1)S(1)} %bitcast.6, f32[1,4096]{1,0:T(1,128)S(1)} %get-tuple-element.15.gain_ref, bf16[512,2048]{1,0:T(8,128)(2,1)S(1)} %get-tuple-element.16.near_ref, ...), custom_call_target="tpu_custom_call" | custom-call | tf_op jit(solution)/shard_map/score/pallas_call | solution.py:312
  19.2 0.0 copy-start.1
  19.2 0.0 copy-start.2
  19.2 0.9 %mix.3 = f32[56,2048]{1,0:T(8,128)S(1)} custom-call(s32[1]{0:T(128)} %bitcast.3.base_ref, bf16[16,4096]{1,0:T(8,128)(2,1)S(1)} %get-tuple-element.19.query_ref, f32[1,4096]{1,0:T(1,128)S(1)} %get-tuple-element.15.gain_ref, bf16[128,4096]{1,0:T(8,128)(2,1)S(1)} %get-tuple-element.20.raw_ref, f32[128,128]{1,0:T(8,128)S(1)} %get-tuple-element.21.cols_ref, ...), custom_call_target="tpu_custom_call" | custom-call | flops 67108864 | bytes 2097152 | tf_op jit(solution)/shard_map/mix/pallas_call | solution.py:334
  20.1 0.1 collective-permute-start
  20.2 4.8 %all-to-all-start.1 = ((f32[16,1,128]{2,1,0:T(1,128)}), f32[16,1,128]{2,1,0:T(1,128)S(1)}, u32[]{:S(2)}, u32[]{:S(2)}) async-start(f32[16,1,128]{2,1,0:T(1,128)} %get-tuple-element.18), calls=%async_computation.1 | async-start | bytes 16384 | tf_op jit(solution)/shard_map/all_to_all | solution.py:272
  25.0 0.9 %mix.2.mine_ref = f32[56,2048]{1,0:T(8,128)S(1)} custom-call(s32[1]{0:T(128)} %bitcast.2.base_ref, bf16[16,4096]{1,0:T(8,128)(2,1)S(1)} %get-tuple-element.19.query_ref, f32[1,4096]{1,0:T(1,128)S(1)} %get-tuple-element.15.gain_ref, bf16[128,4096]{1,0:T(8,128)(2,1)S(1)} %get-tuple-element.20.raw_ref, f32[128,128]{1,0:T(8,128)S(1)} %get-tuple-element.21.cols_ref, ...), custom_call_target="tpu_custom_call" | custom-call | flops 67108864 | bytes 2097152 | tf_op jit(solution)/shard_map/mix/pallas_call | solution.py:334
  25.9 3.2 %all-to-all-done.1.sums_ref = f32[16,1,128]{2,1,0:T(1,128)S(1)} async-done(((f32[16,1,128]{2,1,0:T(1,128)}), f32[16,1,128]{2,1,0:T(1,128)S(1)}, u32[]{:S(2)}, u32[]{:S(2)}) %all-to-all-start.1) | async-done | bytes 8224 | tf_op jit(solution)/shard_map/all_to_all | solution.py:272
  29.1 0.0 collective-permute-done.sibling_ref
  29.1 0.8 %partial.1 = (bf16[128,512]{1,0:T(8,128)(2,1)}, f32[1,128]{1,0:T(1,128)S(1)}) custom-call(f32[16,1,128]{2,1,0:T(1,128)S(1)} %all-to-all-done.1.sums_ref, f32[56,2048]{1,0:T(8,128)S(1)} %mix.2.mine_ref, f32[56,2048]{1,0:T(8,128)S(1)} %collective-permute-done.sibling_ref), custom_call_target="tpu_custom_call" | custom-call | tf_op jit(solution)/shard_map/partial/pallas_call | solution.py:351
  29.9 4.2 %all-to-all-start.2 = ((bf16[16,8,512]{2,1,0:T(8,128)(2,1)}), bf16[16,8,512]{2,1,0:T(8,128)(2,1)S(1)}, u32[]{:S(2)}, u32[]{:S(2)}) async-start(bf16[16,8,512]{2,1,0:T(8,128)(2,1)} %bitcast.4), calls=%async_computation.2 | async-start | bytes 262144 | tf_op jit(solution)/shard_map/all_to_all | solution.py:272
  34.1 4.1 %d_passages.1 = f32[512,4096]{1,0:T(8,128)} custom-call(f32[1,128]{1,0:T(1,128)S(1)} %get-tuple-element.23.total_ref, bf16[16,4096]{1,0:T(8,128)(2,1)S(1)} %get-tuple-element.19.query_ref, f32[1,4096]{1,0:T(1,128)S(1)} %get-tuple-element.15.gain_ref, bf16[128,4096]{1,0:T(8,128)(2,1)S(1)} %get-tuple-element.20.raw_ref, ...), custom_call_target="tpu_custom_call" | custom-call | flops 1073741824 | bytes 8388608 | tf_op jit(solution)/shard_map/d_passages/pallas_call | solution.py:360
  38.2 1.6 %all-to-all-done.2.got_ref = bf16[16,8,512]{2,1,0:T(8,128)(2,1)S(1)} async-done(((bf16[16,8,512]{2,1,0:T(8,128)(2,1)}), bf16[16,8,512]{2,1,0:T(8,128)(2,1)S(1)}, u32[]{:S(2)}, u32[]{:S(2)}) %all-to-all-start.2) | async-done | bytes 131104 | tf_op jit(solution)/shard_map/all_to_all | solution.py:272
  39.8 0.0 copy-done.1
  39.8 0.0 copy-done.2
  39.8 0.9 %final.1 = (f32[1,4096]{1,0:T(1,128)}, f32[1,4096]{1,0:T(1,128)}) custom-call(bf16[16,8,512]{2,1,0:T(8,128)(2,1)S(1)} %all-to-all-done.2.got_ref, bf16[1,4096]{1,0:T(2,128)(2,1)S(1)} %copy-done.2, f32[1,4096]{1,0:T(1,128)S(1)} %bitcast.8), custom_call_target="tpu_custom_call" | custom-call | tf_op jit(solution)/shard_map/final/pallas_call | solution.py:373
Async XLA Ops:
  2.4 13.7 %all-to-all-start = ((bf16[16,8,640]{2,1,0:T(8,128)(2,1)}), bf16[16,8,640]{2,1,0:T(8,128)(2,1)S(1)}, u32[]{:S(2)}, u32[]{:S(2)}) async-start(bf16[16,8,640]{2,1,0:T(8,128)(2,1)} %pack.1), calls=%async_computation | async-start | bytes 327680 | tf_op jit(solution)/shard_map/all_to_all | solution.py:272
  9.9 0.7 %copy-start = (f32[4096]{0:T(1024)S(1)}, f32[4096]{0:T(1024)}, u32[]{:S(2)}) copy-start(f32[4096]{0:T(1024)} %param.7) | copy-start | bytes 49156
  19.2 20.6 %copy-start.1 = (f32[4096]{0:T(1024)S(1)}, f32[4096]{0:T(1024)}, u32[]{:S(2)}) copy-start(f32[4096]{0:T(1024)} %param.7) | copy-start | bytes 49156
  19.2 20.6 %copy-start.2 = (bf16[1,4096]{1,0:T(2,128)(2,1)S(1)}, bf16[1,4096]{1,0:T(2,128)(2,1)}, u32[]{:S(2)}) copy-start(bf16[1,4096]{1,0:T(2,128)(2,1)} %queries_ref.3) | copy-start | bytes 24580
  20.1 9.0 %collective-permute-start = (f32[56,2048]{1,0:T(8,128)S(1)}, f32[56,2048]{1,0:T(8,128)S(1)}, u32[]{:S(2)}, u32[]{:S(2)}) collective-permute-start(f32[56,2048]{1,0:T(8,128)S(1)} %mix.3), channel_id=1, source_target_pairs={{0,1},{1,0},{2,3},{3,2},{4,5},{5,4},{6,7},{7,6},{8,9},{9,8},{10,11... | collective-permute-start | bytes 1376264 | tf_op jit(solution)/shard_map/ppermute | solution.py:347
  20.2 8.9 %all-to-all-start.1 = ((f32[16,1,128]{2,1,0:T(1,128)}), f32[16,1,128]{2,1,0:T(1,128)S(1)}, u32[]{:S(2)}, u32[]{:S(2)}) async-start(f32[16,1,128]{2,1,0:T(1,128)} %get-tuple-element.18), calls=%async_computation.1 | async-start | bytes 16384 | tf_op jit(solution)/shard_map/all_to_all | solution.py:272
  29.9 9.9 %all-to-all-start.2 = ((bf16[16,8,512]{2,1,0:T(8,128)(2,1)}), bf16[16,8,512]{2,1,0:T(8,128)(2,1)S(1)}, u32[]{:S(2)}, u32[]{:S(2)}) async-start(bf16[16,8,512]{2,1,0:T(8,128)(2,1)} %bitcast.4), calls=%async_computation.2 | async-start | bytes 262144 | tf_op jit(solution)/shard_map/all_to_all | solution.py:272

commit v13 on v12

--- a/solution.py
+++ b/solution.py
@@ -106,8 +106,40 @@
         copy.wait()
 
 
+def mix(base, query_ref, gain_ref, raw_ref, cols, lines, out_ref):
+    queries = query_ref.shape[0]
+    pairs = raw_ref.shape[0]
+    chunk = out_ref.shape[1] // 2
+    cos, inverse, query_inverse = cols[:, 2:3], cols[:, 3:4], cols[:, 5:6]
+    own = belongs((queries, pairs), 1)
+    by_weight = split(jnp.where(own, lines[0:1, :], 0.0))
+    by_mark = split(jnp.where(own, lines[1:2, :], 0.0))
+    plain = jnp.concatenate([*by_weight, *by_mark], axis=0)
+    repeat = jnp.where(belongs((pairs, queries), 0), 1.0, 0.0).astype(bf16)
+    for k in range(2):
+        part = slice(k * chunk, (k + 1) * chunk)
+        there = pl.ds(pl.multiple_of(base + k * chunk, 128), chunk)
+        row = (raw_ref[:, there].astype(f32) * gain_ref[:, there] * inverse).astype(bf16)
+        mixed = dot(plain, row, nn_dims)
+        out_ref[:queries, part] = mixed[:queries] + mixed[queries : 2 * queries]
+        out_ref[queries : 2 * queries, part] = mixed[2 * queries : 3 * queries] + mixed[3 * queries :]
+        row = row.astype(f32)
+        query = dot(repeat, query_ref[:, there], nn_dims) * query_inverse
+        turned = row * (query.astype(bf16).astype(f32) - cos * row)
+        mixed = dot(plain, turned.astype(bf16), nn_dims)
+        out_ref[2 * queries : 3 * queries, part] = mixed[:queries] + mixed[queries : 2 * queries]
+        last = jnp.sum(mixed[2 * queries :], axis=0, keepdims=True)
+        out_ref[3 * queries :, part] = jnp.broadcast_to(last, (8, chunk))
+
+
+def mix_kernel(core_ref, query_ref, gain_ref, raw_ref, cols_ref, rows_ref, out_ref):
+    base = core_ref[0] * out_ref.shape[1]
+    mix(base, query_ref, gain_ref, raw_ref, cols_ref[...], rows_ref[...], out_ref)
+
+
 def score_kernel(
-    got_ref, gain_ref, near_ref, far_ref, raw_ref, query_ref, cols_ref, rows_ref, sums_ref, held, wide, sems
+    core_ref, got_ref, gain_ref, near_ref, far_ref,
+    raw_ref, query_ref, cols_ref, rows_ref, sums_ref, theirs_ref, held, wide, sems,
 ):
     queries, width = query_ref.shape
     pairs = queries * 8
@@ -121,6 +153,10 @@
         copies[-1].start()
     tiles = wide.shape[0]
     loaded = [got_ref[:, j * 128 : (j + 1) * 128].astype(f32) for j in range(tiles + 1)]
+    squares = sum(x * x for x in loaded[:-1])
+    squares = jnp.sum(squares, axis=1, keepdims=True).reshape(queries, 8, 1)
+    squares = jnp.broadcast_to(jnp.sum(squares, axis=1, keepdims=True), (queries, 8, 1))
+    query_inverse = 1.0 / jnp.sqrt(squares.reshape(pairs, 1))
     for j in range(tiles):
         wide[j] = loaded[j]
     query = [wide[j, pl.ds(k, queries, stride=8), :] for k in range(8) for j in range(tiles)]
@@ -150,10 +186,6 @@
             size = size + lifted[:, tile] * lifted[:, tile]
             along = along + lifted[:, tile] * repeated[:, tile]
     inverse = 1.0 / jnp.sqrt(jnp.sum(size, axis=1, keepdims=True))
-    squares = sum(x * x for x in loaded[:-1])
-    squares = jnp.sum(squares, axis=1, keepdims=True).reshape(queries, 8, 1)
-    squares = jnp.broadcast_to(jnp.sum(squares, axis=1, keepdims=True), (queries, 8, 1))
-    query_inverse = 1.0 / jnp.sqrt(squares.reshape(pairs, 1))
     cos = jnp.sum(along, axis=1, keepdims=True) * inverse * query_inverse
     weight = jnp.where(mark > 0.0, jnp.exp(cos * score_scale), 0.0)
     lane = lax.broadcasted_iota(jnp.int32, (pairs, 128), 1)
@@ -164,33 +196,8 @@
     flipped = jnp.transpose(cols)[:8]
     rows_ref[...] = flipped
     sums_ref[...] = jnp.broadcast_to(flipped[None, :1], sums_ref.shape)
-
-
-def mix_kernel(base_ref, query_ref, gain_ref, raw_ref, cols_ref, rows_ref, out_ref):
-    queries = query_ref.shape[0]
-    pairs = raw_ref.shape[0]
-    chunk = out_ref.shape[1] // 2
-    cos, inverse = cols_ref[:, 2:3], cols_ref[:, 3:4]
-    weight, mark = rows_ref[0:1, :], rows_ref[1:2, :]
-    own = belongs((queries, pairs), 1)
-    by_weight = split(jnp.where(own, weight, 0.0))
-    by_mark = split(jnp.where(own, mark, 0.0))
-    plain = jnp.concatenate([*by_weight, *by_mark], axis=0)
-    repeat = jnp.where(belongs((pairs, queries), 0), 1.0, 0.0).astype(bf16)
-    for k in range(2):
-        part = slice(k * chunk, (k + 1) * chunk)
-        there = pl.ds(pl.multiple_of(base_ref[0] + k * chunk, 128), chunk)
-        row = (raw_ref[:, there].astype(f32) * gain_ref[:, there] * inverse).astype(bf16)
-        mixed = dot(plain, row, nn_dims)
-        out_ref[:queries, part] = mixed[:queries] + mixed[queries : 2 * queries]
-        out_ref[queries : 2 * queries, part] = mixed[2 * queries : 3 * queries] + mixed[3 * queries :]
-        row = row.astype(f32)
-        query = dot(repeat, query_ref[:, there], nn_dims) * cols_ref[:, 5:6]
-        turned = row * (query.astype(bf16).astype(f32) - cos * row)
-        mixed = dot(plain, turned.astype(bf16), nn_dims)
-        out_ref[2 * queries : 3 * queries, part] = mixed[:queries] + mixed[queries : 2 * queries]
-        last = jnp.sum(mixed[2 * queries :], axis=0, keepdims=True)
-        out_ref[3 * queries :, part] = jnp.broadcast_to(last, (8, chunk))
+    base = (1 - core_ref[0]) * theirs_ref.shape[1]
+    mix(base, query_ref, gain_ref, raw_ref, cols, flipped, theirs_ref)
 
 
 def partial_kernel(sums_ref, mine_ref, sibling_ref, out_ref, total_ref, laid):
@@ -309,15 +316,18 @@
             flops=0, bytes_accessed=4 * rows * width, transcendentals=0
         ),
     )(passages, gain)
-    raw, query, cols, lines, sums = pl.pallas_call(
+    half = width // 2
+    core = (lax.axis_index("hash") % 2).astype(jnp.int32).reshape(1)
+    raw, query, cols, lines, sums, theirs = pl.pallas_call(
         score_kernel,
-        in_specs=[whole(), whole(), whole(), outside()],
+        in_specs=[pl.BlockSpec(memory_space=pltpu.SMEM), whole(), whole(), whole(), outside()],
         out_shape=[
             shape((pairs, width), bf16),
             shape((count, width), bf16),
             shape((pairs, 128)),
             shape((8, pairs)),
             shape((count, 1, pairs)),
+            shape((3 * count + 8, half)),
         ],
         scratch_shapes=[
             pltpu.VMEM((rows, width // 2), bf16),
@@ -326,27 +336,20 @@
         ],
         compiler_params=params(48),
         name="score",
-    )(got, gain_near, near, far)
-
-    half = width // 2
-
-    def mix(base):
-        return pl.pallas_call(
-            mix_kernel,
-            in_specs=[pl.BlockSpec(memory_space=pltpu.SMEM)] + [whole()] * 5,
-            out_shape=shape((3 * count + 8, half)),
-            compiler_params=params(48),
-            name="mix",
-            cost_estimate=pl.CostEstimate(
-                flops=8 * count * pairs * width, bytes_accessed=4 * pairs * width, transcendentals=0
-            ),
-        )(base.astype(jnp.int32).reshape(1), query, gain_near, raw, cols, lines)
-
-    core = lax.axis_index("hash") % 2
-    theirs = mix((1 - core) * half)
+    )(core, got, gain_near, near, far)
+
+    got_sums = exchange(sums)
     sibling = lax.ppermute(theirs, "hash", [(i, i ^ 1) for i in range(count)])
-    mine = mix(core * half)
-    got_sums = exchange(sums)
+    mine = pl.pallas_call(
+        mix_kernel,
+        in_specs=[pl.BlockSpec(memory_space=pltpu.SMEM)] + [whole()] * 5,
+        out_shape=shape((3 * count + 8, half)),
+        compiler_params=params(48),
+        name="mix",
+        cost_estimate=pl.CostEstimate(
+            flops=8 * count * pairs * width, bytes_accessed=4 * pairs * width, transcendentals=0
+        ),
+    )(core, query, gain_near, raw, cols, lines)
 
     partial, total = pl.pallas_call(
         partial_kernel,

time: 41.2 us -> 41.3 us (level)
    pallas_call x3 -> x2, Pallas kernels: 4.81 us -> 4.94 us  [the longest x1 4.07 us: local(): pl.pallas_call(score_kernel, in_specs=[pl.BlockSpec(memory_space=pltpu.SM...]
where the time goes in v13:
time: 41.3 us; the launch traced here: 40.8 us
  starting transfers between devices  16.7 us (40%)
  Pallas kernels  15.2 us (37%)
  waiting for transfers between devices  7.47 us (18%)
  local copies, waits for them, and re-layouts  0.72 us (2%)
  between operations  0.7 us (2%)
    all_to_all x3, starting transfers between devices, exchange(): lax.all_to_all(x, 'hash', split_axis=0, concat_axis=0, axis_index_groups=...  16.6 us
    all_to_all x3, waiting for transfers between devices, exchange(): lax.all_to_all(x, 'hash', split_axis=0, concat_axis=0, axis_index_groups=...  7.47 us
    pallas_call x1, Pallas kernels, local(): pl.pallas_call(score_kernel, in_specs=[pl.BlockSpec(memory_space=pltpu.SM...  4.07 us
    pallas_call x1, Pallas kernels, local(): pl.pallas_call(passage_kernel, in_specs=[whole()] * 6, out_specs=outside(...  4.06 us
    pallas_call x1, Pallas kernels, local(): pl.pallas_call(stage_kernel, in_specs=[outside(), whole()], out_specs=[wh...  2.75 us
    pallas_call x1, Pallas kernels, local(): pl.pallas_call(functools.partial(pack_kernel, rows), out_shape=shape((cou...  1.72 us
    pallas_call x1, Pallas kernels, local(): pl.pallas_call(final_kernel, out_shape=[shape((1, width)), shape((1, widt...  0.87 us
    pallas_call x1, Pallas kernels, local(): pl.pallas_call(mix_kernel, in_specs=[pl.BlockSpec(memory_space=pltpu.SMEM...  0.87 us
  transfers between devices with their start and end apart: 4, of which 3 were waited for; matrix products, arithmetic and copies ran while one was open for 0% of the time, Pallas kernels for 19%

profile of v13, /device:TPU:0, one launch (start us, length us, event | category | flops | bytes accessed | tf_op | source)
XLA Modules:
  0.0 40.8 jit_solution(2939376495597760694)
XLA Ops:
  0.6 1.7 %pack.1 = bf16[16,8,640]{2,1,0:T(8,128)(2,1)} custom-call(bf16[1,4096]{1,0:T(2,128)(2,1)} %queries_ref.3, s32[1,128]{1,0:T(1,128)} %candidates_ref.1, s32[1,128]{1,0:T(1,128)} %teacher_ref.1), custom_call_target="tpu_custom_call" | custom-call | tf_op jit(solution)/shard_map/pack/pallas_call | solution.py:290
  2.4 7.6 %all-to-all-start = ((bf16[16,8,640]{2,1,0:T(8,128)(2,1)}), bf16[16,8,640]{2,1,0:T(8,128)(2,1)S(1)}, u32[]{:S(2)}, u32[]{:S(2)}) async-start(bf16[16,8,640]{2,1,0:T(8,128)(2,1)} %pack.1), calls=%async_computation | async-start | bytes 327680 | tf_op jit(solution)/shard_map/all_to_all | solution.py:279
  9.9 0.0 copy-start
  9.9 0.7 %copy-done = f32[4096]{0:T(1024)S(1)} copy-done((f32[4096]{0:T(1024)S(1)}, f32[4096]{0:T(1024)}, u32[]{:S(2)}) %copy-start) | copy-done | bytes 16408
  10.6 2.8 %stage.1 = (bf16[512,2048]{1,0:T(8,128)(2,1)S(1)}, bf16[5120,2048]{1,0:T(8,128)(2,1)}, f32[1,4096]{1,0:T(1,128)S(1)}) custom-call(bf16[512,4096]{1,0:T(8,128)(2,1)} %passages_ref.1, f32[1,4096]{1,0:T(1,128)S(1)} %bitcast.6), custom_call_target="tpu_custom_call" | custom-call | bytes 8388608 | tf_op jit(solution)/shard_map/stage/pallas_call | solution.py:299
  13.4 2.7 %all-to-all-done = bf16[16,8,640]{2,1,0:T(8,128)(2,1)S(1)} async-done(((bf16[16,8,640]{2,1,0:T(8,128)(2,1)}), bf16[16,8,640]{2,1,0:T(8,128)(2,1)S(1)}, u32[]{:S(2)}, u32[]{:S(2)}) %all-to-all-start) | async-done | bytes 163872 | tf_op jit(solution)/shard_map/all_to_all | solution.py:279
  16.1 4.1 %score.1 = (bf16[128,4096]{1,0:T(8,128)(2,1)S(1)}, bf16[16,4096]{1,0:T(8,128)(2,1)S(1)}, f32[128,128]{1,0:T(8,128)S(1)}, f32[8,128]{1,0:T(8,128)S(1)}, f32[16,1,128]{2,1,0:T(1,128)}, /*index=5*/f32[56,2048]{1,0:T(8,128)}) custom-call(s32[1]{0:T(128)} %bitcast.core_ref, bf16[128,640]{1,0:T(8,128)(2,1)S(1)} %bitcast.5, ...), custom_call_target="tpu_custom_call" | custom-call | tf_op jit(solution)/shard_map/score/pallas_call | solution.py:321
  20.2 0.0 copy-start.1
  20.2 0.0 copy-start.2
  20.2 0.1 collective-permute-start
  20.3 4.8 %all-to-all-start.1 = ((f32[16,1,128]{2,1,0:T(1,128)}), f32[16,1,128]{2,1,0:T(1,128)S(1)}, u32[]{:S(2)}, u32[]{:S(2)}) async-start(f32[16,1,128]{2,1,0:T(1,128)} %get-tuple-element.19), calls=%async_computation.1 | async-start | bytes 16384 | tf_op jit(solution)/shard_map/all_to_all | solution.py:279
  25.1 0.9 %mix.1.mine_ref = f32[56,2048]{1,0:T(8,128)S(1)} custom-call(s32[1]{0:T(128)} %bitcast.core_ref, bf16[16,4096]{1,0:T(8,128)(2,1)S(1)} %get-tuple-element.20.query_ref, f32[1,4096]{1,0:T(1,128)S(1)} %get-tuple-element.16.gain_ref, bf16[128,4096]{1,0:T(8,128)(2,1)S(1)} %get-tuple-element.21.raw_ref, f32[128,128]{1,0:T(8,128)S(1)} %get-tuple-element.22.cols_ref, ...), custom_call_target="tpu_custom_call" | custom-call | flops 67108864 | bytes 2097152 | tf_op jit(solution)/shard_map/mix/pallas_call | solution.py:343
  26.0 3.2 %all-to-all-done.1.sums_ref = f32[16,1,128]{2,1,0:T(1,128)S(1)} async-done(((f32[16,1,128]{2,1,0:T(1,128)}), f32[16,1,128]{2,1,0:T(1,128)S(1)}, u32[]{:S(2)}, u32[]{:S(2)}) %all-to-all-start.1) | async-done | bytes 8224 | tf_op jit(solution)/shard_map/all_to_all | solution.py:279
  29.2 0.0 collective-permute-done.sibling_ref
  29.2 0.8 %partial.1 = (bf16[128,512]{1,0:T(8,128)(2,1)}, f32[1,128]{1,0:T(1,128)S(1)}) custom-call(f32[16,1,128]{2,1,0:T(1,128)S(1)} %all-to-all-done.1.sums_ref, f32[56,2048]{1,0:T(8,128)S(1)} %mix.1.mine_ref, f32[56,2048]{1,0:T(8,128)S(1)} %collective-permute-done.sibling_ref), custom_call_target="tpu_custom_call" | custom-call | tf_op jit(solution)/shard_map/partial/pallas_call | solution.py:354
  30.0 4.2 %all-to-all-start.2 = ((bf16[16,8,512]{2,1,0:T(8,128)(2,1)}), bf16[16,8,512]{2,1,0:T(8,128)(2,1)S(1)}, u32[]{:S(2)}, u32[]{:S(2)}) async-start(bf16[16,8,512]{2,1,0:T(8,128)(2,1)} %bitcast.3), calls=%async_computation.2 | async-start | bytes 262144 | tf_op jit(solution)/shard_map/all_to_all | solution.py:279
  34.3 4.1 %d_passages.1 = f32[512,4096]{1,0:T(8,128)} custom-call(f32[1,128]{1,0:T(1,128)S(1)} %get-tuple-element.25.total_ref, bf16[16,4096]{1,0:T(8,128)(2,1)S(1)} %get-tuple-element.20.query_ref, f32[1,4096]{1,0:T(1,128)S(1)} %get-tuple-element.16.gain_ref, bf16[128,4096]{1,0:T(8,128)(2,1)S(1)} %get-tuple-element.21.raw_ref, ...), custom_call_target="tpu_custom_call" | custom-call | flops 1073741824 | bytes 8388608 | tf_op jit(solution)/shard_map/d_passages/pallas_call | solution.py:363
  38.3 1.6 %all-to-all-done.2.got_ref = bf16[16,8,512]{2,1,0:T(8,128)(2,1)S(1)} async-done(((bf16[16,8,512]{2,1,0:T(8,128)(2,1)}), bf16[16,8,512]{2,1,0:T(8,128)(2,1)S(1)}, u32[]{:S(2)}, u32[]{:S(2)}) %all-to-all-start.2) | async-done | bytes 131104 | tf_op jit(solution)/shard_map/all_to_all | solution.py:279
  39.9 0.0 copy-done.1
  39.9 0.0 copy-done.2
  39.9 0.9 %final.1 = (f32[1,4096]{1,0:T(1,128)}, f32[1,4096]{1,0:T(1,128)}) custom-call(bf16[16,8,512]{2,1,0:T(8,128)(2,1)S(1)} %all-to-all-done.2.got_ref, bf16[1,4096]{1,0:T(2,128)(2,1)S(1)} %copy-done.2, f32[1,4096]{1,0:T(1,128)S(1)} %bitcast.7), custom_call_target="tpu_custom_call" | custom-call | tf_op jit(solution)/shard_map/final/pallas_call | solution.py:376
Async XLA Ops:
  2.4 13.7 %all-to-all-start = ((bf16[16,8,640]{2,1,0:T(8,128)(2,1)}), bf16[16,8,640]{2,1,0:T(8,128)(2,1)S(1)}, u32[]{:S(2)}, u32[]{:S(2)}) async-start(bf16[16,8,640]{2,1,0:T(8,128)(2,1)} %pack.1), calls=%async_computation | async-start | bytes 327680 | tf_op jit(solution)/shard_map/all_to_all | solution.py:279
  9.9 0.7 %copy-start = (f32[4096]{0:T(1024)S(1)}, f32[4096]{0:T(1024)}, u32[]{:S(2)}) copy-start(f32[4096]{0:T(1024)} %param.7) | copy-start | bytes 49156
  20.2 19.7 %copy-start.1 = (f32[4096]{0:T(1024)S(1)}, f32[4096]{0:T(1024)}, u32[]{:S(2)}) copy-start(f32[4096]{0:T(1024)} %param.7) | copy-start | bytes 49156
  20.2 19.7 %copy-start.2 = (bf16[1,4096]{1,0:T(2,128)(2,1)S(1)}, bf16[1,4096]{1,0:T(2,128)(2,1)}, u32[]{:S(2)}) copy-start(bf16[1,4096]{1,0:T(2,128)(2,1)} %queries_ref.3) | copy-start | bytes 24580
  20.2 9.0 %collective-permute-start = (f32[56,2048]{1,0:T(8,128)}, f32[56,2048]{1,0:T(8,128)S(1)}, u32[]{:S(2)}, u32[]{:S(2)}) collective-permute-start(f32[56,2048]{1,0:T(8,128)} %get-tuple-element.24), channel_id=1, source_target_pairs={{0,1},{1,0},{2,3},{3,2},{4,5},{5,4},{6,7},{7,6},{8,9},{9,8},{10,11... | collective-permute-start | bytes 1376264 | tf_op jit(solution)/shard_map/ppermute | solution.py:342
  20.3 8.9 %all-to-all-start.1 = ((f32[16,1,128]{2,1,0:T(1,128)}), f32[16,1,128]{2,1,0:T(1,128)S(1)}, u32[]{:S(2)}, u32[]{:S(2)}) async-start(f32[16,1,128]{2,1,0:T(1,128)} %get-tuple-element.19), calls=%async_computation.1 | async-start | bytes 16384 | tf_op jit(solution)/shard_map/all_to_all | solution.py:279
  30.0 9.9 %all-to-all-start.2 = ((bf16[16,8,512]{2,1,0:T(8,128)(2,1)}), bf16[16,8,512]{2,1,0:T(8,128)(2,1)S(1)}, u32[]{:S(2)}, u32[]{:S(2)}) async-start(bf16[16,8,512]{2,1,0:T(8,128)(2,1)} %bitcast.3), calls=%async_computation.2 | async-start | bytes 262144 | tf_op jit(solution)/shard_map/all_to_all | solution.py:279

commit v14 on v13

--- a/solution.py
+++ b/solution.py
@@ -106,10 +106,11 @@
         copy.wait()
 
 
-def mix(base, query_ref, gain_ref, raw_ref, cols, lines, out_ref):
+def mix(base, first, query_ref, gain_ref, raw_ref, lines, out_ref, before_ref):
     queries = query_ref.shape[0]
     pairs = raw_ref.shape[0]
     chunk = out_ref.shape[1] // 2
+    cols = jnp.transpose(jnp.concatenate([lines, jnp.zeros((120, pairs), f32)], axis=0))
     cos, inverse, query_inverse = cols[:, 2:3], cols[:, 3:4], cols[:, 5:6]
     own = belongs((queries, pairs), 1)
     by_weight = split(jnp.where(own, lines[0:1, :], 0.0))
@@ -119,22 +120,34 @@
     for k in range(2):
         part = slice(k * chunk, (k + 1) * chunk)
         there = pl.ds(pl.multiple_of(base + k * chunk, 128), chunk)
-        row = (raw_ref[:, there].astype(f32) * gain_ref[:, there] * inverse).astype(bf16)
-        mixed = dot(plain, row, nn_dims)
-        out_ref[:queries, part] = mixed[:queries] + mixed[queries : 2 * queries]
-        out_ref[queries : 2 * queries, part] = mixed[2 * queries : 3 * queries] + mixed[3 * queries :]
+        here = pl.ds(pl.multiple_of(first + k * chunk, 128), chunk)
+        row = (raw_ref[:, here].astype(f32) * gain_ref[:, there] * inverse).astype(bf16)
+        plainly = dot(plain, row, nn_dims)
         row = row.astype(f32)
         query = dot(repeat, query_ref[:, there], nn_dims) * query_inverse
         turned = row * (query.astype(bf16).astype(f32) - cos * row)
-        mixed = dot(plain, turned.astype(bf16), nn_dims)
-        out_ref[2 * queries : 3 * queries, part] = mixed[:queries] + mixed[queries : 2 * queries]
-        last = jnp.sum(mixed[2 * queries :], axis=0, keepdims=True)
-        out_ref[3 * queries :, part] = jnp.broadcast_to(last, (8, chunk))
-
-
-def mix_kernel(core_ref, query_ref, gain_ref, raw_ref, cols_ref, rows_ref, out_ref):
+        turned = dot(plain, turned.astype(bf16), nn_dims)
+        last = jnp.sum(turned[2 * queries :], axis=0, keepdims=True)
+        sums = jnp.concatenate(
+            [
+                plainly[:queries] + plainly[queries : 2 * queries],
+                plainly[2 * queries : 3 * queries] + plainly[3 * queries :],
+                turned[:queries] + turned[queries : 2 * queries],
+                jnp.broadcast_to(last, (8, chunk)),
+            ],
+            axis=0,
+        )
+        out_ref[:, part] = sums if before_ref is None else sums + before_ref[:, part]
+
+
+def mine_kernel(core_ref, query_ref, gain_ref, raw_ref, rows_ref, out_ref):
     base = core_ref[0] * out_ref.shape[1]
-    mix(base, query_ref, gain_ref, raw_ref, cols_ref[...], rows_ref[...], out_ref)
+    mix(base, base, query_ref, gain_ref, raw_ref, rows_ref[...], out_ref, None)
+
+
+def both_kernel(core_ref, query_ref, gain_ref, raw_ref, rows_ref, mine_ref, out_ref):
+    base = core_ref[0] * out_ref.shape[1]
+    mix(base, 0, query_ref, gain_ref, raw_ref, rows_ref[...], out_ref, mine_ref)
 
 
 def score_kernel(
@@ -185,6 +198,8 @@
             tile = slice(j * 128, (j + 1) * 128)
             size = size + lifted[:, tile] * lifted[:, tile]
             along = along + lifted[:, tile] * repeated[:, tile]
+    there = theirs_ref.shape[1]
+    theirs_ref[...] = raw_ref[:, pl.ds(pl.multiple_of((1 - core_ref[0]) * there, 128), there)]
     inverse = 1.0 / jnp.sqrt(jnp.sum(size, axis=1, keepdims=True))
     cos = jnp.sum(along, axis=1, keepdims=True) * inverse * query_inverse
     weight = jnp.where(mark > 0.0, jnp.exp(cos * score_scale), 0.0)
@@ -196,18 +211,16 @@
     flipped = jnp.transpose(cols)[:8]
     rows_ref[...] = flipped
     sums_ref[...] = jnp.broadcast_to(flipped[None, :1], sums_ref.shape)
-    base = (1 - core_ref[0]) * theirs_ref.shape[1]
-    mix(base, query_ref, gain_ref, raw_ref, cols, flipped, theirs_ref)
-
-
-def partial_kernel(sums_ref, mine_ref, sibling_ref, out_ref, total_ref, laid):
+
+
+def partial_kernel(sums_ref, both_ref, out_ref, total_ref, laid):
     queries = sums_ref.shape[2] // 8
-    width = mine_ref.shape[1]
+    width = both_ref.shape[1]
     total = jnp.sum(sums_ref[...][:, 0, :], axis=0, keepdims=True)
     total_ref[...] = total
     own = belongs((queries, total.shape[1]), 1)
     inverse = 1.0 / jnp.sum(jnp.where(own, total, 0.0), axis=1, keepdims=True)
-    both = mine_ref[...] + sibling_ref[...]
+    both = both_ref[...]
     partial = coef_scale * (both[:queries] * inverse - both[queries : 2 * queries])
     gain_part = jnp.sum(both[2 * queries : 3 * queries] * inverse, axis=0, keepdims=True)
     gain_part = coef_scale * (gain_part - both[3 * queries : 3 * queries + 1])
@@ -327,7 +340,7 @@
             shape((pairs, 128)),
             shape((8, pairs)),
             shape((count, 1, pairs)),
-            shape((3 * count + 8, half)),
+            shape((pairs, half), bf16),
         ],
         scratch_shapes=[
             pltpu.VMEM((rows, width // 2), bf16),
@@ -339,17 +352,24 @@
     )(core, got, gain_near, near, far)
 
     got_sums = exchange(sums)
-    sibling = lax.ppermute(theirs, "hash", [(i, i ^ 1) for i in range(count)])
-    mine = pl.pallas_call(
-        mix_kernel,
-        in_specs=[pl.BlockSpec(memory_space=pltpu.SMEM)] + [whole()] * 5,
-        out_shape=shape((3 * count + 8, half)),
-        compiler_params=params(48),
-        name="mix",
-        cost_estimate=pl.CostEstimate(
-            flops=8 * count * pairs * width, bytes_accessed=4 * pairs * width, transcendentals=0
-        ),
-    )(core, query, gain_near, raw, cols, lines)
+    swap = [(i, i ^ 1) for i in range(count)]
+    sibling_raw = lax.ppermute(theirs, "hash", swap)
+    sibling_lines = lax.ppermute(lines, "hash", swap)
+
+    def mixed(kernel, *operands):
+        return pl.pallas_call(
+            kernel,
+            in_specs=[pl.BlockSpec(memory_space=pltpu.SMEM)] + [whole()] * (len(operands) + 2),
+            out_shape=shape((3 * count + 8, half)),
+            compiler_params=params(48),
+            name="mix",
+            cost_estimate=pl.CostEstimate(
+                flops=8 * count * pairs * width, bytes_accessed=4 * pairs * width, transcendentals=0
+            ),
+        )(core, query, gain_near, *operands)
+
+    mine = mixed(mine_kernel, raw, lines)
+    both = mixed(both_kernel, sibling_raw, sibling_lines, mine)
 
     partial, total = pl.pallas_call(
         partial_kernel,
@@ -357,7 +377,7 @@
         scratch_shapes=[pltpu.VMEM((half // 512, pairs, 128), f32)],
         compiler_params=params(48),
         name="partial",
-    )(got_sums, mine, sibling)
+    )(got_sums, both)
     got_partial = exchange(partial.reshape(count, 8, half // 4))
 
     d_passages = pl.pallas_call(

time: 41.3 us -> 40.1 us (0.971)
  waiting for transfers between devices: 7.47 us -> 6.31 us
    all_to_all x3, waiting for transfers between devices: 7.47 us -> 6.23 us  [exchange(): lax.all_to_all(x, 'hash', split_axis=0, concat_axis=0, axis_index_groups=...]
    pallas_call x1, Pallas kernels: 4.07 us -> 2.85 us  [local(): pl.pallas_call(score_kernel, in_specs=[pl.BlockSpec(memory_space=pltpu.SM...]
    pallas_call x1 -> x2, Pallas kernels: 0.87 us -> 1.87 us  [mixed(): pl.pallas_call(kernel, in_specs=[pl.BlockSpec(memory_space=pltpu.SMEM)] +...]
  transfers between devices with their start and end apart: 4 -> 5, of which waited for: 3 -> 4; matrix products, arithmetic and copies ran while one was open for 0% -> 0% of each run, Pallas kernels for 19% -> 22%
where the time goes in v14:
time: 40.1 us; the launch traced here: 39.6 us
  starting transfers between devices  16.9 us (42%)
  Pallas kernels  15 us (37%)
  waiting for transfers between devices  6.31 us (16%)
  local copies, waits for them, and re-layouts  0.72 us (2%)
  between operations  0.71 us (2%)
    all_to_all x3, starting transfers between devices, exchange(): lax.all_to_all(x, 'hash', split_axis=0, concat_axis=0, axis_index_groups=...  16.6 us
    all_to_all x3, waiting for transfers between devices, exchange(): lax.all_to_all(x, 'hash', split_axis=0, concat_axis=0, axis_index_groups=...  6.23 us
    pallas_call x1, Pallas kernels, local(): pl.pallas_call(passage_kernel, in_specs=[whole()] * 6, out_specs=outside(...  4.06 us
    pallas_call x1, Pallas kernels, local(): pl.pallas_call(score_kernel, in_specs=[pl.BlockSpec(memory_space=pltpu.SM...  2.85 us
    pallas_call x1, Pallas kernels, local(): pl.pallas_call(stage_kernel, in_specs=[outside(), whole()], out_specs=[wh...  2.75 us
    pallas_call x2, Pallas kernels, mixed(): pl.pallas_call(kernel, in_specs=[pl.BlockSpec(memory_space=pltpu.SMEM)] +...  1.87 us
    pallas_call x1, Pallas kernels, local(): pl.pallas_call(functools.partial(pack_kernel, rows), out_shape=shape((cou...  1.72 us
    pallas_call x1, Pallas kernels, local(): pl.pallas_call(final_kernel, out_shape=[shape((1, width)), shape((1, widt...  0.87 us
  transfers between devices with their start and end apart: 5, of which 4 were waited for; matrix products, arithmetic and copies ran while one was open for 0% of the time, Pallas kernels for 22%

profile of v14, /device:TPU:0, one launch (start us, length us, event | category | flops | bytes accessed | tf_op | source)
XLA Modules:
  0.0 39.6 jit_solution(9085300718568743270)
XLA Ops:
  0.6 1.7 %pack.1 = bf16[16,8,640]{2,1,0:T(8,128)(2,1)} custom-call(bf16[1,4096]{1,0:T(2,128)(2,1)} %queries_ref.3, s32[1,128]{1,0:T(1,128)} %candidates_ref.1, s32[1,128]{1,0:T(1,128)} %teacher_ref.1), custom_call_target="tpu_custom_call" | custom-call | tf_op jit(solution)/shard_map/pack/pallas_call | solution.py:303
  2.4 7.6 %all-to-all-start = ((bf16[16,8,640]{2,1,0:T(8,128)(2,1)}), bf16[16,8,640]{2,1,0:T(8,128)(2,1)S(1)}, u32[]{:S(2)}, u32[]{:S(2)}) async-start(bf16[16,8,640]{2,1,0:T(8,128)(2,1)} %pack.1), calls=%async_computation | async-start | bytes 327680 | tf_op jit(solution)/shard_map/all_to_all | solution.py:292
  9.9 0.0 copy-start
  9.9 0.7 %copy-done = f32[4096]{0:T(1024)S(1)} copy-done((f32[4096]{0:T(1024)S(1)}, f32[4096]{0:T(1024)}, u32[]{:S(2)}) %copy-start) | copy-done | bytes 16408
  10.6 2.8 %stage.1 = (bf16[512,2048]{1,0:T(8,128)(2,1)S(1)}, bf16[5120,2048]{1,0:T(8,128)(2,1)}, f32[1,4096]{1,0:T(1,128)S(1)}) custom-call(bf16[512,4096]{1,0:T(8,128)(2,1)} %passages_ref.1, f32[1,4096]{1,0:T(1,128)S(1)} %bitcast.6), custom_call_target="tpu_custom_call" | custom-call | bytes 8388608 | tf_op jit(solution)/shard_map/stage/pallas_call | solution.py:312
  13.4 2.7 %all-to-all-done = bf16[16,8,640]{2,1,0:T(8,128)(2,1)S(1)} async-done(((bf16[16,8,640]{2,1,0:T(8,128)(2,1)}), bf16[16,8,640]{2,1,0:T(8,128)(2,1)S(1)}, u32[]{:S(2)}, u32[]{:S(2)}) %all-to-all-start) | async-done | bytes 163872 | tf_op jit(solution)/shard_map/all_to_all | solution.py:292
  16.1 2.8 %score.1 = (bf16[128,4096]{1,0:T(8,128)(2,1)S(1)}, bf16[16,4096]{1,0:T(8,128)(2,1)S(1)}, f32[128,128]{1,0:T(8,128)S(1)}, f32[8,128]{1,0:T(8,128)S(1)}, f32[16,1,128]{2,1,0:T(1,128)}, /*index=5*/bf16[128,2048]{1,0:T(8,128)(2,1)}) custom-call(s32[1]{0:T(128)} %bitcast.core_ref, bf16[128,640]{1,0:T(8,128)(2,1)S(1)} %bitcast.5, ...), custom_call_target="tpu_custom_call" | custom-call | tf_op jit(solution)/shard_map/score/pallas_call | solution.py:334
  19.0 0.0 copy-start.1
  19.0 0.0 copy-start.2
  19.0 0.1 collective-permute-start
  19.1 4.8 %all-to-all-start.1 = ((f32[16,1,128]{2,1,0:T(1,128)}), f32[16,1,128]{2,1,0:T(1,128)S(1)}, u32[]{:S(2)}, u32[]{:S(2)}) async-start(f32[16,1,128]{2,1,0:T(1,128)} %get-tuple-element.19), calls=%async_computation.1 | async-start | bytes 16384 | tf_op jit(solution)/shard_map/all_to_all | solution.py:292
  23.9 0.1 collective-permute-start.1
  24.1 0.9 %mix.2.mine_ref = f32[56,2048]{1,0:T(8,128)S(1)} custom-call(s32[1]{0:T(128)} %bitcast.core_ref, bf16[16,4096]{1,0:T(8,128)(2,1)S(1)} %get-tuple-element.20.query_ref, f32[1,4096]{1,0:T(1,128)S(1)} %get-tuple-element.16.gain_ref, bf16[128,4096]{1,0:T(8,128)(2,1)S(1)} %get-tuple-element.23.raw_ref, f32[8,128]{1,0:T(8,128)S(1)} %get-tuple-element.22.rows_ref), custom_call_target="tpu_custom_call" | custom-call | flops 67108864 | bytes 2097152 | tf_op jit(solution)/shard_map/mix/pallas_call | solution.py:360
  25.0 0.1 collective-permute-done.1.rows_ref
  25.1 0.0 collective-permute-done.raw_ref
  25.1 0.9 %mix.3.both_ref = f32[56,2048]{1,0:T(8,128)S(1)} custom-call(s32[1]{0:T(128)} %bitcast.core_ref, bf16[16,4096]{1,0:T(8,128)(2,1)S(1)} %get-tuple-element.20.query_ref, f32[1,4096]{1,0:T(1,128)S(1)} %get-tuple-element.16.gain_ref, bf16[128,2048]{1,0:T(8,128)(2,1)S(1)} %collective-permute-done.raw_ref, f32[8,128]{1,0:T(8,128)S(1)} %collective-permute-done.1.rows_ref, ...), custom_call_target="tpu_custom_call" | custom-call | flops 67108864 | bytes 2097152 | tf_op jit(solution)/shard_map/mix/pallas_call | solution.py:360
  26.0 1.9 %all-to-all-done.1.sums_ref = f32[16,1,128]{2,1,0:T(1,128)S(1)} async-done(((f32[16,1,128]{2,1,0:T(1,128)}), f32[16,1,128]{2,1,0:T(1,128)S(1)}, u32[]{:S(2)}, u32[]{:S(2)}) %all-to-all-start.1) | async-done | bytes 8224 | tf_op jit(solution)/shard_map/all_to_all | solution.py:292
  28.0 0.8 %partial.1 = (bf16[128,512]{1,0:T(8,128)(2,1)}, f32[1,128]{1,0:T(1,128)S(1)}) custom-call(f32[16,1,128]{2,1,0:T(1,128)S(1)} %all-to-all-done.1.sums_ref, f32[56,2048]{1,0:T(8,128)S(1)} %mix.3.both_ref), custom_call_target="tpu_custom_call" | custom-call | tf_op jit(solution)/shard_map/partial/pallas_call | solution.py:374
  28.8 4.2 %all-to-all-start.2 = ((bf16[16,8,512]{2,1,0:T(8,128)(2,1)}), bf16[16,8,512]{2,1,0:T(8,128)(2,1)S(1)}, u32[]{:S(2)}, u32[]{:S(2)}) async-start(bf16[16,8,512]{2,1,0:T(8,128)(2,1)} %bitcast.3), calls=%async_computation.2 | async-start | bytes 262144 | tf_op jit(solution)/shard_map/all_to_all | solution.py:292
  33.0 4.1 %d_passages.1 = f32[512,4096]{1,0:T(8,128)} custom-call(f32[1,128]{1,0:T(1,128)S(1)} %get-tuple-element.24.total_ref, bf16[16,4096]{1,0:T(8,128)(2,1)S(1)} %get-tuple-element.20.query_ref, f32[1,4096]{1,0:T(1,128)S(1)} %get-tuple-element.16.gain_ref, bf16[128,4096]{1,0:T(8,128)(2,1)S(1)} %get-tuple-element.23.raw_ref, ...), custom_call_target="tpu_custom_call" | custom-call | flops 1073741824 | bytes 8388608 | tf_op jit(solution)/shard_map/d_passages/pallas_call | solution.py:383
  37.1 1.6 %all-to-all-done.2.got_ref = bf16[16,8,512]{2,1,0:T(8,128)(2,1)S(1)} async-done(((bf16[16,8,512]{2,1,0:T(8,128)(2,1)}), bf16[16,8,512]{2,1,0:T(8,128)(2,1)S(1)}, u32[]{:S(2)}, u32[]{:S(2)}) %all-to-all-start.2) | async-done | bytes 131104 | tf_op jit(solution)/shard_map/all_to_all | solution.py:292
  38.7 0.0 copy-done.1
  38.7 0.0 copy-done.2
  38.7 0.9 %final.1 = (f32[1,4096]{1,0:T(1,128)}, f32[1,4096]{1,0:T(1,128)}) custom-call(bf16[16,8,512]{2,1,0:T(8,128)(2,1)S(1)} %all-to-all-done.2.got_ref, bf16[1,4096]{1,0:T(2,128)(2,1)S(1)} %copy-done.2, f32[1,4096]{1,0:T(1,128)S(1)} %bitcast.7), custom_call_target="tpu_custom_call" | custom-call | tf_op jit(solution)/shard_map/final/pallas_call | solution.py:396
Async XLA Ops:
  2.4 13.7 %all-to-all-start = ((bf16[16,8,640]{2,1,0:T(8,128)(2,1)}), bf16[16,8,640]{2,1,0:T(8,128)(2,1)S(1)}, u32[]{:S(2)}, u32[]{:S(2)}) async-start(bf16[16,8,640]{2,1,0:T(8,128)(2,1)} %pack.1), calls=%async_computation | async-start | bytes 327680 | tf_op jit(solution)/shard_map/all_to_all | solution.py:292
  9.9 0.7 %copy-start = (f32[4096]{0:T(1024)S(1)}, f32[4096]{0:T(1024)}, u32[]{:S(2)}) copy-start(f32[4096]{0:T(1024)} %param.7) | copy-start | bytes 49156
  19.0 19.7 %copy-start.1 = (f32[4096]{0:T(1024)S(1)}, f32[4096]{0:T(1024)}, u32[]{:S(2)}) copy-start(f32[4096]{0:T(1024)} %param.7) | copy-start | bytes 49156
  19.0 19.7 %copy-start.2 = (bf16[1,4096]{1,0:T(2,128)(2,1)S(1)}, bf16[1,4096]{1,0:T(2,128)(2,1)}, u32[]{:S(2)}) copy-start(bf16[1,4096]{1,0:T(2,128)(2,1)} %queries_ref.3) | copy-start | bytes 24580
  19.0 6.1 %collective-permute-start = (bf16[128,2048]{1,0:T(8,128)(2,1)}, bf16[128,2048]{1,0:T(8,128)(2,1)S(1)}, u32[]{:S(2)}, u32[]{:S(2)}) collective-permute-start(bf16[128,2048]{1,0:T(8,128)(2,1)} %get-tuple-element.21), channel_id=1, source_target_pairs={{0,1},{1,0},{2,3},{3,2},{4,5},{5,4},{6,7},{7,6},{8,9},{9,8},{10,11... | collective-permute-start | bytes 1572872 | tf_op jit(solution)/shard_map/ppermute | solution.py:356
  19.1 8.9 %all-to-all-start.1 = ((f32[16,1,128]{2,1,0:T(1,128)}), f32[16,1,128]{2,1,0:T(1,128)S(1)}, u32[]{:S(2)}, u32[]{:S(2)}) async-start(f32[16,1,128]{2,1,0:T(1,128)} %get-tuple-element.19), calls=%async_computation.1 | async-start | bytes 16384 | tf_op jit(solution)/shard_map/all_to_all | solution.py:292
  23.9 1.2 %collective-permute-start.1 = (f32[8,128]{1,0:T(8,128)S(1)}, f32[8,128]{1,0:T(8,128)S(1)}, u32[]{:S(2)}, u32[]{:S(2)}) collective-permute-start(f32[8,128]{1,0:T(8,128)S(1)} %get-tuple-element.22.rows_ref), channel_id=1, source_target_pairs={{0,1},{1,0},{2,3},{3,2},{4,5},{5,4},{6,7},{7,6},{8,9},{9,8},{10,11... | collective-permute-start | bytes 12296 | tf_op jit(solution)/shard_map/ppermute | solution.py:357
  28.8 9.9 %all-to-all-start.2 = ((bf16[16,8,512]{2,1,0:T(8,128)(2,1)}), bf16[16,8,512]{2,1,0:T(8,128)(2,1)S(1)}, u32[]{:S(2)}, u32[]{:S(2)}) async-start(bf16[16,8,512]{2,1,0:T(8,128)(2,1)} %bitcast.3), calls=%async_computation.2 | async-start | bytes 262144 | tf_op jit(solution)/shard_map/all_to_all | solution.py:292

commit v15 on v14

--- a/solution.py
+++ b/solution.py
@@ -30,7 +30,15 @@
 
 
 def member_order(count):
-    return [(i + count // 2 + 1) % count for i in range(count)]
+    first = count // 2 + 1
+    return [first, *range(0, count, 2), *(i for i in range(1, count, 2) if i != first)]
+
+
+def member_slot(owner, count):
+    first = count // 2 + 1
+    half = owner >> 1
+    odd = 1 + count // 2 + half - jnp.where(owner > first, 1, 0)
+    return jnp.where((owner & 1) == 0, 1 + half, jnp.where(owner == first, 0, odd))
 
 
 def params(megabytes):
@@ -54,7 +62,7 @@
     query = jnp.concatenate([query[:, k * width : (k + 1) * width] for k in range(8)], axis=0)
     owner = lax.div(ids, rows)
     inside = ids - owner * rows
-    slot = lax.rem(owner + (count - member_order(count)[0]), count)
+    slot = member_slot(owner, count)
     marks = jnp.exp(teacher_ref[...].astype(f32) * (1.0 / teacher_div))
     marks = marks / jnp.sum(marks, axis=1, keepdims=True)
     high, low = split(marks)
@@ -180,12 +188,10 @@
     mark = lists[:, 2:3] + lists[:, 3:4]
     lane = lax.broadcasted_iota(jnp.int32, (pairs, rows), 1).astype(f32)
     pick = jnp.where(inside == lane, 1.0, 0.0).astype(bf16)
-    repeat = jnp.where(belongs((pairs, queries), 0), 1.0, 0.0).astype(bf16)
     size = jnp.zeros((pairs, 128), f32)
-    along = jnp.zeros((pairs, 128), f32)
+    along = [jnp.zeros((8, 128), f32)] * queries
     for k in range(chunks):
         part = slice(k * chunk, (k + 1) * chunk)
-        repeated = dot(repeat, query[:, part], nn_dims)
         if k < half:
             passages = near_ref[:, part]
         else:
@@ -197,10 +203,14 @@
         for j in range(chunk // 128):
             tile = slice(j * 128, (j + 1) * 128)
             size = size + lifted[:, tile] * lifted[:, tile]
-            along = along + lifted[:, tile] * repeated[:, tile]
+            eighth, place = divmod(k * chunk // 128 + j, tiles)
+            for i in range(queries):
+                row = wide[place, i * 8 + eighth : i * 8 + eighth + 1, :]
+                along[i] = along[i] + lifted[i * 8 : i * 8 + 8, tile] * row
     there = theirs_ref.shape[1]
     theirs_ref[...] = raw_ref[:, pl.ds(pl.multiple_of((1 - core_ref[0]) * there, 128), there)]
     inverse = 1.0 / jnp.sqrt(jnp.sum(size, axis=1, keepdims=True))
+    along = jnp.concatenate(along, axis=0)
     cos = jnp.sum(along, axis=1, keepdims=True) * inverse * query_inverse
     weight = jnp.where(mark > 0.0, jnp.exp(cos * score_scale), 0.0)
     lane = lax.broadcasted_iota(jnp.int32, (pairs, 128), 1)
@@ -270,10 +280,9 @@
 
 def final_kernel(got_ref, queries_ref, gain_ref, d_queries_ref, d_gain_ref):
     count = got_ref.shape[0]
-    got = got_ref[...].astype(f32).reshape(count // 2, 2, *got_ref.shape[1:])
-    got = jnp.sum(got, axis=0)
-    first = member_order(count)[0] % 2
-    halves = [got[first], got[1 - first]]
+    got = got_ref[...].astype(f32)
+    middle = 1 + count // 2
+    halves = [jnp.sum(got[1:middle], axis=0), got[0] + jnp.sum(got[middle:], axis=0)]
     query = queries_ref[...].astype(f32)
     norm = jnp.sqrt(jnp.sum(query * query, axis=1, keepdims=True))
     unit = query / norm

time: 40.1 us -> 39.3 us (0.980)
  starting transfers between devices: 16.9 us -> 16.4 us
  waiting for transfers between devices: 6.31 us -> 5.82 us
    all_to_all x3, waiting for transfers between devices: 6.23 us -> 5.76 us  [exchange(): lax.all_to_all(x, 'hash', split_axis=0, concat_axis=0, axis_index_groups=...]
    all_to_all x3, starting transfers between devices: 16.6 us -> 16.2 us  [exchange(): lax.all_to_all(x, 'hash', split_axis=0, concat_axis=0, axis_index_groups=...]
where the time goes in v15:
time: 39.3 us; the launch traced here: 38.8 us
  starting transfers between devices  16.4 us (42%)
  Pallas kernels  15.1 us (38%)
  waiting for transfers between devices  5.82 us (15%)
  local copies, waits for them, and re-layouts  0.72 us (2%)
  between operations  0.71 us (2%)
    all_to_all x3, starting transfers between devices, exchange(): lax.all_to_all(x, 'hash', split_axis=0, concat_axis=0, axis_index_groups=...  16.2 us
    all_to_all x3, waiting for transfers between devices, exchange(): lax.all_to_all(x, 'hash', split_axis=0, concat_axis=0, axis_index_groups=...  5.76 us
    pallas_call x1, Pallas kernels, local(): pl.pallas_call(passage_kernel, in_specs=[whole()] * 6, out_specs=outside(...  4.06 us
    pallas_call x1, Pallas kernels, local(): pl.pallas_call(score_kernel, in_specs=[pl.BlockSpec(memory_space=pltpu.SM...  2.95 us
    pallas_call x1, Pallas kernels, local(): pl.pallas_call(stage_kernel, in_specs=[outside(), whole()], out_specs=[wh...  2.75 us
    pallas_call x2, Pallas kernels, mixed(): pl.pallas_call(kernel, in_specs=[pl.BlockSpec(memory_space=pltpu.SMEM)] +...  1.88 us
    pallas_call x1, Pallas kernels, local(): pl.pallas_call(functools.partial(pack_kernel, rows), out_shape=shape((cou...  1.72 us
    pallas_call x1, Pallas kernels, local(): pl.pallas_call(final_kernel, out_shape=[shape((1, width)), shape((1, widt...  0.87 us
  transfers between devices with their start and end apart: 5, of which 4 were waited for; matrix products, arithmetic and copies ran while one was open for 0% of the time, Pallas kernels for 22%

profile of v15, /device:TPU:0, one launch (start us, length us, event | category | flops | bytes accessed | tf_op | source)
XLA Modules:
  0.0 38.8 jit_solution(4925649037834530685)
XLA Ops:
  0.6 1.7 %pack.1 = bf16[16,8,640]{2,1,0:T(8,128)(2,1)} custom-call(bf16[1,4096]{1,0:T(2,128)(2,1)} %queries_ref.3, s32[1,128]{1,0:T(1,128)} %candidates_ref.1, s32[1,128]{1,0:T(1,128)} %teacher_ref.1), custom_call_target="tpu_custom_call" | custom-call | tf_op jit(solution)/shard_map/pack/pallas_call | solution.py:312
  2.4 7.5 %all-to-all-start = ((bf16[16,8,640]{2,1,0:T(8,128)(2,1)}), bf16[16,8,640]{2,1,0:T(8,128)(2,1)S(1)}, u32[]{:S(2)}, u32[]{:S(2)}) async-start(bf16[16,8,640]{2,1,0:T(8,128)(2,1)} %pack.1), calls=%async_computation | async-start | bytes 327680 | tf_op jit(solution)/shard_map/all_to_all | solution.py:301
  9.9 0.0 copy-start
  9.9 0.7 %copy-done = f32[4096]{0:T(1024)S(1)} copy-done((f32[4096]{0:T(1024)S(1)}, f32[4096]{0:T(1024)}, u32[]{:S(2)}) %copy-start) | copy-done | bytes 16408
  10.6 2.8 %stage.1 = (bf16[512,2048]{1,0:T(8,128)(2,1)S(1)}, bf16[5120,2048]{1,0:T(8,128)(2,1)}, f32[1,4096]{1,0:T(1,128)S(1)}) custom-call(bf16[512,4096]{1,0:T(8,128)(2,1)} %passages_ref.1, f32[1,4096]{1,0:T(1,128)S(1)} %bitcast.6), custom_call_target="tpu_custom_call" | custom-call | bytes 8388608 | tf_op jit(solution)/shard_map/stage/pallas_call | solution.py:321
  13.4 2.4 %all-to-all-done = bf16[16,8,640]{2,1,0:T(8,128)(2,1)S(1)} async-done(((bf16[16,8,640]{2,1,0:T(8,128)(2,1)}), bf16[16,8,640]{2,1,0:T(8,128)(2,1)S(1)}, u32[]{:S(2)}, u32[]{:S(2)}) %all-to-all-start) | async-done | bytes 163872 | tf_op jit(solution)/shard_map/all_to_all | solution.py:301
  15.8 2.9 %score.1 = (bf16[128,4096]{1,0:T(8,128)(2,1)S(1)}, bf16[16,4096]{1,0:T(8,128)(2,1)S(1)}, f32[128,128]{1,0:T(8,128)S(1)}, f32[8,128]{1,0:T(8,128)S(1)}, f32[16,1,128]{2,1,0:T(1,128)}, /*index=5*/bf16[128,2048]{1,0:T(8,128)(2,1)}) custom-call(s32[1]{0:T(128)} %bitcast.core_ref, bf16[128,640]{1,0:T(8,128)(2,1)S(1)} %bitcast.5, ...), custom_call_target="tpu_custom_call" | custom-call | tf_op jit(solution)/shard_map/score/pallas_call | solution.py:343
  18.7 0.0 copy-start.1
  18.7 0.0 copy-start.2
  18.8 0.1 collective-permute-start
  18.8 4.5 %all-to-all-start.1 = ((f32[16,1,128]{2,1,0:T(1,128)}), f32[16,1,128]{2,1,0:T(1,128)S(1)}, u32[]{:S(2)}, u32[]{:S(2)}) async-start(f32[16,1,128]{2,1,0:T(1,128)} %get-tuple-element.19), calls=%async_computation.1 | async-start | bytes 16384 | tf_op jit(solution)/shard_map/all_to_all | solution.py:301
  23.4 0.2 collective-permute-start.1
  23.5 0.9 %mix.2.mine_ref = f32[56,2048]{1,0:T(8,128)S(1)} custom-call(s32[1]{0:T(128)} %bitcast.core_ref, bf16[16,4096]{1,0:T(8,128)(2,1)S(1)} %get-tuple-element.20.query_ref, f32[1,4096]{1,0:T(1,128)S(1)} %get-tuple-element.16.gain_ref, bf16[128,4096]{1,0:T(8,128)(2,1)S(1)} %get-tuple-element.23.raw_ref, f32[8,128]{1,0:T(8,128)S(1)} %get-tuple-element.22.rows_ref), custom_call_target="tpu_custom_call" | custom-call | flops 67108864 | bytes 2097152 | tf_op jit(solution)/shard_map/mix/pallas_call | solution.py:369
  24.5 0.1 collective-permute-done.1.rows_ref
  24.5 0.0 collective-permute-done.raw_ref
  24.5 0.9 %mix.3.both_ref = f32[56,2048]{1,0:T(8,128)S(1)} custom-call(s32[1]{0:T(128)} %bitcast.core_ref, bf16[16,4096]{1,0:T(8,128)(2,1)S(1)} %get-tuple-element.20.query_ref, f32[1,4096]{1,0:T(1,128)S(1)} %get-tuple-element.16.gain_ref, bf16[128,2048]{1,0:T(8,128)(2,1)S(1)} %collective-permute-done.raw_ref, f32[8,128]{1,0:T(8,128)S(1)} %collective-permute-done.1.rows_ref, ...), custom_call_target="tpu_custom_call" | custom-call | flops 67108864 | bytes 2097152 | tf_op jit(solution)/shard_map/mix/pallas_call | solution.py:369
  25.5 2.0 %all-to-all-done.1.sums_ref = f32[16,1,128]{2,1,0:T(1,128)S(1)} async-done(((f32[16,1,128]{2,1,0:T(1,128)}), f32[16,1,128]{2,1,0:T(1,128)S(1)}, u32[]{:S(2)}, u32[]{:S(2)}) %all-to-all-start.1) | async-done | bytes 8224 | tf_op jit(solution)/shard_map/all_to_all | solution.py:301
  27.4 0.8 %partial.1 = (bf16[128,512]{1,0:T(8,128)(2,1)}, f32[1,128]{1,0:T(1,128)S(1)}) custom-call(f32[16,1,128]{2,1,0:T(1,128)S(1)} %all-to-all-done.1.sums_ref, f32[56,2048]{1,0:T(8,128)S(1)} %mix.3.both_ref), custom_call_target="tpu_custom_call" | custom-call | tf_op jit(solution)/shard_map/partial/pallas_call | solution.py:383
  28.3 4.1 %all-to-all-start.2 = ((bf16[16,8,512]{2,1,0:T(8,128)(2,1)}), bf16[16,8,512]{2,1,0:T(8,128)(2,1)S(1)}, u32[]{:S(2)}, u32[]{:S(2)}) async-start(bf16[16,8,512]{2,1,0:T(8,128)(2,1)} %bitcast.3), calls=%async_computation.2 | async-start | bytes 262144 | tf_op jit(solution)/shard_map/all_to_all | solution.py:301
  32.4 4.1 %d_passages.1 = f32[512,4096]{1,0:T(8,128)} custom-call(f32[1,128]{1,0:T(1,128)S(1)} %get-tuple-element.24.total_ref, bf16[16,4096]{1,0:T(8,128)(2,1)S(1)} %get-tuple-element.20.query_ref, f32[1,4096]{1,0:T(1,128)S(1)} %get-tuple-element.16.gain_ref, bf16[128,4096]{1,0:T(8,128)(2,1)S(1)} %get-tuple-element.23.raw_ref, ...), custom_call_target="tpu_custom_call" | custom-call | flops 1073741824 | bytes 8388608 | tf_op jit(solution)/shard_map/d_passages/pallas_call | solution.py:392
  36.5 1.4 %all-to-all-done.2.got_ref = bf16[16,8,512]{2,1,0:T(8,128)(2,1)S(1)} async-done(((bf16[16,8,512]{2,1,0:T(8,128)(2,1)}), bf16[16,8,512]{2,1,0:T(8,128)(2,1)S(1)}, u32[]{:S(2)}, u32[]{:S(2)}) %all-to-all-start.2) | async-done | bytes 131104 | tf_op jit(solution)/shard_map/all_to_all | solution.py:301
  37.9 0.0 copy-done.1
  37.9 0.0 copy-done.2
  37.9 0.9 %final.1 = (f32[1,4096]{1,0:T(1,128)}, f32[1,4096]{1,0:T(1,128)}) custom-call(bf16[16,8,512]{2,1,0:T(8,128)(2,1)S(1)} %all-to-all-done.2.got_ref, bf16[1,4096]{1,0:T(2,128)(2,1)S(1)} %copy-done.2, f32[1,4096]{1,0:T(1,128)S(1)} %bitcast.7), custom_call_target="tpu_custom_call" | custom-call | tf_op jit(solution)/shard_map/final/pallas_call | solution.py:405
Async XLA Ops:
  2.4 13.4 %all-to-all-start = ((bf16[16,8,640]{2,1,0:T(8,128)(2,1)}), bf16[16,8,640]{2,1,0:T(8,128)(2,1)S(1)}, u32[]{:S(2)}, u32[]{:S(2)}) async-start(bf16[16,8,640]{2,1,0:T(8,128)(2,1)} %pack.1), calls=%async_computation | async-start | bytes 327680 | tf_op jit(solution)/shard_map/all_to_all | solution.py:301
  9.9 0.7 %copy-start = (f32[4096]{0:T(1024)S(1)}, f32[4096]{0:T(1024)}, u32[]{:S(2)}) copy-start(f32[4096]{0:T(1024)} %param.7) | copy-start | bytes 49156
  18.7 19.2 %copy-start.1 = (f32[4096]{0:T(1024)S(1)}, f32[4096]{0:T(1024)}, u32[]{:S(2)}) copy-start(f32[4096]{0:T(1024)} %param.7) | copy-start | bytes 49156
  18.7 19.1 %copy-start.2 = (bf16[1,4096]{1,0:T(2,128)(2,1)S(1)}, bf16[1,4096]{1,0:T(2,128)(2,1)}, u32[]{:S(2)}) copy-start(bf16[1,4096]{1,0:T(2,128)(2,1)} %queries_ref.3) | copy-start | bytes 24580
  18.8 5.8 %collective-permute-start = (bf16[128,2048]{1,0:T(8,128)(2,1)}, bf16[128,2048]{1,0:T(8,128)(2,1)S(1)}, u32[]{:S(2)}, u32[]{:S(2)}) collective-permute-start(bf16[128,2048]{1,0:T(8,128)(2,1)} %get-tuple-element.21), channel_id=1, source_target_pairs={{0,1},{1,0},{2,3},{3,2},{4,5},{5,4},{6,7},{7,6},{8,9},{9,8},{10,11... | collective-permute-start | bytes 1572872 | tf_op jit(solution)/shard_map/ppermute | solution.py:365
  18.8 8.6 %all-to-all-start.1 = ((f32[16,1,128]{2,1,0:T(1,128)}), f32[16,1,128]{2,1,0:T(1,128)S(1)}, u32[]{:S(2)}, u32[]{:S(2)}) async-start(f32[16,1,128]{2,1,0:T(1,128)} %get-tuple-element.19), calls=%async_computation.1 | async-start | bytes 16384 | tf_op jit(solution)/shard_map/all_to_all | solution.py:301
  23.4 1.2 %collective-permute-start.1 = (f32[8,128]{1,0:T(8,128)S(1)}, f32[8,128]{1,0:T(8,128)S(1)}, u32[]{:S(2)}, u32[]{:S(2)}) collective-permute-start(f32[8,128]{1,0:T(8,128)S(1)} %get-tuple-element.22.rows_ref), channel_id=1, source_target_pairs={{0,1},{1,0},{2,3},{3,2},{4,5},{5,4},{6,7},{7,6},{8,9},{9,8},{10,11... | collective-permute-start | bytes 12296 | tf_op jit(solution)/shard_map/ppermute | solution.py:366
  28.3 9.6 %all-to-all-start.2 = ((bf16[16,8,512]{2,1,0:T(8,128)(2,1)}), bf16[16,8,512]{2,1,0:T(8,128)(2,1)S(1)}, u32[]{:S(2)}, u32[]{:S(2)}) async-start(bf16[16,8,512]{2,1,0:T(8,128)(2,1)} %bitcast.3), calls=%async_computation.2 | async-start | bytes 262144 | tf_op jit(solution)/shard_map/all_to_all | solution.py:301

commit v16 on v15

--- a/solution.py
+++ b/solution.py
@@ -96,11 +96,12 @@
 def stage_kernel(passages_ref, gain_ref, near_ref, far_ref, gain_out_ref, held, sems_in, sems_out):
     gain_out_ref[...] = gain_ref[...]
     rows, width = near_ref.shape
+    rest = held.shape[1]
     piece = rows // chunks
     copies_in, copies_out, copies_near = [], [], []
     for k in range(chunks):
         part = pl.ds(k * piece, piece)
-        far = passages_ref.at[part, pl.ds(width, width)]
+        far = passages_ref.at[part, pl.ds(width, rest)]
         near = passages_ref.at[part, pl.ds(0, width)]
         copies_in.append(pltpu.make_async_copy(far, held.at[part], sems_in.at[k]))
         copies_out.append(pltpu.make_async_copy(held.at[part], far_ref.at[part], sems_out.at[k]))
@@ -166,9 +167,9 @@
     pairs = queries * 8
     rows = held.shape[0]
     chunk = width // chunks
-    half = chunks // 2
+    close = near_ref.shape[1] // chunk
     copies = []
-    for k in range(half):
+    for k in range(chunks - close):
         part = pl.ds(k * chunk, chunk)
         copies.append(pltpu.make_async_copy(far_ref.at[pl.ds(0, rows), part], held.at[:, part], sems.at[k]))
         copies[-1].start()
@@ -192,11 +193,11 @@
     along = [jnp.zeros((8, 128), f32)] * queries
     for k in range(chunks):
         part = slice(k * chunk, (k + 1) * chunk)
-        if k < half:
+        if k < close:
             passages = near_ref[:, part]
         else:
-            copies[k - half].wait()
-            passages = held[:, slice((k - half) * chunk, (k - half + 1) * chunk)]
+            copies[k - close].wait()
+            passages = held[:, slice((k - close) * chunk, (k - close + 1) * chunk)]
         raw = dot(pick, passages, nn_dims)
         raw_ref[:, part] = raw.astype(bf16)
         lifted = raw * gain_ref[:, part]
@@ -323,12 +324,12 @@
         in_specs=[outside(), whole()],
         out_specs=[whole(), outside(), whole()],
         out_shape=[
-            shape((rows, width // 2), bf16),
-            shape((10 * rows, width // 2), bf16),
+            shape((rows, width - width // chunks), bf16),
+            shape((20 * rows, width // chunks), bf16),
             shape((1, width)),
         ],
         scratch_shapes=[
-            pltpu.VMEM((rows, width // 2), bf16),
+            pltpu.VMEM((rows, width // chunks), bf16),
             pltpu.SemaphoreType.DMA((2 * chunks,)),
             pltpu.SemaphoreType.DMA((chunks,)),
         ],
@@ -352,7 +353,7 @@
             shape((pairs, half), bf16),
         ],
         scratch_shapes=[
-            pltpu.VMEM((rows, width // 2), bf16),
+            pltpu.VMEM((rows, width // chunks), bf16),
             pltpu.VMEM((width // 1024, pairs, 128), f32),
             pltpu.SemaphoreType.DMA((chunks // 2,)),
         ],

time: 39.3 us -> 40.7 us (1.036)
  local copies, waits for them, and re-layouts: 0.72 us -> 4.27 us
  waiting for transfers between devices: 5.82 us -> 4.26 us
  Pallas kernels: 15.1 us -> 14.5 us
    unnamed x6 -> x10, local copies, waits for them, and re-layouts: 0.72 us -> 4.27 us
    all_to_all x3, waiting for transfers between devices: 5.76 us -> 4.2 us  [exchange(): lax.all_to_all(x, 'hash', split_axis=0, concat_axis=0, axis_index_groups=...]
    pallas_call x1, Pallas kernels: 2.95 us -> 2.44 us  [local(): pl.pallas_call(score_kernel, in_specs=[pl.BlockSpec(memory_space=pltpu.SM...]
  transfers between devices with their start and end apart: 5 -> 5, of which waited for: 4 -> 4; matrix products, arithmetic and copies ran while one was open for 0% -> 0% of each run, Pallas kernels for 22% -> 21%
where the time goes in v16:
time: 40.7 us; the launch traced here: 40.2 us
  starting transfers between devices  16.4 us (40%)
  Pallas kernels  14.5 us (36%)
  local copies, waits for them, and re-layouts  4.27 us (10%)
  waiting for transfers between devices  4.26 us (10%)
  between operations  0.72 us (2%)
    all_to_all x3, starting transfers between devices, exchange(): lax.all_to_all(x, 'hash', split_axis=0, concat_axis=0, axis_index_groups=...  16.2 us
    unnamed x10, local copies, waits for them, and re-layouts  4.27 us
    all_to_all x3, waiting for transfers between devices, exchange(): lax.all_to_all(x, 'hash', split_axis=0, concat_axis=0, axis_index_groups=...  4.2 us
    pallas_call x1, Pallas kernels, local(): pl.pallas_call(passage_kernel, in_specs=[whole()] * 6, out_specs=outside(...  4.05 us
    pallas_call x1, Pallas kernels, local(): pl.pallas_call(stage_kernel, in_specs=[outside(), whole()], out_specs=[wh...  2.66 us
    pallas_call x1, Pallas kernels, local(): pl.pallas_call(score_kernel, in_specs=[pl.BlockSpec(memory_space=pltpu.SM...  2.44 us
    pallas_call x2, Pallas kernels, mixed(): pl.pallas_call(kernel, in_specs=[pl.BlockSpec(memory_space=pltpu.SMEM)] +...  1.88 us
    pallas_call x1, Pallas kernels, local(): pl.pallas_call(functools.partial(pack_kernel, rows), out_shape=shape((cou...  1.73 us
  transfers between devices with their start and end apart: 5, of which 4 were waited for; matrix products, arithmetic and copies ran while one was open for 0% of the time, Pallas kernels for 21%

profile of v16, /device:TPU:0, one launch (start us, length us, event | category | flops | bytes accessed | tf_op | source)
XLA Modules:
  0.0 40.2 jit_solution(6325103581069709724)
XLA Ops:
  0.6 1.7 %pack.1 = bf16[16,8,640]{2,1,0:T(8,128)(2,1)} custom-call(bf16[1,4096]{1,0:T(2,128)(2,1)} %queries_ref.3, s32[1,128]{1,0:T(1,128)} %candidates_ref.1, s32[1,128]{1,0:T(1,128)} %teacher_ref.1), custom_call_target="tpu_custom_call" | custom-call | tf_op jit(solution)/shard_map/pack/pallas_call | solution.py:313
  2.4 7.5 %all-to-all-start = ((bf16[16,8,640]{2,1,0:T(8,128)(2,1)}), bf16[16,8,640]{2,1,0:T(8,128)(2,1)S(1)}, u32[]{:S(2)}, u32[]{:S(2)}) async-start(bf16[16,8,640]{2,1,0:T(8,128)(2,1)} %pack.1), calls=%async_computation | async-start | bytes 327680 | tf_op jit(solution)/shard_map/all_to_all | solution.py:302
  9.9 0.0 copy-start.2
  9.9 0.7 %copy-done.2 = f32[4096]{0:T(1024)S(1)} copy-done((f32[4096]{0:T(1024)S(1)}, f32[4096]{0:T(1024)}, u32[]{:S(2)}) %copy-start.2) | copy-done | bytes 16408
  10.6 2.7 %stage.1 = (bf16[512,3072]{1,0:T(8,128)(2,1)S(1)}, bf16[10240,1024]{1,0:T(8,128)(2,1)}, f32[1,4096]{1,0:T(1,128)S(1)}) custom-call(bf16[512,4096]{1,0:T(8,128)(2,1)} %passages_ref.1, f32[1,4096]{1,0:T(1,128)S(1)} %bitcast.6), custom_call_target="tpu_custom_call" | custom-call | bytes 8388608 | tf_op jit(solution)/shard_map/stage/pallas_call | solution.py:322
  13.3 0.0 copy-start
  13.3 1.7 %copy-done = bf16[512,3072]{1,0:T(8,128)(2,1)} copy-done((bf16[512,3072]{1,0:T(8,128)(2,1)}, bf16[512,3072]{1,0:T(8,128)(2,1)S(1)}, u32[]{:S(2)}) %copy-start) | copy-done | bytes 3145752
  15.0 0.8 %all-to-all-done = bf16[16,8,640]{2,1,0:T(8,128)(2,1)S(1)} async-done(((bf16[16,8,640]{2,1,0:T(8,128)(2,1)}), bf16[16,8,640]{2,1,0:T(8,128)(2,1)S(1)}, u32[]{:S(2)}, u32[]{:S(2)}) %all-to-all-start) | async-done | bytes 163872 | tf_op jit(solution)/shard_map/all_to_all | solution.py:302
  15.8 0.0 copy-start.1
  15.8 1.9 %copy-done.1 = bf16[512,3072]{1,0:T(8,128)(2,1)S(1)} copy-done((bf16[512,3072]{1,0:T(8,128)(2,1)S(1)}, bf16[512,3072]{1,0:T(8,128)(2,1)}, u32[]{:S(2)}) %copy-start.1) | copy-done | bytes 3145752
  17.7 2.4 %score.1 = (bf16[128,4096]{1,0:T(8,128)(2,1)S(1)}, bf16[16,4096]{1,0:T(8,128)(2,1)S(1)}, f32[128,128]{1,0:T(8,128)S(1)}, f32[8,128]{1,0:T(8,128)S(1)}, f32[16,1,...) custom-call(s32[1]{0:T(128)} %bitcast.core_ref, bf16[128,640]{1,0:T(8,128)(2,1)S(1)} %bitcast.5, ...), custom_call_target="tpu_custom_call" | custom-call | tf_op jit(solution)/shard_map/score/pallas_call | solution.py:344
  20.1 0.0 copy-start.3
  20.1 0.0 copy-start.4
  20.1 0.1 collective-permute-start
  20.2 4.5 %all-to-all-start.1 = ((f32[16,1,128]{2,1,0:T(1,128)}), f32[16,1,128]{2,1,0:T(1,128)S(1)}, u32[]{:S(2)}, u32[]{:S(2)}) async-start(f32[16,1,128]{2,1,0:T(1,128)} %get-tuple-element.19), calls=%async_computation.1 | async-start | bytes 16384 | tf_op jit(solution)/shard_map/all_to_all | solution.py:302
  24.7 0.2 collective-permute-start.1
  24.9 0.9 %mix.2.mine_ref = f32[56,2048]{1,0:T(8,128)S(1)} custom-call(s32[1]{0:T(128)} %bitcast.core_ref, bf16[16,4096]{1,0:T(8,128)(2,1)S(1)} %get-tuple-element.20.query_ref, f32[1,4096]{1,0:T(1,128)S(1)} %get-tuple-element.16.gain_ref, bf16[128,4096]{1,0:T(8,128)(2,1)S(1)} %get-tuple-element.23.raw_ref, f32[8,128]{1,0:T(8,128)S(1)} %get-tuple-element.22.rows_ref), custom_call_target="tpu_custom_call" | custom-call | flops 67108864 | bytes 2097152 | tf_op jit(solution)/shard_map/mix/pallas_call | solution.py:370
  25.9 0.1 collective-permute-done.1.rows_ref
  25.9 0.0 collective-permute-done.raw_ref
  25.9 0.9 %mix.3.both_ref = f32[56,2048]{1,0:T(8,128)S(1)} custom-call(s32[1]{0:T(128)} %bitcast.core_ref, bf16[16,4096]{1,0:T(8,128)(2,1)S(1)} %get-tuple-element.20.query_ref, f32[1,4096]{1,0:T(1,128)S(1)} %get-tuple-element.16.gain_ref, bf16[128,2048]{1,0:T(8,128)(2,1)S(1)} %collective-permute-done.raw_ref, f32[8,128]{1,0:T(8,128)S(1)} %collective-permute-done.1.rows_ref, ...), custom_call_target="tpu_custom_call" | custom-call | flops 67108864 | bytes 2097152 | tf_op jit(solution)/shard_map/mix/pallas_call | solution.py:370
  26.9 2.0 %all-to-all-done.1.sums_ref = f32[16,1,128]{2,1,0:T(1,128)S(1)} async-done(((f32[16,1,128]{2,1,0:T(1,128)}), f32[16,1,128]{2,1,0:T(1,128)S(1)}, u32[]{:S(2)}, u32[]{:S(2)}) %all-to-all-start.1) | async-done | bytes 8224 | tf_op jit(solution)/shard_map/all_to_all | solution.py:302
  28.8 0.9 %partial.1 = (bf16[128,512]{1,0:T(8,128)(2,1)}, f32[1,128]{1,0:T(1,128)S(1)}) custom-call(f32[16,1,128]{2,1,0:T(1,128)S(1)} %all-to-all-done.1.sums_ref, f32[56,2048]{1,0:T(8,128)S(1)} %mix.3.both_ref), custom_call_target="tpu_custom_call" | custom-call | tf_op jit(solution)/shard_map/partial/pallas_call | solution.py:384
  29.7 4.1 %all-to-all-start.2 = ((bf16[16,8,512]{2,1,0:T(8,128)(2,1)}), bf16[16,8,512]{2,1,0:T(8,128)(2,1)S(1)}, u32[]{:S(2)}, u32[]{:S(2)}) async-start(bf16[16,8,512]{2,1,0:T(8,128)(2,1)} %bitcast.3), calls=%async_computation.2 | async-start | bytes 262144 | tf_op jit(solution)/shard_map/all_to_all | solution.py:302
  33.8 4.0 %d_passages.1 = f32[512,4096]{1,0:T(8,128)} custom-call(f32[1,128]{1,0:T(1,128)S(1)} %get-tuple-element.24.total_ref, bf16[16,4096]{1,0:T(8,128)(2,1)S(1)} %get-tuple-element.20.query_ref, f32[1,4096]{1,0:T(1,128)S(1)} %get-tuple-element.16.gain_ref, bf16[128,4096]{1,0:T(8,128)(2,1)S(1)} %get-tuple-element.23.raw_ref, ...), custom_call_target="tpu_custom_call" | custom-call | flops 1073741824 | bytes 8388608 | tf_op jit(solution)/shard_map/d_passages/pallas_call | solution.py:393
  37.9 1.4 %all-to-all-done.2.got_ref = bf16[16,8,512]{2,1,0:T(8,128)(2,1)S(1)} async-done(((bf16[16,8,512]{2,1,0:T(8,128)(2,1)}), bf16[16,8,512]{2,1,0:T(8,128)(2,1)S(1)}, u32[]{:S(2)}, u32[]{:S(2)}) %all-to-all-start.2) | async-done | bytes 131104 | tf_op jit(solution)/shard_map/all_to_all | solution.py:302
  39.3 0.0 copy-done.3
  39.3 0.0 copy-done.4
  39.3 0.9 %final.1 = (f32[1,4096]{1,0:T(1,128)}, f32[1,4096]{1,0:T(1,128)}) custom-call(bf16[16,8,512]{2,1,0:T(8,128)(2,1)S(1)} %all-to-all-done.2.got_ref, bf16[1,4096]{1,0:T(2,128)(2,1)S(1)} %copy-done.4, f32[1,4096]{1,0:T(1,128)S(1)} %bitcast.7), custom_call_target="tpu_custom_call" | custom-call | tf_op jit(solution)/shard_map/final/pallas_call | solution.py:406
Async XLA Ops:
  2.4 13.4 %all-to-all-start = ((bf16[16,8,640]{2,1,0:T(8,128)(2,1)}), bf16[16,8,640]{2,1,0:T(8,128)(2,1)S(1)}, u32[]{:S(2)}, u32[]{:S(2)}) async-start(bf16[16,8,640]{2,1,0:T(8,128)(2,1)} %pack.1), calls=%async_computation | async-start | bytes 327680 | tf_op jit(solution)/shard_map/all_to_all | solution.py:302
  9.9 0.7 %copy-start.2 = (f32[4096]{0:T(1024)S(1)}, f32[4096]{0:T(1024)}, u32[]{:S(2)}) copy-start(f32[4096]{0:T(1024)} %param.7) | copy-start | bytes 49156
  13.3 1.7 %copy-start = (bf16[512,3072]{1,0:T(8,128)(2,1)}, bf16[512,3072]{1,0:T(8,128)(2,1)S(1)}, u32[]{:S(2)}) copy-start(bf16[512,3072]{1,0:T(8,128)(2,1)S(1)} %get-tuple-element.17.near_ref) | copy-start | bytes 9437188
  15.8 1.9 %copy-start.1 = (bf16[512,3072]{1,0:T(8,128)(2,1)S(1)}, bf16[512,3072]{1,0:T(8,128)(2,1)}, u32[]{:S(2)}) copy-start(bf16[512,3072]{1,0:T(8,128)(2,1)} %copy-done) | copy-start | bytes 9437188
  20.1 19.2 %copy-start.3 = (f32[4096]{0:T(1024)S(1)}, f32[4096]{0:T(1024)}, u32[]{:S(2)}) copy-start(f32[4096]{0:T(1024)} %param.7) | copy-start | bytes 49156
  20.1 19.2 %copy-start.4 = (bf16[1,4096]{1,0:T(2,128)(2,1)S(1)}, bf16[1,4096]{1,0:T(2,128)(2,1)}, u32[]{:S(2)}) copy-start(bf16[1,4096]{1,0:T(2,128)(2,1)} %queries_ref.3) | copy-start | bytes 24580
  20.1 5.8 %collective-permute-start = (bf16[128,2048]{1,0:T(8,128)(2,1)S(1)}, bf16[128,2048]{1,0:T(8,128)(2,1)S(1)}, u32[]{:S(2)}, u32[]{:S(2)}) collective-permute-start(bf16[128,2048]{1,0:T(8,128)(2,1)S(1)} %get-tuple-element.21), channel_id=1, source_target_pairs={{0,1},{1,0},{2,3},{3,2},{4,5},{5,4},{6,7},{7,6},{8,9},{9,8},{10,11... | collective-permute-start | bytes 1572872 | tf_op jit(solution)/shard_map/ppermute | solution.py:366
  20.2 8.6 %all-to-all-start.1 = ((f32[16,1,128]{2,1,0:T(1,128)}), f32[16,1,128]{2,1,0:T(1,128)S(1)}, u32[]{:S(2)}, u32[]{:S(2)}) async-start(f32[16,1,128]{2,1,0:T(1,128)} %get-tuple-element.19), calls=%async_computation.1 | async-start | bytes 16384 | tf_op jit(solution)/shard_map/all_to_all | solution.py:302
  24.7 1.2 %collective-permute-start.1 = (f32[8,128]{1,0:T(8,128)S(1)}, f32[8,128]{1,0:T(8,128)S(1)}, u32[]{:S(2)}, u32[]{:S(2)}) collective-permute-start(f32[8,128]{1,0:T(8,128)S(1)} %get-tuple-element.22.rows_ref), channel_id=1, source_target_pairs={{0,1},{1,0},{2,3},{3,2},{4,5},{5,4},{6,7},{7,6},{8,9},{9,8},{10,11... | collective-permute-start | bytes 12296 | tf_op jit(solution)/shard_map/ppermute | solution.py:367
  29.7 9.6 %all-to-all-start.2 = ((bf16[16,8,512]{2,1,0:T(8,128)(2,1)}), bf16[16,8,512]{2,1,0:T(8,128)(2,1)S(1)}, u32[]{:S(2)}, u32[]{:S(2)}) async-start(bf16[16,8,512]{2,1,0:T(8,128)(2,1)} %bitcast.3), calls=%async_computation.2 | async-start | bytes 262144 | tf_op jit(solution)/shard_map/all_to_all | solution.py:302

commit v17 on v16

--- a/solution.py
+++ b/solution.py
@@ -12,6 +12,8 @@
 teacher_div = 2.0
 coef_scale = loss_scale * score_scale
 chunks = 4
+taken = 16
+close = 11
 pieces = 8
 f32 = jnp.float32
 bf16 = jnp.bfloat16
@@ -166,10 +168,9 @@
     queries, width = query_ref.shape
     pairs = queries * 8
     rows = held.shape[0]
-    chunk = width // chunks
-    close = near_ref.shape[1] // chunk
+    chunk = width // taken
     copies = []
-    for k in range(chunks - close):
+    for k in range(taken - close):
         part = pl.ds(k * chunk, chunk)
         copies.append(pltpu.make_async_copy(far_ref.at[pl.ds(0, rows), part], held.at[:, part], sems.at[k]))
         copies[-1].start()
@@ -191,7 +192,7 @@
     pick = jnp.where(inside == lane, 1.0, 0.0).astype(bf16)
     size = jnp.zeros((pairs, 128), f32)
     along = [jnp.zeros((8, 128), f32)] * queries
-    for k in range(chunks):
+    for k in range(taken):
         part = slice(k * chunk, (k + 1) * chunk)
         if k < close:
             passages = near_ref[:, part]
@@ -319,17 +320,18 @@
     got = exchange(packed).reshape(count * 8, width // 8 + listed)
 
     pairs = count * 8
+    far_width = (taken - close) * width // taken
     near, far, gain_near = pl.pallas_call(
         stage_kernel,
         in_specs=[outside(), whole()],
         out_specs=[whole(), outside(), whole()],
         out_shape=[
-            shape((rows, width - width // chunks), bf16),
-            shape((20 * rows, width // chunks), bf16),
+            shape((rows, close * width // taken), bf16),
+            shape((16 * rows, far_width), bf16),
             shape((1, width)),
         ],
         scratch_shapes=[
-            pltpu.VMEM((rows, width // chunks), bf16),
+            pltpu.VMEM((rows, far_width), bf16),
             pltpu.SemaphoreType.DMA((2 * chunks,)),
             pltpu.SemaphoreType.DMA((chunks,)),
         ],
@@ -353,9 +355,9 @@
             shape((pairs, half), bf16),
         ],
         scratch_shapes=[
-            pltpu.VMEM((rows, width // chunks), bf16),
+            pltpu.VMEM((rows, far_width), bf16),
             pltpu.VMEM((width // 1024, pairs, 128), f32),
-            pltpu.SemaphoreType.DMA((chunks // 2,)),
+            pltpu.SemaphoreType.DMA((taken - close,)),
         ],
         compiler_params=params(48),
         name="score",

time: 40.7 us -> 41.7 us (1.025)
  Pallas kernels: 14.5 us -> 15.7 us
    pallas_call x1, Pallas kernels: 2.44 us -> 3.56 us  [local(): pl.pallas_call(score_kernel, in_specs=[pl.BlockSpec(memory_space=pltpu.SM...]
where the time goes in v17:
time: 41.7 us; the launch traced here: 41.2 us
  starting transfers between devices  16.4 us (39%)
  Pallas kernels  15.7 us (38%)
  waiting for transfers between devices  4.24 us (10%)
  local copies, waits for them, and re-layouts  4.11 us (10%)
  between operations  0.72 us (2%)
    all_to_all x3, starting transfers between devices, exchange(): lax.all_to_all(x, 'hash', split_axis=0, concat_axis=0, axis_index_groups=...  16.2 us
    all_to_all x3, waiting for transfers between devices, exchange(): lax.all_to_all(x, 'hash', split_axis=0, concat_axis=0, axis_index_groups=...  4.19 us
    unnamed x10, local copies, waits for them, and re-layouts  4.11 us
    pallas_call x1, Pallas kernels, local(): pl.pallas_call(passage_kernel, in_specs=[whole()] * 6, out_specs=outside(...  4.06 us
    pallas_call x1, Pallas kernels, local(): pl.pallas_call(score_kernel, in_specs=[pl.BlockSpec(memory_space=pltpu.SM...  3.56 us
    pallas_call x1, Pallas kernels, local(): pl.pallas_call(stage_kernel, in_specs=[outside(), whole()], out_specs=[wh...  2.75 us
    pallas_call x2, Pallas kernels, mixed(): pl.pallas_call(kernel, in_specs=[pl.BlockSpec(memory_space=pltpu.SMEM)] +...  1.88 us
    pallas_call x1, Pallas kernels, local(): pl.pallas_call(functools.partial(pack_kernel, rows), out_shape=shape((cou...  1.73 us
  transfers between devices with their start and end apart: 5, of which 4 were waited for; matrix products, arithmetic and copies ran while one was open for 0% of the time, Pallas kernels for 21%

profile of v17, /device:TPU:0, one launch (start us, length us, event | category | flops | bytes accessed | tf_op | source)
XLA Modules:
  0.0 41.2 jit_solution(15848140513502907073)
XLA Ops:
  0.6 1.7 %pack.1 = bf16[16,8,640]{2,1,0:T(8,128)(2,1)} custom-call(bf16[1,4096]{1,0:T(2,128)(2,1)} %queries_ref.3, s32[1,128]{1,0:T(1,128)} %candidates_ref.1, s32[1,128]{1,0:T(1,128)} %teacher_ref.1), custom_call_target="tpu_custom_call" | custom-call | tf_op jit(solution)/shard_map/pack/pallas_call | solution.py:314
  2.4 7.5 %all-to-all-start = ((bf16[16,8,640]{2,1,0:T(8,128)(2,1)}), bf16[16,8,640]{2,1,0:T(8,128)(2,1)S(1)}, u32[]{:S(2)}, u32[]{:S(2)}) async-start(bf16[16,8,640]{2,1,0:T(8,128)(2,1)} %pack.1), calls=%async_computation | async-start | bytes 327680 | tf_op jit(solution)/shard_map/all_to_all | solution.py:303
  9.9 0.0 copy-start.2
  9.9 0.7 %copy-done.2 = f32[4096]{0:T(1024)S(1)} copy-done((f32[4096]{0:T(1024)S(1)}, f32[4096]{0:T(1024)}, u32[]{:S(2)}) %copy-start.2) | copy-done | bytes 16408
  10.6 2.7 %stage.1 = (bf16[512,2816]{1,0:T(8,128)(2,1)S(1)}, bf16[8192,1280]{1,0:T(8,128)(2,1)}, f32[1,4096]{1,0:T(1,128)S(1)}) custom-call(bf16[512,4096]{1,0:T(8,128)(2,1)} %passages_ref.1, f32[1,4096]{1,0:T(1,128)S(1)} %bitcast.6), custom_call_target="tpu_custom_call" | custom-call | bytes 8388608 | tf_op jit(solution)/shard_map/stage/pallas_call | solution.py:324
  13.4 0.0 copy-start
  13.4 1.6 %copy-done = bf16[512,2816]{1,0:T(8,128)(2,1)} copy-done((bf16[512,2816]{1,0:T(8,128)(2,1)}, bf16[512,2816]{1,0:T(8,128)(2,1)S(1)}, u32[]{:S(2)}) %copy-start) | copy-done | bytes 2883608
  15.0 0.8 %all-to-all-done = bf16[16,8,640]{2,1,0:T(8,128)(2,1)S(1)} async-done(((bf16[16,8,640]{2,1,0:T(8,128)(2,1)}), bf16[16,8,640]{2,1,0:T(8,128)(2,1)S(1)}, u32[]{:S(2)}, u32[]{:S(2)}) %all-to-all-start) | async-done | bytes 163872 | tf_op jit(solution)/shard_map/all_to_all | solution.py:303
  15.8 0.0 copy-start.1
  15.8 1.8 %copy-done.1 = bf16[512,2816]{1,0:T(8,128)(2,1)S(1)} copy-done((bf16[512,2816]{1,0:T(8,128)(2,1)S(1)}, bf16[512,2816]{1,0:T(8,128)(2,1)}, u32[]{:S(2)}) %copy-start.1) | copy-done | bytes 2883608
  17.6 3.6 %score.1 = (bf16[128,4096]{1,0:T(8,128)(2,1)S(1)}, bf16[16,4096]{1,0:T(8,128)(2,1)S(1)}, f32[128,128]{1,0:T(8,128)S(1)}, f32[8,128]{1,0:T(8,128)S(1)}, f32[16,1,...) custom-call(s32[1]{0:T(128)} %bitcast.core_ref, bf16[128,640]{1,0:T(8,128)(2,1)S(1)} %bitcast.5, ...), custom_call_target="tpu_custom_call" | custom-call | tf_op jit(solution)/shard_map/score/pallas_call | solution.py:346
  21.2 0.0 copy-start.3
  21.2 0.0 copy-start.4
  21.2 0.1 collective-permute-start
  21.3 4.5 %all-to-all-start.1 = ((f32[16,1,128]{2,1,0:T(1,128)}), f32[16,1,128]{2,1,0:T(1,128)S(1)}, u32[]{:S(2)}, u32[]{:S(2)}) async-start(f32[16,1,128]{2,1,0:T(1,128)} %get-tuple-element.19), calls=%async_computation.1 | async-start | bytes 16384 | tf_op jit(solution)/shard_map/all_to_all | solution.py:303
  25.8 0.2 collective-permute-start.1
  26.0 0.9 %mix.2.mine_ref = f32[56,2048]{1,0:T(8,128)S(1)} custom-call(s32[1]{0:T(128)} %bitcast.core_ref, bf16[16,4096]{1,0:T(8,128)(2,1)S(1)} %get-tuple-element.20.query_ref, f32[1,4096]{1,0:T(1,128)S(1)} %get-tuple-element.16.gain_ref, bf16[128,4096]{1,0:T(8,128)(2,1)S(1)} %get-tuple-element.23.raw_ref, f32[8,128]{1,0:T(8,128)S(1)} %get-tuple-element.22.rows_ref), custom_call_target="tpu_custom_call" | custom-call | flops 67108864 | bytes 2097152 | tf_op jit(solution)/shard_map/mix/pallas_call | solution.py:372
  26.9 0.1 collective-permute-done.1.rows_ref
  26.9 0.0 collective-permute-done.raw_ref
  27.0 0.9 %mix.3.both_ref = f32[56,2048]{1,0:T(8,128)S(1)} custom-call(s32[1]{0:T(128)} %bitcast.core_ref, bf16[16,4096]{1,0:T(8,128)(2,1)S(1)} %get-tuple-element.20.query_ref, f32[1,4096]{1,0:T(1,128)S(1)} %get-tuple-element.16.gain_ref, bf16[128,2048]{1,0:T(8,128)(2,1)S(1)} %collective-permute-done.raw_ref, f32[8,128]{1,0:T(8,128)S(1)} %collective-permute-done.1.rows_ref, ...), custom_call_target="tpu_custom_call" | custom-call | flops 67108864 | bytes 2097152 | tf_op jit(solution)/shard_map/mix/pallas_call | solution.py:372
  27.9 2.0 %all-to-all-done.1.sums_ref = f32[16,1,128]{2,1,0:T(1,128)S(1)} async-done(((f32[16,1,128]{2,1,0:T(1,128)}), f32[16,1,128]{2,1,0:T(1,128)S(1)}, u32[]{:S(2)}, u32[]{:S(2)}) %all-to-all-start.1) | async-done | bytes 8224 | tf_op jit(solution)/shard_map/all_to_all | solution.py:303
  29.9 0.9 %partial.1 = (bf16[128,512]{1,0:T(8,128)(2,1)}, f32[1,128]{1,0:T(1,128)S(1)}) custom-call(f32[16,1,128]{2,1,0:T(1,128)S(1)} %all-to-all-done.1.sums_ref, f32[56,2048]{1,0:T(8,128)S(1)} %mix.3.both_ref), custom_call_target="tpu_custom_call" | custom-call | tf_op jit(solution)/shard_map/partial/pallas_call | solution.py:386
  30.7 4.1 %all-to-all-start.2 = ((bf16[16,8,512]{2,1,0:T(8,128)(2,1)}), bf16[16,8,512]{2,1,0:T(8,128)(2,1)S(1)}, u32[]{:S(2)}, u32[]{:S(2)}) async-start(bf16[16,8,512]{2,1,0:T(8,128)(2,1)} %bitcast.3), calls=%async_computation.2 | async-start | bytes 262144 | tf_op jit(solution)/shard_map/all_to_all | solution.py:303
  34.9 4.1 %d_passages.1 = f32[512,4096]{1,0:T(8,128)} custom-call(f32[1,128]{1,0:T(1,128)S(1)} %get-tuple-element.24.total_ref, bf16[16,4096]{1,0:T(8,128)(2,1)S(1)} %get-tuple-element.20.query_ref, f32[1,4096]{1,0:T(1,128)S(1)} %get-tuple-element.16.gain_ref, bf16[128,4096]{1,0:T(8,128)(2,1)S(1)} %get-tuple-element.23.raw_ref, ...), custom_call_target="tpu_custom_call" | custom-call | flops 1073741824 | bytes 8388608 | tf_op jit(solution)/shard_map/d_passages/pallas_call | solution.py:395
  38.9 1.4 %all-to-all-done.2.got_ref = bf16[16,8,512]{2,1,0:T(8,128)(2,1)S(1)} async-done(((bf16[16,8,512]{2,1,0:T(8,128)(2,1)}), bf16[16,8,512]{2,1,0:T(8,128)(2,1)S(1)}, u32[]{:S(2)}, u32[]{:S(2)}) %all-to-all-start.2) | async-done | bytes 131104 | tf_op jit(solution)/shard_map/all_to_all | solution.py:303
  40.3 0.0 copy-done.3
  40.3 0.0 copy-done.4
  40.3 0.9 %final.1 = (f32[1,4096]{1,0:T(1,128)}, f32[1,4096]{1,0:T(1,128)}) custom-call(bf16[16,8,512]{2,1,0:T(8,128)(2,1)S(1)} %all-to-all-done.2.got_ref, bf16[1,4096]{1,0:T(2,128)(2,1)S(1)} %copy-done.4, f32[1,4096]{1,0:T(1,128)S(1)} %bitcast.7), custom_call_target="tpu_custom_call" | custom-call | tf_op jit(solution)/shard_map/final/pallas_call | solution.py:408
Async XLA Ops:
  2.4 13.4 %all-to-all-start = ((bf16[16,8,640]{2,1,0:T(8,128)(2,1)}), bf16[16,8,640]{2,1,0:T(8,128)(2,1)S(1)}, u32[]{:S(2)}, u32[]{:S(2)}) async-start(bf16[16,8,640]{2,1,0:T(8,128)(2,1)} %pack.1), calls=%async_computation | async-start | bytes 327680 | tf_op jit(solution)/shard_map/all_to_all | solution.py:303
  9.9 0.7 %copy-start.2 = (f32[4096]{0:T(1024)S(1)}, f32[4096]{0:T(1024)}, u32[]{:S(2)}) copy-start(f32[4096]{0:T(1024)} %param.7) | copy-start | bytes 49156
  13.4 1.6 %copy-start = (bf16[512,2816]{1,0:T(8,128)(2,1)}, bf16[512,2816]{1,0:T(8,128)(2,1)S(1)}, u32[]{:S(2)}) copy-start(bf16[512,2816]{1,0:T(8,128)(2,1)S(1)} %get-tuple-element.17.near_ref) | copy-start | bytes 8650756
  15.8 1.8 %copy-start.1 = (bf16[512,2816]{1,0:T(8,128)(2,1)S(1)}, bf16[512,2816]{1,0:T(8,128)(2,1)}, u32[]{:S(2)}) copy-start(bf16[512,2816]{1,0:T(8,128)(2,1)} %copy-done) | copy-start | bytes 8650756
  21.2 19.2 %copy-start.3 = (f32[4096]{0:T(1024)S(1)}, f32[4096]{0:T(1024)}, u32[]{:S(2)}) copy-start(f32[4096]{0:T(1024)} %param.7) | copy-start | bytes 49156
  21.2 19.2 %copy-start.4 = (bf16[1,4096]{1,0:T(2,128)(2,1)S(1)}, bf16[1,4096]{1,0:T(2,128)(2,1)}, u32[]{:S(2)}) copy-start(bf16[1,4096]{1,0:T(2,128)(2,1)} %queries_ref.3) | copy-start | bytes 24580
  21.2 5.8 %collective-permute-start = (bf16[128,2048]{1,0:T(8,128)(2,1)S(1)}, bf16[128,2048]{1,0:T(8,128)(2,1)S(1)}, u32[]{:S(2)}, u32[]{:S(2)}) collective-permute-start(bf16[128,2048]{1,0:T(8,128)(2,1)S(1)} %get-tuple-element.21), channel_id=1, source_target_pairs={{0,1},{1,0},{2,3},{3,2},{4,5},{5,4},{6,7},{7,6},{8,9},{9,8},{10,11... | collective-permute-start | bytes 1572872 | tf_op jit(solution)/shard_map/ppermute | solution.py:368
  21.3 8.6 %all-to-all-start.1 = ((f32[16,1,128]{2,1,0:T(1,128)}), f32[16,1,128]{2,1,0:T(1,128)S(1)}, u32[]{:S(2)}, u32[]{:S(2)}) async-start(f32[16,1,128]{2,1,0:T(1,128)} %get-tuple-element.19), calls=%async_computation.1 | async-start | bytes 16384 | tf_op jit(solution)/shard_map/all_to_all | solution.py:303
  25.8 1.2 %collective-permute-start.1 = (f32[8,128]{1,0:T(8,128)S(1)}, f32[8,128]{1,0:T(8,128)S(1)}, u32[]{:S(2)}, u32[]{:S(2)}) collective-permute-start(f32[8,128]{1,0:T(8,128)S(1)} %get-tuple-element.22.rows_ref), channel_id=1, source_target_pairs={{0,1},{1,0},{2,3},{3,2},{4,5},{5,4},{6,7},{7,6},{8,9},{9,8},{10,11... | collective-permute-start | bytes 12296 | tf_op jit(solution)/shard_map/ppermute | solution.py:369
  30.7 9.6 %all-to-all-start.2 = ((bf16[16,8,512]{2,1,0:T(8,128)(2,1)}), bf16[16,8,512]{2,1,0:T(8,128)(2,1)S(1)}, u32[]{:S(2)}, u32[]{:S(2)}) async-start(bf16[16,8,512]{2,1,0:T(8,128)(2,1)} %bitcast.3), calls=%async_computation.2 | async-start | bytes 262144 | tf_op jit(solution)/shard_map/all_to_all | solution.py:303

commit v18 on v17

--- a/solution.py
+++ b/solution.py
@@ -12,8 +12,8 @@
 teacher_div = 2.0
 coef_scale = loss_scale * score_scale
 chunks = 4
-taken = 16
-close = 11
+taken = 8
+close = 5
 pieces = 8
 f32 = jnp.float32
 bf16 = jnp.bfloat16
@@ -168,12 +168,9 @@
     queries, width = query_ref.shape
     pairs = queries * 8
     rows = held.shape[0]
-    chunk = width // taken
-    copies = []
-    for k in range(taken - close):
-        part = pl.ds(k * chunk, chunk)
-        copies.append(pltpu.make_async_copy(far_ref.at[pl.ds(0, rows), part], held.at[:, part], sems.at[k]))
-        copies[-1].start()
+    split_at = near_ref.shape[1]
+    copy = pltpu.make_async_copy(far_ref.at[pl.ds(0, rows)], held, sems.at[0])
+    copy.start()
     tiles = wide.shape[0]
     loaded = [got_ref[:, j * 128 : (j + 1) * 128].astype(f32) for j in range(tiles + 1)]
     squares = sum(x * x for x in loaded[:-1])
@@ -192,23 +189,19 @@
     pick = jnp.where(inside == lane, 1.0, 0.0).astype(bf16)
     size = jnp.zeros((pairs, 128), f32)
     along = [jnp.zeros((8, 128), f32)] * queries
-    for k in range(taken):
-        part = slice(k * chunk, (k + 1) * chunk)
-        if k < close:
-            passages = near_ref[:, part]
-        else:
-            copies[k - close].wait()
-            passages = held[:, slice((k - close) * chunk, (k - close + 1) * chunk)]
-        raw = dot(pick, passages, nn_dims)
-        raw_ref[:, part] = raw.astype(bf16)
-        lifted = raw * gain_ref[:, part]
-        for j in range(chunk // 128):
-            tile = slice(j * 128, (j + 1) * 128)
-            size = size + lifted[:, tile] * lifted[:, tile]
-            eighth, place = divmod(k * chunk // 128 + j, tiles)
+    for begin, end, source in ((0, split_at, near_ref), (split_at, width, held)):
+        if source is held:
+            copy.wait()
+        raw = dot(pick, source[...], nn_dims)
+        raw_ref[:, begin:end] = raw.astype(bf16)
+        lifted = raw * gain_ref[:, begin:end]
+        for j in range((end - begin) // 128):
+            tile = lifted[:, j * 128 : (j + 1) * 128]
+            size = size + tile * tile
+            eighth, place = divmod(begin // 128 + j, tiles)
             for i in range(queries):
                 row = wide[place, i * 8 + eighth : i * 8 + eighth + 1, :]
-                along[i] = along[i] + lifted[i * 8 : i * 8 + 8, tile] * row
+                along[i] = along[i] + tile[i * 8 : i * 8 + 8] * row
     there = theirs_ref.shape[1]
     theirs_ref[...] = raw_ref[:, pl.ds(pl.multiple_of((1 - core_ref[0]) * there, 128), there)]
     inverse = 1.0 / jnp.sqrt(jnp.sum(size, axis=1, keepdims=True))
@@ -357,7 +350,7 @@
         scratch_shapes=[
             pltpu.VMEM((rows, far_width), bf16),
             pltpu.VMEM((width // 1024, pairs, 128), f32),
-            pltpu.SemaphoreType.DMA((taken - close,)),
+            pltpu.SemaphoreType.DMA((1,)),
         ],
         compiler_params=params(48),
         name="score",

time: 41.7 us -> 41 us (0.983)
  Pallas kernels: 15.7 us -> 15.1 us
    pallas_call x1, Pallas kernels: 3.56 us -> 2.86 us  [local(): pl.pallas_call(score_kernel, in_specs=[pl.BlockSpec(memory_space=pltpu.SM...]
  transfers between devices with their start and end apart: 5 -> 5, of which waited for: 4 -> 4; matrix products, arithmetic and copies ran while one was open for 0% -> 0% of each run, Pallas kernels for 21% -> 22%
where the time goes in v18:
time: 41 us; the launch traced here: 40.4 us
  starting transfers between devices  16.4 us (40%)
  Pallas kernels  15.1 us (37%)
  waiting for transfers between devices  4.23 us (10%)
  local copies, waits for them, and re-layouts  3.95 us (10%)
  between operations  0.72 us (2%)
    all_to_all x3, starting transfers between devices, exchange(): lax.all_to_all(x, 'hash', split_axis=0, concat_axis=0, axis_index_groups=...  16.2 us
    all_to_all x3, waiting for transfers between devices, exchange(): lax.all_to_all(x, 'hash', split_axis=0, concat_axis=0, axis_index_groups=...  4.18 us
    pallas_call x1, Pallas kernels, local(): pl.pallas_call(passage_kernel, in_specs=[whole()] * 6, out_specs=outside(...  4.06 us
    unnamed x10, local copies, waits for them, and re-layouts  3.95 us
    pallas_call x1, Pallas kernels, local(): pl.pallas_call(score_kernel, in_specs=[pl.BlockSpec(memory_space=pltpu.SM...  2.86 us
    pallas_call x1, Pallas kernels, local(): pl.pallas_call(stage_kernel, in_specs=[outside(), whole()], out_specs=[wh...  2.84 us
    pallas_call x2, Pallas kernels, mixed(): pl.pallas_call(kernel, in_specs=[pl.BlockSpec(memory_space=pltpu.SMEM)] +...  1.88 us
    pallas_call x1, Pallas kernels, local(): pl.pallas_call(functools.partial(pack_kernel, rows), out_shape=shape((cou...  1.72 us
  transfers between devices with their start and end apart: 5, of which 4 were waited for; matrix products, arithmetic and copies ran while one was open for 0% of the time, Pallas kernels for 22%

profile of v18, /device:TPU:0, one launch (start us, length us, event | category | flops | bytes accessed | tf_op | source)
XLA Modules:
  0.0 40.4 jit_solution(1537019141098404650)
XLA Ops:
  0.6 1.7 %pack.1 = bf16[16,8,640]{2,1,0:T(8,128)(2,1)} custom-call(bf16[1,4096]{1,0:T(2,128)(2,1)} %queries_ref.3, s32[1,128]{1,0:T(1,128)} %candidates_ref.1, s32[1,128]{1,0:T(1,128)} %teacher_ref.1), custom_call_target="tpu_custom_call" | custom-call | tf_op jit(solution)/shard_map/pack/pallas_call | solution.py:307
  2.3 7.5 %all-to-all-start = ((bf16[16,8,640]{2,1,0:T(8,128)(2,1)}), bf16[16,8,640]{2,1,0:T(8,128)(2,1)S(1)}, u32[]{:S(2)}, u32[]{:S(2)}) async-start(bf16[16,8,640]{2,1,0:T(8,128)(2,1)} %pack.1), calls=%async_computation | async-start | bytes 327680 | tf_op jit(solution)/shard_map/all_to_all | solution.py:296
  9.9 0.0 copy-start.2
  9.9 0.7 %copy-done.2 = f32[4096]{0:T(1024)S(1)} copy-done((f32[4096]{0:T(1024)S(1)}, f32[4096]{0:T(1024)}, u32[]{:S(2)}) %copy-start.2) | copy-done | bytes 16408
  10.6 2.8 %stage.1 = (bf16[512,2560]{1,0:T(8,128)(2,1)S(1)}, bf16[8192,1536]{1,0:T(8,128)(2,1)}, f32[1,4096]{1,0:T(1,128)S(1)}) custom-call(bf16[512,4096]{1,0:T(8,128)(2,1)} %passages_ref.1, f32[1,4096]{1,0:T(1,128)S(1)} %bitcast.6), custom_call_target="tpu_custom_call" | custom-call | bytes 8388608 | tf_op jit(solution)/shard_map/stage/pallas_call | solution.py:317
  13.5 0.0 copy-start
  13.5 1.5 %copy-done = bf16[512,2560]{1,0:T(8,128)(2,1)} copy-done((bf16[512,2560]{1,0:T(8,128)(2,1)}, bf16[512,2560]{1,0:T(8,128)(2,1)S(1)}, u32[]{:S(2)}) %copy-start) | copy-done | bytes 2621464
  15.0 0.8 %all-to-all-done = bf16[16,8,640]{2,1,0:T(8,128)(2,1)S(1)} async-done(((bf16[16,8,640]{2,1,0:T(8,128)(2,1)}), bf16[16,8,640]{2,1,0:T(8,128)(2,1)S(1)}, u32[]{:S(2)}, u32[]{:S(2)}) %all-to-all-start) | async-done | bytes 163872 | tf_op jit(solution)/shard_map/all_to_all | solution.py:296
  15.8 0.0 copy-start.1
  15.8 1.7 %copy-done.1 = bf16[512,2560]{1,0:T(8,128)(2,1)S(1)} copy-done((bf16[512,2560]{1,0:T(8,128)(2,1)S(1)}, bf16[512,2560]{1,0:T(8,128)(2,1)}, u32[]{:S(2)}) %copy-start.1) | copy-done | bytes 2621464
  17.5 2.9 %score.1 = (bf16[128,4096]{1,0:T(8,128)(2,1)S(1)}, bf16[16,4096]{1,0:T(8,128)(2,1)S(1)}, f32[128,128]{1,0:T(8,128)S(1)}, f32[8,128]{1,0:T(8,128)S(1)}, f32[16,1,...) custom-call(s32[1]{0:T(128)} %bitcast.core_ref, bf16[128,640]{1,0:T(8,128)(2,1)S(1)} %bitcast.5, ...), custom_call_target="tpu_custom_call" | custom-call | tf_op jit(solution)/shard_map/score/pallas_call | solution.py:339
  20.4 0.0 copy-start.3
  20.4 0.0 copy-start.4
  20.4 0.1 collective-permute-start
  20.5 4.5 %all-to-all-start.1 = ((f32[16,1,128]{2,1,0:T(1,128)}), f32[16,1,128]{2,1,0:T(1,128)S(1)}, u32[]{:S(2)}, u32[]{:S(2)}) async-start(f32[16,1,128]{2,1,0:T(1,128)} %get-tuple-element.19), calls=%async_computation.1 | async-start | bytes 16384 | tf_op jit(solution)/shard_map/all_to_all | solution.py:296
  25.0 0.2 collective-permute-start.1
  25.2 0.9 %mix.2.mine_ref = f32[56,2048]{1,0:T(8,128)S(1)} custom-call(s32[1]{0:T(128)} %bitcast.core_ref, bf16[16,4096]{1,0:T(8,128)(2,1)S(1)} %get-tuple-element.20.query_ref, f32[1,4096]{1,0:T(1,128)S(1)} %get-tuple-element.16.gain_ref, bf16[128,4096]{1,0:T(8,128)(2,1)S(1)} %get-tuple-element.23.raw_ref, f32[8,128]{1,0:T(8,128)S(1)} %get-tuple-element.22.rows_ref), custom_call_target="tpu_custom_call" | custom-call | flops 67108864 | bytes 2097152 | tf_op jit(solution)/shard_map/mix/pallas_call | solution.py:365
  26.1 0.1 collective-permute-done.1.rows_ref
  26.2 0.0 collective-permute-done.raw_ref
  26.2 0.9 %mix.3.both_ref = f32[56,2048]{1,0:T(8,128)S(1)} custom-call(s32[1]{0:T(128)} %bitcast.core_ref, bf16[16,4096]{1,0:T(8,128)(2,1)S(1)} %get-tuple-element.20.query_ref, f32[1,4096]{1,0:T(1,128)S(1)} %get-tuple-element.16.gain_ref, bf16[128,2048]{1,0:T(8,128)(2,1)S(1)} %collective-permute-done.raw_ref, f32[8,128]{1,0:T(8,128)S(1)} %collective-permute-done.1.rows_ref, ...), custom_call_target="tpu_custom_call" | custom-call | flops 67108864 | bytes 2097152 | tf_op jit(solution)/shard_map/mix/pallas_call | solution.py:365
  27.1 2.0 %all-to-all-done.1.sums_ref = f32[16,1,128]{2,1,0:T(1,128)S(1)} async-done(((f32[16,1,128]{2,1,0:T(1,128)}), f32[16,1,128]{2,1,0:T(1,128)S(1)}, u32[]{:S(2)}, u32[]{:S(2)}) %all-to-all-start.1) | async-done | bytes 8224 | tf_op jit(solution)/shard_map/all_to_all | solution.py:296
  29.1 0.9 %partial.1 = (bf16[128,512]{1,0:T(8,128)(2,1)}, f32[1,128]{1,0:T(1,128)S(1)}) custom-call(f32[16,1,128]{2,1,0:T(1,128)S(1)} %all-to-all-done.1.sums_ref, f32[56,2048]{1,0:T(8,128)S(1)} %mix.3.both_ref), custom_call_target="tpu_custom_call" | custom-call | tf_op jit(solution)/shard_map/partial/pallas_call | solution.py:379
  30.0 4.1 %all-to-all-start.2 = ((bf16[16,8,512]{2,1,0:T(8,128)(2,1)}), bf16[16,8,512]{2,1,0:T(8,128)(2,1)S(1)}, u32[]{:S(2)}, u32[]{:S(2)}) async-start(bf16[16,8,512]{2,1,0:T(8,128)(2,1)} %bitcast.3), calls=%async_computation.2 | async-start | bytes 262144 | tf_op jit(solution)/shard_map/all_to_all | solution.py:296
  34.1 4.1 %d_passages.1 = f32[512,4096]{1,0:T(8,128)} custom-call(f32[1,128]{1,0:T(1,128)S(1)} %get-tuple-element.24.total_ref, bf16[16,4096]{1,0:T(8,128)(2,1)S(1)} %get-tuple-element.20.query_ref, f32[1,4096]{1,0:T(1,128)S(1)} %get-tuple-element.16.gain_ref, bf16[128,4096]{1,0:T(8,128)(2,1)S(1)} %get-tuple-element.23.raw_ref, ...), custom_call_target="tpu_custom_call" | custom-call | flops 1073741824 | bytes 8388608 | tf_op jit(solution)/shard_map/d_passages/pallas_call | solution.py:388
  38.1 1.4 %all-to-all-done.2.got_ref = bf16[16,8,512]{2,1,0:T(8,128)(2,1)S(1)} async-done(((bf16[16,8,512]{2,1,0:T(8,128)(2,1)}), bf16[16,8,512]{2,1,0:T(8,128)(2,1)S(1)}, u32[]{:S(2)}, u32[]{:S(2)}) %all-to-all-start.2) | async-done | bytes 131104 | tf_op jit(solution)/shard_map/all_to_all | solution.py:296
  39.5 0.0 copy-done.3
  39.5 0.0 copy-done.4
  39.5 0.9 %final.1 = (f32[1,4096]{1,0:T(1,128)}, f32[1,4096]{1,0:T(1,128)}) custom-call(bf16[16,8,512]{2,1,0:T(8,128)(2,1)S(1)} %all-to-all-done.2.got_ref, bf16[1,4096]{1,0:T(2,128)(2,1)S(1)} %copy-done.4, f32[1,4096]{1,0:T(1,128)S(1)} %bitcast.7), custom_call_target="tpu_custom_call" | custom-call | tf_op jit(solution)/shard_map/final/pallas_call | solution.py:401
Async XLA Ops:
  2.3 13.4 %all-to-all-start = ((bf16[16,8,640]{2,1,0:T(8,128)(2,1)}), bf16[16,8,640]{2,1,0:T(8,128)(2,1)S(1)}, u32[]{:S(2)}, u32[]{:S(2)}) async-start(bf16[16,8,640]{2,1,0:T(8,128)(2,1)} %pack.1), calls=%async_computation | async-start | bytes 327680 | tf_op jit(solution)/shard_map/all_to_all | solution.py:296
  9.9 0.7 %copy-start.2 = (f32[4096]{0:T(1024)S(1)}, f32[4096]{0:T(1024)}, u32[]{:S(2)}) copy-start(f32[4096]{0:T(1024)} %param.7) | copy-start | bytes 49156
  13.5 1.5 %copy-start = (bf16[512,2560]{1,0:T(8,128)(2,1)}, bf16[512,2560]{1,0:T(8,128)(2,1)S(1)}, u32[]{:S(2)}) copy-start(bf16[512,2560]{1,0:T(8,128)(2,1)S(1)} %get-tuple-element.17.near_ref) | copy-start | bytes 7864324
  15.8 1.7 %copy-start.1 = (bf16[512,2560]{1,0:T(8,128)(2,1)S(1)}, bf16[512,2560]{1,0:T(8,128)(2,1)}, u32[]{:S(2)}) copy-start(bf16[512,2560]{1,0:T(8,128)(2,1)} %copy-done) | copy-start | bytes 7864324
  20.4 19.2 %copy-start.3 = (f32[4096]{0:T(1024)S(1)}, f32[4096]{0:T(1024)}, u32[]{:S(2)}) copy-start(f32[4096]{0:T(1024)} %param.7) | copy-start | bytes 49156
  20.4 19.2 %copy-start.4 = (bf16[1,4096]{1,0:T(2,128)(2,1)S(1)}, bf16[1,4096]{1,0:T(2,128)(2,1)}, u32[]{:S(2)}) copy-start(bf16[1,4096]{1,0:T(2,128)(2,1)} %queries_ref.3) | copy-start | bytes 24580
  20.4 5.8 %collective-permute-start = (bf16[128,2048]{1,0:T(8,128)(2,1)S(1)}, bf16[128,2048]{1,0:T(8,128)(2,1)S(1)}, u32[]{:S(2)}, u32[]{:S(2)}) collective-permute-start(bf16[128,2048]{1,0:T(8,128)(2,1)S(1)} %get-tuple-element.21), channel_id=1, source_target_pairs={{0,1},{1,0},{2,3},{3,2},{4,5},{5,4},{6,7},{7,6},{8,9},{9,8},{10,11... | collective-permute-start | bytes 1572872 | tf_op jit(solution)/shard_map/ppermute | solution.py:361
  20.5 8.6 %all-to-all-start.1 = ((f32[16,1,128]{2,1,0:T(1,128)}), f32[16,1,128]{2,1,0:T(1,128)S(1)}, u32[]{:S(2)}, u32[]{:S(2)}) async-start(f32[16,1,128]{2,1,0:T(1,128)} %get-tuple-element.19), calls=%async_computation.1 | async-start | bytes 16384 | tf_op jit(solution)/shard_map/all_to_all | solution.py:296
  25.0 1.2 %collective-permute-start.1 = (f32[8,128]{1,0:T(8,128)S(1)}, f32[8,128]{1,0:T(8,128)S(1)}, u32[]{:S(2)}, u32[]{:S(2)}) collective-permute-start(f32[8,128]{1,0:T(8,128)S(1)} %get-tuple-element.22.rows_ref), channel_id=1, source_target_pairs={{0,1},{1,0},{2,3},{3,2},{4,5},{5,4},{6,7},{7,6},{8,9},{9,8},{10,11... | collective-permute-start | bytes 12296 | tf_op jit(solution)/shard_map/ppermute | solution.py:362
  30.0 9.6 %all-to-all-start.2 = ((bf16[16,8,512]{2,1,0:T(8,128)(2,1)}), bf16[16,8,512]{2,1,0:T(8,128)(2,1)S(1)}, u32[]{:S(2)}, u32[]{:S(2)}) async-start(bf16[16,8,512]{2,1,0:T(8,128)(2,1)} %bitcast.3), calls=%async_computation.2 | async-start | bytes 262144 | tf_op jit(solution)/shard_map/all_to_all | solution.py:296

commit v19 on v15

--- a/solution.py
+++ b/solution.py
@@ -93,33 +93,40 @@
     return pair == lax.broadcasted_iota(jnp.int32, dims, 1 - pair_axis)
 
 
-def stage_kernel(passages_ref, gain_ref, near_ref, far_ref, gain_out_ref, held, sems_in, sems_out):
-    gain_out_ref[...] = gain_ref[...]
+def stage_kernel(passages_ref, gain_ref, near_ref, far_ref, norms_ref, raw, gains, held, sems_in, sems_out, sem):
     rows, width = near_ref.shape
-    piece = rows // chunks
-    copies_in, copies_out, copies_near = [], [], []
-    for k in range(chunks):
+    piece = rows // pieces
+    gain_copy = pltpu.make_async_copy(gain_ref, gains, sem.at[0])
+    gain_copy.start()
+    copies_in, copies_out, inverses = [], [], []
+    for k in range(pieces):
         part = pl.ds(k * piece, piece)
-        far = passages_ref.at[part, pl.ds(width, width)]
-        near = passages_ref.at[part, pl.ds(0, width)]
-        copies_in.append(pltpu.make_async_copy(far, held.at[part], sems_in.at[k]))
+        copies_in.append(pltpu.make_async_copy(passages_ref.at[part], raw.at[part], sems_in.at[k]))
         copies_out.append(pltpu.make_async_copy(held.at[part], far_ref.at[part], sems_out.at[k]))
-        copies_near.append(pltpu.make_async_copy(near, near_ref.at[part], sems_in.at[chunks + k]))
-    for copy in copies_in + copies_near:
-        copy.start()
-    for k in range(chunks):
+        copies_in[-1].start()
+    gain_copy.wait()
+    for k in range(pieces):
+        part = pl.ds(k * piece, piece)
         copies_in[k].wait()
+        lifted = raw[part, :].astype(f32) * gains[...]
+        inverse = 1.0 / jnp.sqrt(jnp.sum(lifted * lifted, axis=1, keepdims=True))
+        unit = (lifted * inverse).astype(bf16)
+        held[part, :] = unit[:, width:]
         copies_out[k].start()
-    for copy in copies_near + copies_out:
+        near_ref[part, :] = unit[:, :width]
+        inverses.append(inverse)
+    inverse = jnp.concatenate(inverses, axis=0)
+    norms_ref[...] = jnp.transpose(jnp.broadcast_to(inverse, (rows, 128)))[:1, :]
+    for copy in copies_out:
         copy.wait()
 
 
-def mix(base, first, query_ref, gain_ref, raw_ref, lines, out_ref, before_ref):
+def mix(base, first, query_ref, units_ref, lines, out_ref, before_ref):
     queries = query_ref.shape[0]
-    pairs = raw_ref.shape[0]
+    pairs = units_ref.shape[0]
     chunk = out_ref.shape[1] // 2
     cols = jnp.transpose(jnp.concatenate([lines, jnp.zeros((120, pairs), f32)], axis=0))
-    cos, inverse, query_inverse = cols[:, 2:3], cols[:, 3:4], cols[:, 5:6]
+    cos, query_inverse = cols[:, 2:3], cols[:, 5:6]
     own = belongs((queries, pairs), 1)
     by_weight = split(jnp.where(own, lines[0:1, :], 0.0))
     by_mark = split(jnp.where(own, lines[1:2, :], 0.0))
@@ -129,7 +136,7 @@
         part = slice(k * chunk, (k + 1) * chunk)
         there = pl.ds(pl.multiple_of(base + k * chunk, 128), chunk)
         here = pl.ds(pl.multiple_of(first + k * chunk, 128), chunk)
-        row = (raw_ref[:, here].astype(f32) * gain_ref[:, there] * inverse).astype(bf16)
+        row = units_ref[:, here]
         plainly = dot(plain, row, nn_dims)
         row = row.astype(f32)
         query = dot(repeat, query_ref[:, there], nn_dims) * query_inverse
@@ -148,19 +155,19 @@
         out_ref[:, part] = sums if before_ref is None else sums + before_ref[:, part]
 
 
-def mine_kernel(core_ref, query_ref, gain_ref, raw_ref, rows_ref, out_ref):
+def mine_kernel(core_ref, query_ref, units_ref, rows_ref, out_ref):
     base = core_ref[0] * out_ref.shape[1]
-    mix(base, base, query_ref, gain_ref, raw_ref, rows_ref[...], out_ref, None)
-
-
-def both_kernel(core_ref, query_ref, gain_ref, raw_ref, rows_ref, mine_ref, out_ref):
+    mix(base, base, query_ref, units_ref, rows_ref[...], out_ref, None)
+
+
+def both_kernel(core_ref, query_ref, units_ref, rows_ref, mine_ref, out_ref):
     base = core_ref[0] * out_ref.shape[1]
-    mix(base, 0, query_ref, gain_ref, raw_ref, rows_ref[...], out_ref, mine_ref)
+    mix(base, 0, query_ref, units_ref, rows_ref[...], out_ref, mine_ref)
 
 
 def score_kernel(
-    core_ref, got_ref, gain_ref, near_ref, far_ref,
-    raw_ref, query_ref, cols_ref, rows_ref, sums_ref, theirs_ref, held, wide, sems,
+    core_ref, got_ref, norms_ref, near_ref, far_ref,
+    units_ref, query_ref, cols_ref, rows_ref, sums_ref, theirs_ref, held, wide, sems,
 ):
     queries, width = query_ref.shape
     pairs = queries * 8
@@ -187,8 +194,9 @@
     inside = lists[:, 0:1] * 256.0 + lists[:, 1:2]
     mark = lists[:, 2:3] + lists[:, 3:4]
     lane = lax.broadcasted_iota(jnp.int32, (pairs, rows), 1).astype(f32)
-    pick = jnp.where(inside == lane, 1.0, 0.0).astype(bf16)
-    size = jnp.zeros((pairs, 128), f32)
+    here = inside == lane
+    inverse = jnp.sum(jnp.where(here, norms_ref[...], 0.0), axis=1, keepdims=True)
+    pick = jnp.where(here, 1.0, 0.0).astype(bf16)
     along = [jnp.zeros((8, 128), f32)] * queries
     for k in range(chunks):
         part = slice(k * chunk, (k + 1) * chunk)
@@ -197,21 +205,18 @@
         else:
             copies[k - half].wait()
             passages = held[:, slice((k - half) * chunk, (k - half + 1) * chunk)]
-        raw = dot(pick, passages, nn_dims)
-        raw_ref[:, part] = raw.astype(bf16)
-        lifted = raw * gain_ref[:, part]
+        units = dot(pick, passages, nn_dims)
+        units_ref[:, part] = units.astype(bf16)
         for j in range(chunk // 128):
             tile = slice(j * 128, (j + 1) * 128)
-            size = size + lifted[:, tile] * lifted[:, tile]
             eighth, place = divmod(k * chunk // 128 + j, tiles)
             for i in range(queries):
                 row = wide[place, i * 8 + eighth : i * 8 + eighth + 1, :]
-                along[i] = along[i] + lifted[i * 8 : i * 8 + 8, tile] * row
+                along[i] = along[i] + units[i * 8 : i * 8 + 8, tile] * row
     there = theirs_ref.shape[1]
-    theirs_ref[...] = raw_ref[:, pl.ds(pl.multiple_of((1 - core_ref[0]) * there, 128), there)]
-    inverse = 1.0 / jnp.sqrt(jnp.sum(size, axis=1, keepdims=True))
+    theirs_ref[...] = units_ref[:, pl.ds(pl.multiple_of((1 - core_ref[0]) * there, 128), there)]
     along = jnp.concatenate(along, axis=0)
-    cos = jnp.sum(along, axis=1, keepdims=True) * inverse * query_inverse
+    cos = jnp.sum(along, axis=1, keepdims=True) * query_inverse
     weight = jnp.where(mark > 0.0, jnp.exp(cos * score_scale), 0.0)
     lane = lax.broadcasted_iota(jnp.int32, (pairs, 128), 1)
     cols = jnp.zeros((pairs, 128), f32)
@@ -246,9 +251,9 @@
         out_ref[:, tile * 128 : (tile + 1) * 128] = laid[tile].astype(bf16)
 
 
-def passage_kernel(total_ref, query_ref, gain_ref, raw_ref, cols_ref, rows_ref, out_ref, made, sems):
+def passage_kernel(total_ref, query_ref, gain_ref, units_ref, cols_ref, rows_ref, out_ref, made, sems):
     queries, width = query_ref.shape
-    rows, pairs = made.shape[0], raw_ref.shape[0]
+    rows, pairs = made.shape[0], units_ref.shape[0]
     piece = width // pieces
     weight, mark = cols_ref[:, 0:1], cols_ref[:, 1:2]
     cos, inverse = cols_ref[:, 2:3], cols_ref[:, 3:4]
@@ -267,7 +272,7 @@
     for k in range(pieces):
         part = slice(k * piece, (k + 1) * piece)
         gain = gain_ref[:, part]
-        row = (raw_ref[:, part].astype(f32) * gain * inverse).astype(bf16).astype(f32)
+        row = units_ref[:, part].astype(f32)
         query = dot(repeat, query_ref[:, part], nn_dims) * cols_ref[:, 5:6]
         term = (query.astype(bf16).astype(f32) - cos * row) * scale * gain
         made[:, part] = dot(spread, jnp.concatenate(split(term), axis=0), nn_dims)
@@ -318,19 +323,22 @@
     got = exchange(packed).reshape(count * 8, width // 8 + listed)
 
     pairs = count * 8
-    near, far, gain_near = pl.pallas_call(
+    near, far, norms = pl.pallas_call(
         stage_kernel,
-        in_specs=[outside(), whole()],
+        in_specs=[outside(), outside()],
         out_specs=[whole(), outside(), whole()],
         out_shape=[
             shape((rows, width // 2), bf16),
             shape((10 * rows, width // 2), bf16),
-            shape((1, width)),
+            shape((1, rows)),
         ],
         scratch_shapes=[
+            pltpu.VMEM((rows, width), bf16),
+            pltpu.VMEM((1, width), f32),
             pltpu.VMEM((rows, width // 2), bf16),
-            pltpu.SemaphoreType.DMA((2 * chunks,)),
-            pltpu.SemaphoreType.DMA((chunks,)),
+            pltpu.SemaphoreType.DMA((pieces,)),
+            pltpu.SemaphoreType.DMA((pieces,)),
+            pltpu.SemaphoreType.DMA((1,)),
         ],
         compiler_params=params(48),
         name="stage",
@@ -340,7 +348,7 @@
     )(passages, gain)
     half = width // 2
     core = (lax.axis_index("hash") % 2).astype(jnp.int32).reshape(1)
-    raw, query, cols, lines, sums, theirs = pl.pallas_call(
+    units, query, cols, lines, sums, theirs = pl.pallas_call(
         score_kernel,
         in_specs=[pl.BlockSpec(memory_space=pltpu.SMEM), whole(), whole(), whole(), outside()],
         out_shape=[
@@ -358,27 +366,27 @@
         ],
         compiler_params=params(48),
         name="score",
-    )(core, got, gain_near, near, far)
+    )(core, got, norms, near, far)
 
     got_sums = exchange(sums)
     swap = [(i, i ^ 1) for i in range(count)]
-    sibling_raw = lax.ppermute(theirs, "hash", swap)
+    sibling_units = lax.ppermute(theirs, "hash", swap)
     sibling_lines = lax.ppermute(lines, "hash", swap)
 
     def mixed(kernel, *operands):
         return pl.pallas_call(
             kernel,
-            in_specs=[pl.BlockSpec(memory_space=pltpu.SMEM)] + [whole()] * (len(operands) + 2),
+            in_specs=[pl.BlockSpec(memory_space=pltpu.SMEM)] + [whole()] * (len(operands) + 1),
             out_shape=shape((3 * count + 8, half)),
             compiler_params=params(48),
             name="mix",
             cost_estimate=pl.CostEstimate(
                 flops=8 * count * pairs * width, bytes_accessed=4 * pairs * width, transcendentals=0
             ),
-        )(core, query, gain_near, *operands)
-
-    mine = mixed(mine_kernel, raw, lines)
-    both = mixed(both_kernel, sibling_raw, sibling_lines, mine)
+        )(core, query, *operands)
+
+    mine = mixed(mine_kernel, units, lines)
+    both = mixed(both_kernel, sibling_units, sibling_lines, mine)
 
     partial, total = pl.pallas_call(
         partial_kernel,
@@ -400,7 +408,7 @@
         cost_estimate=pl.CostEstimate(
             flops=4 * pairs * rows * width, bytes_accessed=4 * rows * width, transcendentals=0
         ),
-    )(total, query, gain_near, raw, cols, lines)
+    )(total, query, gain, units, cols, lines)
 
     d_queries, d_gain = pl.pallas_call(
         final_kernel,

time: 39.3 us -> 39.5 us (level)
  Pallas kernels: 15.1 us -> 16.3 us
  waiting for transfers between devices: 5.82 us -> 4.82 us
    pallas_call x1, Pallas kernels: 2.75 us -> 3.98 us  [local(): pl.pallas_call(stage_kernel, in_specs=[outside(), outside()], out_specs=[...]
    all_to_all x3, waiting for transfers between devices: 5.76 us -> 4.65 us  [exchange(): lax.all_to_all(x, 'hash', split_axis=0, concat_axis=0, axis_index_groups=...]
  transfers between devices with their start and end apart: 5 -> 5, of which waited for: 4 -> 4; matrix products, arithmetic and copies ran while one was open for 0% -> 0% of each run, Pallas kernels for 22% -> 25%
where the time goes in v19:
time: 39.5 us; the launch traced here: 39 us
  starting transfers between devices  16.4 us (42%)
  Pallas kernels  16.3 us (41%)
  waiting for transfers between devices  4.82 us (12%)
  local copies, waits for them, and re-layouts  0.72 us (2%)
  between operations  0.7 us (2%)
    all_to_all x3, starting transfers between devices, exchange(): lax.all_to_all(x, 'hash', split_axis=0, concat_axis=0, axis_index_groups=...  16.2 us
    all_to_all x3, waiting for transfers between devices, exchange(): lax.all_to_all(x, 'hash', split_axis=0, concat_axis=0, axis_index_groups=...  4.65 us
    pallas_call x1, Pallas kernels, local(): pl.pallas_call(passage_kernel, in_specs=[whole()] * 6, out_specs=outside(...  4.05 us
    pallas_call x1, Pallas kernels, local(): pl.pallas_call(stage_kernel, in_specs=[outside(), outside()], out_specs=[...  3.98 us
    pallas_call x1, Pallas kernels, local(): pl.pallas_call(score_kernel, in_specs=[pl.BlockSpec(memory_space=pltpu.SM...  3.15 us
    pallas_call x1, Pallas kernels, local(): pl.pallas_call(functools.partial(pack_kernel, rows), out_shape=shape((cou...  1.72 us
    pallas_call x2, Pallas kernels, mixed(): pl.pallas_call(kernel, in_specs=[pl.BlockSpec(memory_space=pltpu.SMEM)] +...  1.65 us
    pallas_call x1, Pallas kernels, local(): pl.pallas_call(final_kernel, out_shape=[shape((1, width)), shape((1, widt...  0.87 us
  transfers between devices with their start and end apart: 5, of which 4 were waited for; matrix products, arithmetic and copies ran while one was open for 0% of the time, Pallas kernels for 25%

profile of v19, /device:TPU:0, one launch (start us, length us, event | category | flops | bytes accessed | tf_op | source)
XLA Modules:
  0.0 39.0 jit_solution(8526493244932079393)
XLA Ops:
  0.6 1.7 %pack.1 = bf16[16,8,640]{2,1,0:T(8,128)(2,1)} custom-call(bf16[1,4096]{1,0:T(2,128)(2,1)} %queries_ref.3, s32[1,128]{1,0:T(1,128)} %candidates_ref.1, s32[1,128]{1,0:T(1,128)} %teacher_ref.1), custom_call_target="tpu_custom_call" | custom-call | tf_op jit(solution)/shard_map/pack/pallas_call | solution.py:317
  2.4 7.5 %all-to-all-start = ((bf16[16,8,640]{2,1,0:T(8,128)(2,1)}), bf16[16,8,640]{2,1,0:T(8,128)(2,1)S(1)}, u32[]{:S(2)}, u32[]{:S(2)}) async-start(bf16[16,8,640]{2,1,0:T(8,128)(2,1)} %pack.1), calls=%async_computation | async-start | bytes 327680 | tf_op jit(solution)/shard_map/all_to_all | solution.py:306
  9.9 0.0 copy-start
  9.9 0.7 %copy-done = f32[4096]{0:T(1024)S(1)} copy-done((f32[4096]{0:T(1024)S(1)}, f32[4096]{0:T(1024)}, u32[]{:S(2)}) %copy-start) | copy-done | bytes 16408
  10.6 4.0 %stage.1 = (bf16[512,2048]{1,0:T(8,128)(2,1)S(1)}, bf16[5120,2048]{1,0:T(8,128)(2,1)}, f32[1,512]{1,0:T(1,128)S(1)}) custom-call(bf16[512,4096]{1,0:T(8,128)(2,1)} %passages_ref.1, f32[1,4096]{1,0:T(1,128)S(1)} %bitcast.6), custom_call_target="tpu_custom_call" | custom-call | bytes 8388608 | tf_op jit(solution)/shard_map/stage/pallas_call | solution.py:326
  14.6 1.2 %all-to-all-done = bf16[16,8,640]{2,1,0:T(8,128)(2,1)S(1)} async-done(((bf16[16,8,640]{2,1,0:T(8,128)(2,1)}), bf16[16,8,640]{2,1,0:T(8,128)(2,1)S(1)}, u32[]{:S(2)}, u32[]{:S(2)}) %all-to-all-start) | async-done | bytes 163872 | tf_op jit(solution)/shard_map/all_to_all | solution.py:306
  15.8 0.0 copy-start.1
  15.8 3.2 %score.1 = (bf16[128,4096]{1,0:T(8,128)(2,1)S(1)}, bf16[16,4096]{1,0:T(8,128)(2,1)S(1)}, f32[128,128]{1,0:T(8,128)S(1)}, f32[8,128]{1,0:T(8,128)S(1)}, f32[16,1,128]{2,1,0:T(1,128)}, /*index=5*/bf16[128,2048]{1,0:T(8,128)(2,1)}) custom-call(s32[1]{0:T(128)} %bitcast.core_ref, bf16[128,640]{1,0:T(8,128)(2,1)S(1)} %bitcast.5, ...), custom_call_target="tpu_custom_call" | custom-call | tf_op jit(solution)/shard_map/score/pallas_call | solution.py:351
  18.9 0.0 copy-start.2
  19.0 0.1 collective-permute-start
  19.0 4.5 %all-to-all-start.1 = ((f32[16,1,128]{2,1,0:T(1,128)}), f32[16,1,128]{2,1,0:T(1,128)S(1)}, u32[]{:S(2)}, u32[]{:S(2)}) async-start(f32[16,1,128]{2,1,0:T(1,128)} %get-tuple-element.19), calls=%async_computation.1 | async-start | bytes 16384 | tf_op jit(solution)/shard_map/all_to_all | solution.py:306
  23.6 0.2 collective-permute-start.1
  23.7 0.8 %mix.2.mine_ref = f32[56,2048]{1,0:T(8,128)S(1)} custom-call(s32[1]{0:T(128)} %bitcast.core_ref, bf16[16,4096]{1,0:T(8,128)(2,1)S(1)} %get-tuple-element.20.query_ref, bf16[128,4096]{1,0:T(8,128)(2,1)S(1)} %get-tuple-element.23.units_ref, f32[8,128]{1,0:T(8,128)S(1)} %get-tuple-element.22.rows_ref), custom_call_target="tpu_custom_call" | custom-call | flops 67108864 | bytes 2097152 | tf_op jit(solution)/shard_map/mix/pallas_call | solution.py:377
  24.5 0.2 collective-permute-done.1.rows_ref
  24.7 0.0 collective-permute-done.units_ref
  24.7 0.8 %mix.3.both_ref = f32[56,2048]{1,0:T(8,128)S(1)} custom-call(s32[1]{0:T(128)} %bitcast.core_ref, bf16[16,4096]{1,0:T(8,128)(2,1)S(1)} %get-tuple-element.20.query_ref, bf16[128,2048]{1,0:T(8,128)(2,1)S(1)} %collective-permute-done.units_ref, f32[8,128]{1,0:T(8,128)S(1)} %collective-permute-done.1.rows_ref, f32[56,2048]{1,0:T(8,128)S(1)} %mix.2.mine_ref), custom_call_target="tpu_custom_call" | custom-call | flops 67108864 | bytes 2097152 | tf_op jit(solution)/shard_map/mix/pallas_call | solution.py:377
  25.6 2.1 %all-to-all-done.1.sums_ref = f32[16,1,128]{2,1,0:T(1,128)S(1)} async-done(((f32[16,1,128]{2,1,0:T(1,128)}), f32[16,1,128]{2,1,0:T(1,128)S(1)}, u32[]{:S(2)}, u32[]{:S(2)}) %all-to-all-start.1) | async-done | bytes 8224 | tf_op jit(solution)/shard_map/all_to_all | solution.py:306
  27.6 0.8 %partial.1 = (bf16[128,512]{1,0:T(8,128)(2,1)}, f32[1,128]{1,0:T(1,128)S(1)}) custom-call(f32[16,1,128]{2,1,0:T(1,128)S(1)} %all-to-all-done.1.sums_ref, f32[56,2048]{1,0:T(8,128)S(1)} %mix.3.both_ref), custom_call_target="tpu_custom_call" | custom-call | tf_op jit(solution)/shard_map/partial/pallas_call | solution.py:391
  28.5 4.1 %all-to-all-start.2 = ((bf16[16,8,512]{2,1,0:T(8,128)(2,1)}), bf16[16,8,512]{2,1,0:T(8,128)(2,1)S(1)}, u32[]{:S(2)}, u32[]{:S(2)}) async-start(bf16[16,8,512]{2,1,0:T(8,128)(2,1)} %bitcast.3), calls=%async_computation.2 | async-start | bytes 262144 | tf_op jit(solution)/shard_map/all_to_all | solution.py:306
  32.6 0.0 copy-done.1
  32.6 4.1 %d_passages.1 = f32[512,4096]{1,0:T(8,128)} custom-call(f32[1,128]{1,0:T(1,128)S(1)} %get-tuple-element.24.total_ref, bf16[16,4096]{1,0:T(8,128)(2,1)S(1)} %get-tuple-element.20.query_ref, f32[1,4096]{1,0:T(1,128)S(1)} %bitcast.7, bf16[128,4096]{1,0:T(8,128)(2,1)S(1)} %get-tuple-element.23.units_ref, f32[128,128]{1,0:T(8,128)S(1)} %get-tuple-element.25.cols_ref, ...), custom_call_target="tpu_custom_call" | custom-call | flops 1073741824 | bytes 8388608 | tf_op jit(solution)/shard_map/d_passages/pallas_call | solution.py:400
  36.7 1.4 %all-to-all-done.2.got_ref = bf16[16,8,512]{2,1,0:T(8,128)(2,1)S(1)} async-done(((bf16[16,8,512]{2,1,0:T(8,128)(2,1)}), bf16[16,8,512]{2,1,0:T(8,128)(2,1)S(1)}, u32[]{:S(2)}, u32[]{:S(2)}) %all-to-all-start.2) | async-done | bytes 131104 | tf_op jit(solution)/shard_map/all_to_all | solution.py:306
  38.1 0.0 copy-done.2
  38.1 0.9 %final.1 = (f32[1,4096]{1,0:T(1,128)}, f32[1,4096]{1,0:T(1,128)}) custom-call(bf16[16,8,512]{2,1,0:T(8,128)(2,1)S(1)} %all-to-all-done.2.got_ref, bf16[1,4096]{1,0:T(2,128)(2,1)S(1)} %copy-done.2, f32[1,4096]{1,0:T(1,128)S(1)} %bitcast.8), custom_call_target="tpu_custom_call" | custom-call | tf_op jit(solution)/shard_map/final/pallas_call | solution.py:413
Async XLA Ops:
  2.4 13.4 %all-to-all-start = ((bf16[16,8,640]{2,1,0:T(8,128)(2,1)}), bf16[16,8,640]{2,1,0:T(8,128)(2,1)S(1)}, u32[]{:S(2)}, u32[]{:S(2)}) async-start(bf16[16,8,640]{2,1,0:T(8,128)(2,1)} %pack.1), calls=%async_computation | async-start | bytes 327680 | tf_op jit(solution)/shard_map/all_to_all | solution.py:306
  9.9 0.7 %copy-start = (f32[4096]{0:T(1024)S(1)}, f32[4096]{0:T(1024)}, u32[]{:S(2)}) copy-start(f32[4096]{0:T(1024)} %param.7) | copy-start | bytes 49156
  15.8 16.8 %copy-start.1 = (f32[4096]{0:T(1024)S(1)}, f32[4096]{0:T(1024)}, u32[]{:S(2)}) copy-start(f32[4096]{0:T(1024)} %param.7) | copy-start | bytes 49156
  18.9 19.1 %copy-start.2 = (bf16[1,4096]{1,0:T(2,128)(2,1)S(1)}, bf16[1,4096]{1,0:T(2,128)(2,1)}, u32[]{:S(2)}) copy-start(bf16[1,4096]{1,0:T(2,128)(2,1)} %queries_ref.3) | copy-start | bytes 24580
  19.0 5.8 %collective-permute-start = (bf16[128,2048]{1,0:T(8,128)(2,1)}, bf16[128,2048]{1,0:T(8,128)(2,1)S(1)}, u32[]{:S(2)}, u32[]{:S(2)}) collective-permute-start(bf16[128,2048]{1,0:T(8,128)(2,1)} %get-tuple-element.21), channel_id=1, source_target_pairs={{0,1},{1,0},{2,3},{3,2},{4,5},{5,4},{6,7},{7,6},{8,9},{9,8},{10,11... | collective-permute-start | bytes 1572872 | tf_op jit(solution)/shard_map/ppermute | solution.py:373
  19.0 8.6 %all-to-all-start.1 = ((f32[16,1,128]{2,1,0:T(1,128)}), f32[16,1,128]{2,1,0:T(1,128)S(1)}, u32[]{:S(2)}, u32[]{:S(2)}) async-start(f32[16,1,128]{2,1,0:T(1,128)} %get-tuple-element.19), calls=%async_computation.1 | async-start | bytes 16384 | tf_op jit(solution)/shard_map/all_to_all | solution.py:306
  23.6 1.2 %collective-permute-start.1 = (f32[8,128]{1,0:T(8,128)S(1)}, f32[8,128]{1,0:T(8,128)S(1)}, u32[]{:S(2)}, u32[]{:S(2)}) collective-permute-start(f32[8,128]{1,0:T(8,128)S(1)} %get-tuple-element.22.rows_ref), channel_id=1, source_target_pairs={{0,1},{1,0},{2,3},{3,2},{4,5},{5,4},{6,7},{7,6},{8,9},{9,8},{10,11... | collective-permute-start | bytes 12296 | tf_op jit(solution)/shard_map/ppermute | solution.py:374
  28.5 9.6 %all-to-all-start.2 = ((bf16[16,8,512]{2,1,0:T(8,128)(2,1)}), bf16[16,8,512]{2,1,0:T(8,128)(2,1)S(1)}, u32[]{:S(2)}, u32[]{:S(2)}) async-start(bf16[16,8,512]{2,1,0:T(8,128)(2,1)} %bitcast.3), calls=%async_computation.2 | async-start | bytes 262144 | tf_op jit(solution)/shard_map/all_to_all | solution.py:306

commit v20 on v15

--- a/solution.py
+++ b/solution.py
@@ -168,10 +168,15 @@
     chunk = width // chunks
     half = chunks // 2
     copies = []
+    piece = rows // chunks
     for k in range(half):
         part = pl.ds(k * chunk, chunk)
-        copies.append(pltpu.make_async_copy(far_ref.at[pl.ds(0, rows), part], held.at[:, part], sems.at[k]))
-        copies[-1].start()
+        copies.append([])
+        for j in range(chunks):
+            down = pl.ds(j * piece, piece)
+            there, here = far_ref.at[down, part], held.at[down, part]
+            copies[k].append(pltpu.make_async_copy(there, here, sems.at[k * chunks + j]))
+            copies[k][j].start()
     tiles = wide.shape[0]
     loaded = [got_ref[:, j * 128 : (j + 1) * 128].astype(f32) for j in range(tiles + 1)]
     squares = sum(x * x for x in loaded[:-1])
@@ -195,7 +200,8 @@
         if k < half:
             passages = near_ref[:, part]
         else:
-            copies[k - half].wait()
+            for copy in copies[k - half]:
+                copy.wait()
             passages = held[:, slice((k - half) * chunk, (k - half + 1) * chunk)]
         raw = dot(pick, passages, nn_dims)
         raw_ref[:, part] = raw.astype(bf16)
@@ -354,7 +360,7 @@
         scratch_shapes=[
             pltpu.VMEM((rows, width // 2), bf16),
             pltpu.VMEM((width // 1024, pairs, 128), f32),
-            pltpu.SemaphoreType.DMA((chunks // 2,)),
+            pltpu.SemaphoreType.DMA((chunks // 2 * chunks,)),
         ],
         compiler_params=params(48),
         name="score",

time: 39.3 us -> 39.5 us (level)
  no operation moved by 1% of the time
where the time goes in v20:
time: 39.5 us; the launch traced here: 39 us
  starting transfers between devices  16.4 us (42%)
  Pallas kernels  15.3 us (39%)
  waiting for transfers between devices  5.82 us (15%)
  local copies, waits for them, and re-layouts  0.72 us (2%)
  between operations  0.71 us (2%)
    all_to_all x3, starting transfers between devices, exchange(): lax.all_to_all(x, 'hash', split_axis=0, concat_axis=0, axis_index_groups=...  16.2 us
    all_to_all x3, waiting for transfers between devices, exchange(): lax.all_to_all(x, 'hash', split_axis=0, concat_axis=0, axis_index_groups=...  5.77 us
    pallas_call x1, Pallas kernels, local(): pl.pallas_call(passage_kernel, in_specs=[whole()] * 6, out_specs=outside(...  4.06 us
    pallas_call x1, Pallas kernels, local(): pl.pallas_call(score_kernel, in_specs=[pl.BlockSpec(memory_space=pltpu.SM...  3.22 us
    pallas_call x1, Pallas kernels, local(): pl.pallas_call(stage_kernel, in_specs=[outside(), whole()], out_specs=[wh...  2.75 us
    pallas_call x2, Pallas kernels, mixed(): pl.pallas_call(kernel, in_specs=[pl.BlockSpec(memory_space=pltpu.SMEM)] +...  1.88 us
    pallas_call x1, Pallas kernels, local(): pl.pallas_call(functools.partial(pack_kernel, rows), out_shape=shape((cou...  1.72 us
    pallas_call x1, Pallas kernels, local(): pl.pallas_call(final_kernel, out_shape=[shape((1, width)), shape((1, widt...  0.87 us
  transfers between devices with their start and end apart: 5, of which 4 were waited for; matrix products, arithmetic and copies ran while one was open for 0% of the time, Pallas kernels for 22%

profile of v20, /device:TPU:0, one launch (start us, length us, event | category | flops | bytes accessed | tf_op | source)
XLA Modules:
  0.0 39.0 jit_solution(17905860746519708480)
XLA Ops:
  0.6 1.7 %pack.1 = bf16[16,8,640]{2,1,0:T(8,128)(2,1)} custom-call(bf16[1,4096]{1,0:T(2,128)(2,1)} %queries_ref.3, s32[1,128]{1,0:T(1,128)} %candidates_ref.1, s32[1,128]{1,0:T(1,128)} %teacher_ref.1), custom_call_target="tpu_custom_call" | custom-call | tf_op jit(solution)/shard_map/pack/pallas_call | solution.py:318
  2.4 7.5 %all-to-all-start = ((bf16[16,8,640]{2,1,0:T(8,128)(2,1)}), bf16[16,8,640]{2,1,0:T(8,128)(2,1)S(1)}, u32[]{:S(2)}, u32[]{:S(2)}) async-start(bf16[16,8,640]{2,1,0:T(8,128)(2,1)} %pack.1), calls=%async_computation | async-start | bytes 327680 | tf_op jit(solution)/shard_map/all_to_all | solution.py:307
  9.9 0.0 copy-start
  9.9 0.7 %copy-done = f32[4096]{0:T(1024)S(1)} copy-done((f32[4096]{0:T(1024)S(1)}, f32[4096]{0:T(1024)}, u32[]{:S(2)}) %copy-start) | copy-done | bytes 16408
  10.6 2.8 %stage.1 = (bf16[512,2048]{1,0:T(8,128)(2,1)S(1)}, bf16[5120,2048]{1,0:T(8,128)(2,1)}, f32[1,4096]{1,0:T(1,128)S(1)}) custom-call(bf16[512,4096]{1,0:T(8,128)(2,1)} %passages_ref.1, f32[1,4096]{1,0:T(1,128)S(1)} %bitcast.6), custom_call_target="tpu_custom_call" | custom-call | bytes 8388608 | tf_op jit(solution)/shard_map/stage/pallas_call | solution.py:327
  13.4 2.4 %all-to-all-done = bf16[16,8,640]{2,1,0:T(8,128)(2,1)S(1)} async-done(((bf16[16,8,640]{2,1,0:T(8,128)(2,1)}), bf16[16,8,640]{2,1,0:T(8,128)(2,1)S(1)}, u32[]{:S(2)}, u32[]{:S(2)}) %all-to-all-start) | async-done | bytes 163872 | tf_op jit(solution)/shard_map/all_to_all | solution.py:307
  15.8 3.2 %score.1 = (bf16[128,4096]{1,0:T(8,128)(2,1)S(1)}, bf16[16,4096]{1,0:T(8,128)(2,1)S(1)}, f32[128,128]{1,0:T(8,128)S(1)}, f32[8,128]{1,0:T(8,128)S(1)}, f32[16,1,128]{2,1,0:T(1,128)}, /*index=5*/bf16[128,2048]{1,0:T(8,128)(2,1)}) custom-call(s32[1]{0:T(128)} %bitcast.core_ref, bf16[128,640]{1,0:T(8,128)(2,1)S(1)} %bitcast.5, ...), custom_call_target="tpu_custom_call" | custom-call | tf_op jit(solution)/shard_map/score/pallas_call | solution.py:349
  19.0 0.0 copy-start.1
  19.0 0.0 copy-start.2
  19.0 0.1 collective-permute-start
  19.1 4.5 %all-to-all-start.1 = ((f32[16,1,128]{2,1,0:T(1,128)}), f32[16,1,128]{2,1,0:T(1,128)S(1)}, u32[]{:S(2)}, u32[]{:S(2)}) async-start(f32[16,1,128]{2,1,0:T(1,128)} %get-tuple-element.19), calls=%async_computation.1 | async-start | bytes 16384 | tf_op jit(solution)/shard_map/all_to_all | solution.py:307
  23.6 0.2 collective-permute-start.1
  23.8 0.9 %mix.2.mine_ref = f32[56,2048]{1,0:T(8,128)S(1)} custom-call(s32[1]{0:T(128)} %bitcast.core_ref, bf16[16,4096]{1,0:T(8,128)(2,1)S(1)} %get-tuple-element.20.query_ref, f32[1,4096]{1,0:T(1,128)S(1)} %get-tuple-element.16.gain_ref, bf16[128,4096]{1,0:T(8,128)(2,1)S(1)} %get-tuple-element.23.raw_ref, f32[8,128]{1,0:T(8,128)S(1)} %get-tuple-element.22.rows_ref), custom_call_target="tpu_custom_call" | custom-call | flops 67108864 | bytes 2097152 | tf_op jit(solution)/shard_map/mix/pallas_call | solution.py:375
  24.7 0.1 collective-permute-done.1.rows_ref
  24.8 0.0 collective-permute-done.raw_ref
  24.8 0.9 %mix.3.both_ref = f32[56,2048]{1,0:T(8,128)S(1)} custom-call(s32[1]{0:T(128)} %bitcast.core_ref, bf16[16,4096]{1,0:T(8,128)(2,1)S(1)} %get-tuple-element.20.query_ref, f32[1,4096]{1,0:T(1,128)S(1)} %get-tuple-element.16.gain_ref, bf16[128,2048]{1,0:T(8,128)(2,1)S(1)} %collective-permute-done.raw_ref, f32[8,128]{1,0:T(8,128)S(1)} %collective-permute-done.1.rows_ref, ...), custom_call_target="tpu_custom_call" | custom-call | flops 67108864 | bytes 2097152 | tf_op jit(solution)/shard_map/mix/pallas_call | solution.py:375
  25.7 2.0 %all-to-all-done.1.sums_ref = f32[16,1,128]{2,1,0:T(1,128)S(1)} async-done(((f32[16,1,128]{2,1,0:T(1,128)}), f32[16,1,128]{2,1,0:T(1,128)S(1)}, u32[]{:S(2)}, u32[]{:S(2)}) %all-to-all-start.1) | async-done | bytes 8224 | tf_op jit(solution)/shard_map/all_to_all | solution.py:307
  27.7 0.8 %partial.1 = (bf16[128,512]{1,0:T(8,128)(2,1)}, f32[1,128]{1,0:T(1,128)S(1)}) custom-call(f32[16,1,128]{2,1,0:T(1,128)S(1)} %all-to-all-done.1.sums_ref, f32[56,2048]{1,0:T(8,128)S(1)} %mix.3.both_ref), custom_call_target="tpu_custom_call" | custom-call | tf_op jit(solution)/shard_map/partial/pallas_call | solution.py:389
  28.6 4.1 %all-to-all-start.2 = ((bf16[16,8,512]{2,1,0:T(8,128)(2,1)}), bf16[16,8,512]{2,1,0:T(8,128)(2,1)S(1)}, u32[]{:S(2)}, u32[]{:S(2)}) async-start(bf16[16,8,512]{2,1,0:T(8,128)(2,1)} %bitcast.3), calls=%async_computation.2 | async-start | bytes 262144 | tf_op jit(solution)/shard_map/all_to_all | solution.py:307
  32.7 4.1 %d_passages.1 = f32[512,4096]{1,0:T(8,128)} custom-call(f32[1,128]{1,0:T(1,128)S(1)} %get-tuple-element.24.total_ref, bf16[16,4096]{1,0:T(8,128)(2,1)S(1)} %get-tuple-element.20.query_ref, f32[1,4096]{1,0:T(1,128)S(1)} %get-tuple-element.16.gain_ref, bf16[128,4096]{1,0:T(8,128)(2,1)S(1)} %get-tuple-element.23.raw_ref, ...), custom_call_target="tpu_custom_call" | custom-call | flops 1073741824 | bytes 8388608 | tf_op jit(solution)/shard_map/d_passages/pallas_call | solution.py:398
  36.8 1.4 %all-to-all-done.2.got_ref = bf16[16,8,512]{2,1,0:T(8,128)(2,1)S(1)} async-done(((bf16[16,8,512]{2,1,0:T(8,128)(2,1)}), bf16[16,8,512]{2,1,0:T(8,128)(2,1)S(1)}, u32[]{:S(2)}, u32[]{:S(2)}) %all-to-all-start.2) | async-done | bytes 131104 | tf_op jit(solution)/shard_map/all_to_all | solution.py:307
  38.2 0.0 copy-done.1
  38.2 0.0 copy-done.2
  38.2 0.9 %final.1 = (f32[1,4096]{1,0:T(1,128)}, f32[1,4096]{1,0:T(1,128)}) custom-call(bf16[16,8,512]{2,1,0:T(8,128)(2,1)S(1)} %all-to-all-done.2.got_ref, bf16[1,4096]{1,0:T(2,128)(2,1)S(1)} %copy-done.2, f32[1,4096]{1,0:T(1,128)S(1)} %bitcast.7), custom_call_target="tpu_custom_call" | custom-call | tf_op jit(solution)/shard_map/final/pallas_call | solution.py:411
Async XLA Ops:
  2.4 13.4 %all-to-all-start = ((bf16[16,8,640]{2,1,0:T(8,128)(2,1)}), bf16[16,8,640]{2,1,0:T(8,128)(2,1)S(1)}, u32[]{:S(2)}, u32[]{:S(2)}) async-start(bf16[16,8,640]{2,1,0:T(8,128)(2,1)} %pack.1), calls=%async_computation | async-start | bytes 327680 | tf_op jit(solution)/shard_map/all_to_all | solution.py:307
  9.9 0.7 %copy-start = (f32[4096]{0:T(1024)S(1)}, f32[4096]{0:T(1024)}, u32[]{:S(2)}) copy-start(f32[4096]{0:T(1024)} %param.7) | copy-start | bytes 49156
  19.0 19.2 %copy-start.1 = (f32[4096]{0:T(1024)S(1)}, f32[4096]{0:T(1024)}, u32[]{:S(2)}) copy-start(f32[4096]{0:T(1024)} %param.7) | copy-start | bytes 49156
  19.0 19.1 %copy-start.2 = (bf16[1,4096]{1,0:T(2,128)(2,1)S(1)}, bf16[1,4096]{1,0:T(2,128)(2,1)}, u32[]{:S(2)}) copy-start(bf16[1,4096]{1,0:T(2,128)(2,1)} %queries_ref.3) | copy-start | bytes 24580
  19.0 5.8 %collective-permute-start = (bf16[128,2048]{1,0:T(8,128)(2,1)}, bf16[128,2048]{1,0:T(8,128)(2,1)S(1)}, u32[]{:S(2)}, u32[]{:S(2)}) collective-permute-start(bf16[128,2048]{1,0:T(8,128)(2,1)} %get-tuple-element.21), channel_id=1, source_target_pairs={{0,1},{1,0},{2,3},{3,2},{4,5},{5,4},{6,7},{7,6},{8,9},{9,8},{10,11... | collective-permute-start | bytes 1572872 | tf_op jit(solution)/shard_map/ppermute | solution.py:371
  19.1 8.6 %all-to-all-start.1 = ((f32[16,1,128]{2,1,0:T(1,128)}), f32[16,1,128]{2,1,0:T(1,128)S(1)}, u32[]{:S(2)}, u32[]{:S(2)}) async-start(f32[16,1,128]{2,1,0:T(1,128)} %get-tuple-element.19), calls=%async_computation.1 | async-start | bytes 16384 | tf_op jit(solution)/shard_map/all_to_all | solution.py:307
  23.6 1.2 %collective-permute-start.1 = (f32[8,128]{1,0:T(8,128)S(1)}, f32[8,128]{1,0:T(8,128)S(1)}, u32[]{:S(2)}, u32[]{:S(2)}) collective-permute-start(f32[8,128]{1,0:T(8,128)S(1)} %get-tuple-element.22.rows_ref), channel_id=1, source_target_pairs={{0,1},{1,0},{2,3},{3,2},{4,5},{5,4},{6,7},{7,6},{8,9},{9,8},{10,11... | collective-permute-start | bytes 12296 | tf_op jit(solution)/shard_map/ppermute | solution.py:372
  28.6 9.6 %all-to-all-start.2 = ((bf16[16,8,512]{2,1,0:T(8,128)(2,1)}), bf16[16,8,512]{2,1,0:T(8,128)(2,1)S(1)}, u32[]{:S(2)}, u32[]{:S(2)}) async-start(bf16[16,8,512]{2,1,0:T(8,128)(2,1)} %bitcast.3), calls=%async_computation.2 | async-start | bytes 262144 | tf_op jit(solution)/shard_map/all_to_all | solution.py:307

commit v21 on v15

--- a/solution.py
+++ b/solution.py
@@ -96,6 +96,7 @@
 def stage_kernel(passages_ref, gain_ref, near_ref, far_ref, gain_out_ref, held, sems_in, sems_out):
     gain_out_ref[...] = gain_ref[...]
     rows, width = near_ref.shape
+    half = width // 2
     piece = rows // chunks
     copies_in, copies_out, copies_near = [], [], []
     for k in range(chunks):
@@ -103,13 +104,17 @@
         far = passages_ref.at[part, pl.ds(width, width)]
         near = passages_ref.at[part, pl.ds(0, width)]
         copies_in.append(pltpu.make_async_copy(far, held.at[part], sems_in.at[k]))
-        copies_out.append(pltpu.make_async_copy(held.at[part], far_ref.at[part], sems_out.at[k]))
         copies_near.append(pltpu.make_async_copy(near, near_ref.at[part], sems_in.at[chunks + k]))
+        for j in range(2):
+            there = far_ref.at[pl.ds(j * rows + k * piece, piece)]
+            here = held.at[part, pl.ds(j * half, half)]
+            copies_out.append(pltpu.make_async_copy(here, there, sems_out.at[2 * k + j]))
     for copy in copies_in + copies_near:
         copy.start()
     for k in range(chunks):
         copies_in[k].wait()
-        copies_out[k].start()
+        copies_out[2 * k].start()
+        copies_out[2 * k + 1].start()
     for copy in copies_near + copies_out:
         copy.wait()
 
@@ -164,13 +169,12 @@
 ):
     queries, width = query_ref.shape
     pairs = queries * 8
-    rows = held.shape[0]
+    rows = held.shape[1]
     chunk = width // chunks
     half = chunks // 2
     copies = []
     for k in range(half):
-        part = pl.ds(k * chunk, chunk)
-        copies.append(pltpu.make_async_copy(far_ref.at[pl.ds(0, rows), part], held.at[:, part], sems.at[k]))
+        copies.append(pltpu.make_async_copy(far_ref.at[pl.ds(k * rows, rows)], held.at[k], sems.at[k]))
         copies[-1].start()
     tiles = wide.shape[0]
     loaded = [got_ref[:, j * 128 : (j + 1) * 128].astype(f32) for j in range(tiles + 1)]
@@ -196,7 +200,7 @@
             passages = near_ref[:, part]
         else:
             copies[k - half].wait()
-            passages = held[:, slice((k - half) * chunk, (k - half + 1) * chunk)]
+            passages = held[k - half]
         raw = dot(pick, passages, nn_dims)
         raw_ref[:, part] = raw.astype(bf16)
         lifted = raw * gain_ref[:, part]
@@ -324,13 +328,13 @@
         out_specs=[whole(), outside(), whole()],
         out_shape=[
             shape((rows, width // 2), bf16),
-            shape((10 * rows, width // 2), bf16),
+            shape((20 * rows, width // 4), bf16),
             shape((1, width)),
         ],
         scratch_shapes=[
             pltpu.VMEM((rows, width // 2), bf16),
             pltpu.SemaphoreType.DMA((2 * chunks,)),
-            pltpu.SemaphoreType.DMA((chunks,)),
+            pltpu.SemaphoreType.DMA((2 * chunks,)),
         ],
         compiler_params=params(48),
         name="stage",
@@ -352,7 +356,7 @@
             shape((pairs, half), bf16),
         ],
         scratch_shapes=[
-            pltpu.VMEM((rows, width // 2), bf16),
+            pltpu.VMEM((chunks // 2, rows, width // chunks), bf16),
             pltpu.VMEM((width // 1024, pairs, 128), f32),
             pltpu.SemaphoreType.DMA((chunks // 2,)),
         ],

time: 39.3 us -> 39.1 us (level)
  transfers between devices with their start and end apart: 5 -> 5, of which waited for: 4 -> 4; matrix products, arithmetic and copies ran while one was open for 0% -> 0% of each run, Pallas kernels for 22% -> 23%
where the time goes in v21:
time: 39.1 us; the launch traced here: 38.6 us
  starting transfers between devices  16.4 us (42%)
  Pallas kernels  14.9 us (38%)
  waiting for transfers between devices  5.79 us (15%)
  local copies, waits for them, and re-layouts  0.72 us (2%)
  between operations  0.71 us (2%)
    all_to_all x3, starting transfers between devices, exchange(): lax.all_to_all(x, 'hash', split_axis=0, concat_axis=0, axis_index_groups=...  16.2 us
    all_to_all x3, waiting for transfers between devices, exchange(): lax.all_to_all(x, 'hash', split_axis=0, concat_axis=0, axis_index_groups=...  5.73 us
    pallas_call x1, Pallas kernels, local(): pl.pallas_call(passage_kernel, in_specs=[whole()] * 6, out_specs=outside(...  4.05 us
    pallas_call x1, Pallas kernels, local(): pl.pallas_call(stage_kernel, in_specs=[outside(), whole()], out_specs=[wh...  2.8 us
    pallas_call x1, Pallas kernels, local(): pl.pallas_call(score_kernel, in_specs=[pl.BlockSpec(memory_space=pltpu.SM...  2.77 us
    pallas_call x2, Pallas kernels, mixed(): pl.pallas_call(kernel, in_specs=[pl.BlockSpec(memory_space=pltpu.SMEM)] +...  1.87 us
    pallas_call x1, Pallas kernels, local(): pl.pallas_call(functools.partial(pack_kernel, rows), out_shape=shape((cou...  1.72 us
    pallas_call x1, Pallas kernels, local(): pl.pallas_call(final_kernel, out_shape=[shape((1, width)), shape((1, widt...  0.87 us
  transfers between devices with their start and end apart: 5, of which 4 were waited for; matrix products, arithmetic and copies ran while one was open for 0% of the time, Pallas kernels for 23%

profile of v21, /device:TPU:0, one launch (start us, length us, event | category | flops | bytes accessed | tf_op | source)
XLA Modules:
  0.0 38.6 jit_solution(9894005786350810690)
XLA Ops:
  0.6 1.7 %pack.1 = bf16[16,8,640]{2,1,0:T(8,128)(2,1)} custom-call(bf16[1,4096]{1,0:T(2,128)(2,1)} %queries_ref.3, s32[1,128]{1,0:T(1,128)} %candidates_ref.1, s32[1,128]{1,0:T(1,128)} %teacher_ref.1), custom_call_target="tpu_custom_call" | custom-call | tf_op jit(solution)/shard_map/pack/pallas_call | solution.py:316
  2.4 7.5 %all-to-all-start = ((bf16[16,8,640]{2,1,0:T(8,128)(2,1)}), bf16[16,8,640]{2,1,0:T(8,128)(2,1)S(1)}, u32[]{:S(2)}, u32[]{:S(2)}) async-start(bf16[16,8,640]{2,1,0:T(8,128)(2,1)} %pack.1), calls=%async_computation | async-start | bytes 327680 | tf_op jit(solution)/shard_map/all_to_all | solution.py:305
  9.9 0.0 copy-start
  9.9 0.7 %copy-done = f32[4096]{0:T(1024)S(1)} copy-done((f32[4096]{0:T(1024)S(1)}, f32[4096]{0:T(1024)}, u32[]{:S(2)}) %copy-start) | copy-done | bytes 16408
  10.6 2.8 %stage.1 = (bf16[512,2048]{1,0:T(8,128)(2,1)S(1)}, bf16[10240,1024]{1,0:T(8,128)(2,1)}, f32[1,4096]{1,0:T(1,128)S(1)}) custom-call(bf16[512,4096]{1,0:T(8,128)(2,1)} %passages_ref.1, f32[1,4096]{1,0:T(1,128)S(1)} %bitcast.6), custom_call_target="tpu_custom_call" | custom-call | bytes 8388608 | tf_op jit(solution)/shard_map/stage/pallas_call | solution.py:325
  13.4 2.4 %all-to-all-done = bf16[16,8,640]{2,1,0:T(8,128)(2,1)S(1)} async-done(((bf16[16,8,640]{2,1,0:T(8,128)(2,1)}), bf16[16,8,640]{2,1,0:T(8,128)(2,1)S(1)}, u32[]{:S(2)}, u32[]{:S(2)}) %all-to-all-start) | async-done | bytes 163872 | tf_op jit(solution)/shard_map/all_to_all | solution.py:305
  15.8 2.8 %score.1 = (bf16[128,4096]{1,0:T(8,128)(2,1)S(1)}, bf16[16,4096]{1,0:T(8,128)(2,1)S(1)}, f32[128,128]{1,0:T(8,128)S(1)}, f32[8,128]{1,0:T(8,128)S(1)}, f32[16,1,128]{2,1,0:T(1,128)}, /*index=5*/bf16[128,2048]{1,0:T(8,128)(2,1)}) custom-call(s32[1]{0:T(128)} %bitcast.core_ref, bf16[128,640]{1,0:T(8,128)(2,1)S(1)} %bitcast.5, ...), custom_call_target="tpu_custom_call" | custom-call | tf_op jit(solution)/shard_map/score/pallas_call | solution.py:347
  18.6 0.0 copy-start.1
  18.6 0.0 copy-start.2
  18.6 0.1 collective-permute-start
  18.7 4.5 %all-to-all-start.1 = ((f32[16,1,128]{2,1,0:T(1,128)}), f32[16,1,128]{2,1,0:T(1,128)S(1)}, u32[]{:S(2)}, u32[]{:S(2)}) async-start(f32[16,1,128]{2,1,0:T(1,128)} %get-tuple-element.19), calls=%async_computation.1 | async-start | bytes 16384 | tf_op jit(solution)/shard_map/all_to_all | solution.py:305
  23.2 0.2 collective-permute-start.1
  23.4 0.9 %mix.2.mine_ref = f32[56,2048]{1,0:T(8,128)S(1)} custom-call(s32[1]{0:T(128)} %bitcast.core_ref, bf16[16,4096]{1,0:T(8,128)(2,1)S(1)} %get-tuple-element.20.query_ref, f32[1,4096]{1,0:T(1,128)S(1)} %get-tuple-element.16.gain_ref, bf16[128,4096]{1,0:T(8,128)(2,1)S(1)} %get-tuple-element.23.raw_ref, f32[8,128]{1,0:T(8,128)S(1)} %get-tuple-element.22.rows_ref), custom_call_target="tpu_custom_call" | custom-call | flops 67108864 | bytes 2097152 | tf_op jit(solution)/shard_map/mix/pallas_call | solution.py:373
  24.3 0.1 collective-permute-done.1.rows_ref
  24.3 0.0 collective-permute-done.raw_ref
  24.4 0.9 %mix.3.both_ref = f32[56,2048]{1,0:T(8,128)S(1)} custom-call(s32[1]{0:T(128)} %bitcast.core_ref, bf16[16,4096]{1,0:T(8,128)(2,1)S(1)} %get-tuple-element.20.query_ref, f32[1,4096]{1,0:T(1,128)S(1)} %get-tuple-element.16.gain_ref, bf16[128,2048]{1,0:T(8,128)(2,1)S(1)} %collective-permute-done.raw_ref, f32[8,128]{1,0:T(8,128)S(1)} %collective-permute-done.1.rows_ref, ...), custom_call_target="tpu_custom_call" | custom-call | flops 67108864 | bytes 2097152 | tf_op jit(solution)/shard_map/mix/pallas_call | solution.py:373
  25.3 2.0 %all-to-all-done.1.sums_ref = f32[16,1,128]{2,1,0:T(1,128)S(1)} async-done(((f32[16,1,128]{2,1,0:T(1,128)}), f32[16,1,128]{2,1,0:T(1,128)S(1)}, u32[]{:S(2)}, u32[]{:S(2)}) %all-to-all-start.1) | async-done | bytes 8224 | tf_op jit(solution)/shard_map/all_to_all | solution.py:305
  27.3 0.8 %partial.1 = (bf16[128,512]{1,0:T(8,128)(2,1)}, f32[1,128]{1,0:T(1,128)S(1)}) custom-call(f32[16,1,128]{2,1,0:T(1,128)S(1)} %all-to-all-done.1.sums_ref, f32[56,2048]{1,0:T(8,128)S(1)} %mix.3.both_ref), custom_call_target="tpu_custom_call" | custom-call | tf_op jit(solution)/shard_map/partial/pallas_call | solution.py:387
  28.1 4.1 %all-to-all-start.2 = ((bf16[16,8,512]{2,1,0:T(8,128)(2,1)}), bf16[16,8,512]{2,1,0:T(8,128)(2,1)S(1)}, u32[]{:S(2)}, u32[]{:S(2)}) async-start(bf16[16,8,512]{2,1,0:T(8,128)(2,1)} %bitcast.3), calls=%async_computation.2 | async-start | bytes 262144 | tf_op jit(solution)/shard_map/all_to_all | solution.py:305
  32.2 4.0 %d_passages.1 = f32[512,4096]{1,0:T(8,128)} custom-call(f32[1,128]{1,0:T(1,128)S(1)} %get-tuple-element.24.total_ref, bf16[16,4096]{1,0:T(8,128)(2,1)S(1)} %get-tuple-element.20.query_ref, f32[1,4096]{1,0:T(1,128)S(1)} %get-tuple-element.16.gain_ref, bf16[128,4096]{1,0:T(8,128)(2,1)S(1)} %get-tuple-element.23.raw_ref, ...), custom_call_target="tpu_custom_call" | custom-call | flops 1073741824 | bytes 8388608 | tf_op jit(solution)/shard_map/d_passages/pallas_call | solution.py:396
  36.3 1.4 %all-to-all-done.2.got_ref = bf16[16,8,512]{2,1,0:T(8,128)(2,1)S(1)} async-done(((bf16[16,8,512]{2,1,0:T(8,128)(2,1)}), bf16[16,8,512]{2,1,0:T(8,128)(2,1)S(1)}, u32[]{:S(2)}, u32[]{:S(2)}) %all-to-all-start.2) | async-done | bytes 131104 | tf_op jit(solution)/shard_map/all_to_all | solution.py:305
  37.7 0.0 copy-done.1
  37.7 0.0 copy-done.2
  37.7 0.9 %final.1 = (f32[1,4096]{1,0:T(1,128)}, f32[1,4096]{1,0:T(1,128)}) custom-call(bf16[16,8,512]{2,1,0:T(8,128)(2,1)S(1)} %all-to-all-done.2.got_ref, bf16[1,4096]{1,0:T(2,128)(2,1)S(1)} %copy-done.2, f32[1,4096]{1,0:T(1,128)S(1)} %bitcast.7), custom_call_target="tpu_custom_call" | custom-call | tf_op jit(solution)/shard_map/final/pallas_call | solution.py:409
Async XLA Ops:
  2.4 13.4 %all-to-all-start = ((bf16[16,8,640]{2,1,0:T(8,128)(2,1)}), bf16[16,8,640]{2,1,0:T(8,128)(2,1)S(1)}, u32[]{:S(2)}, u32[]{:S(2)}) async-start(bf16[16,8,640]{2,1,0:T(8,128)(2,1)} %pack.1), calls=%async_computation | async-start | bytes 327680 | tf_op jit(solution)/shard_map/all_to_all | solution.py:305
  9.9 0.7 %copy-start = (f32[4096]{0:T(1024)S(1)}, f32[4096]{0:T(1024)}, u32[]{:S(2)}) copy-start(f32[4096]{0:T(1024)} %param.7) | copy-start | bytes 49156
  18.6 19.2 %copy-start.1 = (f32[4096]{0:T(1024)S(1)}, f32[4096]{0:T(1024)}, u32[]{:S(2)}) copy-start(f32[4096]{0:T(1024)} %param.7) | copy-start | bytes 49156
  18.6 19.1 %copy-start.2 = (bf16[1,4096]{1,0:T(2,128)(2,1)S(1)}, bf16[1,4096]{1,0:T(2,128)(2,1)}, u32[]{:S(2)}) copy-start(bf16[1,4096]{1,0:T(2,128)(2,1)} %queries_ref.3) | copy-start | bytes 24580
  18.6 5.8 %collective-permute-start = (bf16[128,2048]{1,0:T(8,128)(2,1)}, bf16[128,2048]{1,0:T(8,128)(2,1)S(1)}, u32[]{:S(2)}, u32[]{:S(2)}) collective-permute-start(bf16[128,2048]{1,0:T(8,128)(2,1)} %get-tuple-element.21), channel_id=1, source_target_pairs={{0,1},{1,0},{2,3},{3,2},{4,5},{5,4},{6,7},{7,6},{8,9},{9,8},{10,11... | collective-permute-start | bytes 1572872 | tf_op jit(solution)/shard_map/ppermute | solution.py:369
  18.7 8.6 %all-to-all-start.1 = ((f32[16,1,128]{2,1,0:T(1,128)}), f32[16,1,128]{2,1,0:T(1,128)S(1)}, u32[]{:S(2)}, u32[]{:S(2)}) async-start(f32[16,1,128]{2,1,0:T(1,128)} %get-tuple-element.19), calls=%async_computation.1 | async-start | bytes 16384 | tf_op jit(solution)/shard_map/all_to_all | solution.py:305
  23.2 1.2 %collective-permute-start.1 = (f32[8,128]{1,0:T(8,128)S(1)}, f32[8,128]{1,0:T(8,128)S(1)}, u32[]{:S(2)}, u32[]{:S(2)}) collective-permute-start(f32[8,128]{1,0:T(8,128)S(1)} %get-tuple-element.22.rows_ref), channel_id=1, source_target_pairs={{0,1},{1,0},{2,3},{3,2},{4,5},{5,4},{6,7},{7,6},{8,9},{9,8},{10,11... | collective-permute-start | bytes 12296 | tf_op jit(solution)/shard_map/ppermute | solution.py:370
  28.1 9.6 %all-to-all-start.2 = ((bf16[16,8,512]{2,1,0:T(8,128)(2,1)}), bf16[16,8,512]{2,1,0:T(8,128)(2,1)S(1)}, u32[]{:S(2)}, u32[]{:S(2)}) async-start(bf16[16,8,512]{2,1,0:T(8,128)(2,1)} %bitcast.3), calls=%async_computation.2 | async-start | bytes 262144 | tf_op jit(solution)/shard_map/all_to_all | solution.py:305

commit v22 on v21

--- a/solution.py
+++ b/solution.py
@@ -17,6 +17,7 @@
 bf16 = jnp.bfloat16
 vmem = pltpu.VMEM
 nn_dims = (((1,), (0,)), ((), ()))
+nt_dims = (((1,), (1,)), ((), ()))
 
 
 def dot(a, b, dims):
@@ -60,7 +61,7 @@
     width = queries_ref.shape[1] // 8
     query = queries_ref[...].astype(f32)
     query = jnp.concatenate([query[:, k * width : (k + 1) * width] for k in range(8)], axis=0)
-    owner = lax.div(ids, rows)
+    owner = ids >> (rows.bit_length() - 1) if rows & (rows - 1) == 0 else lax.div(ids, rows)
     inside = ids - owner * rows
     slot = member_slot(owner, count)
     marks = jnp.exp(teacher_ref[...].astype(f32) * (1.0 / teacher_div))
@@ -72,7 +73,7 @@
             (inside & 255).astype(f32),
             high.astype(f32),
             low.astype(f32),
-            jnp.zeros((listed - 4, listed), f32),
+            jnp.zeros((12, listed), f32),
         ],
         axis=0,
     )
@@ -83,7 +84,8 @@
     rank = jnp.sum(jnp.where(earlier, 1.0, 0.0), axis=0, keepdims=True)
     place = slot * 8 + rank.astype(jnp.int32)
     spread = jnp.where(place == lax.broadcasted_iota(jnp.int32, (count * 8, listed), 0), 1.0, 0.0)
-    lists = dot(spread.astype(bf16), jnp.transpose(values).astype(bf16), nn_dims)
+    lists = dot(spread.astype(bf16), values.astype(bf16), nt_dims)
+    lists = jnp.concatenate([lists, jnp.zeros((count * 8, listed - 16), f32)], axis=1)
     out_ref[:, :, :width] = jnp.broadcast_to(query.astype(bf16)[None], (count, 8, width))
     out_ref[:, :, width:] = lists.astype(bf16).reshape(count, 8, listed)
 
@@ -119,10 +121,10 @@
         copy.wait()
 
 
-def mix(base, first, query_ref, gain_ref, raw_ref, lines, out_ref, before_ref):
+def mix(base, first, query_ref, gain_ref, raw_ref, lines, width):
     queries = query_ref.shape[0]
     pairs = raw_ref.shape[0]
-    chunk = out_ref.shape[1] // 2
+    chunk = width // 2
     cols = jnp.transpose(jnp.concatenate([lines, jnp.zeros((120, pairs), f32)], axis=0))
     cos, inverse, query_inverse = cols[:, 2:3], cols[:, 3:4], cols[:, 5:6]
     own = belongs((queries, pairs), 1)
@@ -131,7 +133,6 @@
     plain = jnp.concatenate([*by_weight, *by_mark], axis=0)
     repeat = jnp.where(belongs((pairs, queries), 0), 1.0, 0.0).astype(bf16)
     for k in range(2):
-        part = slice(k * chunk, (k + 1) * chunk)
         there = pl.ds(pl.multiple_of(base + k * chunk, 128), chunk)
         here = pl.ds(pl.multiple_of(first + k * chunk, 128), chunk)
         row = (raw_ref[:, here].astype(f32) * gain_ref[:, there] * inverse).astype(bf16)
@@ -150,17 +151,31 @@
             ],
             axis=0,
         )
-        out_ref[:, part] = sums if before_ref is None else sums + before_ref[:, part]
+        yield slice(k * chunk, (k + 1) * chunk), sums
 
 
 def mine_kernel(core_ref, query_ref, gain_ref, raw_ref, rows_ref, out_ref):
-    base = core_ref[0] * out_ref.shape[1]
-    mix(base, base, query_ref, gain_ref, raw_ref, rows_ref[...], out_ref, None)
-
-
-def both_kernel(core_ref, query_ref, gain_ref, raw_ref, rows_ref, mine_ref, out_ref):
-    base = core_ref[0] * out_ref.shape[1]
-    mix(base, 0, query_ref, gain_ref, raw_ref, rows_ref[...], out_ref, mine_ref)
+    width = out_ref.shape[1]
+    base = core_ref[0] * width
+    for part, sums in mix(base, base, query_ref, gain_ref, raw_ref, rows_ref[...], width):
+        out_ref[:, part] = sums
+
+
+def both_kernel(core_ref, query_ref, gain_ref, raw_ref, rows_ref, mine_ref, scaled_ref, plain_ref):
+    queries = query_ref.shape[0]
+    width = mine_ref.shape[1]
+    tiles = scaled_ref.shape[0]
+    base = core_ref[0] * width
+    for part, sums in mix(base, 0, query_ref, gain_ref, raw_ref, rows_ref[...], width):
+        sums = sums + mine_ref[:, part]
+        for j in range((part.stop - part.start) // 128):
+            row, tile = divmod(part.start // 128 + j, tiles)
+            piece = sums[:, j * 128 : (j + 1) * 128]
+            last = piece[3 * queries : 3 * queries + 1] * (1.0 / queries)
+            scaled_ref[tile, pl.ds(row, queries, stride=8), :] = piece[:queries]
+            scaled_ref[tile, pl.ds(4 + row, queries, stride=8), :] = piece[2 * queries : 3 * queries]
+            plain_ref[tile, pl.ds(row, queries, stride=8), :] = piece[queries : 2 * queries]
+            plain_ref[tile, pl.ds(4 + row, queries, stride=8), :] = jnp.broadcast_to(last, (queries, 128))
 
 
 def score_kernel(
@@ -227,27 +242,21 @@
     sums_ref[...] = jnp.broadcast_to(flipped[None, :1], sums_ref.shape)
 
 
-def partial_kernel(sums_ref, both_ref, out_ref, total_ref, laid):
-    queries = sums_ref.shape[2] // 8
-    width = both_ref.shape[1]
+def partial_kernel(sums_ref, scaled_ref, plain_ref, out_ref, total_ref):
+    tiles, pairs, _ = scaled_ref.shape
+    queries = pairs // 8
     total = jnp.sum(sums_ref[...][:, 0, :], axis=0, keepdims=True)
     total_ref[...] = total
-    own = belongs((queries, total.shape[1]), 1)
-    inverse = 1.0 / jnp.sum(jnp.where(own, total, 0.0), axis=1, keepdims=True)
-    both = both_ref[...]
-    partial = coef_scale * (both[:queries] * inverse - both[queries : 2 * queries])
-    gain_part = jnp.sum(both[2 * queries : 3 * queries] * inverse, axis=0, keepdims=True)
-    gain_part = coef_scale * (gain_part - both[3 * queries : 3 * queries + 1])
-    tiles = laid.shape[0]
-    for k in range(width // 128):
-        row, tile = k // tiles, k % tiles
-        part = slice(k * 128, (k + 1) * 128)
-        laid[tile, pl.ds(row, queries, stride=8), :] = partial[:, part]
-        laid[tile, pl.ds(4 + row, queries, stride=8), :] = jnp.broadcast_to(
-            gain_part[:, part], (queries, 128)
-        )
+    alike = (lax.broadcasted_iota(jnp.int32, (pairs, pairs), 0) >> 3) == (
+        lax.broadcasted_iota(jnp.int32, (pairs, pairs), 1) >> 3
+    )
+    inverse = coef_scale / jnp.sum(jnp.where(alike, total, 0.0), axis=1, keepdims=True)
+    single = (lax.broadcasted_iota(jnp.int32, (pairs, 128), 0) & 7) < 4
     for tile in range(tiles):
-        out_ref[:, tile * 128 : (tile + 1) * 128] = laid[tile].astype(bf16)
+        terms = scaled_ref[tile] * inverse - coef_scale * plain_ref[tile]
+        added = jnp.sum(terms.reshape(queries, 8, 128), axis=0, keepdims=True)
+        added = jnp.broadcast_to(added, (queries, 8, 128)).reshape(pairs, 128)
+        out_ref[:, tile * 128 : (tile + 1) * 128] = jnp.where(single, terms, added).astype(bf16)
 
 
 def passage_kernel(total_ref, query_ref, gain_ref, raw_ref, cols_ref, rows_ref, out_ref, made, sems):
@@ -369,11 +378,11 @@
     sibling_raw = lax.ppermute(theirs, "hash", swap)
     sibling_lines = lax.ppermute(lines, "hash", swap)
 
-    def mixed(kernel, *operands):
+    def mixed(kernel, out_shape, *operands):
         return pl.pallas_call(
             kernel,
             in_specs=[pl.BlockSpec(memory_space=pltpu.SMEM)] + [whole()] * (len(operands) + 2),
-            out_shape=shape((3 * count + 8, half)),
+            out_shape=out_shape,
             compiler_params=params(48),
             name="mix",
             cost_estimate=pl.CostEstimate(
@@ -381,16 +390,16 @@
             ),
         )(core, query, gain_near, *operands)
 
-    mine = mixed(mine_kernel, raw, lines)
-    both = mixed(both_kernel, sibling_raw, sibling_lines, mine)
+    mine = mixed(mine_kernel, shape((3 * count + 8, half)), raw, lines)
+    laid = shape((half // 512, pairs, 128))
+    scaled, plain = mixed(both_kernel, [laid, laid], sibling_raw, sibling_lines, mine)
 
     partial, total = pl.pallas_call(
         partial_kernel,
         out_shape=[shape((pairs, half // 4), bf16), shape((1, pairs))],
-        scratch_shapes=[pltpu.VMEM((half // 512, pairs, 128), f32)],
         compiler_params=params(48),
         name="partial",
-    )(got_sums, both)
+    )(got_sums, scaled, plain)
     got_partial = exchange(partial.reshape(count, 8, half // 4))
 
     d_passages = pl.pallas_call(

time: 39.1 us -> 39 us (level)
  no operation moved by 1% of the time
where the time goes in v22:
time: 39 us; the launch traced here: 38.5 us
  starting transfers between devices  16.4 us (42%)
  Pallas kernels  14.9 us (38%)
  waiting for transfers between devices  5.72 us (15%)
  local copies, waits for them, and re-layouts  0.72 us (2%)
  between operations  0.71 us (2%)
    all_to_all x3, starting transfers between devices, exchange(): lax.all_to_all(x, 'hash', split_axis=0, concat_axis=0, axis_index_groups=...  16.2 us
    all_to_all x3, waiting for transfers between devices, exchange(): lax.all_to_all(x, 'hash', split_axis=0, concat_axis=0, axis_index_groups=...  5.66 us
    pallas_call x1, Pallas kernels, local(): pl.pallas_call(passage_kernel, in_specs=[whole()] * 6, out_specs=outside(...  4.06 us
    pallas_call x1, Pallas kernels, local(): pl.pallas_call(stage_kernel, in_specs=[outside(), whole()], out_specs=[wh...  2.8 us
    pallas_call x1, Pallas kernels, local(): pl.pallas_call(score_kernel, in_specs=[pl.BlockSpec(memory_space=pltpu.SM...  2.77 us
    pallas_call x2, Pallas kernels, mixed(): pl.pallas_call(kernel, in_specs=[pl.BlockSpec(memory_space=pltpu.SMEM)] +...  1.94 us
    pallas_call x1, Pallas kernels, local(): pl.pallas_call(functools.partial(pack_kernel, rows), out_shape=shape((cou...  1.67 us
    pallas_call x1, Pallas kernels, local(): pl.pallas_call(final_kernel, out_shape=[shape((1, width)), shape((1, widt...  0.87 us
  transfers between devices with their start and end apart: 5, of which 4 were waited for; matrix products, arithmetic and copies ran while one was open for 0% of the time, Pallas kernels for 23%

profile of v22, /device:TPU:0, one launch (start us, length us, event | category | flops | bytes accessed | tf_op | source)
XLA Modules:
  0.0 38.5 jit_solution(6840156597596633870)
XLA Ops:
  0.6 1.7 %pack.1 = bf16[16,8,640]{2,1,0:T(8,128)(2,1)} custom-call(bf16[1,4096]{1,0:T(2,128)(2,1)} %queries_ref.3, s32[1,128]{1,0:T(1,128)} %candidates_ref.1, s32[1,128]{1,0:T(1,128)} %teacher_ref.1), custom_call_target="tpu_custom_call" | custom-call | tf_op jit(solution)/shard_map/pack/pallas_call | solution.py:325
  2.3 7.5 %all-to-all-start = ((bf16[16,8,640]{2,1,0:T(8,128)(2,1)}), bf16[16,8,640]{2,1,0:T(8,128)(2,1)S(1)}, u32[]{:S(2)}, u32[]{:S(2)}) async-start(bf16[16,8,640]{2,1,0:T(8,128)(2,1)} %pack.1), calls=%async_computation | async-start | bytes 327680 | tf_op jit(solution)/shard_map/all_to_all | solution.py:314
  9.9 0.0 copy-start
  9.9 0.7 %copy-done = f32[4096]{0:T(1024)S(1)} copy-done((f32[4096]{0:T(1024)S(1)}, f32[4096]{0:T(1024)}, u32[]{:S(2)}) %copy-start) | copy-done | bytes 16408
  10.6 2.8 %stage.1 = (bf16[512,2048]{1,0:T(8,128)(2,1)S(1)}, bf16[10240,1024]{1,0:T(8,128)(2,1)}, f32[1,4096]{1,0:T(1,128)S(1)}) custom-call(bf16[512,4096]{1,0:T(8,128)(2,1)} %passages_ref.1, f32[1,4096]{1,0:T(1,128)S(1)} %bitcast.6), custom_call_target="tpu_custom_call" | custom-call | bytes 8388608 | tf_op jit(solution)/shard_map/stage/pallas_call | solution.py:334
  13.4 2.4 %all-to-all-done = bf16[16,8,640]{2,1,0:T(8,128)(2,1)S(1)} async-done(((bf16[16,8,640]{2,1,0:T(8,128)(2,1)}), bf16[16,8,640]{2,1,0:T(8,128)(2,1)S(1)}, u32[]{:S(2)}, u32[]{:S(2)}) %all-to-all-start) | async-done | bytes 163872 | tf_op jit(solution)/shard_map/all_to_all | solution.py:314
  15.7 2.8 %score.1 = (bf16[128,4096]{1,0:T(8,128)(2,1)S(1)}, bf16[16,4096]{1,0:T(8,128)(2,1)S(1)}, f32[128,128]{1,0:T(8,128)S(1)}, f32[8,128]{1,0:T(8,128)S(1)}, f32[16,1,128]{2,1,0:T(1,128)}, /*index=5*/bf16[128,2048]{1,0:T(8,128)(2,1)}) custom-call(s32[1]{0:T(128)} %bitcast.core_ref, bf16[128,640]{1,0:T(8,128)(2,1)S(1)} %bitcast.5, ...), custom_call_target="tpu_custom_call" | custom-call | tf_op jit(solution)/shard_map/score/pallas_call | solution.py:356
  18.5 0.0 copy-start.1
  18.5 0.0 copy-start.2
  18.5 0.1 collective-permute-start
  18.6 4.5 %all-to-all-start.1 = ((f32[16,1,128]{2,1,0:T(1,128)}), f32[16,1,128]{2,1,0:T(1,128)S(1)}, u32[]{:S(2)}, u32[]{:S(2)}) async-start(f32[16,1,128]{2,1,0:T(1,128)} %get-tuple-element.21), calls=%async_computation.1 | async-start | bytes 16384 | tf_op jit(solution)/shard_map/all_to_all | solution.py:314
  23.1 0.2 collective-permute-start.1
  23.3 0.9 %mix.2.mine_ref = f32[56,2048]{1,0:T(8,128)S(1)} custom-call(s32[1]{0:T(128)} %bitcast.core_ref, bf16[16,4096]{1,0:T(8,128)(2,1)S(1)} %get-tuple-element.22.query_ref, f32[1,4096]{1,0:T(1,128)S(1)} %get-tuple-element.18.gain_ref, bf16[128,4096]{1,0:T(8,128)(2,1)S(1)} %get-tuple-element.25.raw_ref, f32[8,128]{1,0:T(8,128)S(1)} %get-tuple-element.24.rows_ref), custom_call_target="tpu_custom_call" | custom-call | flops 67108864 | bytes 2097152 | tf_op jit(solution)/shard_map/mix/pallas_call | solution.py:382
  24.2 0.1 collective-permute-done.1.rows_ref
  24.3 0.0 collective-permute-done.raw_ref
  24.3 1.0 %mix.3 = (f32[4,128,128]{2,1,0:T(8,128)S(1)}, f32[4,128,128]{2,1,0:T(8,128)S(1)}) custom-call(s32[1]{0:T(128)} %bitcast.core_ref, bf16[16,4096]{1,0:T(8,128)(2,1)S(1)} %get-tuple-element.22.query_ref, f32[1,4096]{1,0:T(1,128)S(1)} %get-tuple-element.18.gain_ref, bf16[128,2048]{1,0:T(8,128)(2,1)S(1)} %collective-permute-done.raw_ref, ...), custom_call_target="tpu_custom_call" | custom-call | flops 67108864 | bytes 2097152 | tf_op jit(solution)/shard_map/mix/pallas_call | solution.py:382
  25.3 1.9 %all-to-all-done.1.sums_ref = f32[16,1,128]{2,1,0:T(1,128)S(1)} async-done(((f32[16,1,128]{2,1,0:T(1,128)}), f32[16,1,128]{2,1,0:T(1,128)S(1)}, u32[]{:S(2)}, u32[]{:S(2)}) %all-to-all-start.1) | async-done | bytes 8224 | tf_op jit(solution)/shard_map/all_to_all | solution.py:314
  27.2 0.8 %partial.1 = (bf16[128,512]{1,0:T(8,128)(2,1)}, f32[1,128]{1,0:T(1,128)S(1)}) custom-call(f32[16,1,128]{2,1,0:T(1,128)S(1)} %all-to-all-done.1.sums_ref, f32[4,128,128]{2,1,0:T(8,128)S(1)} %get-tuple-element.26.scaled_ref, f32[4,128,128]{2,1,0:T(8,128)S(1)} %get-tuple-element.27.plain_ref), custom_call_target="tpu_custom_call" | custom-call | tf_op jit(solution)/shard_map/partial/pallas_call | solution.py:397
  28.0 4.1 %all-to-all-start.2 = ((bf16[16,8,512]{2,1,0:T(8,128)(2,1)}), bf16[16,8,512]{2,1,0:T(8,128)(2,1)S(1)}, u32[]{:S(2)}, u32[]{:S(2)}) async-start(bf16[16,8,512]{2,1,0:T(8,128)(2,1)} %bitcast.3), calls=%async_computation.2 | async-start | bytes 262144 | tf_op jit(solution)/shard_map/all_to_all | solution.py:314
  32.2 4.1 %d_passages.1 = f32[512,4096]{1,0:T(8,128)} custom-call(f32[1,128]{1,0:T(1,128)S(1)} %get-tuple-element.28.total_ref, bf16[16,4096]{1,0:T(8,128)(2,1)S(1)} %get-tuple-element.22.query_ref, f32[1,4096]{1,0:T(1,128)S(1)} %get-tuple-element.18.gain_ref, bf16[128,4096]{1,0:T(8,128)(2,1)S(1)} %get-tuple-element.25.raw_ref, ...), custom_call_target="tpu_custom_call" | custom-call | flops 1073741824 | bytes 8388608 | tf_op jit(solution)/shard_map/d_passages/pallas_call | solution.py:405
  36.2 1.4 %all-to-all-done.2.got_ref = bf16[16,8,512]{2,1,0:T(8,128)(2,1)S(1)} async-done(((bf16[16,8,512]{2,1,0:T(8,128)(2,1)}), bf16[16,8,512]{2,1,0:T(8,128)(2,1)S(1)}, u32[]{:S(2)}, u32[]{:S(2)}) %all-to-all-start.2) | async-done | bytes 131104 | tf_op jit(solution)/shard_map/all_to_all | solution.py:314
  37.6 0.0 copy-done.1
  37.6 0.0 copy-done.2
  37.6 0.9 %final.1 = (f32[1,4096]{1,0:T(1,128)}, f32[1,4096]{1,0:T(1,128)}) custom-call(bf16[16,8,512]{2,1,0:T(8,128)(2,1)S(1)} %all-to-all-done.2.got_ref, bf16[1,4096]{1,0:T(2,128)(2,1)S(1)} %copy-done.2, f32[1,4096]{1,0:T(1,128)S(1)} %bitcast.7), custom_call_target="tpu_custom_call" | custom-call | tf_op jit(solution)/shard_map/final/pallas_call | solution.py:418
Async XLA Ops:
  2.3 13.4 %all-to-all-start = ((bf16[16,8,640]{2,1,0:T(8,128)(2,1)}), bf16[16,8,640]{2,1,0:T(8,128)(2,1)S(1)}, u32[]{:S(2)}, u32[]{:S(2)}) async-start(bf16[16,8,640]{2,1,0:T(8,128)(2,1)} %pack.1), calls=%async_computation | async-start | bytes 327680 | tf_op jit(solution)/shard_map/all_to_all | solution.py:314
  9.9 0.7 %copy-start = (f32[4096]{0:T(1024)S(1)}, f32[4096]{0:T(1024)}, u32[]{:S(2)}) copy-start(f32[4096]{0:T(1024)} %param.7) | copy-start | bytes 49156
  18.5 19.1 %copy-start.1 = (f32[4096]{0:T(1024)S(1)}, f32[4096]{0:T(1024)}, u32[]{:S(2)}) copy-start(f32[4096]{0:T(1024)} %param.7) | copy-start | bytes 49156
  18.5 19.1 %copy-start.2 = (bf16[1,4096]{1,0:T(2,128)(2,1)S(1)}, bf16[1,4096]{1,0:T(2,128)(2,1)}, u32[]{:S(2)}) copy-start(bf16[1,4096]{1,0:T(2,128)(2,1)} %queries_ref.3) | copy-start | bytes 24580
  18.5 5.8 %collective-permute-start = (bf16[128,2048]{1,0:T(8,128)(2,1)}, bf16[128,2048]{1,0:T(8,128)(2,1)S(1)}, u32[]{:S(2)}, u32[]{:S(2)}) collective-permute-start(bf16[128,2048]{1,0:T(8,128)(2,1)} %get-tuple-element.23), channel_id=1, source_target_pairs={{0,1},{1,0},{2,3},{3,2},{4,5},{5,4},{6,7},{7,6},{8,9},{9,8},{10,11... | collective-permute-start | bytes 1572872 | tf_op jit(solution)/shard_map/ppermute | solution.py:378
  18.6 8.6 %all-to-all-start.1 = ((f32[16,1,128]{2,1,0:T(1,128)}), f32[16,1,128]{2,1,0:T(1,128)S(1)}, u32[]{:S(2)}, u32[]{:S(2)}) async-start(f32[16,1,128]{2,1,0:T(1,128)} %get-tuple-element.21), calls=%async_computation.1 | async-start | bytes 16384 | tf_op jit(solution)/shard_map/all_to_all | solution.py:314
  23.1 1.2 %collective-permute-start.1 = (f32[8,128]{1,0:T(8,128)S(1)}, f32[8,128]{1,0:T(8,128)S(1)}, u32[]{:S(2)}, u32[]{:S(2)}) collective-permute-start(f32[8,128]{1,0:T(8,128)S(1)} %get-tuple-element.24.rows_ref), channel_id=1, source_target_pairs={{0,1},{1,0},{2,3},{3,2},{4,5},{5,4},{6,7},{7,6},{8,9},{9,8},{10,11... | collective-permute-start | bytes 12296 | tf_op jit(solution)/shard_map/ppermute | solution.py:379
  28.0 9.6 %all-to-all-start.2 = ((bf16[16,8,512]{2,1,0:T(8,128)(2,1)}), bf16[16,8,512]{2,1,0:T(8,128)(2,1)S(1)}, u32[]{:S(2)}, u32[]{:S(2)}) async-start(bf16[16,8,512]{2,1,0:T(8,128)(2,1)} %bitcast.3), calls=%async_computation.2 | async-start | bytes 262144 | tf_op jit(solution)/shard_map/all_to_all | solution.py:314

commit v23 on v21

--- a/solution.py
+++ b/solution.py
@@ -153,7 +153,13 @@
         out_ref[:, part] = sums if before_ref is None else sums + before_ref[:, part]
 
 
-def mine_kernel(core_ref, query_ref, gain_ref, raw_ref, rows_ref, out_ref):
+def mine_kernel(core_ref, got_ref, gain_ref, raw_ref, rows_ref, out_ref, query_ref, wide):
+    queries = query_ref.shape[0]
+    tiles = wide.shape[0]
+    for j in range(tiles):
+        wide[j] = got_ref[:, j * 128 : (j + 1) * 128].astype(f32)
+    query = [wide[j, pl.ds(k, queries, stride=8), :] for k in range(8) for j in range(tiles)]
+    query_ref[...] = jnp.concatenate(query, axis=1).astype(bf16)
     base = core_ref[0] * out_ref.shape[1]
     mix(base, base, query_ref, gain_ref, raw_ref, rows_ref[...], out_ref, None)
 
@@ -165,10 +171,10 @@
 
 def score_kernel(
     core_ref, got_ref, gain_ref, near_ref, far_ref,
-    raw_ref, query_ref, cols_ref, rows_ref, sums_ref, theirs_ref, held, wide, sems,
+    raw_ref, cols_ref, rows_ref, sums_ref, theirs_ref, held, wide, sems,
 ):
-    queries, width = query_ref.shape
-    pairs = queries * 8
+    pairs, width = raw_ref.shape
+    queries = pairs // 8
     rows = held.shape[1]
     chunk = width // chunks
     half = chunks // 2
@@ -184,9 +190,6 @@
     query_inverse = 1.0 / jnp.sqrt(squares.reshape(pairs, 1))
     for j in range(tiles):
         wide[j] = loaded[j]
-    query = [wide[j, pl.ds(k, queries, stride=8), :] for k in range(8) for j in range(tiles)]
-    query = jnp.concatenate(query, axis=1).astype(bf16)
-    query_ref[...] = query
     lists = loaded[-1]
     inside = lists[:, 0:1] * 256.0 + lists[:, 1:2]
     mark = lists[:, 2:3] + lists[:, 3:4]
@@ -344,12 +347,11 @@
     )(passages, gain)
     half = width // 2
     core = (lax.axis_index("hash") % 2).astype(jnp.int32).reshape(1)
-    raw, query, cols, lines, sums, theirs = pl.pallas_call(
+    raw, cols, lines, sums, theirs = pl.pallas_call(
         score_kernel,
         in_specs=[pl.BlockSpec(memory_space=pltpu.SMEM), whole(), whole(), whole(), outside()],
         out_shape=[
             shape((pairs, width), bf16),
-            shape((count, width), bf16),
             shape((pairs, 128)),
             shape((8, pairs)),
             shape((count, 1, pairs)),
@@ -369,20 +371,25 @@
     sibling_raw = lax.ppermute(theirs, "hash", swap)
     sibling_lines = lax.ppermute(lines, "hash", swap)
 
-    def mixed(kernel, *operands):
+    def mixed(kernel, out_shape, scratch, *operands):
         return pl.pallas_call(
             kernel,
-            in_specs=[pl.BlockSpec(memory_space=pltpu.SMEM)] + [whole()] * (len(operands) + 2),
-            out_shape=shape((3 * count + 8, half)),
+            in_specs=[pl.BlockSpec(memory_space=pltpu.SMEM)] + [whole()] * len(operands),
+            out_shape=out_shape,
+            scratch_shapes=scratch,
             compiler_params=params(48),
             name="mix",
             cost_estimate=pl.CostEstimate(
                 flops=8 * count * pairs * width, bytes_accessed=4 * pairs * width, transcendentals=0
             ),
-        )(core, query, gain_near, *operands)
-
-    mine = mixed(mine_kernel, raw, lines)
-    both = mixed(both_kernel, sibling_raw, sibling_lines, mine)
+        )(core, *operands)
+
+    wide = [pltpu.VMEM((width // 1024, pairs, 128), f32)]
+    added = shape((3 * count + 8, half))
+    mine, query = mixed(
+        mine_kernel, [added, shape((count, width), bf16)], wide, got, gain_near, raw, lines
+    )
+    both = mixed(both_kernel, added, [], query, gain_near, sibling_raw, sibling_lines, mine)
 
     partial, total = pl.pallas_call(
         partial_kernel,

time: 39.1 us -> 39.1 us (level)
  transfers between devices with their start and end apart: 5 -> 5, of which waited for: 4 -> 3; matrix products, arithmetic and copies ran while one was open for 0% -> 0% of each run, Pallas kernels for 23% -> 23%
where the time goes in v23:
time: 39.1 us; the launch traced here: 38.6 us
  starting transfers between devices  16.4 us (42%)
  Pallas kernels  15 us (38%)
  waiting for transfers between devices  5.74 us (15%)
  local copies, waits for them, and re-layouts  0.72 us (2%)
  between operations  0.71 us (2%)
    all_to_all x3, starting transfers between devices, exchange(): lax.all_to_all(x, 'hash', split_axis=0, concat_axis=0, axis_index_groups=...  16.2 us
    all_to_all x3, waiting for transfers between devices, exchange(): lax.all_to_all(x, 'hash', split_axis=0, concat_axis=0, axis_index_groups=...  5.72 us
    pallas_call x1, Pallas kernels, local(): pl.pallas_call(passage_kernel, in_specs=[whole()] * 6, out_specs=outside(...  4.06 us
    pallas_call x1, Pallas kernels, local(): pl.pallas_call(stage_kernel, in_specs=[outside(), whole()], out_specs=[wh...  2.8 us
    pallas_call x1, Pallas kernels, local(): pl.pallas_call(score_kernel, in_specs=[pl.BlockSpec(memory_space=pltpu.SM...  2.78 us
    pallas_call x2, Pallas kernels, mixed(): pl.pallas_call(kernel, in_specs=[pl.BlockSpec(memory_space=pltpu.SMEM)] +...  1.91 us
    pallas_call x1, Pallas kernels, local(): pl.pallas_call(functools.partial(pack_kernel, rows), out_shape=shape((cou...  1.72 us
    pallas_call x1, Pallas kernels, local(): pl.pallas_call(final_kernel, out_shape=[shape((1, width)), shape((1, widt...  0.87 us
  transfers between devices with their start and end apart: 5, of which 3 were waited for; matrix products, arithmetic and copies ran while one was open for 0% of the time, Pallas kernels for 23%

profile of v23, /device:TPU:0, one launch (start us, length us, event | category | flops | bytes accessed | tf_op | source)
XLA Modules:
  0.0 38.6 jit_solution(5927526638426815848)
XLA Ops:
  0.6 1.7 %pack.1 = bf16[16,8,640]{2,1,0:T(8,128)(2,1)} custom-call(bf16[1,4096]{1,0:T(2,128)(2,1)} %queries_ref.3, s32[1,128]{1,0:T(1,128)} %candidates_ref.1, s32[1,128]{1,0:T(1,128)} %teacher_ref.1), custom_call_target="tpu_custom_call" | custom-call | tf_op jit(solution)/shard_map/pack/pallas_call | solution.py:319
  2.4 7.5 %all-to-all-start = ((bf16[16,8,640]{2,1,0:T(8,128)(2,1)}), bf16[16,8,640]{2,1,0:T(8,128)(2,1)S(1)}, u32[]{:S(2)}, u32[]{:S(2)}) async-start(bf16[16,8,640]{2,1,0:T(8,128)(2,1)} %pack.1), calls=%async_computation | async-start | bytes 327680 | tf_op jit(solution)/shard_map/all_to_all | solution.py:308
  9.9 0.0 copy-start
  9.9 0.7 %copy-done = f32[4096]{0:T(1024)S(1)} copy-done((f32[4096]{0:T(1024)S(1)}, f32[4096]{0:T(1024)}, u32[]{:S(2)}) %copy-start) | copy-done | bytes 16408
  10.6 2.8 %stage.1 = (bf16[512,2048]{1,0:T(8,128)(2,1)S(1)}, bf16[10240,1024]{1,0:T(8,128)(2,1)}, f32[1,4096]{1,0:T(1,128)S(1)}) custom-call(bf16[512,4096]{1,0:T(8,128)(2,1)} %passages_ref.1, f32[1,4096]{1,0:T(1,128)S(1)} %bitcast.7), custom_call_target="tpu_custom_call" | custom-call | bytes 8388608 | tf_op jit(solution)/shard_map/stage/pallas_call | solution.py:328
  13.4 2.4 %all-to-all-done = bf16[16,8,640]{2,1,0:T(8,128)(2,1)S(1)} async-done(((bf16[16,8,640]{2,1,0:T(8,128)(2,1)}), bf16[16,8,640]{2,1,0:T(8,128)(2,1)S(1)}, u32[]{:S(2)}, u32[]{:S(2)}) %all-to-all-start) | async-done | bytes 163872 | tf_op jit(solution)/shard_map/all_to_all | solution.py:308
  15.8 2.8 %score.1 = (bf16[128,4096]{1,0:T(8,128)(2,1)S(1)}, f32[128,128]{1,0:T(8,128)S(1)}, f32[8,128]{1,0:T(8,128)S(1)}, f32[16,1,128]{2,1,0:T(1,128)}, bf16[128,2048]{1,0:T(8,128)(2,1)}) custom-call(s32[1]{0:T(128)} %bitcast.core_ref, bf16[128,640]{1,0:T(8,128)(2,1)S(1)} %bitcast.5, f32[1,4096]{1,0:T(1,128)S(1)} %get-tuple-element.17.gain_ref, ...), custom_call_target="tpu_custom_call" | custom-call | tf_op jit(solution)/shard_map/score/pallas_call | solution.py:350
  18.6 0.0 copy-start.1
  18.6 0.0 copy-start.2
  18.6 0.1 collective-permute-start
  18.7 4.5 %all-to-all-start.1 = ((f32[16,1,128]{2,1,0:T(1,128)}), f32[16,1,128]{2,1,0:T(1,128)S(1)}, u32[]{:S(2)}, u32[]{:S(2)}) async-start(f32[16,1,128]{2,1,0:T(1,128)} %get-tuple-element.20), calls=%async_computation.1 | async-start | bytes 16384 | tf_op jit(solution)/shard_map/all_to_all | solution.py:308
  23.2 0.2 collective-permute-start.1
  23.4 1.0 %mix.2 = (f32[56,2048]{1,0:T(8,128)S(1)}, bf16[16,4096]{1,0:T(8,128)(2,1)S(1)}) custom-call(s32[1]{0:T(128)} %bitcast.core_ref, bf16[128,640]{1,0:T(8,128)(2,1)S(1)} %bitcast.6, f32[1,4096]{1,0:T(1,128)S(1)} %get-tuple-element.17.gain_ref, bf16[128,4096]{1,0:T(8,128)(2,1)S(1)} %get-tuple-element.21.raw_ref, f32[8,128]{1,0:T(8,128)S(1)} %get-tuple-element.22.rows_ref), custom_call_target="tpu_custom_call" | custom-call | flops 67108864 | bytes 2097152 | tf_op jit(solution)/shard_map/mix/pallas_call | solution.py:375
  24.3 0.0 collective-permute-done.1.rows_ref
  24.4 0.0 collective-permute-done.raw_ref
  24.4 0.9 %mix.3.both_ref = f32[56,2048]{1,0:T(8,128)S(1)} custom-call(s32[1]{0:T(128)} %bitcast.core_ref, bf16[16,4096]{1,0:T(8,128)(2,1)S(1)} %get-tuple-element.23.query_ref, f32[1,4096]{1,0:T(1,128)S(1)} %get-tuple-element.17.gain_ref, bf16[128,2048]{1,0:T(8,128)(2,1)S(1)} %collective-permute-done.raw_ref, f32[8,128]{1,0:T(8,128)S(1)} %collective-permute-done.1.rows_ref, ...), custom_call_target="tpu_custom_call" | custom-call | flops 67108864 | bytes 2097152 | tf_op jit(solution)/shard_map/mix/pallas_call | solution.py:375
  25.3 2.0 %all-to-all-done.1.sums_ref = f32[16,1,128]{2,1,0:T(1,128)S(1)} async-done(((f32[16,1,128]{2,1,0:T(1,128)}), f32[16,1,128]{2,1,0:T(1,128)S(1)}, u32[]{:S(2)}, u32[]{:S(2)}) %all-to-all-start.1) | async-done | bytes 8224 | tf_op jit(solution)/shard_map/all_to_all | solution.py:308
  27.3 0.9 %partial.1 = (bf16[128,512]{1,0:T(8,128)(2,1)}, f32[1,128]{1,0:T(1,128)S(1)}) custom-call(f32[16,1,128]{2,1,0:T(1,128)S(1)} %all-to-all-done.1.sums_ref, f32[56,2048]{1,0:T(8,128)S(1)} %mix.3.both_ref), custom_call_target="tpu_custom_call" | custom-call | tf_op jit(solution)/shard_map/partial/pallas_call | solution.py:394
  28.1 4.1 %all-to-all-start.2 = ((bf16[16,8,512]{2,1,0:T(8,128)(2,1)}), bf16[16,8,512]{2,1,0:T(8,128)(2,1)S(1)}, u32[]{:S(2)}, u32[]{:S(2)}) async-start(bf16[16,8,512]{2,1,0:T(8,128)(2,1)} %bitcast.3), calls=%async_computation.2 | async-start | bytes 262144 | tf_op jit(solution)/shard_map/all_to_all | solution.py:308
  32.3 4.1 %d_passages.1 = f32[512,4096]{1,0:T(8,128)} custom-call(f32[1,128]{1,0:T(1,128)S(1)} %get-tuple-element.26.total_ref, bf16[16,4096]{1,0:T(8,128)(2,1)S(1)} %get-tuple-element.23.query_ref, f32[1,4096]{1,0:T(1,128)S(1)} %get-tuple-element.17.gain_ref, bf16[128,4096]{1,0:T(8,128)(2,1)S(1)} %get-tuple-element.21.raw_ref, ...), custom_call_target="tpu_custom_call" | custom-call | flops 1073741824 | bytes 8388608 | tf_op jit(solution)/shard_map/d_passages/pallas_call | solution.py:403
  36.3 1.4 %all-to-all-done.2.got_ref = bf16[16,8,512]{2,1,0:T(8,128)(2,1)S(1)} async-done(((bf16[16,8,512]{2,1,0:T(8,128)(2,1)}), bf16[16,8,512]{2,1,0:T(8,128)(2,1)S(1)}, u32[]{:S(2)}, u32[]{:S(2)}) %all-to-all-start.2) | async-done | bytes 131104 | tf_op jit(solution)/shard_map/all_to_all | solution.py:308
  37.7 0.0 copy-done.1
  37.7 0.0 copy-done.2
  37.7 0.9 %final.1 = (f32[1,4096]{1,0:T(1,128)}, f32[1,4096]{1,0:T(1,128)}) custom-call(bf16[16,8,512]{2,1,0:T(8,128)(2,1)S(1)} %all-to-all-done.2.got_ref, bf16[1,4096]{1,0:T(2,128)(2,1)S(1)} %copy-done.2, f32[1,4096]{1,0:T(1,128)S(1)} %bitcast.8), custom_call_target="tpu_custom_call" | custom-call | tf_op jit(solution)/shard_map/final/pallas_call | solution.py:416
Async XLA Ops:
  2.4 13.4 %all-to-all-start = ((bf16[16,8,640]{2,1,0:T(8,128)(2,1)}), bf16[16,8,640]{2,1,0:T(8,128)(2,1)S(1)}, u32[]{:S(2)}, u32[]{:S(2)}) async-start(bf16[16,8,640]{2,1,0:T(8,128)(2,1)} %pack.1), calls=%async_computation | async-start | bytes 327680 | tf_op jit(solution)/shard_map/all_to_all | solution.py:308
  9.9 0.7 %copy-start = (f32[4096]{0:T(1024)S(1)}, f32[4096]{0:T(1024)}, u32[]{:S(2)}) copy-start(f32[4096]{0:T(1024)} %param.7) | copy-start | bytes 49156
  18.6 19.2 %copy-start.1 = (f32[4096]{0:T(1024)S(1)}, f32[4096]{0:T(1024)}, u32[]{:S(2)}) copy-start(f32[4096]{0:T(1024)} %param.7) | copy-start | bytes 49156
  18.6 19.2 %copy-start.2 = (bf16[1,4096]{1,0:T(2,128)(2,1)S(1)}, bf16[1,4096]{1,0:T(2,128)(2,1)}, u32[]{:S(2)}) copy-start(bf16[1,4096]{1,0:T(2,128)(2,1)} %queries_ref.3) | copy-start | bytes 24580
  18.6 5.8 %collective-permute-start = (bf16[128,2048]{1,0:T(8,128)(2,1)}, bf16[128,2048]{1,0:T(8,128)(2,1)S(1)}, u32[]{:S(2)}, u32[]{:S(2)}) collective-permute-start(bf16[128,2048]{1,0:T(8,128)(2,1)} %get-tuple-element.24), channel_id=1, source_target_pairs={{0,1},{1,0},{2,3},{3,2},{4,5},{5,4},{6,7},{7,6},{8,9},{9,8},{10,11... | collective-permute-start | bytes 1572872 | tf_op jit(solution)/shard_map/ppermute | solution.py:371
  18.7 8.6 %all-to-all-start.1 = ((f32[16,1,128]{2,1,0:T(1,128)}), f32[16,1,128]{2,1,0:T(1,128)S(1)}, u32[]{:S(2)}, u32[]{:S(2)}) async-start(f32[16,1,128]{2,1,0:T(1,128)} %get-tuple-element.20), calls=%async_computation.1 | async-start | bytes 16384 | tf_op jit(solution)/shard_map/all_to_all | solution.py:308
  23.2 1.2 %collective-permute-start.1 = (f32[8,128]{1,0:T(8,128)S(1)}, f32[8,128]{1,0:T(8,128)S(1)}, u32[]{:S(2)}, u32[]{:S(2)}) collective-permute-start(f32[8,128]{1,0:T(8,128)S(1)} %get-tuple-element.22.rows_ref), channel_id=1, source_target_pairs={{0,1},{1,0},{2,3},{3,2},{4,5},{5,4},{6,7},{7,6},{8,9},{9,8},{10,11... | collective-permute-start | bytes 12296 | tf_op jit(solution)/shard_map/ppermute | solution.py:372
  28.1 9.6 %all-to-all-start.2 = ((bf16[16,8,512]{2,1,0:T(8,128)(2,1)}), bf16[16,8,512]{2,1,0:T(8,128)(2,1)S(1)}, u32[]{:S(2)}, u32[]{:S(2)}) async-start(bf16[16,8,512]{2,1,0:T(8,128)(2,1)} %bitcast.3), calls=%async_computation.2 | async-start | bytes 262144 | tf_op jit(solution)/shard_map/all_to_all | solution.py:308

commit v24 on v23

--- a/solution.py
+++ b/solution.py
@@ -157,7 +157,7 @@
     queries = query_ref.shape[0]
     tiles = wide.shape[0]
     for j in range(tiles):
-        wide[j] = got_ref[:, j * 128 : (j + 1) * 128].astype(f32)
+        wide[j, : 8 * queries, :] = got_ref[:, j * 128 : (j + 1) * 128].astype(f32)
     query = [wide[j, pl.ds(k, queries, stride=8), :] for k in range(8) for j in range(tiles)]
     query_ref[...] = jnp.concatenate(query, axis=1).astype(bf16)
     base = core_ref[0] * out_ref.shape[1]
@@ -189,7 +189,7 @@
     squares = jnp.broadcast_to(jnp.sum(squares, axis=1, keepdims=True), (queries, 8, 1))
     query_inverse = 1.0 / jnp.sqrt(squares.reshape(pairs, 1))
     for j in range(tiles):
-        wide[j] = loaded[j]
+        wide[j, :pairs, :] = loaded[j]
     lists = loaded[-1]
     inside = lists[:, 0:1] * 256.0 + lists[:, 1:2]
     mark = lists[:, 2:3] + lists[:, 3:4]
@@ -250,7 +250,7 @@
             gain_part[:, part], (queries, 128)
         )
     for tile in range(tiles):
-        out_ref[:, tile * 128 : (tile + 1) * 128] = laid[tile].astype(bf16)
+        out_ref[:, tile * 128 : (tile + 1) * 128] = laid[tile, : 8 * queries, :].astype(bf16)
 
 
 def passage_kernel(total_ref, query_ref, gain_ref, raw_ref, cols_ref, rows_ref, out_ref, made, sems):
@@ -359,7 +359,7 @@
         ],
         scratch_shapes=[
             pltpu.VMEM((chunks // 2, rows, width // chunks), bf16),
-            pltpu.VMEM((width // 1024, pairs, 128), f32),
+            pltpu.VMEM((width // 1024, pairs + 8, 128), f32),
             pltpu.SemaphoreType.DMA((chunks // 2,)),
         ],
         compiler_params=params(48),
@@ -384,7 +384,7 @@
             ),
         )(core, *operands)
 
-    wide = [pltpu.VMEM((width // 1024, pairs, 128), f32)]
+    wide = [pltpu.VMEM((width // 1024, pairs + 8, 128), f32)]
     added = shape((3 * count + 8, half))
     mine, query = mixed(
         mine_kernel, [added, shape((count, width), bf16)], wide, got, gain_near, raw, lines
@@ -394,7 +394,7 @@
     partial, total = pl.pallas_call(
         partial_kernel,
         out_shape=[shape((pairs, half // 4), bf16), shape((1, pairs))],
-        scratch_shapes=[pltpu.VMEM((half // 512, pairs, 128), f32)],
+        scratch_shapes=[pltpu.VMEM((half // 512, pairs + 8, 128), f32)],
         compiler_params=params(48),
         name="partial",
     )(got_sums, both)

time: 39.1 us -> 39.1 us (level)
  no operation moved by 1% of the time
where the time goes in v24:
time: 39.1 us; the launch traced here: 38.6 us
  starting transfers between devices  16.4 us (42%)
  Pallas kernels  15 us (38%)
  waiting for transfers between devices  5.74 us (15%)
  local copies, waits for them, and re-layouts  0.72 us (2%)
  between operations  0.71 us (2%)
    all_to_all x3, starting transfers between devices, exchange(): lax.all_to_all(x, 'hash', split_axis=0, concat_axis=0, axis_index_groups=...  16.2 us
    all_to_all x3, waiting for transfers between devices, exchange(): lax.all_to_all(x, 'hash', split_axis=0, concat_axis=0, axis_index_groups=...  5.72 us
    pallas_call x1, Pallas kernels, local(): pl.pallas_call(passage_kernel, in_specs=[whole()] * 6, out_specs=outside(...  4.06 us
    pallas_call x1, Pallas kernels, local(): pl.pallas_call(stage_kernel, in_specs=[outside(), whole()], out_specs=[wh...  2.8 us
    pallas_call x1, Pallas kernels, local(): pl.pallas_call(score_kernel, in_specs=[pl.BlockSpec(memory_space=pltpu.SM...  2.78 us
    pallas_call x2, Pallas kernels, mixed(): pl.pallas_call(kernel, in_specs=[pl.BlockSpec(memory_space=pltpu.SMEM)] +...  1.91 us
    pallas_call x1, Pallas kernels, local(): pl.pallas_call(functools.partial(pack_kernel, rows), out_shape=shape((cou...  1.72 us
    pallas_call x1, Pallas kernels, local(): pl.pallas_call(final_kernel, out_shape=[shape((1, width)), shape((1, widt...  0.87 us
  transfers between devices with their start and end apart: 5, of which 3 were waited for; matrix products, arithmetic and copies ran while one was open for 0% of the time, Pallas kernels for 23%

profile of v24, /device:TPU:0, one launch (start us, length us, event | category | flops | bytes accessed | tf_op | source)
XLA Modules:
  0.0 38.6 jit_solution(11886841583294272588)
XLA Ops:
  0.6 1.7 %pack.1 = bf16[16,8,640]{2,1,0:T(8,128)(2,1)} custom-call(bf16[1,4096]{1,0:T(2,128)(2,1)} %queries_ref.3, s32[1,128]{1,0:T(1,128)} %candidates_ref.1, s32[1,128]{1,0:T(1,128)} %teacher_ref.1), custom_call_target="tpu_custom_call" | custom-call | tf_op jit(solution)/shard_map/pack/pallas_call | solution.py:319
  2.4 7.5 %all-to-all-start = ((bf16[16,8,640]{2,1,0:T(8,128)(2,1)}), bf16[16,8,640]{2,1,0:T(8,128)(2,1)S(1)}, u32[]{:S(2)}, u32[]{:S(2)}) async-start(bf16[16,8,640]{2,1,0:T(8,128)(2,1)} %pack.1), calls=%async_computation | async-start | bytes 327680 | tf_op jit(solution)/shard_map/all_to_all | solution.py:308
  9.9 0.0 copy-start
  9.9 0.7 %copy-done = f32[4096]{0:T(1024)S(1)} copy-done((f32[4096]{0:T(1024)S(1)}, f32[4096]{0:T(1024)}, u32[]{:S(2)}) %copy-start) | copy-done | bytes 16408
  10.6 2.8 %stage.1 = (bf16[512,2048]{1,0:T(8,128)(2,1)S(1)}, bf16[10240,1024]{1,0:T(8,128)(2,1)}, f32[1,4096]{1,0:T(1,128)S(1)}) custom-call(bf16[512,4096]{1,0:T(8,128)(2,1)} %passages_ref.1, f32[1,4096]{1,0:T(1,128)S(1)} %bitcast.7), custom_call_target="tpu_custom_call" | custom-call | bytes 8388608 | tf_op jit(solution)/shard_map/stage/pallas_call | solution.py:328
  13.4 2.4 %all-to-all-done = bf16[16,8,640]{2,1,0:T(8,128)(2,1)S(1)} async-done(((bf16[16,8,640]{2,1,0:T(8,128)(2,1)}), bf16[16,8,640]{2,1,0:T(8,128)(2,1)S(1)}, u32[]{:S(2)}, u32[]{:S(2)}) %all-to-all-start) | async-done | bytes 163872 | tf_op jit(solution)/shard_map/all_to_all | solution.py:308
  15.8 2.8 %score.1 = (bf16[128,4096]{1,0:T(8,128)(2,1)S(1)}, f32[128,128]{1,0:T(8,128)S(1)}, f32[8,128]{1,0:T(8,128)S(1)}, f32[16,1,128]{2,1,0:T(1,128)}, bf16[128,2048]{1,0:T(8,128)(2,1)}) custom-call(s32[1]{0:T(128)} %bitcast.core_ref, bf16[128,640]{1,0:T(8,128)(2,1)S(1)} %bitcast.5, f32[1,4096]{1,0:T(1,128)S(1)} %get-tuple-element.17.gain_ref, ...), custom_call_target="tpu_custom_call" | custom-call | tf_op jit(solution)/shard_map/score/pallas_call | solution.py:350
  18.6 0.0 copy-start.1
  18.6 0.0 copy-start.2
  18.6 0.1 collective-permute-start
  18.7 4.5 %all-to-all-start.1 = ((f32[16,1,128]{2,1,0:T(1,128)}), f32[16,1,128]{2,1,0:T(1,128)S(1)}, u32[]{:S(2)}, u32[]{:S(2)}) async-start(f32[16,1,128]{2,1,0:T(1,128)} %get-tuple-element.20), calls=%async_computation.1 | async-start | bytes 16384 | tf_op jit(solution)/shard_map/all_to_all | solution.py:308
  23.2 0.2 collective-permute-start.1
  23.4 1.0 %mix.2 = (f32[56,2048]{1,0:T(8,128)S(1)}, bf16[16,4096]{1,0:T(8,128)(2,1)S(1)}) custom-call(s32[1]{0:T(128)} %bitcast.core_ref, bf16[128,640]{1,0:T(8,128)(2,1)S(1)} %bitcast.6, f32[1,4096]{1,0:T(1,128)S(1)} %get-tuple-element.17.gain_ref, bf16[128,4096]{1,0:T(8,128)(2,1)S(1)} %get-tuple-element.21.raw_ref, f32[8,128]{1,0:T(8,128)S(1)} %get-tuple-element.22.rows_ref), custom_call_target="tpu_custom_call" | custom-call | flops 67108864 | bytes 2097152 | tf_op jit(solution)/shard_map/mix/pallas_call | solution.py:375
  24.3 0.0 collective-permute-done.1.rows_ref
  24.4 0.0 collective-permute-done.raw_ref
  24.4 0.9 %mix.3.both_ref = f32[56,2048]{1,0:T(8,128)S(1)} custom-call(s32[1]{0:T(128)} %bitcast.core_ref, bf16[16,4096]{1,0:T(8,128)(2,1)S(1)} %get-tuple-element.23.query_ref, f32[1,4096]{1,0:T(1,128)S(1)} %get-tuple-element.17.gain_ref, bf16[128,2048]{1,0:T(8,128)(2,1)S(1)} %collective-permute-done.raw_ref, f32[8,128]{1,0:T(8,128)S(1)} %collective-permute-done.1.rows_ref, ...), custom_call_target="tpu_custom_call" | custom-call | flops 67108864 | bytes 2097152 | tf_op jit(solution)/shard_map/mix/pallas_call | solution.py:375
  25.3 2.0 %all-to-all-done.1.sums_ref = f32[16,1,128]{2,1,0:T(1,128)S(1)} async-done(((f32[16,1,128]{2,1,0:T(1,128)}), f32[16,1,128]{2,1,0:T(1,128)S(1)}, u32[]{:S(2)}, u32[]{:S(2)}) %all-to-all-start.1) | async-done | bytes 8224 | tf_op jit(solution)/shard_map/all_to_all | solution.py:308
  27.3 0.9 %partial.1 = (bf16[128,512]{1,0:T(8,128)(2,1)}, f32[1,128]{1,0:T(1,128)S(1)}) custom-call(f32[16,1,128]{2,1,0:T(1,128)S(1)} %all-to-all-done.1.sums_ref, f32[56,2048]{1,0:T(8,128)S(1)} %mix.3.both_ref), custom_call_target="tpu_custom_call" | custom-call | tf_op jit(solution)/shard_map/partial/pallas_call | solution.py:394
  28.1 4.1 %all-to-all-start.2 = ((bf16[16,8,512]{2,1,0:T(8,128)(2,1)}), bf16[16,8,512]{2,1,0:T(8,128)(2,1)S(1)}, u32[]{:S(2)}, u32[]{:S(2)}) async-start(bf16[16,8,512]{2,1,0:T(8,128)(2,1)} %bitcast.3), calls=%async_computation.2 | async-start | bytes 262144 | tf_op jit(solution)/shard_map/all_to_all | solution.py:308
  32.3 4.1 %d_passages.1 = f32[512,4096]{1,0:T(8,128)} custom-call(f32[1,128]{1,0:T(1,128)S(1)} %get-tuple-element.26.total_ref, bf16[16,4096]{1,0:T(8,128)(2,1)S(1)} %get-tuple-element.23.query_ref, f32[1,4096]{1,0:T(1,128)S(1)} %get-tuple-element.17.gain_ref, bf16[128,4096]{1,0:T(8,128)(2,1)S(1)} %get-tuple-element.21.raw_ref, ...), custom_call_target="tpu_custom_call" | custom-call | flops 1073741824 | bytes 8388608 | tf_op jit(solution)/shard_map/d_passages/pallas_call | solution.py:403
  36.3 1.4 %all-to-all-done.2.got_ref = bf16[16,8,512]{2,1,0:T(8,128)(2,1)S(1)} async-done(((bf16[16,8,512]{2,1,0:T(8,128)(2,1)}), bf16[16,8,512]{2,1,0:T(8,128)(2,1)S(1)}, u32[]{:S(2)}, u32[]{:S(2)}) %all-to-all-start.2) | async-done | bytes 131104 | tf_op jit(solution)/shard_map/all_to_all | solution.py:308
  37.7 0.0 copy-done.1
  37.7 0.0 copy-done.2
  37.7 0.9 %final.1 = (f32[1,4096]{1,0:T(1,128)}, f32[1,4096]{1,0:T(1,128)}) custom-call(bf16[16,8,512]{2,1,0:T(8,128)(2,1)S(1)} %all-to-all-done.2.got_ref, bf16[1,4096]{1,0:T(2,128)(2,1)S(1)} %copy-done.2, f32[1,4096]{1,0:T(1,128)S(1)} %bitcast.8), custom_call_target="tpu_custom_call" | custom-call | tf_op jit(solution)/shard_map/final/pallas_call | solution.py:416
Async XLA Ops:
  2.4 13.4 %all-to-all-start = ((bf16[16,8,640]{2,1,0:T(8,128)(2,1)}), bf16[16,8,640]{2,1,0:T(8,128)(2,1)S(1)}, u32[]{:S(2)}, u32[]{:S(2)}) async-start(bf16[16,8,640]{2,1,0:T(8,128)(2,1)} %pack.1), calls=%async_computation | async-start | bytes 327680 | tf_op jit(solution)/shard_map/all_to_all | solution.py:308
  9.9 0.7 %copy-start = (f32[4096]{0:T(1024)S(1)}, f32[4096]{0:T(1024)}, u32[]{:S(2)}) copy-start(f32[4096]{0:T(1024)} %param.7) | copy-start | bytes 49156
  18.6 19.2 %copy-start.1 = (f32[4096]{0:T(1024)S(1)}, f32[4096]{0:T(1024)}, u32[]{:S(2)}) copy-start(f32[4096]{0:T(1024)} %param.7) | copy-start | bytes 49156
  18.6 19.2 %copy-start.2 = (bf16[1,4096]{1,0:T(2,128)(2,1)S(1)}, bf16[1,4096]{1,0:T(2,128)(2,1)}, u32[]{:S(2)}) copy-start(bf16[1,4096]{1,0:T(2,128)(2,1)} %queries_ref.3) | copy-start | bytes 24580
  18.6 5.8 %collective-permute-start = (bf16[128,2048]{1,0:T(8,128)(2,1)}, bf16[128,2048]{1,0:T(8,128)(2,1)S(1)}, u32[]{:S(2)}, u32[]{:S(2)}) collective-permute-start(bf16[128,2048]{1,0:T(8,128)(2,1)} %get-tuple-element.24), channel_id=1, source_target_pairs={{0,1},{1,0},{2,3},{3,2},{4,5},{5,4},{6,7},{7,6},{8,9},{9,8},{10,11... | collective-permute-start | bytes 1572872 | tf_op jit(solution)/shard_map/ppermute | solution.py:371
  18.7 8.6 %all-to-all-start.1 = ((f32[16,1,128]{2,1,0:T(1,128)}), f32[16,1,128]{2,1,0:T(1,128)S(1)}, u32[]{:S(2)}, u32[]{:S(2)}) async-start(f32[16,1,128]{2,1,0:T(1,128)} %get-tuple-element.20), calls=%async_computation.1 | async-start | bytes 16384 | tf_op jit(solution)/shard_map/all_to_all | solution.py:308
  23.2 1.2 %collective-permute-start.1 = (f32[8,128]{1,0:T(8,128)S(1)}, f32[8,128]{1,0:T(8,128)S(1)}, u32[]{:S(2)}, u32[]{:S(2)}) collective-permute-start(f32[8,128]{1,0:T(8,128)S(1)} %get-tuple-element.22.rows_ref), channel_id=1, source_target_pairs={{0,1},{1,0},{2,3},{3,2},{4,5},{5,4},{6,7},{7,6},{8,9},{9,8},{10,11... | collective-permute-start | bytes 12296 | tf_op jit(solution)/shard_map/ppermute | solution.py:372
  28.1 9.6 %all-to-all-start.2 = ((bf16[16,8,512]{2,1,0:T(8,128)(2,1)}), bf16[16,8,512]{2,1,0:T(8,128)(2,1)S(1)}, u32[]{:S(2)}, u32[]{:S(2)}) async-start(bf16[16,8,512]{2,1,0:T(8,128)(2,1)} %bitcast.3), calls=%async_computation.2 | async-start | bytes 262144 | tf_op jit(solution)/shard_map/all_to_all | solution.py:308

commit v25 on v24

--- a/solution.py
+++ b/solution.py
@@ -96,12 +96,13 @@
 def stage_kernel(passages_ref, gain_ref, near_ref, far_ref, gain_out_ref, held, sems_in, sems_out):
     gain_out_ref[...] = gain_ref[...]
     rows, width = near_ref.shape
-    half = width // 2
+    rest = held.shape[1]
+    half = rest // 2
     piece = rows // chunks
     copies_in, copies_out, copies_near = [], [], []
     for k in range(chunks):
         part = pl.ds(k * piece, piece)
-        far = passages_ref.at[part, pl.ds(width, width)]
+        far = passages_ref.at[part, pl.ds(width, rest)]
         near = passages_ref.at[part, pl.ds(0, width)]
         copies_in.append(pltpu.make_async_copy(far, held.at[part], sems_in.at[k]))
         copies_near.append(pltpu.make_async_copy(near, near_ref.at[part], sems_in.at[chunks + k]))
@@ -197,8 +198,10 @@
     pick = jnp.where(inside == lane, 1.0, 0.0).astype(bf16)
     size = jnp.zeros((pairs, 128), f32)
     along = [jnp.zeros((8, 128), f32)] * queries
+    close, chunk = near_ref.shape[1] // 2, held.shape[2]
+    ends = [0, close, 2 * close, 2 * close + chunk, width]
     for k in range(chunks):
-        part = slice(k * chunk, (k + 1) * chunk)
+        part = slice(ends[k], ends[k + 1])
         if k < half:
             passages = near_ref[:, part]
         else:
@@ -207,10 +210,10 @@
         raw = dot(pick, passages, nn_dims)
         raw_ref[:, part] = raw.astype(bf16)
         lifted = raw * gain_ref[:, part]
-        for j in range(chunk // 128):
+        for j in range((ends[k + 1] - ends[k]) // 128):
             tile = slice(j * 128, (j + 1) * 128)
             size = size + lifted[:, tile] * lifted[:, tile]
-            eighth, place = divmod(k * chunk // 128 + j, tiles)
+            eighth, place = divmod(ends[k] // 128 + j, tiles)
             for i in range(queries):
                 row = wide[place, i * 8 + eighth : i * 8 + eighth + 1, :]
                 along[i] = along[i] + lifted[i * 8 : i * 8 + 8, tile] * row
@@ -330,12 +333,12 @@
         in_specs=[outside(), whole()],
         out_specs=[whole(), outside(), whole()],
         out_shape=[
-            shape((rows, width // 2), bf16),
-            shape((20 * rows, width // 4), bf16),
+            shape((rows, 9 * width // 16), bf16),
+            shape((24 * rows, 7 * width // 32), bf16),
             shape((1, width)),
         ],
         scratch_shapes=[
-            pltpu.VMEM((rows, width // 2), bf16),
+            pltpu.VMEM((rows, 7 * width // 16), bf16),
             pltpu.SemaphoreType.DMA((2 * chunks,)),
             pltpu.SemaphoreType.DMA((2 * chunks,)),
         ],
@@ -358,7 +361,7 @@
             shape((pairs, half), bf16),
         ],
         scratch_shapes=[
-            pltpu.VMEM((chunks // 2, rows, width // chunks), bf16),
+            pltpu.VMEM((chunks // 2, rows, 7 * width // 32), bf16),
             pltpu.VMEM((width // 1024, pairs + 8, 128), f32),
             pltpu.SemaphoreType.DMA((chunks // 2,)),
         ],

time: 39.1 us -> 40.9 us (1.046)
  local copies, waits for them, and re-layouts: 0.72 us -> 3.24 us
  waiting for transfers between devices: 5.74 us -> 4.72 us
    unnamed x6 -> x12, local copies, waits for them, and re-layouts: 0.72 us -> 3.24 us
    all_to_all x3, waiting for transfers between devices: 5.72 us -> 4.71 us  [exchange(): lax.all_to_all(x, 'hash', split_axis=0, concat_axis=0, axis_index_groups=...]
  transfers between devices with their start and end apart: 5 -> 5, of which waited for: 3 -> 3; matrix products, arithmetic and copies ran while one was open for 0% -> 0% of each run, Pallas kernels for 23% -> 22%
where the time goes in v25:
time: 40.9 us; the launch traced here: 40.3 us
  starting transfers between devices  16.4 us (40%)
  Pallas kernels  15.2 us (37%)
  waiting for transfers between devices  4.72 us (12%)
  local copies, waits for them, and re-layouts  3.24 us (8%)
  between operations  0.72 us (2%)
    all_to_all x3, starting transfers between devices, exchange(): lax.all_to_all(x, 'hash', split_axis=0, concat_axis=0, axis_index_groups=...  16.2 us
    all_to_all x3, waiting for transfers between devices, exchange(): lax.all_to_all(x, 'hash', split_axis=0, concat_axis=0, axis_index_groups=...  4.71 us
    pallas_call x1, Pallas kernels, local(): pl.pallas_call(passage_kernel, in_specs=[whole()] * 6, out_specs=outside(...  4.06 us
    unnamed x12, local copies, waits for them, and re-layouts  3.24 us
    pallas_call x1, Pallas kernels, local(): pl.pallas_call(score_kernel, in_specs=[pl.BlockSpec(memory_space=pltpu.SM...  2.89 us
    pallas_call x1, Pallas kernels, local(): pl.pallas_call(stage_kernel, in_specs=[outside(), whole()], out_specs=[wh...  2.88 us
    pallas_call x2, Pallas kernels, mixed(): pl.pallas_call(kernel, in_specs=[pl.BlockSpec(memory_space=pltpu.SMEM)] +...  1.92 us
    pallas_call x1, Pallas kernels, local(): pl.pallas_call(functools.partial(pack_kernel, rows), out_shape=shape((cou...  1.72 us
  transfers between devices with their start and end apart: 5, of which 3 were waited for; matrix products, arithmetic and copies ran while one was open for 0% of the time, Pallas kernels for 22%

profile of v25, /device:TPU:0, one launch (start us, length us, event | category | flops | bytes accessed | tf_op | source)
XLA Modules:
  0.0 40.3 jit_solution(1431903005664294867)
XLA Ops:
  0.6 1.7 %pack.1 = bf16[16,8,640]{2,1,0:T(8,128)(2,1)} custom-call(bf16[1,4096]{1,0:T(2,128)(2,1)} %queries_ref.3, s32[1,128]{1,0:T(1,128)} %candidates_ref.1, s32[1,128]{1,0:T(1,128)} %teacher_ref.1), custom_call_target="tpu_custom_call" | custom-call | tf_op jit(solution)/shard_map/pack/pallas_call | solution.py:322
  2.4 7.5 %all-to-all-start = ((bf16[16,8,640]{2,1,0:T(8,128)(2,1)}), bf16[16,8,640]{2,1,0:T(8,128)(2,1)S(1)}, u32[]{:S(2)}, u32[]{:S(2)}) async-start(bf16[16,8,640]{2,1,0:T(8,128)(2,1)} %pack.1), calls=%async_computation | async-start | bytes 327680 | tf_op jit(solution)/shard_map/all_to_all | solution.py:311
  9.9 0.0 copy-start.3
  9.9 0.7 %copy-done.3 = f32[4096]{0:T(1024)S(1)} copy-done((f32[4096]{0:T(1024)S(1)}, f32[4096]{0:T(1024)}, u32[]{:S(2)}) %copy-start.3) | copy-done | bytes 16408
  10.6 2.9 %stage.1 = (bf16[512,2304]{1,0:T(8,128)(2,1)S(1)}, bf16[12288,896]{1,0:T(8,128)(2,1)}, f32[1,4096]{1,0:T(1,128)S(1)}) custom-call(bf16[512,4096]{1,0:T(8,128)(2,1)} %passages_ref.1, f32[1,4096]{1,0:T(1,128)S(1)} %bitcast.7), custom_call_target="tpu_custom_call" | custom-call | bytes 8388608 | tf_op jit(solution)/shard_map/stage/pallas_call | solution.py:331
  13.5 2.3 %all-to-all-done = bf16[16,8,640]{2,1,0:T(8,128)(2,1)S(1)} async-done(((bf16[16,8,640]{2,1,0:T(8,128)(2,1)}), bf16[16,8,640]{2,1,0:T(8,128)(2,1)S(1)}, u32[]{:S(2)}, u32[]{:S(2)}) %all-to-all-start) | async-done | bytes 163872 | tf_op jit(solution)/shard_map/all_to_all | solution.py:311
  15.8 0.0 copy-start
  15.8 0.7 %copy-done = bf16[16,8,640]{2,1,0:T(8,128)(2,1)} copy-done((bf16[16,8,640]{2,1,0:T(8,128)(2,1)}, bf16[16,8,640]{2,1,0:T(8,128)(2,1)S(1)}, u32[]{:S(2)}) %copy-start) | copy-done | bytes 163864
  16.5 0.0 copy-start.1
  16.5 0.9 %copy-done.1 = bf16[16,8,640]{2,1,0:T(8,128)(2,1)S(1)} copy-done((bf16[16,8,640]{2,1,0:T(8,128)(2,1)S(1)}, bf16[16,8,640]{2,1,0:T(8,128)(2,1)}, u32[]{:S(2)}) %copy-start.1) | copy-done | bytes 163864
  17.4 0.0 copy-start.5
  17.4 2.9 %score.1 = (bf16[128,4096]{1,0:T(8,128)(2,1)S(1)}, f32[128,128]{1,0:T(8,128)S(1)}, f32[8,128]{1,0:T(8,128)S(1)}, f32[16,1,128]{2,1,0:T(1,128)}, bf16[128,2048]{1,0:T(8,128)(2,1)}) custom-call(s32[1]{0:T(128)} %bitcast.core_ref, bf16[128,640]{1,0:T(8,128)(2,1)S(1)} %bitcast.5, f32[1,4096]{1,0:T(1,128)S(1)} %get-tuple-element.17.gain_ref, ...), custom_call_target="tpu_custom_call" | custom-call | tf_op jit(solution)/shard_map/score/pallas_call | solution.py:353
  20.3 0.0 copy-start.4
  20.3 0.1 collective-permute-start
  20.4 4.5 %all-to-all-start.1 = ((f32[16,1,128]{2,1,0:T(1,128)}), f32[16,1,128]{2,1,0:T(1,128)S(1)}, u32[]{:S(2)}, u32[]{:S(2)}) async-start(f32[16,1,128]{2,1,0:T(1,128)} %get-tuple-element.20), calls=%async_computation.1 | async-start | bytes 16384 | tf_op jit(solution)/shard_map/all_to_all | solution.py:311
  24.9 0.2 collective-permute-start.1
  25.1 0.0 copy-start.2
  25.1 0.9 %copy-done.2 = bf16[16,8,640]{2,1,0:T(8,128)(2,1)S(1)} copy-done((bf16[16,8,640]{2,1,0:T(8,128)(2,1)S(1)}, bf16[16,8,640]{2,1,0:T(8,128)(2,1)}, u32[]{:S(2)}) %copy-start.2) | copy-done | bytes 163864
  26.0 1.0 %mix.2 = (f32[56,2048]{1,0:T(8,128)S(1)}, bf16[16,4096]{1,0:T(8,128)(2,1)S(1)}) custom-call(s32[1]{0:T(128)} %bitcast.core_ref, bf16[128,640]{1,0:T(8,128)(2,1)S(1)} %bitcast.6, f32[1,4096]{1,0:T(1,128)S(1)} %get-tuple-element.17.gain_ref, bf16[128,4096]{1,0:T(8,128)(2,1)S(1)} %get-tuple-element.21.raw_ref, f32[8,128]{1,0:T(8,128)S(1)} %get-tuple-element.22.rows_ref), custom_call_target="tpu_custom_call" | custom-call | flops 67108864 | bytes 2097152 | tf_op jit(solution)/shard_map/mix/pallas_call | solution.py:378
  27.0 0.0 collective-permute-done.1.rows_ref
  27.0 0.0 collective-permute-done.raw_ref
  27.0 0.9 %mix.3.both_ref = f32[56,2048]{1,0:T(8,128)S(1)} custom-call(s32[1]{0:T(128)} %bitcast.core_ref, bf16[16,4096]{1,0:T(8,128)(2,1)S(1)} %get-tuple-element.23.query_ref, f32[1,4096]{1,0:T(1,128)S(1)} %get-tuple-element.17.gain_ref, bf16[128,2048]{1,0:T(8,128)(2,1)S(1)} %collective-permute-done.raw_ref, f32[8,128]{1,0:T(8,128)S(1)} %collective-permute-done.1.rows_ref, ...), custom_call_target="tpu_custom_call" | custom-call | flops 67108864 | bytes 2097152 | tf_op jit(solution)/shard_map/mix/pallas_call | solution.py:378
  27.9 1.1 %all-to-all-done.1.sums_ref = f32[16,1,128]{2,1,0:T(1,128)S(1)} async-done(((f32[16,1,128]{2,1,0:T(1,128)}), f32[16,1,128]{2,1,0:T(1,128)S(1)}, u32[]{:S(2)}, u32[]{:S(2)}) %all-to-all-start.1) | async-done | bytes 8224 | tf_op jit(solution)/shard_map/all_to_all | solution.py:311
  29.0 0.9 %partial.1 = (bf16[128,512]{1,0:T(8,128)(2,1)}, f32[1,128]{1,0:T(1,128)S(1)}) custom-call(f32[16,1,128]{2,1,0:T(1,128)S(1)} %all-to-all-done.1.sums_ref, f32[56,2048]{1,0:T(8,128)S(1)} %mix.3.both_ref), custom_call_target="tpu_custom_call" | custom-call | tf_op jit(solution)/shard_map/partial/pallas_call | solution.py:397
  29.8 4.1 %all-to-all-start.2 = ((bf16[16,8,512]{2,1,0:T(8,128)(2,1)}), bf16[16,8,512]{2,1,0:T(8,128)(2,1)S(1)}, u32[]{:S(2)}, u32[]{:S(2)}) async-start(bf16[16,8,512]{2,1,0:T(8,128)(2,1)} %bitcast.3), calls=%async_computation.2 | async-start | bytes 262144 | tf_op jit(solution)/shard_map/all_to_all | solution.py:311
  34.0 4.1 %d_passages.1 = f32[512,4096]{1,0:T(8,128)} custom-call(f32[1,128]{1,0:T(1,128)S(1)} %get-tuple-element.26.total_ref, bf16[16,4096]{1,0:T(8,128)(2,1)S(1)} %get-tuple-element.23.query_ref, f32[1,4096]{1,0:T(1,128)S(1)} %get-tuple-element.17.gain_ref, bf16[128,4096]{1,0:T(8,128)(2,1)S(1)} %get-tuple-element.21.raw_ref, ...), custom_call_target="tpu_custom_call" | custom-call | flops 1073741824 | bytes 8388608 | tf_op jit(solution)/shard_map/d_passages/pallas_call | solution.py:406
  38.0 1.4 %all-to-all-done.2.got_ref = bf16[16,8,512]{2,1,0:T(8,128)(2,1)S(1)} async-done(((bf16[16,8,512]{2,1,0:T(8,128)(2,1)}), bf16[16,8,512]{2,1,0:T(8,128)(2,1)S(1)}, u32[]{:S(2)}, u32[]{:S(2)}) %all-to-all-start.2) | async-done | bytes 131104 | tf_op jit(solution)/shard_map/all_to_all | solution.py:311
  39.4 0.0 copy-done.5
  39.4 0.0 copy-done.4
  39.4 0.9 %final.1 = (f32[1,4096]{1,0:T(1,128)}, f32[1,4096]{1,0:T(1,128)}) custom-call(bf16[16,8,512]{2,1,0:T(8,128)(2,1)S(1)} %all-to-all-done.2.got_ref, bf16[1,4096]{1,0:T(2,128)(2,1)S(1)} %copy-done.5, f32[1,4096]{1,0:T(1,128)S(1)} %bitcast.8), custom_call_target="tpu_custom_call" | custom-call | tf_op jit(solution)/shard_map/final/pallas_call | solution.py:419
Async XLA Ops:
  2.4 13.4 %all-to-all-start = ((bf16[16,8,640]{2,1,0:T(8,128)(2,1)}), bf16[16,8,640]{2,1,0:T(8,128)(2,1)S(1)}, u32[]{:S(2)}, u32[]{:S(2)}) async-start(bf16[16,8,640]{2,1,0:T(8,128)(2,1)} %pack.1), calls=%async_computation | async-start | bytes 327680 | tf_op jit(solution)/shard_map/all_to_all | solution.py:311
  9.9 0.7 %copy-start.3 = (f32[4096]{0:T(1024)S(1)}, f32[4096]{0:T(1024)}, u32[]{:S(2)}) copy-start(f32[4096]{0:T(1024)} %param.7) | copy-start | bytes 49156
  15.8 0.7 %copy-start = (bf16[16,8,640]{2,1,0:T(8,128)(2,1)}, bf16[16,8,640]{2,1,0:T(8,128)(2,1)S(1)}, u32[]{:S(2)}) copy-start(bf16[16,8,640]{2,1,0:T(8,128)(2,1)S(1)} %all-to-all-done) | copy-start | bytes 491524
  16.5 0.9 %copy-start.1 = (bf16[16,8,640]{2,1,0:T(8,128)(2,1)S(1)}, bf16[16,8,640]{2,1,0:T(8,128)(2,1)}, u32[]{:S(2)}) copy-start(bf16[16,8,640]{2,1,0:T(8,128)(2,1)} %copy-done) | copy-start | bytes 491524
  17.4 22.1 %copy-start.5 = (bf16[1,4096]{1,0:T(2,128)(2,1)S(1)}, bf16[1,4096]{1,0:T(2,128)(2,1)}, u32[]{:S(2)}) copy-start(bf16[1,4096]{1,0:T(2,128)(2,1)} %queries_ref.3) | copy-start | bytes 24580
  20.3 19.2 %copy-start.4 = (f32[4096]{0:T(1024)S(1)}, f32[4096]{0:T(1024)}, u32[]{:S(2)}) copy-start(f32[4096]{0:T(1024)} %param.7) | copy-start | bytes 49156
  20.3 6.7 %collective-permute-start = (bf16[128,2048]{1,0:T(8,128)(2,1)}, bf16[128,2048]{1,0:T(8,128)(2,1)S(1)}, u32[]{:S(2)}, u32[]{:S(2)}) collective-permute-start(bf16[128,2048]{1,0:T(8,128)(2,1)} %get-tuple-element.24), channel_id=1, source_target_pairs={{0,1},{1,0},{2,3},{3,2},{4,5},{5,4},{6,7},{7,6},{8,9},{9,8},{10,11... | collective-permute-start | bytes 1572872 | tf_op jit(solution)/shard_map/ppermute | solution.py:374
  20.4 8.6 %all-to-all-start.1 = ((f32[16,1,128]{2,1,0:T(1,128)}), f32[16,1,128]{2,1,0:T(1,128)S(1)}, u32[]{:S(2)}, u32[]{:S(2)}) async-start(f32[16,1,128]{2,1,0:T(1,128)} %get-tuple-element.20), calls=%async_computation.1 | async-start | bytes 16384 | tf_op jit(solution)/shard_map/all_to_all | solution.py:311
  24.9 2.1 %collective-permute-start.1 = (f32[8,128]{1,0:T(8,128)S(1)}, f32[8,128]{1,0:T(8,128)S(1)}, u32[]{:S(2)}, u32[]{:S(2)}) collective-permute-start(f32[8,128]{1,0:T(8,128)S(1)} %get-tuple-element.22.rows_ref), channel_id=1, source_target_pairs={{0,1},{1,0},{2,3},{3,2},{4,5},{5,4},{6,7},{7,6},{8,9},{9,8},{10,11... | collective-permute-start | bytes 12296 | tf_op jit(solution)/shard_map/ppermute | solution.py:375
  25.1 0.9 %copy-start.2 = (bf16[16,8,640]{2,1,0:T(8,128)(2,1)S(1)}, bf16[16,8,640]{2,1,0:T(8,128)(2,1)}, u32[]{:S(2)}) copy-start(bf16[16,8,640]{2,1,0:T(8,128)(2,1)} %copy-done) | copy-start | bytes 491524
  29.8 9.6 %all-to-all-start.2 = ((bf16[16,8,512]{2,1,0:T(8,128)(2,1)}), bf16[16,8,512]{2,1,0:T(8,128)(2,1)S(1)}, u32[]{:S(2)}, u32[]{:S(2)}) async-start(bf16[16,8,512]{2,1,0:T(8,128)(2,1)} %bitcast.3), calls=%async_computation.2 | async-start | bytes 262144 | tf_op jit(solution)/shard_map/all_to_all | solution.py:311
